TPU v7x, 32 devices: a whole 2x2x4 slice. The times are simulated.
32 devices in a mesh: ctx: 8 (over y, x, core), tp: 4 (over z).
Axes of the slice: x: 2, y: 2, z: 4, core: 2. Of those that a mesh axis runs over, the one named last changes fastest.
Arguments:
- x_in: bfloat16 [4096, 8192], P('ctx', 'tp'), may hold values from -6 to 6
- gate_z: bfloat16 [4096, 8192], P('ctx', 'tp'), may hold values from -6 to 6
- b_in: bfloat16 [4096, 1024], P('ctx', 'tp'), may hold values from -1.5 to 1.5
- c_in: bfloat16 [4096, 1024], P('ctx', 'tp'), may hold values from -1.5 to 1.5
- step_size: float32 [4096, 128], P('ctx', 'tp'), may hold values from 0 to 2
- log_decay: float32 [4096, 128], P('ctx', 'tp'), may hold values from -1 to 0
- skip: float32 [128], P('tp'), may hold values from 0.5 to 2
- norm_gain: float32 [8192], P('tp'), may hold values from 0.1 to 1.9
- out_weight: bfloat16 [8192, 4096], P('tp'), may hold values from -0.0625 to 0.0625
Outputs:
- layer_out: bfloat16 [4096, 4096], P(('ctx', 'tp'))
All inputs are finite; a program needn't handle non-finite values.
Results may differ from a plain program's by a relative error of at most 0.023.
Values may be sent and summed in bfloat16 or wider, within the bound.
No kernel may reach another device: no remote copies, remote signals or barrier semaphores. Data moves between devices by JAX's collectives and lax.ppermute only.
A program may use at most 128 MiB of HBM per device.

v0:
```python
from functools import partial

import jax
import jax.numpy as jnp
from jax import lax
from jax.sharding import PartitionSpec as P

HEAD_DIM = 64
STATE = 128
SPAN = 256


def from_behind(block, axis, distance):
    devices = range(lax.axis_size(axis))
    route = [(i - distance, i) for i in devices if i - distance in devices]
    return lax.ppermute(block, axis, route)


def block_pass(states, inputs, per_group):
    scaled, decay_log, b_block, c_block = inputs
    block_len = decay_log.shape[0]
    head_count = decay_log.shape[1]
    group_count = b_block.shape[1]
    running = jnp.cumsum(decay_log, axis=0)
    scores = jnp.einsum("tgn,sgn->gts", c_block, b_block, preferred_element_type=jnp.float32)
    scores = jnp.repeat(scores, per_group, axis=0)
    run_heads = running.T
    spread = run_heads[:, :, None] - run_heads[:, None, :]
    causal = lax.broadcasted_iota(jnp.int32, (block_len, block_len), 0) >= lax.broadcasted_iota(
        jnp.int32, (block_len, block_len), 1
    )
    decays = jnp.where(causal[None], jnp.exp(jnp.where(causal[None], spread, 0.0)), 0.0)
    weights = scores * decays
    within = jnp.einsum("hts,shp->thp", weights, scaled, precision=lax.Precision.HIGHEST)
    c_wide = c_block.astype(jnp.float32)
    grouped = states.reshape(group_count, per_group, states.shape[1], states.shape[2])
    carried = jnp.einsum("tgn,gkpn->tgkp", c_wide, grouped, precision=lax.Precision.HIGHEST)
    carried = carried.reshape(block_len, head_count, states.shape[1]) * jnp.exp(running)[:, :, None]
    tail_decay = jnp.exp(running[-1][None, :] - running)
    weighted = (scaled * tail_decay[:, :, None]).reshape(
        block_len, group_count, per_group, states.shape[1]
    )
    fresh_in = jnp.einsum(
        "sgn,sgkp->gkpn", b_block.astype(jnp.float32), weighted, precision=lax.Precision.HIGHEST
    )
    new_states = states * jnp.exp(running[-1])[:, None, None] + fresh_in.reshape(states.shape)
    return (new_states, within + carried)


def on_device(x_in, gate_z, b_in, c_in, step_size, log_decay, skip, norm_gain, out_weight):
    rows_here = x_in.shape[0]
    head_count = step_size.shape[1]
    group_count = b_in.shape[1] // STATE
    per_group = head_count // group_count
    blocks = rows_here // SPAN
    inputs = x_in.astype(jnp.float32).reshape(rows_here, head_count, HEAD_DIM)
    scaled = inputs * step_size[:, :, None]
    b_groups = b_in.reshape(rows_here, group_count, STATE)
    c_groups = c_in.reshape(rows_here, group_count, STATE)
    start_state = jnp.zeros((head_count, HEAD_DIM, STATE), jnp.float32)
    end_state, local_out = lax.scan(
        partial(block_pass, per_group=per_group),
        start_state,
        (
            scaled.reshape(blocks, SPAN, head_count, HEAD_DIM),
            log_decay.reshape(blocks, SPAN, head_count),
            b_groups.reshape(blocks, SPAN, group_count, STATE),
            c_groups.reshape(blocks, SPAN, group_count, STATE),
        ),
    )
    local_out = local_out.reshape(rows_here, head_count, HEAD_DIM)
    running = jnp.cumsum(log_decay, axis=0)
    total = running[-1]

    def relay(turn_index, incoming):
        outgoing = incoming * jnp.exp(total)[:, None, None] + end_state
        return from_behind(outgoing.astype(jnp.bfloat16), "ctx", 1).astype(outgoing.dtype)

    incoming = lax.fori_loop(0, lax.axis_size("ctx") - 1, relay, start_state)
    grouped = incoming.reshape(group_count, per_group, HEAD_DIM, STATE)
    carried = jnp.einsum(
        "tgn,gkpn->tgkp", c_groups.astype(jnp.float32), grouped, precision=lax.Precision.HIGHEST
    )
    carried = carried.reshape(rows_here, head_count, HEAD_DIM) * jnp.exp(running)[:, :, None]
    mixed = (local_out + carried + skip[None, :, None] * inputs).reshape(
        rows_here, head_count * HEAD_DIM
    )
    mixed = mixed * jax.nn.silu(gate_z.astype(jnp.float32))
    by_group = mixed.reshape(rows_here, group_count, -1)
    meansq = jnp.mean(by_group * by_group, axis=2, keepdims=True)
    normed = (
        (by_group * lax.rsqrt(meansq + 1e-05)).reshape(rows_here, -1) * norm_gain[None, :]
    ).astype(jnp.bfloat16)
    return lax.psum_scatter(
        jnp.dot(normed, out_weight, preferred_element_type=jnp.float32).astype(jnp.bfloat16),
        "tp",
        scatter_dimension=0,
        tiled=True,
    )


def solution(mesh):
    placed = (
        P("ctx", "tp"),
        P("ctx", "tp"),
        P("ctx", "tp"),
        P("ctx", "tp"),
        P("ctx", "tp"),
        P("ctx", "tp"),
        P("tp"),
        P("tp"),
        P("tp", None),
    )
    return jax.shard_map(
        on_device, mesh=mesh, in_specs=placed, out_specs=P(("ctx", "tp"), None), check_vma=False
    )
```

profile of v0, /device:TPU:0, one launch (start us, length us, event | category | flops | bytes accessed | tf_op | source)
XLA Modules:
  0.0 359.8 jit_solution(15015075584027880502)
XLA Ops:
  14.1 2.9 copy.32
  17.0 4.0 %reshape.129 = f32[2,256,32,64]{1,0,3,2:T(2,128)} reshape(bf16[512,2048]{0,1:T(8,128)(2,1)S(1)} %copy.32) | data formatting | bytes 6291456 | tf_op jit(solution)/shard_map/reshape | solution.py:56
  22.6 6.9 %broadcast_multiply_fusion = f32[2,256,32,64]{1,0,3,2:T(2,128)} fusion(f32[2,256,32,64]{1,0,3,2:T(2,128)} %reshape.129, f32[2,256,32]{1,0,2:T(2,128)S(1)} %mul.113), kind=kLoop, calls=%fused_computation.53 | loop fusion | flops 1048576 | bytes 8454144 | tf_op jit(solution)/shard_map/mul | solution.py:57
  29.5 133.7 %while.26 = (s32[]{:T(128)}, f32[32,64,128]{2,1,0:T(8,128)S(1)}, f32[2,256,32,64]{1,0,3,2:T(2,128)}, f32[2,256,32]{1,0,2:T(2,128)S(1)}, f32[2,256,32,64]{1,0,3,2...) while((s32[]{:T(128)}, f32[32,64,128]{2,1,0:T(8,128)S(1)}, ...), condition=%wide.region_3.4_spmd.clone, body=%wide.region_0.3_spmd.clone.sunk | while | flops 3266658304 | bytes 53054468 | solution.py:61
  31.9 4.4 %constant_dynamic-slice_fusion.7 = f32[1,256,32,64]{1,0,3,2:T(1,128)S(1)} fusion(f32[2,256,32,64]{1,0,3,2:T(2,128)} %get-tuple-element.289, s32[]{:T(128)} %get-tuple-element.275), kind=kLoop, calls=%fused_computation.34.clone.1 | loop fusion | bytes 4194308 | tf_op jit(solution)/shard_map/while/body/jit(dynamic_index_in_dim)/dynamic_slice | solution.py:61
  43.3 8.4 %fusion.68 = f32[1,256,32,64]{1,3,2,0:T(8,128)S(1)} fusion(f32[2,256,16,64]{1,3,2,0:T(8,128)S(1)} %fusion.66, f32[32,256,256]{2,1,0:T(8,128)S(1)} %bitcast_multiply_fusion.5, f32[256,32]{0,1:T(8,128)S(1)} %get-tuple-element.260, f32[1,256,32,64]{1,0,3,2:T(1,128)S(1)} %constant_dynamic-slice_fusion.7), kind=kOutput, calls=%fused_computation.10.clone.1 | convolution fusion | flops 1611661312 | bytes 14712832 | tf_op jit(solution)/shard_map/while/body/eval_jaxpr/hts,shp->thp/dot_general | solution.py:34
  51.6 2.2 copy.118
  53.8 42.6 %dynamic_update_slice.6 = f32[2,256,32,64]{1,0,3,2:T(2,128)} dynamic-update-slice(f32[2,256,32,64]{1,0,3,2:T(2,128)} %get-tuple-element.277, f32[1,256,32,64]{1,0,3,2:T(1,128)S(1)} %copy.118, s32[]{:T(128)} %get-tuple-element.275, s32[]{:T(128)} %constant.40.clone.1..sunk, s32[]{:T(128)} %constant.40.clone.1..sunk, s32[]{:T(128)} %constant.40.clone.1..sunk) | dynamic-update-slice | bytes 4194308 | tf_op jit(solution)/shard_map/while/body/jit(dynamic_update_index_in_dim)/dynamic_update_slice | solution.py:61
  98.7 4.4 %constant_dynamic-slice_fusion.7 = f32[1,256,32,64]{1,0,3,2:T(1,128)S(1)} fusion(f32[2,256,32,64]{1,0,3,2:T(2,128)} %get-tuple-element.289, s32[]{:T(128)} %get-tuple-element.275), kind=kLoop, calls=%fused_computation.34.clone.1 | loop fusion | bytes 4194308 | tf_op jit(solution)/shard_map/while/body/jit(dynamic_index_in_dim)/dynamic_slice | solution.py:61
  110.1 8.4 %fusion.68 = f32[1,256,32,64]{1,3,2,0:T(8,128)S(1)} fusion(f32[2,256,16,64]{1,3,2,0:T(8,128)S(1)} %fusion.66, f32[32,256,256]{2,1,0:T(8,128)S(1)} %bitcast_multiply_fusion.5, f32[256,32]{0,1:T(8,128)S(1)} %get-tuple-element.260, f32[1,256,32,64]{1,0,3,2:T(1,128)S(1)} %constant_dynamic-slice_fusion.7), kind=kOutput, calls=%fused_computation.10.clone.1 | convolution fusion | flops 1611661312 | bytes 14712832 | tf_op jit(solution)/shard_map/while/body/eval_jaxpr/hts,shp->thp/dot_general | solution.py:34
  120.7 42.6 %dynamic_update_slice.6 = f32[2,256,32,64]{1,0,3,2:T(2,128)} dynamic-update-slice(f32[2,256,32,64]{1,0,3,2:T(2,128)} %get-tuple-element.277, f32[1,256,32,64]{1,0,3,2:T(1,128)S(1)} %copy.118, s32[]{:T(128)} %get-tuple-element.275, s32[]{:T(128)} %constant.40.clone.1..sunk, s32[]{:T(128)} %constant.40.clone.1..sunk, s32[]{:T(128)} %constant.40.clone.1..sunk) | dynamic-update-slice | bytes 4194308 | tf_op jit(solution)/shard_map/while/body/jit(dynamic_update_index_in_dim)/dynamic_update_slice | solution.py:61
  163.2 4.6 %copy.60 = f32[256,8,2,256]{3,1,2,0:T(8,128)} copy(f32[256,8,2,256]{3,2,1,0:T(2,128)} %bitcast.178) | data formatting | bytes 8388608
  167.8 4.0 %copy.41 = bf16[512,2048]{0,1:T(8,128)(2,1)} copy(bf16[512,2048]{1,0:T(8,128)(2,1)} %param.14) | data formatting | bytes 4194304 | tf_op args[1]
  172.0 69.3 %while.27 = (s32[]{:T(128)}, f32[32,64,128]{2,1,0:T(8,128)S(1)}, f32[32,1,1]{0,2,1:T(1,128)S(1)}, f32[32,64,128]{2,1,0:T(8,128)S(1)}, s32[]{:T(128)}, /*index=5*/s32[]{:T(128)}) while((s32[]{:T(128)}, f32[32,64,128]{2,1,0:T(8,128)S(1)}, f32[32,1,1]{0,2,1:T(1,128)S(1)}, f32[32,64,128]{2,1,0:T(8,128)S(1)}, s32[]{:T(128)}, ...), condition=%wide.region_7.8_spmd.clone, body=%wide.region_6.7_spmd.clone.sunk | while | flops 1310723 | bytes 6291703 | solution.py:79
  172.2 2.4 collective-permute-start
  176.4 9.1 %collective-permute-start = (bf16[32,64,128]{2,1,0:T(8,128)(2,1)S(1)}, bf16[32,64,128]{2,1,0:T(8,128)(2,1)S(1)}, u32[]{:S(2)}, u32[]{:S(2)}) collective-permute-start(bf16[32,64,128]{2,1,0:T(8,128)(2,1)S(1)} %fusion.69), channel_id=1, source_target_pairs={{0,4},{4,8},{8,12},{12,16},{16,20},{20,24},{24,28},{1,5},{5,9},{9,... | collective-permute-start | bytes 1572872 | tf_op jit(solution)/shard_map/while/body/eval_jaxpr/ppermute | solution.py:16
  187.3 9.0 %collective-permute-start = (bf16[32,64,128]{2,1,0:T(8,128)(2,1)S(1)}, bf16[32,64,128]{2,1,0:T(8,128)(2,1)S(1)}, u32[]{:S(2)}, u32[]{:S(2)}) collective-permute-start(bf16[32,64,128]{2,1,0:T(8,128)(2,1)S(1)} %fusion.69), channel_id=1, source_target_pairs={{0,4},{4,8},{8,12},{12,16},{16,20},{20,24},{24,28},{1,5},{5,9},{9,... | collective-permute-start | bytes 1572872 | tf_op jit(solution)/shard_map/while/body/eval_jaxpr/ppermute | solution.py:16
  198.2 9.0 %collective-permute-start = (bf16[32,64,128]{2,1,0:T(8,128)(2,1)S(1)}, bf16[32,64,128]{2,1,0:T(8,128)(2,1)S(1)}, u32[]{:S(2)}, u32[]{:S(2)}) collective-permute-start(bf16[32,64,128]{2,1,0:T(8,128)(2,1)S(1)} %fusion.69), channel_id=1, source_target_pairs={{0,4},{4,8},{8,12},{12,16},{16,20},{20,24},{24,28},{1,5},{5,9},{9,... | collective-permute-start | bytes 1572872 | tf_op jit(solution)/shard_map/while/body/eval_jaxpr/ppermute | solution.py:16
  209.0 9.0 %collective-permute-start = (bf16[32,64,128]{2,1,0:T(8,128)(2,1)S(1)}, bf16[32,64,128]{2,1,0:T(8,128)(2,1)S(1)}, u32[]{:S(2)}, u32[]{:S(2)}) collective-permute-start(bf16[32,64,128]{2,1,0:T(8,128)(2,1)S(1)} %fusion.69), channel_id=1, source_target_pairs={{0,4},{4,8},{8,12},{12,16},{16,20},{20,24},{24,28},{1,5},{5,9},{9,... | collective-permute-start | bytes 1572872 | tf_op jit(solution)/shard_map/while/body/eval_jaxpr/ppermute | solution.py:16
  219.8 9.0 %collective-permute-start = (bf16[32,64,128]{2,1,0:T(8,128)(2,1)S(1)}, bf16[32,64,128]{2,1,0:T(8,128)(2,1)S(1)}, u32[]{:S(2)}, u32[]{:S(2)}) collective-permute-start(bf16[32,64,128]{2,1,0:T(8,128)(2,1)S(1)} %fusion.69), channel_id=1, source_target_pairs={{0,4},{4,8},{8,12},{12,16},{16,20},{20,24},{24,28},{1,5},{5,9},{9,... | collective-permute-start | bytes 1572872 | tf_op jit(solution)/shard_map/while/body/eval_jaxpr/ppermute | solution.py:16
  230.7 9.0 %collective-permute-start = (bf16[32,64,128]{2,1,0:T(8,128)(2,1)S(1)}, bf16[32,64,128]{2,1,0:T(8,128)(2,1)S(1)}, u32[]{:S(2)}, u32[]{:S(2)}) collective-permute-start(bf16[32,64,128]{2,1,0:T(8,128)(2,1)S(1)} %fusion.69), channel_id=1, source_target_pairs={{0,4},{4,8},{8,12},{12,16},{16,20},{20,24},{24,28},{1,5},{5,9},{9,... | collective-permute-start | bytes 1572872 | tf_op jit(solution)/shard_map/while/body/eval_jaxpr/ppermute | solution.py:16
  243.5 3.6 %bitcast_reduce_fusion = (f32[512,2]{0,1:T(2,128)S(1)}, f32[512,2048]{0,1:T(8,128)S(1)}) fusion(bf16[512,2048]{0,1:T(8,128)(2,1)S(1)} %copy-done.3, bf16[512,2048]{0,1:T(8,128)(2,1)S(1)} %copy-done.2, f32[2048]{0:T(1024)S(1)} %mul.120, f32[512,2048]{0,1:T(8,128)} %bitcast.177, f32[512,32]{0,1:T(8,128)S(1)} %copy-done.5, f32[2,16,64,512]{3,2,1,0:T(8,128)S(1)} %fusion.33), kind=kLoop, calls=%fused_computation.52 | loop fusion | flops 13630464 | bytes 16855040 | tf_op jit(solution)/shard_map/reduce_sum | solution.py:90
  247.6 13.9 %convolution_convert_fusion = bf16[512,4096]{1,0:T(8,128)(2,1)} fusion(bf16[512,2048]{0,1:T(8,128)(2,1)S(1)} %fusion.32, bf16[2048,4096]{1,0:T(8,128)(2,1)} %param.21), kind=kOutput, calls=%fused_computation.39 | convolution fusion | flops 8592031744 | bytes 23068672 | tf_op jit(solution)/shard_map/dot_general | solution.py:95
  261.5 91.5 %reduce-scatter.2.cloned.1.call-done = bf16[128,4096]{1,0:T(8,128)(2,1)} async-done(((bf16[512,4096]{1,0:T(8,128)(2,1)}), bf16[128,4096]{1,0:T(8,128)(2,1)}) %reduce-scatter.2.cloned.1.call-update) | async-done | bytes 1048592 | tf_op jit(solution)/shard_map/reduce_scatter | solution.py:94
  (99 shorter events, 45.2 us)
Async XLA Ops:
  6.5 346.4 %reduce-scatter.2.cloned.1.call-start = ((), (), s32[]{:S(2)}) async-start(), calls=%async_computation.1 | async-start | bytes 5242880 | tf_op jit(solution)/shard_map/reduce_scatter | solution.py:94
  16.9 12.6 %copy-start.1 = (bf16[512,2048]{0,1:T(8,128)(2,1)}, bf16[512,2048]{0,1:T(8,128)(2,1)S(1)}, u32[]{:S(2)}) copy-start(bf16[512,2048]{0,1:T(8,128)(2,1)S(1)} %copy.32) | copy-start | bytes 6291460
  16.9 4.9 %copy-start.6 = (bf16[512,256]{1,0:T(8,128)(2,1)S(1)}, bf16[512,256]{1,0:T(8,128)(2,1)}, u32[]{:S(2)}) copy-start(bf16[512,256]{1,0:T(8,128)(2,1)} %param.15) | copy-start | bytes 786436
  167.8 4.0 %copy-start.8 = (f32[32]{0:T(128)S(1)}, f32[32]{0:T(128)}, u32[]{:S(2)}) copy-start(f32[32]{0:T(128)} %param.19) | copy-start | bytes 388
  167.8 4.2 %copy-start = (f32[32,64,128]{2,1,0:T(8,128)S(1)}, f32[32,64,128]{2,1,0:T(8,128)}, u32[]{:S(2)}) copy-start(f32[32,64,128]{2,1,0:T(8,128)} %custom-call.1) | copy-start | bytes 3145732
  172.0 69.3 %copy-start.4 = (bf16[512,2,128]{2,1,0:T(2,128)(2,1)S(1)}, bf16[512,2,128]{2,1,0:T(2,128)(2,1)}, u32[]{:S(2)}) copy-start(bf16[512,2,128]{2,1,0:T(2,128)(2,1)} %reshape.134) | copy-start | bytes 786436
  172.2 3.9 %collective-permute-start = (bf16[32,64,128]{2,1,0:T(8,128)(2,1)S(1)}, bf16[32,64,128]{2,1,0:T(8,128)(2,1)S(1)}, u32[]{:S(2)}, u32[]{:S(2)}) collective-permute-start(bf16[32,64,128]{2,1,0:T(8,128)(2,1)S(1)} %fusion.69), channel_id=1, source_target_pairs={{0,4},{4,8},{8,12},{12,16},{16,20},{20,24},{24,28},{1,5},{5,9},{9,... | collective-permute-start | bytes 1572872 | tf_op jit(solution)/shard_map/while/body/eval_jaxpr/ppermute | solution.py:16
  176.4 10.6 %collective-permute-start = (bf16[32,64,128]{2,1,0:T(8,128)(2,1)S(1)}, bf16[32,64,128]{2,1,0:T(8,128)(2,1)S(1)}, u32[]{:S(2)}, u32[]{:S(2)}) collective-permute-start(bf16[32,64,128]{2,1,0:T(8,128)(2,1)S(1)} %fusion.69), channel_id=1, source_target_pairs={{0,4},{4,8},{8,12},{12,16},{16,20},{20,24},{24,28},{1,5},{5,9},{9,... | collective-permute-start | bytes 1572872 | tf_op jit(solution)/shard_map/while/body/eval_jaxpr/ppermute | solution.py:16
  187.3 10.5 %collective-permute-start = (bf16[32,64,128]{2,1,0:T(8,128)(2,1)S(1)}, bf16[32,64,128]{2,1,0:T(8,128)(2,1)S(1)}, u32[]{:S(2)}, u32[]{:S(2)}) collective-permute-start(bf16[32,64,128]{2,1,0:T(8,128)(2,1)S(1)} %fusion.69), channel_id=1, source_target_pairs={{0,4},{4,8},{8,12},{12,16},{16,20},{20,24},{24,28},{1,5},{5,9},{9,... | collective-permute-start | bytes 1572872 | tf_op jit(solution)/shard_map/while/body/eval_jaxpr/ppermute | solution.py:16
  198.2 10.5 %collective-permute-start = (bf16[32,64,128]{2,1,0:T(8,128)(2,1)S(1)}, bf16[32,64,128]{2,1,0:T(8,128)(2,1)S(1)}, u32[]{:S(2)}, u32[]{:S(2)}) collective-permute-start(bf16[32,64,128]{2,1,0:T(8,128)(2,1)S(1)} %fusion.69), channel_id=1, source_target_pairs={{0,4},{4,8},{8,12},{12,16},{16,20},{20,24},{24,28},{1,5},{5,9},{9,... | collective-permute-start | bytes 1572872 | tf_op jit(solution)/shard_map/while/body/eval_jaxpr/ppermute | solution.py:16
  209.0 10.5 %collective-permute-start = (bf16[32,64,128]{2,1,0:T(8,128)(2,1)S(1)}, bf16[32,64,128]{2,1,0:T(8,128)(2,1)S(1)}, u32[]{:S(2)}, u32[]{:S(2)}) collective-permute-start(bf16[32,64,128]{2,1,0:T(8,128)(2,1)S(1)} %fusion.69), channel_id=1, source_target_pairs={{0,4},{4,8},{8,12},{12,16},{16,20},{20,24},{24,28},{1,5},{5,9},{9,... | collective-permute-start | bytes 1572872 | tf_op jit(solution)/shard_map/while/body/eval_jaxpr/ppermute | solution.py:16
  219.8 10.5 %collective-permute-start = (bf16[32,64,128]{2,1,0:T(8,128)(2,1)S(1)}, bf16[32,64,128]{2,1,0:T(8,128)(2,1)S(1)}, u32[]{:S(2)}, u32[]{:S(2)}) collective-permute-start(bf16[32,64,128]{2,1,0:T(8,128)(2,1)S(1)} %fusion.69), channel_id=1, source_target_pairs={{0,4},{4,8},{8,12},{12,16},{16,20},{20,24},{24,28},{1,5},{5,9},{9,... | collective-permute-start | bytes 1572872 | tf_op jit(solution)/shard_map/while/body/eval_jaxpr/ppermute | solution.py:16
  230.7 10.5 %collective-permute-start = (bf16[32,64,128]{2,1,0:T(8,128)(2,1)S(1)}, bf16[32,64,128]{2,1,0:T(8,128)(2,1)S(1)}, u32[]{:S(2)}, u32[]{:S(2)}) collective-permute-start(bf16[32,64,128]{2,1,0:T(8,128)(2,1)S(1)} %fusion.69), channel_id=1, source_target_pairs={{0,4},{4,8},{8,12},{12,16},{16,20},{20,24},{24,28},{1,5},{5,9},{9,... | collective-permute-start | bytes 1572872 | tf_op jit(solution)/shard_map/while/body/eval_jaxpr/ppermute | solution.py:16
  241.3 1.8 copy-start.2
  241.3 2.2 copy-start.3
  241.3 2.2 copy-start.5
  243.5 3.6 %copy-start.7 = (f32[2048]{0:T(1024)S(1)}, f32[2048]{0:T(1024)}, u32[]{:S(2)}) copy-start(f32[2048]{0:T(1024)} %param.20) | copy-start | bytes 24580
Sparse Core Ops, SparseCore 0:
  261.6 91.3 reduce-scatter.1
where the time goes:
time: 367 us; the launch traced here: 360 us
  local copies, waits for them, and re-layouts  125 us (34%)
  waiting for transfers between devices  102 us (28%)
  starting transfers between devices  56.5 us (15%)
  matrix products  39.1 us (11%)
  other arithmetic  23.4 us (6%)
  between operations  13.5 us (4%)
    reduce_scatter x1, waiting for transfers between devices, on_device(): lax.psum_scatter(jnp.dot(normed, out_weight, preferred_element_type=jnp.f...  91.5 us
    dynamic_update_slice x4, local copies, waits for them, and re-layouts, on_device(): lax.scan(partial(block_pass, per_group=per_group), start_state, (scaled.r...  89.4 us
    ppermute x7, starting transfers between devices, from_behind(): return lax.ppermute(block, axis, route)  56.5 us
    dot_general x2, matrix products, block_pass(): jnp.einsum('hts,shp->thp', weights, scaled, precision=lax.Precision.HIGHEST)  16.7 us
    dot_general x1, matrix products, on_device(): jnp.dot(normed, out_weight, preferred_element_type=jnp.float32)  13.9 us
    unnamed x21, local copies, waits for them, and re-layouts  11.8 us
    dynamic_slice x8, local copies, waits for them, and re-layouts, on_device(): lax.scan(partial(block_pass, per_group=per_group), start_state, (scaled.r...  11.6 us
    ppermute x7, waiting for transfers between devices, from_behind(): return lax.ppermute(block, axis, route)  10.4 us
  transfers between devices with their start and end apart: 8, of which 8 were waited for; matrix products, arithmetic and copies ran while one was open for 0% of the time, Pallas kernels for 0%

commit v1 on v0

v1 whole, which is shorter than its diff:
```python
from functools import partial

import jax
import jax.numpy as jnp
from jax import lax
from jax.experimental import pallas as pl
from jax.experimental.pallas import tpu as pltpu
from jax.sharding import PartitionSpec as P

HEAD_DIM = 64
STATE = 128
CHUNK = 128
MIDDLE = CHUNK // 2 - 1
EXTRA = 16
COLUMN_TILE = 512
HALVES = 2
VMEM = 56 * 2**20
F32 = jnp.float32
BF16 = jnp.bfloat16


def params():
    return pltpu.CompilerParams(vmem_limit_bytes=VMEM)


def dot(a, b):
    return jnp.dot(a, b, preferred_element_type=F32)


def dot_exact(a, b):
    return jnp.dot(a, b, preferred_element_type=F32, precision=lax.Precision.HIGHEST)


def head_map(heads, channels):
    head = lax.broadcasted_iota(jnp.int32, (2 * heads, channels), 0) & (heads - 1)
    place = lax.broadcasted_iota(jnp.int32, (2 * heads, channels), 1) >> 6
    return jnp.where(head == place, 1.0, 0.0).astype(BF16)


def high_low(values, heads):
    high = values.astype(BF16).astype(F32)
    lane = lax.broadcasted_iota(jnp.int32, values.shape, 1)
    return jnp.where(lane < heads, high, values - high).astype(BF16)


def twice(values):
    return jnp.concatenate([values, values], axis=1)


def pieces(values, rows):
    first = values.astype(BF16).astype(F32)
    second = (values - first).astype(BF16).astype(F32)
    third = values - first - second
    row = lax.broadcasted_iota(jnp.int32, (rows, values.shape[1]), 0)
    stacked = jnp.where(row == 0, first, jnp.where(row == 1, second, jnp.where(row == 2, third, 0.0)))
    return stacked.astype(BF16)


def state_kernel(groups, core_ref, x_ref, b_ref, step_ref, decay_ref, rhs_ref, inner_ref, outer_ref, send_ref, keep_ref,
                 state, sums, spread):
    chunk = pl.program_id(0)
    heads, channels = step_ref.shape[1], x_ref.shape[1]
    width = channels // groups

    @pl.when(chunk == 0)
    def _():
        state[...] = jnp.zeros_like(state)
        sums[...] = jnp.zeros_like(sums)
        spread[...] = head_map(heads, channels)

    row = lax.broadcasted_iota(jnp.int32, (CHUNK, CHUNK), 0)
    column = lax.broadcasted_iota(jnp.int32, (CHUNK, CHUNK), 1)
    lower = jnp.where(row >= column, 1.0, 0.0)
    running = dot_exact(lower, twice(decay_ref[...]))
    middle, total = running[MIDDLE : MIDDLE + 1], running[CHUNK - 1 : CHUNK]
    before = sums[0:1]
    inner = running - middle
    inner_ref[...] = high_low(jnp.exp(inner), heads)
    outer_ref[...] = high_low(jnp.exp(before + running), heads)
    weight = twice(step_ref[...]) * jnp.exp(-inner)
    factor_row = lax.broadcasted_iota(jnp.int32, (EXTRA, 2 * heads), 0)
    factors = jnp.exp(jnp.where(factor_row == 0, total, jnp.where(factor_row == 1, total - middle, middle)))
    wide = dot(jnp.concatenate([high_low(weight, heads), high_low(factors, heads)], axis=0), spread[...])
    weighted = (x_ref[...].astype(F32) * wide[:CHUNK]).astype(BF16)
    old = state[...]
    rhs_ref[:CHUNK, :] = weighted
    rhs_ref[CHUNK:, :] = (old * wide[CHUNK + 2 : CHUNK + 3]).astype(BF16)
    for g in range(groups):
        cut = slice(g * width, (g + 1) * width)
        fresh = lax.dot_general(
            b_ref[:, g * STATE : (g + 1) * STATE],
            weighted[:, cut],
            (((0,), (0,)), ((), ())),
            preferred_element_type=F32,
        )
        state[:, cut] = old[:, cut] * wide[CHUNK : CHUNK + 1, cut] + fresh * wide[CHUNK + 1 : CHUNK + 2, cut]
    sums[0:1] = before + total

    @pl.when(chunk == pl.num_programs(0) - 1)
    def _():
        end = state[...].astype(BF16)
        logs = dot(pieces(sums[0:1, :heads], EXTRA), spread[:heads, :]).astype(BF16)
        half = channels // 2
        for core in range(2):

            @pl.when(core_ref[0] == core)
            def _():
                own = slice(core * half, (core + 1) * half)
                other = slice((1 - core) * half, (2 - core) * half)
                keep_ref[:STATE, :] = end[:, own]
                keep_ref[STATE:, :] = logs[:, own]
                send_ref[:STATE, :] = end[:, other]
                send_ref[STATE:, :] = logs[:, other]


def log_of(ref):
    return jnp.sum(ref[STATE:, :].astype(F32), axis=0, keepdims=True)


def pair_kernel(core_ref, own_ref, sibling_ref, pair_ref):
    own_log, sibling_log = log_of(own_ref), log_of(sibling_ref)
    early = core_ref[0] == 0
    own_scale = jnp.where(early, jnp.exp(sibling_log), 1.0)
    sibling_scale = jnp.where(early, 1.0, jnp.exp(own_log))
    pair = own_ref[:STATE, :].astype(F32) * own_scale + sibling_ref[:STATE, :].astype(F32) * sibling_scale
    pair_ref[:STATE, :] = pair.astype(BF16)
    pair_ref[STATE:, :] = pieces(own_log + sibling_log, EXTRA)


def join_kernel(late_ref, early_ref, out_ref):
    late_log, early_log = log_of(late_ref), log_of(early_ref)
    out_ref[:STATE, :] = (
        late_ref[:STATE, :].astype(F32) + early_ref[:STATE, :].astype(F32) * jnp.exp(late_log)
    ).astype(BF16)
    out_ref[STATE:, :] = pieces(late_log + early_log, EXTRA)


def last_kernel(core_ref, near_ref, far_ref, own_ref, sibling_ref, keep_ref, send_ref):
    near = near_ref[:STATE, :].astype(F32)
    chip = near + far_ref[:STATE, :].astype(F32) * jnp.exp(log_of(near_ref))
    for core, first, mine, other in ((0, own_ref, 0, 1), (1, sibling_ref, 1, 0)):

        @pl.when(core_ref[0] == core)
        def _():
            after = chip * jnp.exp(log_of(first)) + first[:STATE, :].astype(F32)
            both = (chip.astype(BF16), after.astype(BF16))
            keep_ref[...] = both[mine]
            send_ref[...] = both[other]


def local_kernel(groups, x_ref, gate_ref, b_ref, c_ref, rhs_ref, inner_ref, outer_ref, skip_ref, mixed_ref, scale_ref,
                 spread):
    heads, channels = skip_ref.shape[1], x_ref.shape[1]
    width = channels // groups

    @pl.when(pl.program_id(0) == 0)
    def _():
        spread[...] = head_map(heads, channels)

    row = lax.broadcasted_iota(jnp.int32, (CHUNK, CHUNK), 0)
    column = lax.broadcasted_iota(jnp.int32, (CHUNK, CHUNK), 1)
    skip = high_low(jnp.broadcast_to(twice(skip_ref[...]), (EXTRA, 2 * heads)), heads)
    for g in range(groups):
        cut = slice(g * width, (g + 1) * width)
        part = slice(g * STATE, (g + 1) * STATE)
        to_wide = spread[:, cut]
        scores = lax.dot_general(
            c_ref[:, part], b_ref[:, part], (((1,), (1,)), ((), ())), preferred_element_type=F32
        )
        scores = jnp.where(row >= column, scores, 0.0).astype(BF16)
        within = dot(jnp.concatenate([scores, c_ref[:, part]], axis=1), rhs_ref[:, cut])
        gate = gate_ref[:, cut].astype(F32)
        gate = gate / (1.0 + jnp.exp(-gate))
        passed = x_ref[:, cut].astype(F32) * dot(skip, to_wide)[0:1]
        mixed_ref[:, cut] = (within * dot(inner_ref[...], to_wide) + passed) * gate
        scale_ref[:, cut] = dot(outer_ref[...], to_wide) * gate


def norm_rows(groups, state, mixed, scale, c_rows, gain):
    width = mixed.shape[1] // groups
    parts = []
    for g in range(groups):
        cut = slice(g * width, (g + 1) * width)
        carried = dot(c_rows[:, g * STATE : (g + 1) * STATE], state[:, cut])
        whole = mixed[:, cut] + scale[:, cut] * carried
        meansq = jnp.mean(whole * whole, axis=1, keepdims=True)
        parts.append((whole * lax.rsqrt(meansq + 1e-05) * gain[:, cut]).astype(BF16))
    return parts


def fill_state(core_ref, keep_ref, recv_ref, state):
    half = keep_ref.shape[1]
    for core in range(2):

        @pl.when(core_ref[0] == core)
        def _():
            state[:, core * half : (core + 1) * half] = keep_ref[...]
            state[:, (1 - core) * half : (2 - core) * half] = recv_ref[...]


def first_kernel(groups, place_ref, mixed_ref, scale_ref, c_ref, keep_ref, recv_ref, gain_ref, w_ref, out_ref, normed_ref,
                 state, normed):
    @pl.when(pl.program_id(0) == 0)
    def _():
        fill_state(place_ref, keep_ref, recv_ref, state)
        width = normed.shape[1] // groups
        rows = norm_rows(groups, state, mixed_ref, scale_ref, c_ref, gain_ref)
        for g, part in enumerate(rows):
            normed[:, g * width : (g + 1) * width] = part
        normed_ref[...] = normed[...]

    out_ref[...] = dot(normed[...], w_ref[...]).astype(BF16)


def second_kernel(normed_ref, w_ref, out_ref):
    out_ref[...] = dot(normed_ref[...], w_ref[...]).astype(BF16)


def rest_kernel(groups, blocks, place_ref, mixed_ref, scale_ref, c_ref, keep_ref, recv_ref, gain_ref, w_ref, a_ref, b_ref,
                out_ref, state, normed):
    step = pl.program_id(0)
    size = a_ref.shape[0]

    @pl.when(step == 0)
    def _():
        fill_state(place_ref, keep_ref, recv_ref, state)
        width = normed.shape[1] // groups
        for n in range(1, blocks):
            here = pl.ds(pl.multiple_of(place_ref[1 + n] * size, size), size)
            rows = norm_rows(groups, state, mixed_ref.at[here, :], scale_ref.at[here, :], c_ref.at[here, :], gain_ref)
            for g, part in enumerate(rows):
                normed[(n - 1) * size : n * size, g * width : (g + 1) * width] = part

    product = dot(normed[...], w_ref[...]).astype(BF16)
    for n in range(1, blocks):
        here = pl.ds(pl.multiple_of(place_ref[1 + n] * size, size), size)
        out_ref[here, :] = product[(n - 1) * size : n * size]
    here = pl.ds(pl.multiple_of(place_ref[1] * size, size), size)
    in_first = step < pl.num_programs(0) // 2

    @pl.when(in_first)
    def _():
        out_ref[here, :] = a_ref[...]

    @pl.when(jnp.logical_not(in_first))
    def _():
        out_ref[here, :] = b_ref[...]


def whole_block(shape):
    return pl.BlockSpec(shape, lambda *_: (0,) * len(shape))


def shape_of(shape, kind=BF16):
    return jax.ShapeDtypeStruct(shape, kind)


def block_order(here, count):
    table = []
    for i in range(count):
        order = []
        for step in range(1, count):
            for block, sends in ((count - step + i, i <= step - 1), (step - count + i, i >= count - step)):
                if sends and block not in order:
                    order.append(block)
        table.append(order + [b for b in range(count) if b not in order])
    return jnp.asarray(table, jnp.int32)[here]


def line_reduce(first, partial_sums, size, columns):
    count = lax.axis_size("tp")
    here = lax.axis_index("tp")
    done = []
    for half in range(HALVES):
        cut = columns // HALVES

        def own(block, half=half, cut=cut):
            block = jnp.clip(block, 0, count - 1)
            return lax.dynamic_slice(partial_sums, (block * size, half * cut), (size, cut))

        right = left = None
        for step in range(1, count):
            to_right = [(i, i + 1) for i in range(step)]
            to_left = [(i, i - 1) for i in range(count - step, count)]
            if step == 1 and count > 3:
                both = lax.ppermute(first[half], "tp", to_right + to_left)
                right = jnp.where(here == 1, both, jnp.zeros_like(both))
                left = jnp.where(here == count - 2, both, jnp.zeros_like(both))
                continue
            if step == 1:
                send_right = send_left = first[half]
            else:
                send_right = (own(count - step + here).astype(F32) + right.astype(F32)).astype(BF16)
                send_left = (own(step - count + here).astype(F32) + left.astype(F32)).astype(BF16)
            right = lax.ppermute(send_right, "tp", to_right)
            left = lax.ppermute(send_left, "tp", to_left)
        done.append((own(here).astype(F32) + right.astype(F32) + left.astype(F32)).astype(BF16))
    return jnp.concatenate(done, axis=1)


def on_device(x_in, gate_z, b_in, c_in, step_size, log_decay, skip, norm_gain, out_weight):
    rows, channels = x_in.shape
    heads = step_size.shape[1]
    groups = b_in.shape[1] // STATE
    chunks = rows // CHUNK
    columns = out_weight.shape[1]
    half = channels // 2
    devices = lax.axis_size("ctx")
    chips = devices // 2
    core = lax.rem(lax.axis_index("ctx"), 2).astype(jnp.int32).reshape(1)
    message = (STATE + EXTRA, half)

    by_chunk = lambda width: pl.BlockSpec((CHUNK, width), lambda i, *_: (i, 0))
    rhs, inner, outer, send, own = pl.pallas_call(
        partial(state_kernel, groups),
        grid_spec=pltpu.PrefetchScalarGridSpec(
            num_scalar_prefetch=1,
            grid=(chunks,),
            in_specs=[by_chunk(channels), by_chunk(groups * STATE), by_chunk(heads), by_chunk(heads)],
            out_specs=[
                pl.BlockSpec((CHUNK + STATE, channels), lambda i, *_: (i, 0)),
                by_chunk(2 * heads),
                by_chunk(2 * heads),
                whole_block(message),
                whole_block(message),
            ],
            scratch_shapes=[
                pltpu.VMEM((STATE, channels), F32),
                pltpu.VMEM((8, 2 * heads), F32),
                pltpu.VMEM((2 * heads, channels), BF16),
            ],
        ),
        out_shape=[
            shape_of((chunks * (CHUNK + STATE), channels)),
            shape_of((rows, 2 * heads)),
            shape_of((rows, 2 * heads)),
            shape_of(message),
            shape_of(message),
        ],
        compiler_params=params(),
        name="chunk_states",
    )(core, x_in, b_in, step_size, log_decay)

    swap = [(i, i ^ 1) for i in range(devices)]
    scalar = pl.BlockSpec(memory_space=pltpu.SMEM)
    block = whole_block(message)

    def small(kernel, name, ins, outs):
        return pl.pallas_call(
            kernel,
            in_specs=[scalar if v.dtype == jnp.int32 else whole_block(v.shape) for v in ins],
            out_specs=[whole_block(s) for s in outs],
            out_shape=[shape_of(s) for s in outs],
            compiler_params=params(),
            name=name,
        )(*ins)

    def local_part(first, count, x_in):
        at = lambda width, size=CHUNK: pl.BlockSpec((size, width), lambda i: (first + i, 0))
        to = lambda width: pl.BlockSpec((CHUNK, width), lambda i: (i, 0))
        return pl.pallas_call(
            partial(local_kernel, groups),
            grid=(count,),
            in_specs=[
                at(channels),
                at(channels),
                at(groups * STATE),
                at(groups * STATE),
                at(channels, CHUNK + STATE),
                at(2 * heads),
                at(2 * heads),
                whole_block((1, heads)),
            ],
            out_specs=[to(channels), to(channels)],
            out_shape=[shape_of((count * CHUNK, channels), F32)] * 2,
            scratch_shapes=[pltpu.VMEM((2 * heads, channels), BF16)],
            compiler_params=params(),
            cost_estimate=pl.CostEstimate(flops=count * 2 * 10**9, bytes_accessed=count * 5 * 10**6, transcendentals=0),
            name="local_part",
        )(x_in, gate_z, b_in, c_in, rhs, inner, outer, skip.reshape(1, heads))

    sibling = lax.ppermute(send, "ctx", swap)
    (pair,) = small(pair_kernel, "pair", (core, own, sibling), (message,))
    x_late, pair = lax.optimization_barrier((x_in, pair))
    near, far = None, lax.ppermute(pair, "ctx", [(i, i + 2) for i in range(devices - 2)])
    mixed, scale = local_part(0, chunks, x_late)
    distance = 2
    while distance < chips:
        (near,) = (far,) if near is None else small(join_kernel, "join", (near, far), (message,))
        (outgoing,) = small(join_kernel, "join", (pair, near), (message,))
        far = lax.ppermute(outgoing, "ctx", [(i, i + 2 * distance) for i in range(devices - 2 * distance)])
        distance *= 2
    state_shape = (STATE, half)
    keep, send = small(last_kernel, "incoming", (core, near, far, own, sibling), (state_shape, state_shape))
    recv = lax.ppermute(send, "ctx", swap)

    count = lax.axis_size("tp")
    size = rows // count
    place = jnp.concatenate([core, block_order(lax.axis_index("tp"), count)])
    gain = norm_gain.reshape(1, channels)
    tiles = columns // COLUMN_TILE
    row_block = lambda width: pl.BlockSpec((size, width), lambda j, p: (p[1], 0))
    first_a, normed = pl.pallas_call(
        partial(first_kernel, groups),
        grid_spec=pltpu.PrefetchScalarGridSpec(
            num_scalar_prefetch=1,
            grid=(tiles // 2,),
            in_specs=[
                row_block(channels),
                row_block(channels),
                row_block(groups * STATE),
                whole_block(state_shape),
                whole_block(state_shape),
                whole_block((1, channels)),
                pl.BlockSpec((channels, COLUMN_TILE), lambda j, p: (0, j)),
            ],
            out_specs=[pl.BlockSpec((size, COLUMN_TILE), lambda j, p: (0, j)), whole_block((size, channels))],
            scratch_shapes=[pltpu.VMEM((STATE, channels), BF16), pltpu.VMEM((size, channels), BF16)],
        ),
        out_shape=[shape_of((size, columns // 2)), shape_of((size, channels))],
        compiler_params=params(),
        name="first_block",
    )(place, mixed, scale, c_in, keep, recv, gain, out_weight)
    first_b = pl.pallas_call(
        second_kernel,
        grid=(tiles // 2,),
        in_specs=[
            whole_block((size, channels)),
            pl.BlockSpec((channels, COLUMN_TILE), lambda j: (0, tiles // 2 + j)),
        ],
        out_specs=pl.BlockSpec((size, COLUMN_TILE), lambda j: (0, j)),
        out_shape=shape_of((size, columns // 2)),
        compiler_params=params(),
        cost_estimate=pl.CostEstimate(
            flops=size * channels * columns, bytes_accessed=channels * columns, transcendentals=0
        ),
        name="first_block_rest",
    )(normed, out_weight)
    partial_sums = pl.pallas_call(
        partial(rest_kernel, groups, count),
        grid_spec=pltpu.PrefetchScalarGridSpec(
            num_scalar_prefetch=1,
            grid=(tiles,),
            in_specs=[
                whole_block((rows, channels)),
                whole_block((rows, channels)),
                whole_block((rows, groups * STATE)),
                whole_block(state_shape),
                whole_block(state_shape),
                whole_block((1, channels)),
                pl.BlockSpec((channels, COLUMN_TILE), lambda j, p: (0, j)),
                pl.BlockSpec((size, COLUMN_TILE), lambda j, p: (0, jnp.minimum(j, tiles // 2 - 1))),
                pl.BlockSpec((size, COLUMN_TILE), lambda j, p: (0, jnp.maximum(j - tiles // 2, 0))),
            ],
            out_specs=pl.BlockSpec((rows, COLUMN_TILE), lambda j, p: (0, j)),
            scratch_shapes=[pltpu.VMEM((STATE, channels), BF16), pltpu.VMEM((rows - size, channels), BF16)],
        ),
        out_shape=shape_of((rows, columns)),
        compiler_params=params(),
        cost_estimate=pl.CostEstimate(
            flops=2 * (rows - size) * channels * columns, bytes_accessed=2 * channels * columns, transcendentals=0
        ),
        name="other_blocks",
    )(place, mixed, scale, c_in, keep, recv, gain, out_weight, first_a, first_b)
    return line_reduce((first_a, first_b), partial_sums, size, columns)


def solution(mesh):
    placed = (
        P("ctx", "tp"),
        P("ctx", "tp"),
        P("ctx", "tp"),
        P("ctx", "tp"),
        P("ctx", "tp"),
        P("ctx", "tp"),
        P("tp"),
        P("tp"),
        P("tp", None),
    )
    return jax.shard_map(
        on_device, mesh=mesh, in_specs=placed, out_specs=P(("ctx", "tp"), None), check_vma=False
    )
```

time: 367 us -> 162 us (0.44); the launches traced: 360 us -> 161 us
  local copies, waits for them, and re-layouts: 125 us -> 6.9 us
  Pallas kernels: 0 us -> 53.1 us
  waiting for transfers between devices: 102 us -> 54.7 us
  matrix products: 39.1 us -> 0 us
  starting transfers between devices: 56.5 us -> 36.5 us
  other arithmetic: 23.4 us -> 9.56 us
  between operations: 13.5 us -> 0.17 us
    reduce_scatter x1 -> x0, waiting for transfers between devices: 91.5 us -> none  [on_device(): lax.psum_scatter(jnp.dot(normed, out_weight, preferred_element_type=jnp.f...]
    dynamic_update_slice x4 -> x0, local copies, waits for them, and re-layouts: 89.4 us -> none  [on_device(): lax.scan(partial(block_pass, per_group=per_group), start_state, (scaled.r...]
    pallas_call x0 -> x8, Pallas kernels: none -> 53.1 us  [the longest x1 17.9 us: on_device(): pl.pallas_call(partial(rest_kernel, groups, count), grid_spec=pltpu.Prefe...]
    ppermute x7 -> x14, waiting for transfers between devices: 10.4 us -> 54.7 us  [the longest x4 36.8 us: line_reduce(): right = lax.ppermute(send_right, 'tp', to_right)]
    dot_general x10 -> x0, matrix products: 39.1 us -> none  [the longest x2 16.7 us: block_pass(): jnp.einsum('hts,shp->thp', weights, scaled, precision=lax.Precision.HIGHEST)]
    ppermute x7 -> x14, starting transfers between devices: 56.5 us -> 36.5 us  [the longest x4 17.2 us: line_reduce(): right = lax.ppermute(send_right, 'tp', to_right)]
    dynamic_slice x8 -> x0, local copies, waits for them, and re-layouts: 11.6 us -> none  [on_device(): lax.scan(partial(block_pass, per_group=per_group), start_state, (scaled.r...]
    mul x3 -> x0, other arithmetic: 10.8 us -> none  [the longest x1 6.91 us: on_device(): scaled = inputs * step_size[:, :, None]]
  transfers between devices with their start and end apart: 8 -> 14, of which waited for: 8 -> 9; matrix products, arithmetic and copies ran while one was open for 0% -> 2% of each run, Pallas kernels for 0% -> 17%
where the time goes in v1:
time: 162 us; the launch traced here: 161 us
  waiting for transfers between devices  54.7 us (34%)
  Pallas kernels  53.1 us (33%)
  starting transfers between devices  36.5 us (23%)
  other arithmetic  9.56 us (6%)
  local copies, waits for them, and re-layouts  6.9 us (4%)
    ppermute x4, waiting for transfers between devices, line_reduce(): right = lax.ppermute(send_right, 'tp', to_right)  36.8 us
    pallas_call x1, Pallas kernels, on_device(): pl.pallas_call(partial(rest_kernel, groups, count), grid_spec=pltpu.Prefe...  17.9 us
    ppermute x4, starting transfers between devices, line_reduce(): right = lax.ppermute(send_right, 'tp', to_right)  17.2 us
    pallas_call x1, Pallas kernels, local_part(): pl.pallas_call(partial(local_kernel, groups), grid=(count,), in_specs=[at...  9.22 us
    pallas_call x1, Pallas kernels, on_device(): pl.pallas_call(partial(first_kernel, groups), grid_spec=pltpu.PrefetchSca...  7.51 us
    ppermute x1, waiting for transfers between devices, on_device(): lax.ppermute(pair, 'ctx', [(i, i + 2) for i in range(devices - 2)])  6.85 us
    pallas_call x1, Pallas kernels, on_device(): pl.pallas_call(partial(state_kernel, groups), grid_spec=pltpu.PrefetchSca...  6.62 us
    unnamed x12, local copies, waits for them, and re-layouts  6.21 us
  transfers between devices with their start and end apart: 14, of which 9 were waited for; matrix products, arithmetic and copies ran while one was open for 2% of the time, Pallas kernels for 17%

profile of v1, /device:TPU:0, one launch (start us, length us, event | category | flops | bytes accessed | tf_op | source)
XLA Modules:
  0.0 161.0 jit_solution(13121479342837479141)
XLA Ops:
  0.0 1.7 %copy.11.step_ref = f32[512,32]{1,0:T(8,128)} copy(f32[512,32]{0,1:T(8,128)} %param.14) | data formatting | bytes 131072 | tf_op args[4]
  3.3 6.6 %chunk_states.1 = (bf16[1024,2048]{1,0:T(8,128)(2,1)}, bf16[512,64]{1,0:T(8,128)(2,1)}, bf16[512,64]{1,0:T(8,128)(2,1)}, bf16[144,1024]{1,0:T(8,128)(2,1)}, bf16[144,1024]{1,0:T(8,128)(2,1)}) custom-call(s32[1]{0:T(128)} %bitcast.core_ref, bf16[512,2048]{1,0:T(8,128)(2,1)} %x_ref.2, bf16[512,256]{1,0:T(8,128)(2,1)} %b_ref.3, f32[512,32]{1,0:T(8,128)} %copy.11.step_ref, ...), custom_call_target="tpu_custom_call" | custom-call | tf_op jit(solution)/shard_map/chunk_states/pallas_call | solution.py:314
  12.7 1.9 %pair.1.late_ref = bf16[144,1024]{1,0:T(8,128)(2,1)} custom-call(s32[1]{0:T(128)} %bitcast.core_ref, bf16[144,1024]{1,0:T(8,128)(2,1)} %get-tuple-element.18.own_ref, bf16[144,1024]{1,0:T(8,128)(2,1)} %copy-done), custom_call_target="tpu_custom_call" | custom-call | tf_op jit(solution)/shard_map/pair/pallas_call | solution.py:349
  14.6 4.7 %collective-permute-start.1 = (bf16[144,1024]{1,0:T(8,128)(2,1)}, bf16[144,1024]{1,0:T(8,128)(2,1)S(1)}, u32[]{:S(2)}, u32[]{:S(2)}) collective-permute-start(bf16[144,1024]{1,0:T(8,128)(2,1)} %pair.1.late_ref), channel_id=1, source_target_pairs={{0,8},{4,12},{8,16},{12,20},{16,24},{20,28},{1,9},{5,13},{9,17},{1... | collective-permute-start | bytes 884744 | tf_op jit(solution)/shard_map/ppermute | solution.py:385
  19.3 6.8 %collective-permute-done.1.early_ref.near_ref = bf16[144,1024]{1,0:T(8,128)(2,1)S(1)} collective-permute-done((bf16[144,1024]{1,0:T(8,128)(2,1)}, bf16[144,1024]{1,0:T(8,128)(2,1)S(1)}, u32[]{:S(2)}, u32[]{:S(2)}) %collective-permute-start.1) | collective-permute-done | bytes 294944 | tf_op jit(solution)/shard_map/ppermute | solution.py:385
  26.9 1.9 %join.1 = bf16[144,1024]{1,0:T(8,128)(2,1)} custom-call(bf16[144,1024]{1,0:T(8,128)(2,1)} %pair.1.late_ref, bf16[144,1024]{1,0:T(8,128)(2,1)} %copy-done.1), custom_call_target="tpu_custom_call" | custom-call | tf_op jit(solution)/shard_map/join/pallas_call | solution.py:349
  28.8 5.2 %collective-permute-start.2 = (bf16[144,1024]{1,0:T(8,128)(2,1)}, bf16[144,1024]{1,0:T(8,128)(2,1)S(1)}, u32[]{:S(2)}, u32[]{:S(2)}) collective-permute-start(bf16[144,1024]{1,0:T(8,128)(2,1)} %join.1), channel_id=1, source_target_pairs={{0,16},{4,20},{8,24},{12,28},{1,17},{5,21},{9,25},{13,29},{2,18},{... | collective-permute-start | bytes 884744 | tf_op jit(solution)/shard_map/ppermute | solution.py:391
  35.3 4.7 %collective-permute-done.2.far_ref = bf16[144,1024]{1,0:T(8,128)(2,1)S(1)} collective-permute-done((bf16[144,1024]{1,0:T(8,128)(2,1)}, bf16[144,1024]{1,0:T(8,128)(2,1)S(1)}, u32[]{:S(2)}, u32[]{:S(2)}) %collective-permute-start.2) | collective-permute-done | bytes 294944 | tf_op jit(solution)/shard_map/ppermute | solution.py:391
  40.7 2.3 %incoming.1 = (bf16[128,1024]{1,0:T(8,128)(2,1)}, bf16[128,1024]{1,0:T(8,128)(2,1)}) custom-call(s32[1]{0:T(128)} %bitcast.core_ref, bf16[144,1024]{1,0:T(8,128)(2,1)} %copy-done.1, bf16[144,1024]{1,0:T(8,128)(2,1)} %copy-done.4, bf16[144,1024]{1,0:T(8,128)(2,1)} %get-tuple-element.18.own_ref, bf16[144,1024]{1,0:T(8,128)(2,1)} %copy-done), custom_call_target="tpu_custom_call" | custom-call | tf_op jit(solution)/shard_map/incoming/pallas_call | solution.py:349
  43.0 9.2 %local_part.1 = (f32[512,2048]{1,0:T(8,128)}, f32[512,2048]{1,0:T(8,128)}) custom-call(bf16[512,2048]{1,0:T(8,128)(2,1)} %x_ref.2, bf16[512,2048]{1,0:T(8,128)(2,1)} %gate_ref.1, bf16[512,256]{1,0:T(8,128)(2,1)} %b_ref.3, bf16[512,256]{1,0:T(8,128)(2,1)} %c_ref.5, bf16[1024,2048]{1,0:T(8,128)(2,1)} %get-tuple-element.21.rhs_ref, ...), custom_call_target="tpu_custom_call" | custom-call | flops 8000000000 | bytes 20000000 | tf_op jit(solution)/shard_map/local_part/pallas_call | solution.py:361
  53.0 7.5 %first_block.1 = (bf16[128,2048]{1,0:T(8,128)(2,1)}, bf16[128,2048]{1,0:T(8,128)(2,1)}) custom-call(s32[5]{0:T(128)} %pad_add_fusion.place_ref, f32[512,2048]{1,0:T(8,128)} %get-tuple-element.24.mixed_ref, f32[512,2048]{1,0:T(8,128)} %get-tuple-element.25.scale_ref, bf16[512,256]{1,0:T(8,128)(2,1)} %c_ref.5, bf16[128,1024]{1,0:T(8,128)(2,1)} %get-tuple-element.27.keep_ref, ...), custom_call_target="tpu_custom_call" | custom-call | tf_op jit(solution)/shard_map/first_block/pallas_call | solution.py:403
  60.5 5.8 %first_block_rest.1.b_ref = bf16[128,2048]{1,0:T(8,128)(2,1)} custom-call(bf16[128,2048]{1,0:T(8,128)(2,1)} %get-tuple-element.30.normed_ref, bf16[2048,4096]{1,0:T(8,128)(2,1)} %w_ref.5), custom_call_target="tpu_custom_call" | custom-call | flops 1073741824 | bytes 8388608 | tf_op jit(solution)/shard_map/first_block_rest/pallas_call | solution.py:424
  66.3 3.5 %collective-permute-start.4 = (bf16[128,2048]{1,0:T(8,128)(2,1)S(1)}, bf16[128,2048]{1,0:T(8,128)(2,1)S(1)}, u32[]{:S(2)}, u32[]{:S(2)}) collective-permute-start(bf16[128,2048]{1,0:T(8,128)(2,1)S(1)} %copy-done.3), channel_id=1, source_target_pairs={{0,1},{3,2},{4,5},{7,6},{8,9},{11,10},{12,13},{15,14},{16,17},{19,... | collective-permute-start | bytes 1572872 | tf_op jit(solution)/shard_map/ppermute | solution.py:286
  71.2 17.9 %other_blocks.1 = bf16[512,4096]{1,0:T(8,128)(2,1)} custom-call(s32[5]{0:T(128)} %pad_add_fusion.place_ref, f32[512,2048]{1,0:T(8,128)} %get-tuple-element.24.mixed_ref, f32[512,2048]{1,0:T(8,128)} %get-tuple-element.25.scale_ref, bf16[512,256]{1,0:T(8,128)(2,1)} %c_ref.5, bf16[128,1024]{1,0:T(8,128)(2,1)} %get-tuple-element.27.keep_ref, ...), custom_call_target="tpu_custom_call" | custom-call | flops 6442450944 | bytes 16777216 | tf_op jit(solution)/shard_map/other_blocks/pallas_call | solution.py:439
  93.4 10.7 %collective-permute-done.5 = bf16[128,2048]{1,0:T(8,128)(2,1)S(1)} collective-permute-done((bf16[128,2048]{1,0:T(8,128)(2,1)S(1)}, bf16[128,2048]{1,0:T(8,128)(2,1)S(1)}, u32[]{:S(2)}, u32[]{:S(2)}) %collective-permute-start.5) | collective-permute-done | bytes 524320 | tf_op jit(solution)/shard_map/ppermute | solution.py:295
  104.1 3.0 %add_convert_fusion.4 = (bf16[128,2048]{1,0:T(8,128)(2,1)}, bf16[128,2048]{1,0:T(8,128)(2,1)S(1)}, bf16[128,2048]{1,0:T(8,128)(2,1)S(1)}, bf16[128,2048]{1,0:T(8,128)(2,1)S(1)}) fusion(bf16[128,2048]{1,0:T(8,128)(2,1)S(1)} %collective-permute-done.9, bf16[512,4096]{1,0:T(8,128)(2,1)} %other_blocks.1, s32[]{:T(128)S(6)} %select_n.48, pred[]{:T(512)S(6)} %eq.8, ...), kind=kLoop, calls=%fused_computation.5 | loop fusion | flops 4718592 | bytes 5767186 | tf_op jit(solution)/shard_map/convert_element_type | solution.py:293
  107.1 7.1 %collective-permute-start.10 = (bf16[128,2048]{1,0:T(8,128)(2,1)}, bf16[128,2048]{1,0:T(8,128)(2,1)S(1)}, u32[]{:S(2)}, u32[]{:S(2)}) collective-permute-start(bf16[128,2048]{1,0:T(8,128)(2,1)} %get-tuple-element.33), channel_id=1, source_target_pairs={{0,1},{1,2},{4,5},{5,6},{8,9},{9,10},{12,13},{13,14},{16,17},{17,1... | collective-permute-start | bytes 1572872 | tf_op jit(solution)/shard_map/ppermute | solution.py:295
  114.9 2.5 %collective-permute-start.6 = (bf16[128,2048]{1,0:T(8,128)(2,1)S(1)}, bf16[128,2048]{1,0:T(8,128)(2,1)S(1)}, u32[]{:S(2)}, u32[]{:S(2)}) collective-permute-start(bf16[128,2048]{1,0:T(8,128)(2,1)S(1)} %get-tuple-element.38), channel_id=1, source_target_pairs={{0,1},{1,2},{2,3},{4,5},{5,6},{6,7},{8,9},{9,10},{10,11},{12,13},{... | collective-permute-start | bytes 1572872 | tf_op jit(solution)/shard_map/ppermute | solution.py:295
  118.8 8.1 %collective-permute-done.10 = bf16[128,2048]{1,0:T(8,128)(2,1)S(1)} collective-permute-done((bf16[128,2048]{1,0:T(8,128)(2,1)}, bf16[128,2048]{1,0:T(8,128)(2,1)S(1)}, u32[]{:S(2)}, u32[]{:S(2)}) %collective-permute-start.10) | collective-permute-done | bytes 524320 | tf_op jit(solution)/shard_map/ppermute | solution.py:295
  126.9 9.5 %collective-permute-done.6 = bf16[128,2048]{1,0:T(8,128)(2,1)S(1)} collective-permute-done((bf16[128,2048]{1,0:T(8,128)(2,1)S(1)}, bf16[128,2048]{1,0:T(8,128)(2,1)S(1)}, u32[]{:S(2)}, u32[]{:S(2)}) %collective-permute-start.6) | collective-permute-done | bytes 524320 | tf_op jit(solution)/shard_map/ppermute | solution.py:295
  136.4 2.1 %add_convert_fusion.5 = (bf16[128,2048]{1,0:T(8,128)(2,1)S(1)}, bf16[128,2048]{1,0:T(8,128)(2,1)S(1)}, bf16[128,2048]{1,0:T(8,128)(2,1)S(1)}) fusion(bf16[128,2048]{1,0:T(8,128)(2,1)} %collective-permute-done.8, bf16[128,2048]{1,0:T(8,128)(2,1)S(1)} %collective-permute-done.6, bf16[512,4096]{1,0:T(8,128)(2,1)} %other_blocks.1, s32[]{:T(128)S(6)} %select_n.46, ...), kind=kLoop, calls=%fused_computation.6 | loop fusion | flops 3670016 | bytes 5242892 | tf_op jit(solution)/shard_map/convert_element_type | solution.py:297
  138.5 6.2 %collective-permute-start.11 = (bf16[128,2048]{1,0:T(8,128)(2,1)S(1)}, bf16[128,2048]{1,0:T(8,128)(2,1)S(1)}, u32[]{:S(2)}, u32[]{:S(2)}) collective-permute-start(bf16[128,2048]{1,0:T(8,128)(2,1)S(1)} %get-tuple-element.37), channel_id=1, source_target_pairs={{0,1},{1,2},{2,3},{4,5},{5,6},{6,7},{8,9},{9,10},{10,11},{12,13},{... | collective-permute-start | bytes 1572872 | tf_op jit(solution)/shard_map/ppermute | solution.py:295
  146.0 8.5 %collective-permute-done.11 = bf16[128,2048]{1,0:T(8,128)(2,1)S(1)} collective-permute-done((bf16[128,2048]{1,0:T(8,128)(2,1)S(1)}, bf16[128,2048]{1,0:T(8,128)(2,1)S(1)}, u32[]{:S(2)}, u32[]{:S(2)}) %collective-permute-start.11) | collective-permute-done | bytes 524320 | tf_op jit(solution)/shard_map/ppermute | solution.py:295
  154.5 4.1 %collective-permute-done.13 = bf16[128,2048]{1,0:T(8,128)(2,1)S(1)} collective-permute-done((bf16[128,2048]{1,0:T(8,128)(2,1)S(1)}, bf16[128,2048]{1,0:T(8,128)(2,1)S(1)}, u32[]{:S(2)}, u32[]{:S(2)}) %collective-permute-start.13) | collective-permute-done | bytes 524320 | tf_op jit(solution)/shard_map/ppermute | solution.py:296
  (31 shorter events, 19.0 us)
Async XLA Ops:
  10.0 2.0 %collective-permute-start = (bf16[144,1024]{1,0:T(8,128)(2,1)}, bf16[144,1024]{1,0:T(8,128)(2,1)S(1)}, u32[]{:S(2)}, u32[]{:S(2)}) collective-permute-start(bf16[144,1024]{1,0:T(8,128)(2,1)} %get-tuple-element.19), channel_id=1, source_target_pairs={{0,4},{4,0},{8,12},{12,8},{16,20},{20,16},{24,28},{28,24},{1,5},{5... | collective-permute-start | bytes 884744 | tf_op jit(solution)/shard_map/ppermute | solution.py:382
  11.9 0.7 copy-start
  14.6 11.6 %collective-permute-start.1 = (bf16[144,1024]{1,0:T(8,128)(2,1)}, bf16[144,1024]{1,0:T(8,128)(2,1)S(1)}, u32[]{:S(2)}, u32[]{:S(2)}) collective-permute-start(bf16[144,1024]{1,0:T(8,128)(2,1)} %pair.1.late_ref), channel_id=1, source_target_pairs={{0,8},{4,12},{8,16},{12,20},{16,24},{20,28},{1,9},{5,13},{9,17},{1... | collective-permute-start | bytes 884744 | tf_op jit(solution)/shard_map/ppermute | solution.py:385
  26.2 0.7 copy-start.1
  28.8 11.2 %collective-permute-start.2 = (bf16[144,1024]{1,0:T(8,128)(2,1)}, bf16[144,1024]{1,0:T(8,128)(2,1)S(1)}, u32[]{:S(2)}, u32[]{:S(2)}) collective-permute-start(bf16[144,1024]{1,0:T(8,128)(2,1)} %join.1), channel_id=1, source_target_pairs={{0,16},{4,20},{8,24},{12,28},{1,17},{5,21},{9,25},{13,29},{2,18},{... | collective-permute-start | bytes 884744 | tf_op jit(solution)/shard_map/ppermute | solution.py:391
  40.0 0.7 copy-start.4
  43.0 9.2 %collective-permute-start.3 = (bf16[128,1024]{1,0:T(8,128)(2,1)}, bf16[128,1024]{1,0:T(8,128)(2,1)S(1)}, u32[]{:S(2)}, u32[]{:S(2)}) collective-permute-start(bf16[128,1024]{1,0:T(8,128)(2,1)} %get-tuple-element.28), channel_id=1, source_target_pairs={{0,4},{4,0},{8,12},{12,8},{16,20},{20,16},{24,28},{28,24},{1,5},{5... | collective-permute-start | bytes 786440 | tf_op jit(solution)/shard_map/ppermute | solution.py:395
  52.3 0.7 copy-start.2
  60.5 5.8 %copy-start.3 = (bf16[128,2048]{1,0:T(8,128)(2,1)S(1)}, bf16[128,2048]{1,0:T(8,128)(2,1)}, u32[]{:S(2)}) copy-start(bf16[128,2048]{1,0:T(8,128)(2,1)} %get-tuple-element.29.a_ref) | copy-start | bytes 1572868
  66.3 22.7 %collective-permute-start.4 = (bf16[128,2048]{1,0:T(8,128)(2,1)S(1)}, bf16[128,2048]{1,0:T(8,128)(2,1)S(1)}, u32[]{:S(2)}, u32[]{:S(2)}) collective-permute-start(bf16[128,2048]{1,0:T(8,128)(2,1)S(1)} %copy-done.3), channel_id=1, source_target_pairs={{0,1},{3,2},{4,5},{7,6},{8,9},{11,10},{12,13},{15,14},{16,17},{19,... | collective-permute-start | bytes 1572872 | tf_op jit(solution)/shard_map/ppermute | solution.py:286
  69.8 23.5 %collective-permute-start.9 = (bf16[128,2048]{1,0:T(8,128)(2,1)}, bf16[128,2048]{1,0:T(8,128)(2,1)S(1)}, u32[]{:S(2)}, u32[]{:S(2)}) collective-permute-start(bf16[128,2048]{1,0:T(8,128)(2,1)} %first_block_rest.1.b_ref), channel_id=1, source_target_pairs={{0,1},{3,2},{4,5},{7,6},{8,9},{11,10},{12,13},{15,14},{16,17},{19,... | collective-permute-start | bytes 1572872 | tf_op jit(solution)/shard_map/ppermute | solution.py:286
  90.5 13.5 %collective-permute-start.5 = (bf16[128,2048]{1,0:T(8,128)(2,1)S(1)}, bf16[128,2048]{1,0:T(8,128)(2,1)S(1)}, u32[]{:S(2)}, u32[]{:S(2)}) collective-permute-start(bf16[128,2048]{1,0:T(8,128)(2,1)S(1)} %get-tuple-element.31), channel_id=1, source_target_pairs={{0,1},{1,2},{4,5},{5,6},{8,9},{9,10},{12,13},{13,14},{16,17},{17,1... | collective-permute-start | bytes 1572872 | tf_op jit(solution)/shard_map/ppermute | solution.py:295
  91.9 12.2 %collective-permute-start.7 = (bf16[128,2048]{1,0:T(8,128)(2,1)S(1)}, bf16[128,2048]{1,0:T(8,128)(2,1)S(1)}, u32[]{:S(2)}, u32[]{:S(2)}) collective-permute-start(bf16[128,2048]{1,0:T(8,128)(2,1)S(1)} %get-tuple-element.32), channel_id=1, source_target_pairs={{2,1},{3,2},{6,5},{7,6},{10,9},{11,10},{14,13},{15,14},{18,17},{19... | collective-permute-start | bytes 1572872 | tf_op jit(solution)/shard_map/ppermute | solution.py:296
  107.1 19.8 %collective-permute-start.10 = (bf16[128,2048]{1,0:T(8,128)(2,1)}, bf16[128,2048]{1,0:T(8,128)(2,1)S(1)}, u32[]{:S(2)}, u32[]{:S(2)}) collective-permute-start(bf16[128,2048]{1,0:T(8,128)(2,1)} %get-tuple-element.33), channel_id=1, source_target_pairs={{0,1},{1,2},{4,5},{5,6},{8,9},{9,10},{12,13},{13,14},{16,17},{17,1... | collective-permute-start | bytes 1572872 | tf_op jit(solution)/shard_map/ppermute | solution.py:295
  114.2 12.6 %collective-permute-start.12 = (bf16[128,2048]{1,0:T(8,128)(2,1)S(1)}, bf16[128,2048]{1,0:T(8,128)(2,1)S(1)}, u32[]{:S(2)}, u32[]{:S(2)}) collective-permute-start(bf16[128,2048]{1,0:T(8,128)(2,1)S(1)} %get-tuple-element.34), channel_id=1, source_target_pairs={{2,1},{3,2},{6,5},{7,6},{10,9},{11,10},{14,13},{15,14},{18,17},{19... | collective-permute-start | bytes 1572872 | tf_op jit(solution)/shard_map/ppermute | solution.py:296
  114.9 21.4 %collective-permute-start.6 = (bf16[128,2048]{1,0:T(8,128)(2,1)S(1)}, bf16[128,2048]{1,0:T(8,128)(2,1)S(1)}, u32[]{:S(2)}, u32[]{:S(2)}) collective-permute-start(bf16[128,2048]{1,0:T(8,128)(2,1)S(1)} %get-tuple-element.38), channel_id=1, source_target_pairs={{0,1},{1,2},{2,3},{4,5},{5,6},{6,7},{8,9},{9,10},{10,11},{12,13},{... | collective-permute-start | bytes 1572872 | tf_op jit(solution)/shard_map/ppermute | solution.py:295
  117.5 18.9 %collective-permute-start.8 = (bf16[128,2048]{1,0:T(8,128)(2,1)S(1)}, bf16[128,2048]{1,0:T(8,128)(2,1)}, u32[]{:S(2)}, u32[]{:S(2)}) collective-permute-start(bf16[128,2048]{1,0:T(8,128)(2,1)S(1)} %get-tuple-element.39), channel_id=1, source_target_pairs={{1,0},{2,1},{3,2},{5,4},{6,5},{7,6},{9,8},{10,9},{11,10},{13,12},{... | collective-permute-start | bytes 1572872 | tf_op jit(solution)/shard_map/ppermute | solution.py:296
  138.5 16.0 %collective-permute-start.11 = (bf16[128,2048]{1,0:T(8,128)(2,1)S(1)}, bf16[128,2048]{1,0:T(8,128)(2,1)S(1)}, u32[]{:S(2)}, u32[]{:S(2)}) collective-permute-start(bf16[128,2048]{1,0:T(8,128)(2,1)S(1)} %get-tuple-element.37), channel_id=1, source_target_pairs={{0,1},{1,2},{2,3},{4,5},{5,6},{6,7},{8,9},{9,10},{10,11},{12,13},{... | collective-permute-start | bytes 1572872 | tf_op jit(solution)/shard_map/ppermute | solution.py:295
  144.7 13.9 %collective-permute-start.13 = (bf16[128,2048]{1,0:T(8,128)(2,1)S(1)}, bf16[128,2048]{1,0:T(8,128)(2,1)S(1)}, u32[]{:S(2)}, u32[]{:S(2)}) collective-permute-start(bf16[128,2048]{1,0:T(8,128)(2,1)S(1)} %get-tuple-element.36), channel_id=1, source_target_pairs={{1,0},{2,1},{3,2},{5,4},{6,5},{7,6},{9,8},{10,9},{11,10},{13,12},{... | collective-permute-start | bytes 1572872 | tf_op jit(solution)/shard_map/ppermute | solution.py:296

commit v2 on v0

v2 whole, which is shorter than its diff:
```python
from functools import partial

import jax
import jax.numpy as jnp
from jax import lax
from jax.experimental import pallas as pl
from jax.experimental.pallas import tpu as pltpu
from jax.sharding import PartitionSpec as P

HEAD_DIM = 64
STATE = 128
CHUNK = 128
MIDDLE = CHUNK // 2 - 1
EXTRA = 16
COLUMN_TILE = 512
HALVES = 2
WEIGHT_COPIES = 8
F32 = jnp.float32
BF16 = jnp.bfloat16


def dot(a, b):
    return jnp.dot(a, b, preferred_element_type=F32)


def dot_exact(a, b):
    return jnp.dot(a, b, preferred_element_type=F32, precision=lax.Precision.HIGHEST)


def head_map(heads, channels):
    head = lax.broadcasted_iota(jnp.int32, (2 * heads, channels), 0) & (heads - 1)
    place = lax.broadcasted_iota(jnp.int32, (2 * heads, channels), 1) >> 6
    return jnp.where(head == place, 1.0, 0.0).astype(BF16)


def high_low(values):
    high = values.astype(BF16).astype(F32)
    return jnp.concatenate([high, values - high], axis=0)


def pieces(values, rows):
    first = values.astype(BF16).astype(F32)
    second = (values - first).astype(BF16).astype(F32)
    third = values - first - second
    row = lax.broadcasted_iota(jnp.int32, (rows, values.shape[1]), 0)
    stacked = jnp.where(row == 0, first, jnp.where(row == 1, second, jnp.where(row == 2, third, 0.0)))
    return stacked.astype(BF16)


def load(pairs, semaphores):
    copies = [pltpu.make_async_copy(src, dst, semaphores.at[n]) for n, (src, dst) in enumerate(pairs)]
    for copy in copies:
        copy.start()
    return copies


def rows_of(chunk, size=CHUNK):
    return slice(chunk * size, (chunk + 1) * size)


def state_kernel(groups, core_ref, x_hbm, b_hbm, step_hbm, decay_hbm, rhs_ref, inner_ref, outer_ref, send_ref, keep_ref,
                 x_ref, b_ref, step_ref, decay_ref, semaphores):
    rows, channels = x_ref.shape
    heads = step_ref.shape[0]
    width = channels // groups
    chunks = rows // CHUNK
    small = load([(decay_hbm, decay_ref), (step_hbm, step_ref), (b_hbm, b_ref)], semaphores)
    large = load(
        [(x_hbm.at[rows_of(n), :], x_ref.at[rows_of(n), :]) for n in range(chunks)], semaphores.at[pl.ds(3, chunks)]
    )
    spread = head_map(heads, channels)
    row = lax.broadcasted_iota(jnp.int32, (CHUNK, CHUNK), 0)
    column = lax.broadcasted_iota(jnp.int32, (CHUNK, CHUNK), 1)
    upper = jnp.where(row <= column, 1.0, 0.0)
    lane = lax.broadcasted_iota(jnp.int32, (heads, CHUNK), 1)
    before = jnp.zeros((heads, 1), F32)
    state = [jnp.zeros((STATE, width), F32)] * groups
    for copy in small:
        copy.wait()
    for n in range(chunks):
        here = rows_of(n)
        running = dot_exact(decay_ref[:, here], upper)
        middle, total = running[:, MIDDLE : MIDDLE + 1], running[:, CHUNK - 1 :]
        inner = running - middle
        inner_ref[:, here] = high_low(jnp.exp(inner)).astype(BF16)
        outer_ref[:, here] = high_low(jnp.exp(before + running)).astype(BF16)
        weight = step_ref[:, here] * jnp.exp(-inner)
        factors = jnp.exp(jnp.where(lane == 0, total, jnp.where(lane == 1, total - middle, middle)))
        stacked = jnp.concatenate([jnp.transpose(high_low(weight)), jnp.transpose(high_low(factors))[:EXTRA]], axis=0)
        stacked = stacked.astype(BF16)
        before = before + total
        large[n].wait()
        to_rhs = n * (CHUNK + STATE)
        for g in range(groups):
            cut = slice(g * width, (g + 1) * width)
            wide = dot(stacked, spread[:, cut])
            weighted = (x_ref[here, cut].astype(F32) * wide[:CHUNK]).astype(BF16)
            rhs_ref[to_rhs : to_rhs + CHUNK, cut] = weighted
            rhs_ref[to_rhs + CHUNK : to_rhs + CHUNK + STATE, cut] = (state[g] * wide[CHUNK + 2 : CHUNK + 3]).astype(BF16)
            fresh = lax.dot_general(
                b_ref[here, g * STATE : (g + 1) * STATE],
                weighted,
                (((0,), (0,)), ((), ())),
                preferred_element_type=F32,
            )
            state[g] = state[g] * wide[CHUNK : CHUNK + 1] + fresh * wide[CHUNK + 1 : CHUNK + 2]

    first = before.astype(BF16).astype(F32)
    second = (before - first).astype(BF16).astype(F32)
    third = before - first - second
    stacked = jnp.where(lane == 0, first, jnp.where(lane == 1, second, jnp.where(lane == 2, third, 0.0)))
    logs = dot(jnp.transpose(stacked)[:EXTRA].astype(BF16), spread[:heads, :]).astype(BF16)
    end = jnp.concatenate([part.astype(BF16) for part in state], axis=1)
    half = channels // 2
    for core in range(2):

        @pl.when(core_ref[0] == core)
        def _():
            own = slice(core * half, (core + 1) * half)
            other = slice((1 - core) * half, (2 - core) * half)
            keep_ref[:STATE, :] = end[:, own]
            keep_ref[STATE:, :] = logs[:, own]
            send_ref[:STATE, :] = end[:, other]
            send_ref[STATE:, :] = logs[:, other]


def log_of(ref):
    return jnp.sum(ref[STATE:, :].astype(F32), axis=0, keepdims=True)


def pair_kernel(core_ref, own_ref, sibling_ref, pair_ref):
    own_log, sibling_log = log_of(own_ref), log_of(sibling_ref)
    early = core_ref[0] == 0
    own_scale = jnp.where(early, jnp.exp(sibling_log), 1.0)
    sibling_scale = jnp.where(early, 1.0, jnp.exp(own_log))
    pair = own_ref[:STATE, :].astype(F32) * own_scale + sibling_ref[:STATE, :].astype(F32) * sibling_scale
    pair_ref[:STATE, :] = pair.astype(BF16)
    pair_ref[STATE:, :] = pieces(own_log + sibling_log, EXTRA)


def joined(stretches):
    total, log = stretches[0][:STATE, :].astype(F32), log_of(stretches[0])
    for ref in stretches[1:]:
        total = total + ref[:STATE, :].astype(F32) * jnp.exp(log)
        log = log + log_of(ref)
    return total, log


def join_kernel(*refs):
    total, log = joined(refs[:-1])
    refs[-1][:STATE, :] = total.astype(BF16)
    refs[-1][STATE:, :] = pieces(log, EXTRA)


def last_kernel(core_ref, own_ref, sibling_ref, *refs):
    keep_ref, send_ref = refs[-2:]
    chip = joined(refs[:-2])[0]
    for core, first, mine, other in ((0, own_ref, 0, 1), (1, sibling_ref, 1, 0)):

        @pl.when(core_ref[0] == core)
        def _():
            after = chip * jnp.exp(log_of(first)) + first[:STATE, :].astype(F32)
            both = (chip.astype(BF16), after.astype(BF16))
            keep_ref[...] = both[mine]
            send_ref[...] = both[other]


def widened(parts, spread):
    return lax.dot_general(parts, spread, (((0,), (0,)), ((), ())), preferred_element_type=F32)


def local_kernel(groups, x_hbm, gate_hbm, b_hbm, c_hbm, w_hbm, rhs_ref, inner_ref, outer_ref, skip_ref, mixed_ref, scale_ref,
                 w_ref, x_ref, gate_ref, b_ref, c_ref, semaphores):
    heads = skip_ref.shape[1]
    rows, channels = x_ref.shape
    width = channels // groups
    chunks = rows // CHUNK
    small = load([(b_hbm, b_ref), (c_hbm, c_ref)], semaphores)
    large = []
    for n in range(chunks):
        here = rows_of(n)
        pairs = [(x_hbm.at[here, :], x_ref.at[here, :]), (gate_hbm.at[here, :], gate_ref.at[here, :])]
        large.append(load(pairs, semaphores.at[pl.ds(2 + 2 * n, 2)]))
    size = channels // WEIGHT_COPIES
    weights = [(w_hbm.at[rows_of(n, size), :], w_ref.at[rows_of(n, size), :]) for n in range(WEIGHT_COPIES)]
    weights = load(weights, semaphores.at[pl.ds(2 + 2 * chunks, WEIGHT_COPIES)])

    spread = head_map(heads, channels)
    row = lax.broadcasted_iota(jnp.int32, (CHUNK, CHUNK), 0)
    column = lax.broadcasted_iota(jnp.int32, (CHUNK, CHUNK), 1)
    skip = jnp.sum(dot(pieces(skip_ref[...], EXTRA), spread[:heads, :]), axis=0, keepdims=True)
    for copy in small:
        copy.wait()
    for n in range(chunks):
        here = rows_of(n)
        for copy in large[n]:
            copy.wait()
        for g in range(groups):
            cut = slice(g * width, (g + 1) * width)
            part = slice(g * STATE, (g + 1) * STATE)
            to_wide = spread[:, cut]
            scores = lax.dot_general(
                c_ref[here, part], b_ref[here, part], (((1,), (1,)), ((), ())), preferred_element_type=F32
            )
            scores = jnp.where(row >= column, scores, 0.0).astype(BF16)
            within = dot(jnp.concatenate([scores, c_ref[here, part]], axis=1), rhs_ref[rows_of(n, CHUNK + STATE), cut])
            gate = gate_ref[here, cut].astype(F32)
            gate = gate / (1.0 + jnp.exp(-gate))
            passed = x_ref[here, cut].astype(F32) * skip[:, cut]
            mixed_ref[here, cut] = (within * widened(inner_ref[:, here], to_wide) + passed) * gate
            scale_ref[here, cut] = widened(outer_ref[:, here], to_wide) * gate
    for copy in weights:
        copy.wait()


def norm_rows(groups, state, mixed, scale, c_rows, gain):
    width = mixed.shape[1] // groups
    parts = []
    for g in range(groups):
        cut = slice(g * width, (g + 1) * width)
        carried = dot(c_rows[:, g * STATE : (g + 1) * STATE], state[:, cut])
        whole = mixed[:, cut] + scale[:, cut] * carried
        meansq = jnp.mean(whole * whole, axis=1, keepdims=True)
        parts.append((whole * lax.rsqrt(meansq + 1e-05) * gain[:, cut]).astype(BF16))
    return parts


def fill_state(core_ref, keep_ref, recv_ref, state):
    half = keep_ref.shape[1]
    for core in range(2):

        @pl.when(core_ref[0] == core)
        def _():
            state[:, core * half : (core + 1) * half] = keep_ref[...]
            state[:, (1 - core) * half : (2 - core) * half] = recv_ref[...]


def block_at(here, position, count, size):
    block = 0
    for i in range(count):
        block = jnp.where(here == i, block_order(i, count)[position], block)
    return pl.ds(pl.multiple_of(block * size, size), size)


def first_kernel(groups, count, core_ref, here_ref, mixed_ref, scale_ref, c_ref, keep_ref, recv_ref, gain_ref, w_ref, out_ref,
                 normed_ref, state):
    fill_state(core_ref, keep_ref, recv_ref, state)
    width = normed_ref.shape[1] // groups
    here = block_at(here_ref[0], 0, count, normed_ref.shape[0])
    rows = norm_rows(groups, state, mixed_ref.at[here, :], scale_ref.at[here, :], c_ref.at[here, :], gain_ref)
    for g, part in enumerate(rows):
        normed_ref[:, g * width : (g + 1) * width] = part

    @pl.loop(0, out_ref.shape[1] // COLUMN_TILE)
    def _(j):
        cut = pl.ds(pl.multiple_of(j * COLUMN_TILE, COLUMN_TILE), COLUMN_TILE)
        out_ref[:, cut] = dot(normed_ref[...], w_ref[:, cut]).astype(BF16)


def second_kernel(normed_ref, w_ref, out_ref):
    start = w_ref.shape[1] - out_ref.shape[1]

    @pl.loop(0, out_ref.shape[1] // COLUMN_TILE)
    def _(j):
        cut = pl.ds(pl.multiple_of(j * COLUMN_TILE, COLUMN_TILE), COLUMN_TILE)
        from_ = pl.ds(pl.multiple_of(start + j * COLUMN_TILE, COLUMN_TILE), COLUMN_TILE)
        out_ref[:, cut] = dot(normed_ref[...], w_ref[:, from_]).astype(BF16)


def rest_kernel(groups, count, core_ref, here_ref, mixed_ref, scale_ref, c_ref, keep_ref, recv_ref, gain_ref, w_ref, a_ref,
                b_ref, out_ref, state, normed):
    size, half = a_ref.shape
    blocks = [block_at(here_ref[0], n, count, size) for n in range(count)]
    out_ref[blocks[0], :half] = a_ref[...]
    out_ref[blocks[0], half:] = b_ref[...]
    fill_state(core_ref, keep_ref, recv_ref, state)
    width = normed.shape[1] // groups
    for n in range(1, count):
        here = blocks[n]
        rows = norm_rows(groups, state, mixed_ref.at[here, :], scale_ref.at[here, :], c_ref.at[here, :], gain_ref)
        for g, part in enumerate(rows):
            normed[(n - 1) * size : n * size, g * width : (g + 1) * width] = part

    @pl.loop(0, out_ref.shape[1] // COLUMN_TILE)
    def _(j):
        cut = pl.ds(pl.multiple_of(j * COLUMN_TILE, COLUMN_TILE), COLUMN_TILE)
        product = dot(normed[...], w_ref[:, cut]).astype(BF16)
        for n in range(1, count):
            out_ref[blocks[n], cut] = product[(n - 1) * size : n * size]


def pass_kernel(count, step, column, here_ref, right_ref, left_ref, sums_ref, to_right_ref, to_left_ref):
    size, width = right_ref.shape
    for shift, came, out in ((count - step, right_ref, to_right_ref), (step - count, left_ref, to_left_ref)):
        block = jnp.clip(here_ref[0] + shift, 0, count - 1)
        rows = pl.ds(pl.multiple_of(block * size, size), size)
        own = sums_ref[rows, column : column + width].astype(F32)
        out[...] = (own + came[...].astype(F32)).astype(BF16)


def sum_kernel(column, here_ref, right_ref, left_ref, sums_ref, out_ref):
    size, width = right_ref.shape
    rows = pl.ds(pl.multiple_of(here_ref[0] * size, size), size)
    own = sums_ref[rows, column : column + width].astype(F32)
    out_ref[...] = (own + right_ref[...].astype(F32) + left_ref[...].astype(F32)).astype(BF16)


def block_order(here, count):
    order = []
    for step in range(1, count):
        for block, sends in ((count - step + here, here <= step - 1), (step - count + here, here >= count - step)):
            if sends and block not in order:
                order.append(block)
    return order + [b for b in range(count) if b not in order]


def in_vmem(kernel, name, ins, outs, scratch=(), vmem=8, flops=1):
    vm = pl.BlockSpec(memory_space=pltpu.VMEM)
    specs, arrays = [], []
    for v in ins:
        if isinstance(v, tuple):
            specs.append(pl.BlockSpec(memory_space=pltpu.HBM))
            arrays.append(pltpu.with_memory_space_constraint(v[0], pltpu.HBM))
        elif v.dtype == jnp.int32:
            specs.append(pl.BlockSpec(memory_space=pltpu.SMEM))
            arrays.append(v)
        else:
            specs.append(vm)
            arrays.append(pltpu.with_memory_space_constraint(v, pltpu.VMEM))
    return pl.pallas_call(
        kernel,
        in_specs=specs,
        out_specs=[vm for _ in outs],
        out_shape=[pltpu.VMEM(shape, kind) for shape, kind in outs],
        scratch_shapes=list(scratch),
        compiler_params=pltpu.CompilerParams(vmem_limit_bytes=vmem * 2**20),
        cost_estimate=pl.CostEstimate(flops=flops, bytes_accessed=1, transcendentals=0),
        name=name,
    )(*arrays)


def line_reduce(first, partial_sums, here, size, columns):
    count = lax.axis_size("tp")
    width = columns // HALVES
    block = ((size, width), BF16)
    right = [None] * HALVES
    left = [None] * HALVES
    for step in range(1, count):
        to_right = [(i, i + 1) for i in range(step)]
        to_left = [(i, i - 1) for i in range(count - step, count)]
        for half in range(HALVES):
            if step == 1:
                right[half] = left[half] = lax.ppermute(first[half], "tp", to_right + to_left)
                continue
            ins = (here, right[half], left[half], partial_sums)
            send_right, send_left = in_vmem(partial(pass_kernel, count, step, half * width), "pass_on", ins, (block, block))
            right[half] = lax.ppermute(send_right, "tp", to_right)
            left[half] = lax.ppermute(send_left, "tp", to_left)
    done = []
    for half in range(HALVES):
        ins = (here, right[half], left[half], partial_sums)
        done.extend(in_vmem(partial(sum_kernel, half * width), "sum_up", ins, (block,)))
    return jnp.concatenate(done, axis=1)


def on_device(x_in, gate_z, b_in, c_in, step_size, log_decay, skip, norm_gain, out_weight):
    rows, channels = x_in.shape
    heads = step_size.shape[1]
    groups = b_in.shape[1] // STATE
    chunks = rows // CHUNK
    columns = out_weight.shape[1]
    half = channels // 2
    devices = lax.axis_size("ctx")
    chips = devices // 2
    count = lax.axis_size("tp")
    size = rows // count
    core = lax.rem(lax.axis_index("ctx"), 2).astype(jnp.int32).reshape(1)
    here = lax.axis_index("tp").astype(jnp.int32).reshape(1)
    message = ((STATE + EXTRA, half), BF16)
    by_head = ((2 * heads, rows), BF16)
    whole = ((rows, channels), F32)

    rhs, inner, outer, send, own = in_vmem(
        partial(state_kernel, groups),
        "chunk_states",
        (core, (x_in,), (b_in,), (step_size.T,), (log_decay.T,)),
        (((chunks * (CHUNK + STATE), channels), BF16), by_head, by_head, message, message),
        scratch=[
            pltpu.VMEM((rows, channels), BF16),
            pltpu.VMEM((rows, groups * STATE), BF16),
            pltpu.VMEM((heads, rows), F32),
            pltpu.VMEM((heads, rows), F32),
            pltpu.SemaphoreType.DMA((3 + chunks,)),
        ],
        vmem=20,
    )

    swap = [(i, i ^ 1) for i in range(devices)]
    sibling = lax.ppermute(send, "ctx", swap)
    (pair,) = in_vmem(pair_kernel, "pair", (core, own, sibling), (message,))
    x_late, pair = lax.optimization_barrier((x_in, pair))
    incoming, outgoing, distance = [], pair, 1
    while distance < chips:
        if incoming:
            (outgoing,) = in_vmem(join_kernel, "join", (pair, *incoming), (message,))
        for far in range(distance, min(chips, 4 * distance), distance):
            incoming.append(lax.ppermute(outgoing, "ctx", [(i, i + 2 * far) for i in range(devices - 2 * far)]))
        distance *= 4
    mixed, scale, weight = in_vmem(
        partial(local_kernel, groups),
        "local_part",
        ((x_late,), (gate_z,), (b_in,), (c_in,), (out_weight,), rhs, inner, outer, skip.reshape(1, heads)),
        (whole, whole, (out_weight.shape, BF16)),
        scratch=[
            pltpu.VMEM((rows, channels), BF16),
            pltpu.VMEM((rows, channels), BF16),
            pltpu.VMEM((rows, groups * STATE), BF16),
            pltpu.VMEM((rows, groups * STATE), BF16),
            pltpu.SemaphoreType.DMA((2 + 2 * chunks + WEIGHT_COPIES,)),
        ],
        vmem=20,
        flops=8 * 10**9,
    )
    mixed, scale, weight, *incoming = lax.optimization_barrier((mixed, scale, weight, *incoming))
    state = ((STATE, half), BF16)
    keep, send = in_vmem(last_kernel, "incoming", (core, own, sibling, *incoming), (state, state))
    recv = lax.ppermute(send, "ctx", swap)

    first = ((size, columns // 2), BF16)
    gain = norm_gain.reshape(1, channels)
    inputs = (core, here, mixed, scale, c_in, keep, recv, gain, weight)
    whole_state = pltpu.VMEM((STATE, channels), BF16)
    first_a, normed = in_vmem(
        partial(first_kernel, groups, count), "first_block", inputs, (first, ((size, channels), BF16)), [whole_state]
    )
    (first_b,) = in_vmem(second_kernel, "first_block_rest", (normed, weight), (first,))
    (partial_sums,) = in_vmem(
        partial(rest_kernel, groups, count),
        "other_blocks",
        (*inputs, first_a, first_b),
        (((rows, columns), BF16),),
        [whole_state, pltpu.VMEM((rows - size, channels), BF16)],
        vmem=16,
    )
    return line_reduce((first_a, first_b), partial_sums, here, size, columns)


def solution(mesh):
    placed = (
        P("ctx", "tp"),
        P("ctx", "tp"),
        P("ctx", "tp"),
        P("ctx", "tp"),
        P("ctx", "tp"),
        P("ctx", "tp"),
        P("tp"),
        P("tp"),
        P("tp", None),
    )
    return jax.shard_map(
        on_device, mesh=mesh, in_specs=placed, out_specs=P(("ctx", "tp"), None), check_vma=False
    )
```

time: 367 us -> 122 us (0.33); the launches traced: 360 us -> 121 us
  local copies, waits for them, and re-layouts: 125 us -> 20.5 us
  waiting for transfers between devices: 102 us -> 35 us
  matrix products: 39.1 us -> 0 us
  Pallas kernels: 0 us -> 27.9 us
  other arithmetic: 23.4 us -> 1.06 us
  starting transfers between devices: 56.5 us -> 36.6 us
  between operations: 13.5 us -> 0.27 us
    reduce_scatter x1 -> x0, waiting for transfers between devices: 91.5 us -> none  [on_device(): lax.psum_scatter(jnp.dot(normed, out_weight, preferred_element_type=jnp.f...]
    dynamic_update_slice x4 -> x0, local copies, waits for them, and re-layouts: 89.4 us -> none  [on_device(): lax.scan(partial(block_pass, per_group=per_group), start_state, (scaled.r...]
    dot_general x10 -> x0, matrix products: 39.1 us -> none  [the longest x2 16.7 us: block_pass(): jnp.einsum('hts,shp->thp', weights, scaled, precision=lax.Precision.HIGHEST)]
    pallas_call x0 -> x13, Pallas kernels: none -> 27.9 us  [in_vmem(): pl.pallas_call(kernel, in_specs=specs, out_specs=[vm for _ in outs], out_...]
    ppermute x7 -> x15, waiting for transfers between devices: 10.4 us -> 35 us  [the longest x4 26.4 us: line_reduce(): right[half] = lax.ppermute(send_right, 'tp', to_right)]
    ppermute x7 -> x15, starting transfers between devices: 56.5 us -> 36.6 us  [the longest x4 15.5 us: line_reduce(): right[half] = lax.ppermute(send_right, 'tp', to_right)]
    dynamic_slice x8 -> x0, local copies, waits for them, and re-layouts: 11.6 us -> none  [on_device(): lax.scan(partial(block_pass, per_group=per_group), start_state, (scaled.r...]
    mul x3 -> x0, other arithmetic: 10.8 us -> none  [the longest x1 6.91 us: on_device(): scaled = inputs * step_size[:, :, None]]
  transfers between devices with their start and end apart: 8 -> 15, of which waited for: 8 -> 7; matrix products, arithmetic and copies ran while one was open for 0% -> 0% of each run, Pallas kernels for 0% -> 16%
where the time goes in v2:
time: 122 us; the launch traced here: 121 us
  starting transfers between devices  36.6 us (30%)
  waiting for transfers between devices  35 us (29%)
  Pallas kernels  27.9 us (23%)
  local copies, waits for them, and re-layouts  20.5 us (17%)
    pallas_call x13, Pallas kernels, in_vmem(): pl.pallas_call(kernel, in_specs=specs, out_specs=[vm for _ in outs], out_...  27.9 us
    ppermute x4, waiting for transfers between devices, line_reduce(): right[half] = lax.ppermute(send_right, 'tp', to_right)  26.4 us
    unnamed x24, local copies, waits for them, and re-layouts  20.5 us
    ppermute x4, starting transfers between devices, line_reduce(): right[half] = lax.ppermute(send_right, 'tp', to_right)  15.5 us
    ppermute x3, starting transfers between devices, on_device(): lax.ppermute(outgoing, 'ctx', [(i, i + 2 * far) for i in range(devices -...  9.52 us
    ppermute x2, starting transfers between devices, line_reduce(): lax.ppermute(first[half], 'tp', to_right + to_left)  7.02 us
    ppermute x2, waiting for transfers between devices, line_reduce(): lax.ppermute(first[half], 'tp', to_right + to_left)  5.81 us
    ppermute x4, starting transfers between devices, line_reduce(): left[half] = lax.ppermute(send_left, 'tp', to_left)  3.97 us
  transfers between devices with their start and end apart: 15, of which 7 were waited for; matrix products, arithmetic and copies ran while one was open for 0% of the time, Pallas kernels for 16%

profile of v2, /device:TPU:0, one launch (start us, length us, event | category | flops | bytes accessed | tf_op | source)
XLA Modules:
  0.0 121.4 jit_solution(7491571586647150591)
XLA Ops:
  0.0 5.1 %chunk_states.1 = (bf16[1024,2048]{1,0:T(8,128)(2,1)S(1)}, bf16[64,512]{1,0:T(8,128)(2,1)S(1)}, bf16[64,512]{1,0:T(8,128)(2,1)S(1)}, bf16[144,1024]{1,0:T(8,128)(2,1)S(1)}, bf16[144,1024]{1,0:T(8,128)(2,1)S(1)}) custom-call(s32[1]{0:T(128)} %bitcast.1.core_ref, bf16[512,2048]{1,0:T(8,128)(2,1)} %x_hbm.2, bf16[512,256]{1,0:T(8,128)(2,1)} %b_hbm.3, ...), custom_call_target="tpu_custom_call" | custom-call | flops 1 | bytes 1 | tf_op jit(solution)/shard_map/chunk_states/pallas_call | solution.py:330
  6.9 4.8 %collective-permute-start.1 = (bf16[144,1024]{1,0:T(8,128)(2,1)S(1)}, bf16[144,1024]{1,0:T(8,128)(2,1)S(1)}, u32[]{:S(2)}, u32[]{:S(2)}) collective-permute-start(bf16[144,1024]{1,0:T(8,128)(2,1)S(1)} %pair.1), channel_id=1, source_target_pairs={{0,8},{4,12},{8,16},{12,20},{16,24},{20,28},{1,9},{5,13},{9,17},{1... | collective-permute-start | bytes 884744 | tf_op jit(solution)/shard_map/ppermute | solution.py:407
  11.7 3.4 %collective-permute-start.2 = (bf16[144,1024]{1,0:T(8,128)(2,1)S(1)}, bf16[144,1024]{1,0:T(8,128)(2,1)S(1)}, u32[]{:S(2)}, u32[]{:S(2)}) collective-permute-start(bf16[144,1024]{1,0:T(8,128)(2,1)S(1)} %pair.1), channel_id=1, source_target_pairs={{0,16},{4,20},{8,24},{12,28},{1,17},{5,21},{9,25},{13,29},{2,18},{... | collective-permute-start | bytes 884744 | tf_op jit(solution)/shard_map/ppermute | solution.py:407
  17.1 7.4 %local_part.1 = (f32[512,2048]{1,0:T(8,128)S(1)}, f32[512,2048]{1,0:T(8,128)S(1)}, bf16[2048,4096]{1,0:T(8,128)(2,1)S(1)}) custom-call(bf16[512,2048]{1,0:T(8,128)(2,1)} %x_hbm.2, bf16[512,2048]{1,0:T(8,128)(2,1)} %gate_hbm.1, bf16[512,256]{1,0:T(8,128)(2,1)} %b_hbm.3, bf16[512,256]{1,0:T(8,128)(2,1)} %c_ref.3, bf16[2048,4096]{1,0:T(8,128)(2,1)} %w_hbm.1, ...), custom_call_target="tpu_custom_call" | custom-call | flops 8000000000 | bytes 1 | tf_op jit(solution)/shard_map/local_part/pallas_call | solution.py:330
  24.6 5.7 %copy-done = bf16[2048,4096]{1,0:T(8,128)(2,1)} copy-done((bf16[2048,4096]{1,0:T(8,128)(2,1)}, bf16[2048,4096]{1,0:T(8,128)(2,1)S(1)}, u32[]{:S(2)}) %copy-start) | copy-done | bytes 16777240
  30.3 2.0 %copy-done.3 = f32[512,2048]{1,0:T(8,128)} copy-done((f32[512,2048]{1,0:T(8,128)}, f32[512,2048]{1,0:T(8,128)S(1)}, u32[]{:S(2)}) %copy-start.3) | copy-done | bytes 4194328
  32.3 2.0 %copy-done.6 = f32[512,2048]{1,0:T(8,128)} copy-done((f32[512,2048]{1,0:T(8,128)}, f32[512,2048]{1,0:T(8,128)S(1)}, u32[]{:S(2)}) %copy-start.6) | copy-done | bytes 4194328
  36.2 5.8 %copy-done.1 = bf16[2048,4096]{1,0:T(8,128)(2,1)S(1)} copy-done((bf16[2048,4096]{1,0:T(8,128)(2,1)S(1)}, bf16[2048,4096]{1,0:T(8,128)(2,1)}, u32[]{:S(2)}) %copy-start.1) | copy-done | bytes 16777240
  42.0 2.2 %copy-done.4 = f32[512,2048]{1,0:T(8,128)S(1)} copy-done((f32[512,2048]{1,0:T(8,128)S(1)}, f32[512,2048]{1,0:T(8,128)}, u32[]{:S(2)}) %copy-start.4) | copy-done | bytes 4194328
  44.2 2.2 %copy-done.7 = f32[512,2048]{1,0:T(8,128)S(1)} copy-done((f32[512,2048]{1,0:T(8,128)S(1)}, f32[512,2048]{1,0:T(8,128)}, u32[]{:S(2)}) %copy-start.7) | copy-done | bytes 4194328
  46.4 2.3 %first_block.1 = (bf16[128,2048]{1,0:T(8,128)(2,1)S(1)}, bf16[128,2048]{1,0:T(8,128)(2,1)S(1)}) custom-call(s32[1]{0:T(128)} %bitcast.1.core_ref, s32[1]{0:T(128)} %bitcast.here_ref, f32[512,2048]{1,0:T(8,128)S(1)} %copy-done.4, f32[512,2048]{1,0:T(8,128)S(1)} %copy-done.7, bf16[512,256]{1,0:T(8,128)(2,1)S(1)} %copy-done.9, ...), custom_call_target="tpu_custom_call" | custom-call | flops 1 | bytes 1 | tf_op jit(solution)/shard_map/first_block/pallas_call | solution.py:330
  48.7 3.8 %collective-permute-start.5 = (bf16[128,2048]{1,0:T(8,128)(2,1)S(1)}, bf16[128,2048]{1,0:T(8,128)(2,1)S(1)}, u32[]{:S(2)}, u32[]{:S(2)}) collective-permute-start(bf16[128,2048]{1,0:T(8,128)(2,1)S(1)} %get-tuple-element.51.a_ref), channel_id=1, source_target_pairs={{0,1},{3,2},{4,5},{7,6},{8,9},{11,10},{12,13},{15,14},{16,17},{19,... | collective-permute-start | bytes 1572872 | tf_op jit(solution)/shard_map/ppermute | solution.py:353
  52.6 1.9 %first_block_rest.1.b_ref = bf16[128,2048]{1,0:T(8,128)(2,1)S(1)} custom-call(bf16[128,2048]{1,0:T(8,128)(2,1)S(1)} %get-tuple-element.52.normed_ref, bf16[2048,4096]{1,0:T(8,128)(2,1)S(1)} %copy-done.2), custom_call_target="tpu_custom_call" | custom-call | flops 1 | bytes 1 | tf_op jit(solution)/shard_map/first_block_rest/pallas_call | solution.py:330
  54.4 3.2 %collective-permute-start.10 = (bf16[128,2048]{1,0:T(8,128)(2,1)S(1)}, bf16[128,2048]{1,0:T(8,128)(2,1)S(1)}, u32[]{:S(2)}, u32[]{:S(2)}) collective-permute-start(bf16[128,2048]{1,0:T(8,128)(2,1)S(1)} %first_block_rest.1.b_ref), channel_id=1, source_target_pairs={{0,1},{3,2},{4,5},{7,6},{8,9},{11,10},{12,13},{15,14},{16,17},{19,... | collective-permute-start | bytes 1572872 | tf_op jit(solution)/shard_map/ppermute | solution.py:353
  57.7 9.2 %other_blocks.1.sums_ref = bf16[512,4096]{1,0:T(8,128)(2,1)S(1)} custom-call(s32[1]{0:T(128)} %bitcast.1.core_ref, s32[1]{0:T(128)} %bitcast.here_ref, f32[512,2048]{1,0:T(8,128)S(1)} %copy-done.5, f32[512,2048]{1,0:T(8,128)S(1)} %copy-done.8, bf16[512,256]{1,0:T(8,128)(2,1)S(1)} %copy-done.9, bf16[128,1024]{1,0:T(8,128)(2,1)S(1)} %get-tuple-element.48.keep_ref, ...), custom_call_target="tpu_custom_call" | custom-call | flops 1 | bytes 1 | tf_op jit(solution)/shard_map/other_blocks/pallas_call | solution.py:330
  67.2 2.3 %collective-permute-start.6 = (bf16[128,2048]{1,0:T(8,128)(2,1)S(1)}, bf16[128,2048]{1,0:T(8,128)(2,1)S(1)}, u32[]{:S(2)}, u32[]{:S(2)}) collective-permute-start(bf16[128,2048]{1,0:T(8,128)(2,1)S(1)} %get-tuple-element.53), channel_id=1, source_target_pairs={{0,1},{1,2},{4,5},{5,6},{8,9},{9,10},{12,13},{13,14},{16,17},{17,1... | collective-permute-start | bytes 1572872 | tf_op jit(solution)/shard_map/ppermute | solution.py:357
  70.2 5.8 %collective-permute-done.10.right_ref.left_ref = bf16[128,2048]{1,0:T(8,128)(2,1)S(1)} collective-permute-done((bf16[128,2048]{1,0:T(8,128)(2,1)S(1)}, bf16[128,2048]{1,0:T(8,128)(2,1)S(1)}, u32[]{:S(2)}, u32[]{:S(2)}) %collective-permute-start.10) | collective-permute-done | bytes 524320 | tf_op jit(solution)/shard_map/ppermute | solution.py:353
  76.3 4.4 %collective-permute-start.11 = (bf16[128,2048]{1,0:T(8,128)(2,1)S(1)}, bf16[128,2048]{1,0:T(8,128)(2,1)S(1)}, u32[]{:S(2)}, u32[]{:S(2)}) collective-permute-start(bf16[128,2048]{1,0:T(8,128)(2,1)S(1)} %get-tuple-element.57), channel_id=1, source_target_pairs={{0,1},{1,2},{4,5},{5,6},{8,9},{9,10},{12,13},{13,14},{16,17},{17,1... | collective-permute-start | bytes 1572872 | tf_op jit(solution)/shard_map/ppermute | solution.py:357
  81.4 5.8 %collective-permute-done.6.right_ref = bf16[128,2048]{1,0:T(8,128)(2,1)S(1)} collective-permute-done((bf16[128,2048]{1,0:T(8,128)(2,1)S(1)}, bf16[128,2048]{1,0:T(8,128)(2,1)S(1)}, u32[]{:S(2)}, u32[]{:S(2)}) %collective-permute-start.6) | collective-permute-done | bytes 524320 | tf_op jit(solution)/shard_map/ppermute | solution.py:357
  87.5 4.4 %collective-permute-start.8 = (bf16[128,2048]{1,0:T(8,128)(2,1)S(1)}, bf16[128,2048]{1,0:T(8,128)(2,1)S(1)}, u32[]{:S(2)}, u32[]{:S(2)}) collective-permute-start(bf16[128,2048]{1,0:T(8,128)(2,1)S(1)} %get-tuple-element.55), channel_id=1, source_target_pairs={{0,1},{1,2},{2,3},{4,5},{5,6},{6,7},{8,9},{9,10},{10,11},{12,13},{... | collective-permute-start | bytes 1572872 | tf_op jit(solution)/shard_map/ppermute | solution.py:357
  93.3 5.2 %collective-permute-done.11.right_ref = bf16[128,2048]{1,0:T(8,128)(2,1)S(1)} collective-permute-done((bf16[128,2048]{1,0:T(8,128)(2,1)S(1)}, bf16[128,2048]{1,0:T(8,128)(2,1)S(1)}, u32[]{:S(2)}, u32[]{:S(2)}) %collective-permute-start.11) | collective-permute-done | bytes 524320 | tf_op jit(solution)/shard_map/ppermute | solution.py:357
  98.8 4.4 %collective-permute-start.13 = (bf16[128,2048]{1,0:T(8,128)(2,1)S(1)}, bf16[128,2048]{1,0:T(8,128)(2,1)S(1)}, u32[]{:S(2)}, u32[]{:S(2)}) collective-permute-start(bf16[128,2048]{1,0:T(8,128)(2,1)S(1)} %get-tuple-element.59), channel_id=1, source_target_pairs={{0,1},{1,2},{2,3},{4,5},{5,6},{6,7},{8,9},{9,10},{10,11},{12,13},{... | collective-permute-start | bytes 1572872 | tf_op jit(solution)/shard_map/ppermute | solution.py:357
  104.5 5.2 %collective-permute-done.8.right_ref = bf16[128,2048]{1,0:T(8,128)(2,1)S(1)} collective-permute-done((bf16[128,2048]{1,0:T(8,128)(2,1)S(1)}, bf16[128,2048]{1,0:T(8,128)(2,1)S(1)}, u32[]{:S(2)}, u32[]{:S(2)}) %collective-permute-start.8) | collective-permute-done | bytes 524320 | tf_op jit(solution)/shard_map/ppermute | solution.py:357
  109.9 10.2 %collective-permute-done.13.right_ref = bf16[128,2048]{1,0:T(8,128)(2,1)S(1)} collective-permute-done((bf16[128,2048]{1,0:T(8,128)(2,1)S(1)}, bf16[128,2048]{1,0:T(8,128)(2,1)S(1)}, u32[]{:S(2)}, u32[]{:S(2)}) %collective-permute-start.13) | collective-permute-done | bytes 524320 | tf_op jit(solution)/shard_map/ppermute | solution.py:357
  (44 shorter events, 12.4 us)
Async XLA Ops:
  5.1 1.7 %collective-permute-start = (bf16[144,1024]{1,0:T(8,128)(2,1)S(1)}, bf16[144,1024]{1,0:T(8,128)(2,1)S(1)}, u32[]{:S(2)}, u32[]{:S(2)}) collective-permute-start(bf16[144,1024]{1,0:T(8,128)(2,1)S(1)} %get-tuple-element.34), channel_id=1, source_target_pairs={{0,4},{4,0},{8,12},{12,8},{16,20},{20,16},{24,28},{28,24},{1,5},{5... | collective-permute-start | bytes 884744 | tf_op jit(solution)/shard_map/ppermute | solution.py:399
  6.9 27.4 %collective-permute-start.1 = (bf16[144,1024]{1,0:T(8,128)(2,1)S(1)}, bf16[144,1024]{1,0:T(8,128)(2,1)S(1)}, u32[]{:S(2)}, u32[]{:S(2)}) collective-permute-start(bf16[144,1024]{1,0:T(8,128)(2,1)S(1)} %pair.1), channel_id=1, source_target_pairs={{0,8},{4,12},{8,16},{12,20},{16,24},{20,28},{1,9},{5,13},{9,17},{1... | collective-permute-start | bytes 884744 | tf_op jit(solution)/shard_map/ppermute | solution.py:407
  11.7 22.6 %collective-permute-start.2 = (bf16[144,1024]{1,0:T(8,128)(2,1)S(1)}, bf16[144,1024]{1,0:T(8,128)(2,1)S(1)}, u32[]{:S(2)}, u32[]{:S(2)}) collective-permute-start(bf16[144,1024]{1,0:T(8,128)(2,1)S(1)} %pair.1), channel_id=1, source_target_pairs={{0,16},{4,20},{8,24},{12,28},{1,17},{5,21},{9,25},{13,29},{2,18},{... | collective-permute-start | bytes 884744 | tf_op jit(solution)/shard_map/ppermute | solution.py:407
  15.2 19.1 %collective-permute-start.3 = (bf16[144,1024]{1,0:T(8,128)(2,1)S(1)}, bf16[144,1024]{1,0:T(8,128)(2,1)S(1)}, u32[]{:S(2)}, u32[]{:S(2)}) collective-permute-start(bf16[144,1024]{1,0:T(8,128)(2,1)S(1)} %pair.1), channel_id=1, source_target_pairs={{0,24},{4,28},{1,25},{5,29},{2,26},{6,30},{3,27},{7,31}} | collective-permute-start | bytes 884744 | tf_op jit(solution)/shard_map/ppermute | solution.py:407
  17.1 19.1 %copy-start.9 = (bf16[512,256]{1,0:T(8,128)(2,1)S(1)}, bf16[512,256]{1,0:T(8,128)(2,1)}, u32[]{:S(2)}) copy-start(bf16[512,256]{1,0:T(8,128)(2,1)} %c_ref.3) | copy-start | bytes 786436
  17.1 19.1 %copy-start.10 = (f32[2048]{0:T(1024)S(1)}, f32[2048]{0:T(1024)}, u32[]{:S(2)}) copy-start(f32[2048]{0:T(1024)} %param.16) | copy-start | bytes 24580
  24.6 5.8 %copy-start = (bf16[2048,4096]{1,0:T(8,128)(2,1)}, bf16[2048,4096]{1,0:T(8,128)(2,1)S(1)}, u32[]{:S(2)}) copy-start(bf16[2048,4096]{1,0:T(8,128)(2,1)S(1)} %get-tuple-element.50.w_ref) | copy-start | bytes 50331652
  34.6 1.6 %collective-permute-start.4 = (bf16[128,1024]{1,0:T(8,128)(2,1)S(1)}, bf16[128,1024]{1,0:T(8,128)(2,1)S(1)}, u32[]{:S(2)}, u32[]{:S(2)}) collective-permute-start(bf16[128,1024]{1,0:T(8,128)(2,1)S(1)} %get-tuple-element.49), channel_id=1, source_target_pairs={{0,4},{4,0},{8,12},{12,8},{16,20},{20,16},{24,28},{28,24},{1,5},{5... | collective-permute-start | bytes 786440 | tf_op jit(solution)/shard_map/ppermute | solution.py:427
  36.2 5.8 %copy-start.1 = (bf16[2048,4096]{1,0:T(8,128)(2,1)S(1)}, bf16[2048,4096]{1,0:T(8,128)(2,1)}, u32[]{:S(2)}) copy-start(bf16[2048,4096]{1,0:T(8,128)(2,1)} %copy-done) | copy-start | bytes 50331652
  42.0 2.2 %copy-start.4 = (f32[512,2048]{1,0:T(8,128)S(1)}, f32[512,2048]{1,0:T(8,128)}, u32[]{:S(2)}) copy-start(f32[512,2048]{1,0:T(8,128)} %copy-done.3) | copy-start | bytes 12582916
  44.2 2.2 %copy-start.7 = (f32[512,2048]{1,0:T(8,128)S(1)}, f32[512,2048]{1,0:T(8,128)}, u32[]{:S(2)}) copy-start(f32[512,2048]{1,0:T(8,128)} %copy-done.6) | copy-start | bytes 12582916
  46.4 6.1 %copy-start.2 = (bf16[2048,4096]{1,0:T(8,128)(2,1)S(1)}, bf16[2048,4096]{1,0:T(8,128)(2,1)}, u32[]{:S(2)}) copy-start(bf16[2048,4096]{1,0:T(8,128)(2,1)} %copy-done) | copy-start | bytes 50331652
  48.7 18.1 %collective-permute-start.5 = (bf16[128,2048]{1,0:T(8,128)(2,1)S(1)}, bf16[128,2048]{1,0:T(8,128)(2,1)S(1)}, u32[]{:S(2)}, u32[]{:S(2)}) collective-permute-start(bf16[128,2048]{1,0:T(8,128)(2,1)S(1)} %get-tuple-element.51.a_ref), channel_id=1, source_target_pairs={{0,1},{3,2},{4,5},{7,6},{8,9},{11,10},{12,13},{15,14},{16,17},{19,... | collective-permute-start | bytes 1572872 | tf_op jit(solution)/shard_map/ppermute | solution.py:353
  52.5 5.1 %copy-start.5 = (f32[512,2048]{1,0:T(8,128)S(1)}, f32[512,2048]{1,0:T(8,128)}, u32[]{:S(2)}) copy-start(f32[512,2048]{1,0:T(8,128)} %copy-done.3) | copy-start | bytes 12582916
  52.6 5.1 %copy-start.8 = (f32[512,2048]{1,0:T(8,128)S(1)}, f32[512,2048]{1,0:T(8,128)}, u32[]{:S(2)}) copy-start(f32[512,2048]{1,0:T(8,128)} %copy-done.6) | copy-start | bytes 12582916
  54.4 21.6 %collective-permute-start.10 = (bf16[128,2048]{1,0:T(8,128)(2,1)S(1)}, bf16[128,2048]{1,0:T(8,128)(2,1)S(1)}, u32[]{:S(2)}, u32[]{:S(2)}) collective-permute-start(bf16[128,2048]{1,0:T(8,128)(2,1)S(1)} %first_block_rest.1.b_ref), channel_id=1, source_target_pairs={{0,1},{3,2},{4,5},{7,6},{8,9},{11,10},{12,13},{15,14},{16,17},{19,... | collective-permute-start | bytes 1572872 | tf_op jit(solution)/shard_map/ppermute | solution.py:353
  67.2 20.0 %collective-permute-start.6 = (bf16[128,2048]{1,0:T(8,128)(2,1)S(1)}, bf16[128,2048]{1,0:T(8,128)(2,1)S(1)}, u32[]{:S(2)}, u32[]{:S(2)}) collective-permute-start(bf16[128,2048]{1,0:T(8,128)(2,1)S(1)} %get-tuple-element.53), channel_id=1, source_target_pairs={{0,1},{1,2},{4,5},{5,6},{8,9},{9,10},{12,13},{13,14},{16,17},{17,1... | collective-permute-start | bytes 1572872 | tf_op jit(solution)/shard_map/ppermute | solution.py:357
  69.5 17.7 %collective-permute-start.7 = (bf16[128,2048]{1,0:T(8,128)(2,1)S(1)}, bf16[128,2048]{1,0:T(8,128)(2,1)S(1)}, u32[]{:S(2)}, u32[]{:S(2)}) collective-permute-start(bf16[128,2048]{1,0:T(8,128)(2,1)S(1)} %get-tuple-element.54), channel_id=1, source_target_pairs={{2,1},{3,2},{6,5},{7,6},{10,9},{11,10},{14,13},{15,14},{18,17},{19... | collective-permute-start | bytes 1572872 | tf_op jit(solution)/shard_map/ppermute | solution.py:358
  76.3 22.2 %collective-permute-start.11 = (bf16[128,2048]{1,0:T(8,128)(2,1)S(1)}, bf16[128,2048]{1,0:T(8,128)(2,1)S(1)}, u32[]{:S(2)}, u32[]{:S(2)}) collective-permute-start(bf16[128,2048]{1,0:T(8,128)(2,1)S(1)} %get-tuple-element.57), channel_id=1, source_target_pairs={{0,1},{1,2},{4,5},{5,6},{8,9},{9,10},{12,13},{13,14},{16,17},{17,1... | collective-permute-start | bytes 1572872 | tf_op jit(solution)/shard_map/ppermute | solution.py:357
  80.7 17.7 %collective-permute-start.12 = (bf16[128,2048]{1,0:T(8,128)(2,1)S(1)}, bf16[128,2048]{1,0:T(8,128)(2,1)S(1)}, u32[]{:S(2)}, u32[]{:S(2)}) collective-permute-start(bf16[128,2048]{1,0:T(8,128)(2,1)S(1)} %get-tuple-element.58), channel_id=1, source_target_pairs={{2,1},{3,2},{6,5},{7,6},{10,9},{11,10},{14,13},{15,14},{18,17},{19... | collective-permute-start | bytes 1572872 | tf_op jit(solution)/shard_map/ppermute | solution.py:358
  87.5 22.2 %collective-permute-start.8 = (bf16[128,2048]{1,0:T(8,128)(2,1)S(1)}, bf16[128,2048]{1,0:T(8,128)(2,1)S(1)}, u32[]{:S(2)}, u32[]{:S(2)}) collective-permute-start(bf16[128,2048]{1,0:T(8,128)(2,1)S(1)} %get-tuple-element.55), channel_id=1, source_target_pairs={{0,1},{1,2},{2,3},{4,5},{5,6},{6,7},{8,9},{9,10},{10,11},{12,13},{... | collective-permute-start | bytes 1572872 | tf_op jit(solution)/shard_map/ppermute | solution.py:357
  92.0 17.7 %collective-permute-start.9 = (bf16[128,2048]{1,0:T(8,128)(2,1)S(1)}, bf16[128,2048]{1,0:T(8,128)(2,1)S(1)}, u32[]{:S(2)}, u32[]{:S(2)}) collective-permute-start(bf16[128,2048]{1,0:T(8,128)(2,1)S(1)} %get-tuple-element.56), channel_id=1, source_target_pairs={{1,0},{2,1},{3,2},{5,4},{6,5},{7,6},{9,8},{10,9},{11,10},{13,12},{... | collective-permute-start | bytes 1572872 | tf_op jit(solution)/shard_map/ppermute | solution.py:358
  98.8 21.4 %collective-permute-start.13 = (bf16[128,2048]{1,0:T(8,128)(2,1)S(1)}, bf16[128,2048]{1,0:T(8,128)(2,1)S(1)}, u32[]{:S(2)}, u32[]{:S(2)}) collective-permute-start(bf16[128,2048]{1,0:T(8,128)(2,1)S(1)} %get-tuple-element.59), channel_id=1, source_target_pairs={{0,1},{1,2},{2,3},{4,5},{5,6},{6,7},{8,9},{9,10},{10,11},{12,13},{... | collective-permute-start | bytes 1572872 | tf_op jit(solution)/shard_map/ppermute | solution.py:357
  103.2 16.9 %collective-permute-start.14 = (bf16[128,2048]{1,0:T(8,128)(2,1)S(1)}, bf16[128,2048]{1,0:T(8,128)(2,1)S(1)}, u32[]{:S(2)}, u32[]{:S(2)}) collective-permute-start(bf16[128,2048]{1,0:T(8,128)(2,1)S(1)} %get-tuple-element.60), channel_id=1, source_target_pairs={{1,0},{2,1},{3,2},{5,4},{6,5},{7,6},{9,8},{10,9},{11,10},{13,12},{... | collective-permute-start | bytes 1572872 | tf_op jit(solution)/shard_map/ppermute | solution.py:358
  (3 other events, 4.6 us)

commit v3 on v2

--- a/solution.py
+++ b/solution.py
@@ -58,7 +58,7 @@
     return slice(chunk * size, (chunk + 1) * size)
 
 
-def state_kernel(groups, core_ref, x_hbm, b_hbm, step_hbm, decay_hbm, rhs_ref, inner_ref, outer_ref, send_ref, keep_ref,
+def state_kernel(groups, core_ref, here_ref, x_hbm, b_hbm, step_hbm, decay_hbm, rhs_ref, inner_ref, outer_ref, send_ref, keep_ref,
                  x_ref, b_ref, step_ref, decay_ref, semaphores):
     rows, channels = x_ref.shape
     heads = step_ref.shape[0]
@@ -152,7 +152,7 @@
     refs[-1][STATE:, :] = pieces(log, EXTRA)
 
 
-def last_kernel(core_ref, own_ref, sibling_ref, *refs):
+def last_kernel(core_ref, own_ref, sibling_ref, after_ref, *refs):
     keep_ref, send_ref = refs[-2:]
     chip = joined(refs[:-2])[0]
     for core, first, mine, other in ((0, own_ref, 0, 1), (1, sibling_ref, 1, 0)):
@@ -169,8 +169,9 @@
     return lax.dot_general(parts, spread, (((0,), (0,)), ((), ())), preferred_element_type=F32)
 
 
-def local_kernel(groups, x_hbm, gate_hbm, b_hbm, c_hbm, w_hbm, rhs_ref, inner_ref, outer_ref, skip_ref, mixed_ref, scale_ref,
-                 w_ref, x_ref, gate_ref, b_ref, c_ref, semaphores):
+def local_kernel(groups, x_hbm, gate_hbm, b_hbm, c_hbm, w_hbm, rhs_ref, inner_ref, outer_ref, skip_ref, after_ref, mixed_ref,
+                 scale_ref, w_ref, token_ref, x_ref, gate_ref, b_ref, c_ref, semaphores):
+    token_ref[...] = jnp.zeros_like(token_ref)
     heads = skip_ref.shape[1]
     rows, channels = x_ref.shape
     width = channels // groups
@@ -314,7 +315,7 @@
     return order + [b for b in range(count) if b not in order]
 
 
-def in_vmem(kernel, name, ins, outs, scratch=(), vmem=8, flops=1):
+def in_vmem(kernel, name, ins, outs, scratch=(), vmem=4, flops=1):
     vm = pl.BlockSpec(memory_space=pltpu.VMEM)
     specs, arrays = [], []
     for v in ins:
@@ -383,7 +384,7 @@
     rhs, inner, outer, send, own = in_vmem(
         partial(state_kernel, groups),
         "chunk_states",
-        (core, (x_in,), (b_in,), (step_size.T,), (log_decay.T,)),
+        (core, here, (x_in,), (b_in,), (step_size.T,), (log_decay.T,)),
         (((chunks * (CHUNK + STATE), channels), BF16), by_head, by_head, message, message),
         scratch=[
             pltpu.VMEM((rows, channels), BF16),
@@ -392,13 +393,12 @@
             pltpu.VMEM((heads, rows), F32),
             pltpu.SemaphoreType.DMA((3 + chunks,)),
         ],
-        vmem=20,
+        vmem=8,
     )
 
     swap = [(i, i ^ 1) for i in range(devices)]
     sibling = lax.ppermute(send, "ctx", swap)
     (pair,) = in_vmem(pair_kernel, "pair", (core, own, sibling), (message,))
-    x_late, pair = lax.optimization_barrier((x_in, pair))
     incoming, outgoing, distance = [], pair, 1
     while distance < chips:
         if incoming:
@@ -406,11 +406,11 @@
         for far in range(distance, min(chips, 4 * distance), distance):
             incoming.append(lax.ppermute(outgoing, "ctx", [(i, i + 2 * far) for i in range(devices - 2 * far)]))
         distance *= 4
-    mixed, scale, weight = in_vmem(
+    mixed, scale, weight, token = in_vmem(
         partial(local_kernel, groups),
         "local_part",
-        ((x_late,), (gate_z,), (b_in,), (c_in,), (out_weight,), rhs, inner, outer, skip.reshape(1, heads)),
-        (whole, whole, (out_weight.shape, BF16)),
+        ((x_in,), (gate_z,), (b_in,), (c_in,), (out_weight,), rhs, inner, outer, skip.reshape(1, heads), pair),
+        (whole, whole, (out_weight.shape, BF16), ((EXTRA, STATE), BF16)),
         scratch=[
             pltpu.VMEM((rows, channels), BF16),
             pltpu.VMEM((rows, channels), BF16),
@@ -418,12 +418,11 @@
             pltpu.VMEM((rows, groups * STATE), BF16),
             pltpu.SemaphoreType.DMA((2 + 2 * chunks + WEIGHT_COPIES,)),
         ],
-        vmem=20,
+        vmem=10,
         flops=8 * 10**9,
     )
-    mixed, scale, weight, *incoming = lax.optimization_barrier((mixed, scale, weight, *incoming))
     state = ((STATE, half), BF16)
-    keep, send = in_vmem(last_kernel, "incoming", (core, own, sibling, *incoming), (state, state))
+    keep, send = in_vmem(last_kernel, "incoming", (core, own, sibling, token, *incoming), (state, state))
     recv = lax.ppermute(send, "ctx", swap)
 
     first = ((size, columns // 2), BF16)
@@ -440,7 +439,7 @@
         (*inputs, first_a, first_b),
         (((rows, columns), BF16),),
         [whole_state, pltpu.VMEM((rows - size, channels), BF16)],
-        vmem=16,
+        vmem=6,
     )
     return line_reduce((first_a, first_b), partial_sums, here, size, columns)
 

time: 122 us -> 103 us (0.84)
  local copies, waits for them, and re-layouts: 20.5 us -> 0.66 us
    unnamed x24 -> x6, local copies, waits for them, and re-layouts: 20.5 us -> 0.66 us
    ppermute x2, starting transfers between devices: 7.02 us -> 4.84 us  [line_reduce(): lax.ppermute(first[half], 'tp', to_right + to_left)]
    ppermute x4, starting transfers between devices: 15.5 us -> 17.5 us  [line_reduce(): right[half] = lax.ppermute(send_right, 'tp', to_right)]
  transfers between devices with their start and end apart: 15 -> 15, of which waited for: 7 -> 8; matrix products, arithmetic and copies ran while one was open for 0% -> 0% of each run, Pallas kernels for 16% -> 19%
where the time goes in v3:
time: 103 us; the launch traced here: 102 us
  starting transfers between devices  36.4 us (35%)
  waiting for transfers between devices  36 us (35%)
  Pallas kernels  27.8 us (27%)
  other arithmetic  1.06 us (1%)
    pallas_call x13, Pallas kernels, in_vmem(): pl.pallas_call(kernel, in_specs=specs, out_specs=[vm for _ in outs], out_...  27.8 us
    ppermute x4, waiting for transfers between devices, line_reduce(): right[half] = lax.ppermute(send_right, 'tp', to_right)  26.5 us
    ppermute x4, starting transfers between devices, line_reduce(): right[half] = lax.ppermute(send_right, 'tp', to_right)  17.5 us
    ppermute x3, starting transfers between devices, on_device(): lax.ppermute(outgoing, 'ctx', [(i, i + 2 * far) for i in range(devices -...  9.52 us
    ppermute x2, waiting for transfers between devices, line_reduce(): lax.ppermute(first[half], 'tp', to_right + to_left)  5.87 us
    ppermute x2, starting transfers between devices, line_reduce(): lax.ppermute(first[half], 'tp', to_right + to_left)  4.84 us
    ppermute x4, starting transfers between devices, line_reduce(): left[half] = lax.ppermute(send_left, 'tp', to_left)  3.97 us
  transfers between devices with their start and end apart: 15, of which 8 were waited for; matrix products, arithmetic and copies ran while one was open for 0% of the time, Pallas kernels for 19%

profile of v3, /device:TPU:0, one launch (start us, length us, event | category | flops | bytes accessed | tf_op | source)
XLA Modules:
  0.0 102.2 jit_solution(13302403413588411393)
XLA Ops:
  0.0 5.0 %chunk_states.1 = (bf16[1024,2048]{1,0:T(8,128)(2,1)S(1)}, bf16[64,512]{1,0:T(8,128)(2,1)S(1)}, bf16[64,512]{1,0:T(8,128)(2,1)S(1)}, bf16[144,1024]{1,0:T(8,128)(2,1)S(1)}, bf16[144,1024]{1,0:T(8,128)(2,1)S(1)}) custom-call(s32[1]{0:T(128)} %bitcast.1.core_ref, s32[1]{0:T(128)} %bitcast.here_ref, bf16[512,2048]{1,0:T(8,128)(2,1)} %x_hbm.3, ...), custom_call_target="tpu_custom_call" | custom-call | flops 1 | bytes 1 | tf_op jit(solution)/shard_map/chunk_states/pallas_call | solution.py:331
  5.6 1.2 %collective-permute-done.sibling_ref = bf16[144,1024]{1,0:T(8,128)(2,1)S(1)} collective-permute-done((bf16[144,1024]{1,0:T(8,128)(2,1)S(1)}, bf16[144,1024]{1,0:T(8,128)(2,1)S(1)}, u32[]{:S(2)}, u32[]{:S(2)}) %collective-permute-start) | collective-permute-done | bytes 294944 | tf_op jit(solution)/shard_map/ppermute | solution.py:400
  6.9 4.8 %collective-permute-start.1 = (bf16[144,1024]{1,0:T(8,128)(2,1)S(1)}, bf16[144,1024]{1,0:T(8,128)(2,1)S(1)}, u32[]{:S(2)}, u32[]{:S(2)}) collective-permute-start(bf16[144,1024]{1,0:T(8,128)(2,1)S(1)} %pair.1.after_ref), channel_id=1, source_target_pairs={{0,8},{4,12},{8,16},{12,20},{16,24},{20,28},{1,9},{5,13},{9,17},{1... | collective-permute-start | bytes 884744 | tf_op jit(solution)/shard_map/ppermute | solution.py:407
  11.7 3.4 %collective-permute-start.2 = (bf16[144,1024]{1,0:T(8,128)(2,1)S(1)}, bf16[144,1024]{1,0:T(8,128)(2,1)S(1)}, u32[]{:S(2)}, u32[]{:S(2)}) collective-permute-start(bf16[144,1024]{1,0:T(8,128)(2,1)S(1)} %pair.1.after_ref), channel_id=1, source_target_pairs={{0,16},{4,20},{8,24},{12,28},{1,17},{5,21},{9,25},{13,29},{2,18},{... | collective-permute-start | bytes 884744 | tf_op jit(solution)/shard_map/ppermute | solution.py:407
  15.2 1.3 %collective-permute-start.3 = (bf16[144,1024]{1,0:T(8,128)(2,1)S(1)}, bf16[144,1024]{1,0:T(8,128)(2,1)S(1)}, u32[]{:S(2)}, u32[]{:S(2)}) collective-permute-start(bf16[144,1024]{1,0:T(8,128)(2,1)S(1)} %pair.1.after_ref), channel_id=1, source_target_pairs={{0,24},{4,28},{1,25},{5,29},{2,26},{6,30},{3,27},{7,31}} | collective-permute-start | bytes 884744 | tf_op jit(solution)/shard_map/ppermute | solution.py:407
  17.1 7.4 %local_part.1 = (f32[512,2048]{1,0:T(8,128)S(1)}, f32[512,2048]{1,0:T(8,128)S(1)}, bf16[2048,4096]{1,0:T(8,128)(2,1)S(1)}, bf16[16,128]{1,0:T(8,128)(2,1)S(1)}) custom-call(bf16[512,2048]{1,0:T(8,128)(2,1)} %x_hbm.3, bf16[512,2048]{1,0:T(8,128)(2,1)} %gate_hbm.1, bf16[512,256]{1,0:T(8,128)(2,1)} %b_hbm.3, bf16[512,256]{1,0:T(8,128)(2,1)} %c_ref.3, ...), custom_call_target="tpu_custom_call" | custom-call | flops 8000000000 | bytes 1 | tf_op jit(solution)/shard_map/local_part/pallas_call | solution.py:331
  25.9 1.5 %collective-permute-done.4.recv_ref = bf16[128,1024]{1,0:T(8,128)(2,1)S(1)} collective-permute-done((bf16[128,1024]{1,0:T(8,128)(2,1)S(1)}, bf16[128,1024]{1,0:T(8,128)(2,1)S(1)}, u32[]{:S(2)}, u32[]{:S(2)}) %collective-permute-start.4) | collective-permute-done | bytes 262176 | tf_op jit(solution)/shard_map/ppermute | solution.py:426
  27.4 2.3 %first_block.1 = (bf16[128,2048]{1,0:T(8,128)(2,1)S(1)}, bf16[128,2048]{1,0:T(8,128)(2,1)S(1)}) custom-call(s32[1]{0:T(128)} %bitcast.1.core_ref, s32[1]{0:T(128)} %bitcast.here_ref, f32[512,2048]{1,0:T(8,128)S(1)} %get-tuple-element.31.mixed_ref, f32[512,2048]{1,0:T(8,128)S(1)} %get-tuple-element.32.scale_ref, bf16[512,256]{1,0:T(8,128)(2,1)S(1)} %copy-done, ...), custom_call_target="tpu_custom_call" | custom-call | flops 1 | bytes 1 | tf_op jit(solution)/shard_map/first_block/pallas_call | solution.py:331
  29.8 3.5 %collective-permute-start.5 = (bf16[128,2048]{1,0:T(8,128)(2,1)S(1)}, bf16[128,2048]{1,0:T(8,128)(2,1)S(1)}, u32[]{:S(2)}, u32[]{:S(2)}) collective-permute-start(bf16[128,2048]{1,0:T(8,128)(2,1)S(1)} %get-tuple-element.37.a_ref), channel_id=1, source_target_pairs={{0,1},{3,2},{4,5},{7,6},{8,9},{11,10},{12,13},{15,14},{16,17},{19,... | collective-permute-start | bytes 1572872 | tf_op jit(solution)/shard_map/ppermute | solution.py:354
  33.3 1.8 %first_block_rest.1.b_ref = bf16[128,2048]{1,0:T(8,128)(2,1)S(1)} custom-call(bf16[128,2048]{1,0:T(8,128)(2,1)S(1)} %get-tuple-element.38.normed_ref, bf16[2048,4096]{1,0:T(8,128)(2,1)S(1)} %get-tuple-element.36.w_ref), custom_call_target="tpu_custom_call" | custom-call | flops 1 | bytes 1 | tf_op jit(solution)/shard_map/first_block_rest/pallas_call | solution.py:331
  35.1 1.3 %collective-permute-start.10 = (bf16[128,2048]{1,0:T(8,128)(2,1)S(1)}, bf16[128,2048]{1,0:T(8,128)(2,1)S(1)}, u32[]{:S(2)}, u32[]{:S(2)}) collective-permute-start(bf16[128,2048]{1,0:T(8,128)(2,1)S(1)} %first_block_rest.1.b_ref), channel_id=1, source_target_pairs={{0,1},{3,2},{4,5},{7,6},{8,9},{11,10},{12,13},{15,14},{16,17},{19,... | collective-permute-start | bytes 1572872 | tf_op jit(solution)/shard_map/ppermute | solution.py:354
  36.5 9.2 %other_blocks.1.sums_ref = bf16[512,4096]{1,0:T(8,128)(2,1)S(1)} custom-call(s32[1]{0:T(128)} %bitcast.1.core_ref, s32[1]{0:T(128)} %bitcast.here_ref, f32[512,2048]{1,0:T(8,128)S(1)} %get-tuple-element.31.mixed_ref, f32[512,2048]{1,0:T(8,128)S(1)} %get-tuple-element.32.scale_ref, bf16[512,256]{1,0:T(8,128)(2,1)S(1)} %copy-done, ...), custom_call_target="tpu_custom_call" | custom-call | flops 1 | bytes 1 | tf_op jit(solution)/shard_map/other_blocks/pallas_call | solution.py:331
  45.9 4.3 %collective-permute-start.6 = (bf16[128,2048]{1,0:T(8,128)(2,1)S(1)}, bf16[128,2048]{1,0:T(8,128)(2,1)S(1)}, u32[]{:S(2)}, u32[]{:S(2)}) collective-permute-start(bf16[128,2048]{1,0:T(8,128)(2,1)S(1)} %get-tuple-element.39), channel_id=1, source_target_pairs={{0,1},{1,2},{4,5},{5,6},{8,9},{9,10},{12,13},{13,14},{16,17},{17,1... | collective-permute-start | bytes 1572872 | tf_op jit(solution)/shard_map/ppermute | solution.py:358
  50.9 5.9 %collective-permute-done.10.right_ref.left_ref = bf16[128,2048]{1,0:T(8,128)(2,1)S(1)} collective-permute-done((bf16[128,2048]{1,0:T(8,128)(2,1)S(1)}, bf16[128,2048]{1,0:T(8,128)(2,1)S(1)}, u32[]{:S(2)}, u32[]{:S(2)}) %collective-permute-start.10) | collective-permute-done | bytes 524320 | tf_op jit(solution)/shard_map/ppermute | solution.py:354
  57.0 4.4 %collective-permute-start.11 = (bf16[128,2048]{1,0:T(8,128)(2,1)S(1)}, bf16[128,2048]{1,0:T(8,128)(2,1)S(1)}, u32[]{:S(2)}, u32[]{:S(2)}) collective-permute-start(bf16[128,2048]{1,0:T(8,128)(2,1)S(1)} %get-tuple-element.43), channel_id=1, source_target_pairs={{0,1},{1,2},{4,5},{5,6},{8,9},{9,10},{12,13},{13,14},{16,17},{17,1... | collective-permute-start | bytes 1572872 | tf_op jit(solution)/shard_map/ppermute | solution.py:358
  62.1 5.9 %collective-permute-done.6.right_ref = bf16[128,2048]{1,0:T(8,128)(2,1)S(1)} collective-permute-done((bf16[128,2048]{1,0:T(8,128)(2,1)S(1)}, bf16[128,2048]{1,0:T(8,128)(2,1)S(1)}, u32[]{:S(2)}, u32[]{:S(2)}) %collective-permute-start.6) | collective-permute-done | bytes 524320 | tf_op jit(solution)/shard_map/ppermute | solution.py:358
  68.3 4.4 %collective-permute-start.8 = (bf16[128,2048]{1,0:T(8,128)(2,1)S(1)}, bf16[128,2048]{1,0:T(8,128)(2,1)S(1)}, u32[]{:S(2)}, u32[]{:S(2)}) collective-permute-start(bf16[128,2048]{1,0:T(8,128)(2,1)S(1)} %get-tuple-element.41), channel_id=1, source_target_pairs={{0,1},{1,2},{2,3},{4,5},{5,6},{6,7},{8,9},{9,10},{10,11},{12,13},{... | collective-permute-start | bytes 1572872 | tf_op jit(solution)/shard_map/ppermute | solution.py:358
  72.7 1.3 %collective-permute-start.9 = (bf16[128,2048]{1,0:T(8,128)(2,1)S(1)}, bf16[128,2048]{1,0:T(8,128)(2,1)S(1)}, u32[]{:S(2)}, u32[]{:S(2)}) collective-permute-start(bf16[128,2048]{1,0:T(8,128)(2,1)S(1)} %get-tuple-element.42), channel_id=1, source_target_pairs={{1,0},{2,1},{3,2},{5,4},{6,5},{7,6},{9,8},{10,9},{11,10},{13,12},{... | collective-permute-start | bytes 1572872 | tf_op jit(solution)/shard_map/ppermute | solution.py:359
  74.0 5.2 %collective-permute-done.11.right_ref = bf16[128,2048]{1,0:T(8,128)(2,1)S(1)} collective-permute-done((bf16[128,2048]{1,0:T(8,128)(2,1)S(1)}, bf16[128,2048]{1,0:T(8,128)(2,1)S(1)}, u32[]{:S(2)}, u32[]{:S(2)}) %collective-permute-start.11) | collective-permute-done | bytes 524320 | tf_op jit(solution)/shard_map/ppermute | solution.py:358
  79.5 4.4 %collective-permute-start.13 = (bf16[128,2048]{1,0:T(8,128)(2,1)S(1)}, bf16[128,2048]{1,0:T(8,128)(2,1)S(1)}, u32[]{:S(2)}, u32[]{:S(2)}) collective-permute-start(bf16[128,2048]{1,0:T(8,128)(2,1)S(1)} %get-tuple-element.45), channel_id=1, source_target_pairs={{0,1},{1,2},{2,3},{4,5},{5,6},{6,7},{8,9},{9,10},{10,11},{12,13},{... | collective-permute-start | bytes 1572872 | tf_op jit(solution)/shard_map/ppermute | solution.py:358
  84.0 1.3 %collective-permute-start.14 = (bf16[128,2048]{1,0:T(8,128)(2,1)S(1)}, bf16[128,2048]{1,0:T(8,128)(2,1)S(1)}, u32[]{:S(2)}, u32[]{:S(2)}) collective-permute-start(bf16[128,2048]{1,0:T(8,128)(2,1)S(1)} %get-tuple-element.46), channel_id=1, source_target_pairs={{1,0},{2,1},{3,2},{5,4},{6,5},{7,6},{9,8},{10,9},{11,10},{13,12},{... | collective-permute-start | bytes 1572872 | tf_op jit(solution)/shard_map/ppermute | solution.py:359
  85.3 5.2 %collective-permute-done.8.right_ref = bf16[128,2048]{1,0:T(8,128)(2,1)S(1)} collective-permute-done((bf16[128,2048]{1,0:T(8,128)(2,1)S(1)}, bf16[128,2048]{1,0:T(8,128)(2,1)S(1)}, u32[]{:S(2)}, u32[]{:S(2)}) %collective-permute-start.8) | collective-permute-done | bytes 524320 | tf_op jit(solution)/shard_map/ppermute | solution.py:358
  90.7 10.2 %collective-permute-done.13.right_ref = bf16[128,2048]{1,0:T(8,128)(2,1)S(1)} collective-permute-done((bf16[128,2048]{1,0:T(8,128)(2,1)S(1)}, bf16[128,2048]{1,0:T(8,128)(2,1)S(1)}, u32[]{:S(2)}, u32[]{:S(2)}) %collective-permute-start.13) | collective-permute-done | bytes 524320 | tf_op jit(solution)/shard_map/ppermute | solution.py:358
  101.1 1.1 %pad_maximum_fusion = bf16[128,4096]{1,0:T(8,128)(2,1)} fusion(bf16[128,2048]{1,0:T(8,128)(2,1)S(1)} %sum_up.3, bf16[128,2048]{1,0:T(8,128)(2,1)S(1)} %sum_up.2), kind=kLoop, calls=%fused_computation | loop fusion | flops 2097152 | bytes 2097152 | tf_op jit(solution)/shard_map/concatenate | solution.py:364
  (26 shorter events, 5.6 us)
Async XLA Ops:
  5.1 1.7 %collective-permute-start = (bf16[144,1024]{1,0:T(8,128)(2,1)S(1)}, bf16[144,1024]{1,0:T(8,128)(2,1)S(1)}, u32[]{:S(2)}, u32[]{:S(2)}) collective-permute-start(bf16[144,1024]{1,0:T(8,128)(2,1)S(1)} %get-tuple-element.30), channel_id=1, source_target_pairs={{0,4},{4,0},{8,12},{12,8},{16,20},{20,16},{24,28},{28,24},{1,5},{5... | collective-permute-start | bytes 884744 | tf_op jit(solution)/shard_map/ppermute | solution.py:400
  6.9 17.6 %collective-permute-start.1 = (bf16[144,1024]{1,0:T(8,128)(2,1)S(1)}, bf16[144,1024]{1,0:T(8,128)(2,1)S(1)}, u32[]{:S(2)}, u32[]{:S(2)}) collective-permute-start(bf16[144,1024]{1,0:T(8,128)(2,1)S(1)} %pair.1.after_ref), channel_id=1, source_target_pairs={{0,8},{4,12},{8,16},{12,20},{16,24},{20,28},{1,9},{5,13},{9,17},{1... | collective-permute-start | bytes 884744 | tf_op jit(solution)/shard_map/ppermute | solution.py:407
  11.7 13.8 %collective-permute-start.2 = (bf16[144,1024]{1,0:T(8,128)(2,1)S(1)}, bf16[144,1024]{1,0:T(8,128)(2,1)S(1)}, u32[]{:S(2)}, u32[]{:S(2)}) collective-permute-start(bf16[144,1024]{1,0:T(8,128)(2,1)S(1)} %pair.1.after_ref), channel_id=1, source_target_pairs={{0,16},{4,20},{8,24},{12,28},{1,17},{5,21},{9,25},{13,29},{2,18},{... | collective-permute-start | bytes 884744 | tf_op jit(solution)/shard_map/ppermute | solution.py:407
  15.2 10.3 %collective-permute-start.3 = (bf16[144,1024]{1,0:T(8,128)(2,1)S(1)}, bf16[144,1024]{1,0:T(8,128)(2,1)S(1)}, u32[]{:S(2)}, u32[]{:S(2)}) collective-permute-start(bf16[144,1024]{1,0:T(8,128)(2,1)S(1)} %pair.1.after_ref), channel_id=1, source_target_pairs={{0,24},{4,28},{1,25},{5,29},{2,26},{6,30},{3,27},{7,31}} | collective-permute-start | bytes 884744 | tf_op jit(solution)/shard_map/ppermute | solution.py:407
  16.5 0.7 copy-start.2
  17.1 10.3 %copy-start = (bf16[512,256]{1,0:T(8,128)(2,1)S(1)}, bf16[512,256]{1,0:T(8,128)(2,1)}, u32[]{:S(2)}) copy-start(bf16[512,256]{1,0:T(8,128)(2,1)} %c_ref.3) | copy-start | bytes 786436
  17.1 10.3 %copy-start.1 = (f32[2048]{0:T(1024)S(1)}, f32[2048]{0:T(1024)}, u32[]{:S(2)}) copy-start(f32[2048]{0:T(1024)} %param.16) | copy-start | bytes 24580
  25.8 1.6 %collective-permute-start.4 = (bf16[128,1024]{1,0:T(8,128)(2,1)S(1)}, bf16[128,1024]{1,0:T(8,128)(2,1)S(1)}, u32[]{:S(2)}, u32[]{:S(2)}) collective-permute-start(bf16[128,1024]{1,0:T(8,128)(2,1)S(1)} %get-tuple-element.35), channel_id=1, source_target_pairs={{0,4},{4,0},{8,12},{12,8},{16,20},{20,16},{24,28},{28,24},{1,5},{5... | collective-permute-start | bytes 786440 | tf_op jit(solution)/shard_map/ppermute | solution.py:426
  29.8 15.9 %collective-permute-start.5 = (bf16[128,2048]{1,0:T(8,128)(2,1)S(1)}, bf16[128,2048]{1,0:T(8,128)(2,1)S(1)}, u32[]{:S(2)}, u32[]{:S(2)}) collective-permute-start(bf16[128,2048]{1,0:T(8,128)(2,1)S(1)} %get-tuple-element.37.a_ref), channel_id=1, source_target_pairs={{0,1},{3,2},{4,5},{7,6},{8,9},{11,10},{12,13},{15,14},{16,17},{19,... | collective-permute-start | bytes 1572872 | tf_op jit(solution)/shard_map/ppermute | solution.py:354
  35.1 21.6 %collective-permute-start.10 = (bf16[128,2048]{1,0:T(8,128)(2,1)S(1)}, bf16[128,2048]{1,0:T(8,128)(2,1)S(1)}, u32[]{:S(2)}, u32[]{:S(2)}) collective-permute-start(bf16[128,2048]{1,0:T(8,128)(2,1)S(1)} %first_block_rest.1.b_ref), channel_id=1, source_target_pairs={{0,1},{3,2},{4,5},{7,6},{8,9},{11,10},{12,13},{15,14},{16,17},{19,... | collective-permute-start | bytes 1572872 | tf_op jit(solution)/shard_map/ppermute | solution.py:354
  45.9 22.1 %collective-permute-start.6 = (bf16[128,2048]{1,0:T(8,128)(2,1)S(1)}, bf16[128,2048]{1,0:T(8,128)(2,1)S(1)}, u32[]{:S(2)}, u32[]{:S(2)}) collective-permute-start(bf16[128,2048]{1,0:T(8,128)(2,1)S(1)} %get-tuple-element.39), channel_id=1, source_target_pairs={{0,1},{1,2},{4,5},{5,6},{8,9},{9,10},{12,13},{13,14},{16,17},{17,1... | collective-permute-start | bytes 1572872 | tf_op jit(solution)/shard_map/ppermute | solution.py:358
  50.2 17.8 %collective-permute-start.7 = (bf16[128,2048]{1,0:T(8,128)(2,1)S(1)}, bf16[128,2048]{1,0:T(8,128)(2,1)S(1)}, u32[]{:S(2)}, u32[]{:S(2)}) collective-permute-start(bf16[128,2048]{1,0:T(8,128)(2,1)S(1)} %get-tuple-element.40), channel_id=1, source_target_pairs={{2,1},{3,2},{6,5},{7,6},{10,9},{11,10},{14,13},{15,14},{18,17},{19... | collective-permute-start | bytes 1572872 | tf_op jit(solution)/shard_map/ppermute | solution.py:359
  57.0 22.2 %collective-permute-start.11 = (bf16[128,2048]{1,0:T(8,128)(2,1)S(1)}, bf16[128,2048]{1,0:T(8,128)(2,1)S(1)}, u32[]{:S(2)}, u32[]{:S(2)}) collective-permute-start(bf16[128,2048]{1,0:T(8,128)(2,1)S(1)} %get-tuple-element.43), channel_id=1, source_target_pairs={{0,1},{1,2},{4,5},{5,6},{8,9},{9,10},{12,13},{13,14},{16,17},{17,1... | collective-permute-start | bytes 1572872 | tf_op jit(solution)/shard_map/ppermute | solution.py:358
  61.4 17.8 %collective-permute-start.12 = (bf16[128,2048]{1,0:T(8,128)(2,1)S(1)}, bf16[128,2048]{1,0:T(8,128)(2,1)S(1)}, u32[]{:S(2)}, u32[]{:S(2)}) collective-permute-start(bf16[128,2048]{1,0:T(8,128)(2,1)S(1)} %get-tuple-element.44), channel_id=1, source_target_pairs={{2,1},{3,2},{6,5},{7,6},{10,9},{11,10},{14,13},{15,14},{18,17},{19... | collective-permute-start | bytes 1572872 | tf_op jit(solution)/shard_map/ppermute | solution.py:359
  68.3 22.2 %collective-permute-start.8 = (bf16[128,2048]{1,0:T(8,128)(2,1)S(1)}, bf16[128,2048]{1,0:T(8,128)(2,1)S(1)}, u32[]{:S(2)}, u32[]{:S(2)}) collective-permute-start(bf16[128,2048]{1,0:T(8,128)(2,1)S(1)} %get-tuple-element.41), channel_id=1, source_target_pairs={{0,1},{1,2},{2,3},{4,5},{5,6},{6,7},{8,9},{9,10},{10,11},{12,13},{... | collective-permute-start | bytes 1572872 | tf_op jit(solution)/shard_map/ppermute | solution.py:358
  72.7 17.7 %collective-permute-start.9 = (bf16[128,2048]{1,0:T(8,128)(2,1)S(1)}, bf16[128,2048]{1,0:T(8,128)(2,1)S(1)}, u32[]{:S(2)}, u32[]{:S(2)}) collective-permute-start(bf16[128,2048]{1,0:T(8,128)(2,1)S(1)} %get-tuple-element.42), channel_id=1, source_target_pairs={{1,0},{2,1},{3,2},{5,4},{6,5},{7,6},{9,8},{10,9},{11,10},{13,12},{... | collective-permute-start | bytes 1572872 | tf_op jit(solution)/shard_map/ppermute | solution.py:359
  79.5 21.4 %collective-permute-start.13 = (bf16[128,2048]{1,0:T(8,128)(2,1)S(1)}, bf16[128,2048]{1,0:T(8,128)(2,1)S(1)}, u32[]{:S(2)}, u32[]{:S(2)}) collective-permute-start(bf16[128,2048]{1,0:T(8,128)(2,1)S(1)} %get-tuple-element.45), channel_id=1, source_target_pairs={{0,1},{1,2},{2,3},{4,5},{5,6},{6,7},{8,9},{9,10},{10,11},{12,13},{... | collective-permute-start | bytes 1572872 | tf_op jit(solution)/shard_map/ppermute | solution.py:358
  84.0 16.9 %collective-permute-start.14 = (bf16[128,2048]{1,0:T(8,128)(2,1)S(1)}, bf16[128,2048]{1,0:T(8,128)(2,1)S(1)}, u32[]{:S(2)}, u32[]{:S(2)}) collective-permute-start(bf16[128,2048]{1,0:T(8,128)(2,1)S(1)} %get-tuple-element.46), channel_id=1, source_target_pairs={{1,0},{2,1},{3,2},{5,4},{6,5},{7,6},{9,8},{10,9},{11,10},{13,12},{... | collective-permute-start | bytes 1572872 | tf_op jit(solution)/shard_map/ppermute | solution.py:359

commit v4 on v3

v4 whole, which is shorter than its diff:
```python
from functools import partial

import jax
import jax.numpy as jnp
from jax import lax
from jax.experimental import pallas as pl
from jax.experimental.pallas import tpu as pltpu
from jax.sharding import PartitionSpec as P

HEAD_DIM = 64
STATE = 128
CHUNK = 128
MIDDLE = CHUNK // 2 - 1
EXTRA = 16
COLUMN_TILE = 512
HALVES = 2
WEIGHT_COPIES = 8
SUM_COPIES = 4
F32 = jnp.float32
BF16 = jnp.bfloat16


def dot(a, b):
    return jnp.dot(a, b, preferred_element_type=F32)


def dot_exact(a, b):
    return jnp.dot(a, b, preferred_element_type=F32, precision=lax.Precision.HIGHEST)


def head_map(channels):
    head = lax.broadcasted_iota(jnp.int32, (128, channels), 0) & 63
    place = lax.broadcasted_iota(jnp.int32, (128, channels), 1) >> 6
    return jnp.where(head == place, 1.0, 0.0).astype(BF16)


def padded(values):
    return jnp.concatenate([values, jnp.zeros((64 - values.shape[0], values.shape[1]), F32)], axis=0)


def by_row(values):
    high = values.astype(BF16).astype(F32)
    return jnp.transpose(jnp.concatenate([padded(high), padded(values - high)], axis=0)).astype(BF16)


def pieces(values, axis):
    first = values.astype(BF16).astype(F32)
    second = (values - first).astype(BF16).astype(F32)
    third = values - first - second
    shape = (EXTRA, values.shape[1]) if axis == 0 else (values.shape[0], 128)
    at = lax.broadcasted_iota(jnp.int32, shape, axis)
    return jnp.where(at == 0, first, jnp.where(at == 1, second, jnp.where(at == 2, third, 0.0)))


def running_sums(decay):
    row = lax.broadcasted_iota(jnp.int32, (CHUNK, CHUNK), 0)
    column = lax.broadcasted_iota(jnp.int32, (CHUNK, CHUNK), 1)
    upper = jnp.where(row <= column, 1.0, 0.0)
    return [dot_exact(decay[:, rows_of(n)], upper) for n in range(decay.shape[1] // CHUNK)]


def load(pairs, semaphores):
    copies = [pltpu.make_async_copy(src, dst, semaphores.at[n]) for n, (src, dst) in enumerate(pairs)]
    for copy in copies:
        copy.start()
    return copies


def rows_of(chunk, size=CHUNK):
    return slice(chunk * size, (chunk + 1) * size)


def put_message(ref, state, logs):
    for j in range(state.shape[1] // 128):
        ref[j * STATE : (j + 1) * STATE, :] = state[:, j * 128 : (j + 1) * 128].astype(BF16)
    ref[state.shape[1] :, :] = logs.astype(BF16)


def state_of(ref):
    count = (ref.shape[0] - EXTRA) // STATE
    return jnp.concatenate([ref[j * STATE : (j + 1) * STATE, :] for j in range(count)], axis=1).astype(F32)


def logs_of(ref):
    return ref[ref.shape[0] - EXTRA :, :]


def wide_log(logs, spread):
    return jnp.sum(dot(logs, spread), axis=0, keepdims=True)


def end_state(groups, half, x_ref, b_ref, step_ref, decay_ref, weighted, message_ref, spread):
    rows, width = weighted.shape
    heads = width // HEAD_DIM
    of_heads = pl.ds(pl.multiple_of(half * heads, heads), heads)
    of_channels = pl.ds(pl.multiple_of(half * width, width), width)
    of_group = pl.ds(pl.multiple_of((half * groups // 2) * STATE, STATE), STATE)
    before, running = jnp.zeros((heads, 1), F32), []
    for sums in running_sums(decay_ref[of_heads, :]):
        running.append(before + sums)
        before = before + sums[:, CHUNK - 1 :]
    for n, sums in enumerate(running):
        here = rows_of(n)
        factor = dot(by_row(step_ref[of_heads, here] * jnp.exp(before - sums)), spread)
        weighted[here, :] = (x_ref[here, of_channels].astype(F32) * factor).astype(BF16)
    state = lax.dot_general(
        b_ref[:, of_group], weighted[...], (((0,), (0,)), ((), ())), preferred_element_type=F32
    )
    logs = jnp.concatenate([pieces(before, 1), jnp.zeros((128 - heads, 128), F32)], axis=0)
    put_message(message_ref, state, jnp.transpose(logs)[:EXTRA])


def send_kernel(groups, core_ref, here_ref, x_hbm, b_hbm, step_hbm, decay_hbm, send_ref, x_ref, b_ref, step_ref, decay_ref,
                spread_ref, weighted, semaphores):
    width = weighted.shape[1]
    other = 1 - core_ref[0]
    of_channels = [pl.ds(pl.multiple_of(half * width, width), width) for half in (other, core_ref[0])]
    copies = load(
        [(decay_hbm, decay_ref), (step_hbm, step_ref), (b_hbm, b_ref)]
        + [(x_hbm.at[:, cut], x_ref.at[:, cut]) for cut in of_channels],
        semaphores,
    )
    spread = head_map(width)
    spread_ref[...] = spread
    for copy in copies[:4]:
        copy.wait()
    end_state(groups, other, x_ref, b_ref, step_ref, decay_ref, weighted, send_ref, spread)
    copies[4].wait()


def keep_kernel(groups, core_ref, x_ref, b_ref, step_ref, decay_ref, spread_ref, keep_ref, weighted):
    end_state(groups, core_ref[0], x_ref, b_ref, step_ref, decay_ref, weighted, keep_ref, spread_ref[...])


def pair_kernel(core_ref, spread_ref, own_ref, sibling_ref, pair_ref):
    spread = spread_ref[...]
    own_log, sibling_log = wide_log(logs_of(own_ref), spread), wide_log(logs_of(sibling_ref), spread)
    early = core_ref[0] == 0
    own_scale = jnp.where(early, jnp.exp(sibling_log), 1.0)
    sibling_scale = jnp.where(early, 1.0, jnp.exp(own_log))
    logs = logs_of(own_ref).astype(F32) + logs_of(sibling_ref).astype(F32)
    logs = pieces(jnp.sum(logs, axis=0, keepdims=True), 0)
    put_message(pair_ref, state_of(own_ref) * own_scale + state_of(sibling_ref) * sibling_scale, logs)


def joined(stretches, spread):
    total, log = state_of(stretches[0]), 0.0
    for late, early in zip(stretches, stretches[1:]):
        log = log + wide_log(logs_of(late), spread)
        total = total + state_of(early) * jnp.exp(log)
    return total


def join_kernel(spread_ref, *refs):
    logs = sum(jnp.sum(logs_of(ref).astype(F32), axis=0, keepdims=True) for ref in refs[:-1])
    put_message(refs[-1], joined(refs[:-1], spread_ref[...]), pieces(logs, 0))


def last_kernel(core_ref, after_ref, spread_ref, own_ref, sibling_ref, *refs):
    keep_ref, send_ref = refs[-2:]
    spread = spread_ref[...]
    chip = joined(refs[:-2], spread)
    for core, first, mine, other in ((0, own_ref, 0, 1), (1, sibling_ref, 1, 0)):

        @pl.when(core_ref[0] == core)
        def _():
            after = chip * jnp.exp(wide_log(logs_of(first), spread)) + state_of(first)
            both = (chip.astype(BF16), after.astype(BF16))
            keep_ref[...] = both[mine]
            send_ref[...] = both[other]


def local_kernel(groups, gate_hbm, c_hbm, w_hbm, x_ref, b_ref, step_ref, decay_ref, skip_ref, after_ref, mixed_ref, scale_ref,
                 w_ref, c_ref, token_ref, gate_ref, semaphores):
    token_ref[...] = jnp.zeros_like(token_ref)
    rows, channels = x_ref.shape
    heads = step_ref.shape[0]
    width = channels // groups
    chunks = rows // CHUNK
    small = load([(c_hbm, c_ref)], semaphores)
    gates = [(gate_hbm.at[rows_of(n), :], gate_ref.at[rows_of(n), :]) for n in range(chunks)]
    gates = load(gates, semaphores.at[pl.ds(1, chunks)])
    size = channels // WEIGHT_COPIES
    weights = [(w_hbm.at[rows_of(n, size), :], w_ref.at[rows_of(n, size), :]) for n in range(WEIGHT_COPIES)]
    weights = load(weights, semaphores.at[pl.ds(1 + chunks, WEIGHT_COPIES)])

    spread = head_map(channels)
    row = lax.broadcasted_iota(jnp.int32, (CHUNK, CHUNK), 0)
    column = lax.broadcasted_iota(jnp.int32, (CHUNK, CHUNK), 1)
    lane = lax.broadcasted_iota(jnp.int32, (heads, CHUNK), 1)
    skip = jnp.concatenate([pieces(skip_ref[...], 0), jnp.zeros((EXTRA, 128 - heads), F32)], axis=1)
    skip = wide_log(skip.astype(BF16), spread)
    before = jnp.zeros((heads, 1), F32)
    state = [jnp.zeros((STATE, width), F32)] * groups
    small[0].wait()
    for n, running in enumerate(running_sums(decay_ref[...])):
        here = rows_of(n)
        middle, total = running[:, MIDDLE : MIDDLE + 1], running[:, CHUNK - 1 :]
        inner = running - middle
        factors = jnp.exp(jnp.where(lane == 0, total, jnp.where(lane == 1, total - middle, middle)))
        factors = jnp.concatenate(
            [
                by_row(step_ref[:, here] * jnp.exp(-inner)),
                by_row(jnp.exp(inner)),
                by_row(jnp.exp(before + running)),
                by_row(factors)[:EXTRA],
            ],
            axis=0,
        )
        before = before + total
        gates[n].wait()
        for g in range(groups):
            cut = slice(g * width, (g + 1) * width)
            part = slice(g * STATE, (g + 1) * STATE)
            wide = dot(factors, spread[:, cut])
            to_state, to_fresh, to_middle = (wide[3 * CHUNK + n : 3 * CHUNK + n + 1] for n in range(3))
            x = x_ref[here, cut].astype(F32)
            weighted = (x * wide[:CHUNK]).astype(BF16)
            started = jnp.concatenate([weighted, (state[g] * to_middle).astype(BF16)], axis=0)
            scores = lax.dot_general(
                c_ref[here, part], b_ref[here, part], (((1,), (1,)), ((), ())), preferred_element_type=F32
            )
            scores = jnp.where(row >= column, scores, 0.0).astype(BF16)
            within = dot(jnp.concatenate([scores, c_ref[here, part]], axis=1), started)
            if n < chunks - 1:
                fresh = lax.dot_general(
                    b_ref[here, part], weighted, (((0,), (0,)), ((), ())), preferred_element_type=F32
                )
                state[g] = state[g] * to_state + fresh * to_fresh
            gate = gate_ref[here, cut].astype(F32)
            gate = gate / (1.0 + jnp.exp(-gate))
            mixed_ref[here, cut] = (within * wide[CHUNK : 2 * CHUNK] + x * skip[:, cut]) * gate
            scale_ref[here, cut] = wide[2 * CHUNK : 3 * CHUNK] * gate
    for copy in weights:
        copy.wait()


def norm_rows(groups, state, mixed, scale, c_rows, gain):
    width = mixed.shape[1] // groups
    parts = []
    for g in range(groups):
        cut = slice(g * width, (g + 1) * width)
        carried = dot(c_rows[:, g * STATE : (g + 1) * STATE], state[:, cut])
        whole = mixed[:, cut] + scale[:, cut] * carried
        meansq = jnp.mean(whole * whole, axis=1, keepdims=True)
        parts.append((whole * lax.rsqrt(meansq + 1e-05) * gain[:, cut]).astype(BF16))
    return parts


def fill_state(core_ref, keep_ref, recv_ref, state):
    half = keep_ref.shape[1]
    for core in range(2):

        @pl.when(core_ref[0] == core)
        def _():
            state[:, core * half : (core + 1) * half] = keep_ref[...]
            state[:, (1 - core) * half : (2 - core) * half] = recv_ref[...]


def block_at(here, position, count, size):
    block = 0
    for i in range(count):
        block = jnp.where(here == i, block_order(i, count)[position], block)
    return pl.ds(pl.multiple_of(block * size, size), size)


def first_kernel(groups, count, core_ref, here_ref, mixed_ref, scale_ref, c_ref, keep_ref, recv_ref, gain_ref, w_ref, out_ref,
                 normed_ref, state):
    fill_state(core_ref, keep_ref, recv_ref, state)
    width = normed_ref.shape[1] // groups
    here = block_at(here_ref[0], 0, count, normed_ref.shape[0])
    rows = norm_rows(groups, state, mixed_ref.at[here, :], scale_ref.at[here, :], c_ref.at[here, :], gain_ref)
    for g, part in enumerate(rows):
        normed_ref[:, g * width : (g + 1) * width] = part

    @pl.loop(0, out_ref.shape[1] // COLUMN_TILE)
    def _(j):
        cut = pl.ds(pl.multiple_of(j * COLUMN_TILE, COLUMN_TILE), COLUMN_TILE)
        out_ref[:, cut] = dot(normed_ref[...], w_ref[:, cut]).astype(BF16)


def second_kernel(normed_ref, w_ref, out_ref):
    start = w_ref.shape[1] - out_ref.shape[1]

    @pl.loop(0, out_ref.shape[1] // COLUMN_TILE)
    def _(j):
        cut = pl.ds(pl.multiple_of(j * COLUMN_TILE, COLUMN_TILE), COLUMN_TILE)
        from_ = pl.ds(pl.multiple_of(start + j * COLUMN_TILE, COLUMN_TILE), COLUMN_TILE)
        out_ref[:, cut] = dot(normed_ref[...], w_ref[:, from_]).astype(BF16)


def rest_kernel(groups, count, core_ref, here_ref, mixed_ref, scale_ref, c_ref, keep_ref, recv_ref, gain_ref, w_ref, a_ref,
                b_ref, out_ref, state, normed):
    size, half = a_ref.shape
    blocks = [block_at(here_ref[0], n, count, size) for n in range(count)]
    out_ref[blocks[0], :half] = a_ref[...]
    out_ref[blocks[0], half:] = b_ref[...]
    fill_state(core_ref, keep_ref, recv_ref, state)
    width = normed.shape[1] // groups
    for n in range(1, count):
        here = blocks[n]
        rows = norm_rows(groups, state, mixed_ref.at[here, :], scale_ref.at[here, :], c_ref.at[here, :], gain_ref)
        for g, part in enumerate(rows):
            normed[(n - 1) * size : n * size, g * width : (g + 1) * width] = part

    @pl.loop(0, out_ref.shape[1] // COLUMN_TILE)
    def _(j):
        cut = pl.ds(pl.multiple_of(j * COLUMN_TILE, COLUMN_TILE), COLUMN_TILE)
        product = dot(normed[...], w_ref[:, cut]).astype(BF16)
        for n in range(1, count):
            out_ref[blocks[n], cut] = product[(n - 1) * size : n * size]


def pass_kernel(count, step, column, here_ref, right_ref, left_ref, sums_ref, to_right_ref, to_left_ref):
    size, width = right_ref.shape
    for shift, came, out in ((count - step, right_ref, to_right_ref), (step - count, left_ref, to_left_ref)):
        block = jnp.clip(here_ref[0] + shift, 0, count - 1)
        rows = pl.ds(pl.multiple_of(block * size, size), size)
        own = sums_ref[rows, column : column + width].astype(F32)
        out[...] = (own + came[...].astype(F32)).astype(BF16)


def sum_kernel(column, here_ref, right_ref, left_ref, sums_ref, *refs):
    out_hbm, total, semaphores = refs[-3:]
    size, width = right_ref.shape
    rows = pl.ds(pl.multiple_of(here_ref[0] * size, size), size)
    copies = []
    for n in range(SUM_COPIES):
        part = rows_of(n, size // SUM_COPIES)
        own = sums_ref[rows, column : column + width][part, :].astype(F32)
        total[part, :] = (own + right_ref[part, :].astype(F32) + left_ref[part, :].astype(F32)).astype(BF16)
        to = out_hbm.at[part, column : column + width]
        copies.extend(load([(total.at[part, :], to)], semaphores.at[pl.ds(n, 1)]))
    for copy in copies:
        copy.wait()


def block_order(here, count):
    order = []
    for step in range(1, count):
        for block, sends in ((count - step + here, here <= step - 1), (step - count + here, here >= count - step)):
            if sends and block not in order:
                order.append(block)
    return order + [b for b in range(count) if b not in order]


def in_vmem(kernel, name, ins, outs, scratch=(), vmem=4, flops=1, result=None):
    vm = pl.BlockSpec(memory_space=pltpu.VMEM)
    specs, arrays = [], []
    for v in ins:
        if isinstance(v, tuple):
            specs.append(pl.BlockSpec(memory_space=pltpu.HBM))
            arrays.append(pltpu.with_memory_space_constraint(v[0], pltpu.HBM))
        elif v.dtype == jnp.int32:
            specs.append(pl.BlockSpec(memory_space=pltpu.SMEM))
            arrays.append(v)
        else:
            specs.append(vm)
            arrays.append(pltpu.with_memory_space_constraint(v, pltpu.VMEM))
    in_hbm = outs is None
    return pl.pallas_call(
        kernel,
        in_specs=specs,
        out_specs=[pl.BlockSpec(memory_space=pltpu.HBM)] if in_hbm else [vm for _ in outs],
        out_shape=[pltpu.HBM(*result)] if in_hbm else [pltpu.VMEM(shape, kind) for shape, kind in outs],
        scratch_shapes=list(scratch),
        input_output_aliases={len(ins) - 1: 0} if in_hbm and isinstance(ins[-1], tuple) else {},
        compiler_params=pltpu.CompilerParams(vmem_limit_bytes=vmem * 2**20),
        cost_estimate=pl.CostEstimate(flops=flops, bytes_accessed=1, transcendentals=0),
        name=name,
    )(*arrays)


def line_reduce(first, partial_sums, here, size, columns):
    count = lax.axis_size("tp")
    width = columns // HALVES
    block = ((size, width), BF16)
    right = [None] * HALVES
    left = [None] * HALVES
    for step in range(1, count):
        to_right = [(i, i + 1) for i in range(step)]
        to_left = [(i, i - 1) for i in range(count - step, count)]
        for half in range(HALVES):
            if step == 1:
                right[half] = left[half] = lax.ppermute(first[half], "tp", to_right + to_left)
                continue
            ins = (here, right[half], left[half], partial_sums)
            send_right, send_left = in_vmem(partial(pass_kernel, count, step, half * width), "pass_on", ins, (block, block))
            right[half] = lax.ppermute(send_right, "tp", to_right)
            left[half] = lax.ppermute(send_left, "tp", to_left)
    out = ()
    for half in range(HALVES):
        ins = (here, right[half], left[half], partial_sums, *out)
        scratch = [pltpu.VMEM((size, width), BF16), pltpu.SemaphoreType.DMA((SUM_COPIES,))]
        kernel = partial(sum_kernel, half * width)
        out = (tuple(in_vmem(kernel, "sum_up", ins, None, scratch, result=((size, columns), BF16))),)
    return out[0][0]


def on_device(x_in, gate_z, b_in, c_in, step_size, log_decay, skip, norm_gain, out_weight):
    rows, channels = x_in.shape
    heads = step_size.shape[1]
    groups = b_in.shape[1] // STATE
    chunks = rows // CHUNK
    columns = out_weight.shape[1]
    half = channels // 2
    devices = lax.axis_size("ctx")
    chips = devices // 2
    count = lax.axis_size("tp")
    size = rows // count
    core = lax.rem(lax.axis_index("ctx"), 2).astype(jnp.int32).reshape(1)
    here = lax.axis_index("tp").astype(jnp.int32).reshape(1)
    message = ((half + EXTRA, 128), BF16)
    whole = ((rows, channels), F32)
    by_head = ((heads, rows), F32)
    maps = ((rows, groups * STATE), BF16)
    weighted = pltpu.VMEM((rows, half), BF16)

    send, x_here, b_here, step, decay, spread = in_vmem(
        partial(send_kernel, groups),
        "end_state_sent",
        (core, here, (x_in,), (b_in,), (step_size.T,), (log_decay.T,)),
        (message, ((rows, channels), BF16), maps, by_head, by_head, ((128, half), BF16)),
        scratch=[weighted, pltpu.SemaphoreType.DMA((5,))],
        vmem=6,
    )
    swap = [(i, i ^ 1) for i in range(devices)]
    sibling = lax.ppermute(send, "ctx", swap)
    (own,) = in_vmem(
        partial(keep_kernel, groups), "end_state_kept", (core, x_here, b_here, step, decay, spread), (message,), [weighted],
        vmem=6, flops=10**9,
    )
    (pair,) = in_vmem(pair_kernel, "pair", (core, spread, own, sibling), (message,))
    incoming, outgoing, distance = [], pair, 1
    while distance < chips:
        if incoming:
            (outgoing,) = in_vmem(join_kernel, "join", (spread, pair, *incoming), (message,))
        reach = list(range(distance, min(chips, 4 * distance), distance))
        arrived = {}
        for far in reversed(reach):
            arrived[far] = lax.ppermute(outgoing, "ctx", [(i, i + 2 * far) for i in range(devices - 2 * far)])
        incoming.extend(arrived[far] for far in reach)
        distance *= 4
    mixed, scale, weight, c_here, token = in_vmem(
        partial(local_kernel, groups),
        "local_part",
        ((gate_z,), (c_in,), (out_weight,), x_here, b_here, step, decay, skip.reshape(1, heads), pair),
        (whole, whole, (out_weight.shape, BF16), maps, ((EXTRA, 128), BF16)),
        scratch=[pltpu.VMEM((rows, channels), BF16), pltpu.SemaphoreType.DMA((1 + chunks + WEIGHT_COPIES,))],
        vmem=12,
        flops=8 * 10**9,
    )
    state = ((STATE, half), BF16)
    keep, send = in_vmem(last_kernel, "incoming", (core, token, spread, own, sibling, *incoming), (state, state))
    recv = lax.ppermute(send, "ctx", swap)

    first = ((size, columns // 2), BF16)
    gain = norm_gain.reshape(1, channels)
    inputs = (core, here, mixed, scale, c_here, keep, recv, gain, weight)
    whole_state = pltpu.VMEM((STATE, channels), BF16)
    first_a, normed = in_vmem(
        partial(first_kernel, groups, count), "first_block", inputs, (first, ((size, channels), BF16)), [whole_state]
    )
    (first_b,) = in_vmem(second_kernel, "first_block_rest", (normed, weight), (first,))
    (partial_sums,) = in_vmem(
        partial(rest_kernel, groups, count),
        "other_blocks",
        (*inputs, first_a, first_b),
        (((rows, columns), BF16),),
        [whole_state, pltpu.VMEM((rows - size, channels), BF16)],
        vmem=6,
    )
    return line_reduce((first_a, first_b), partial_sums, here, size, columns)


def solution(mesh):
    placed = (
        P("ctx", "tp"),
        P("ctx", "tp"),
        P("ctx", "tp"),
        P("ctx", "tp"),
        P("ctx", "tp"),
        P("ctx", "tp"),
        P("tp"),
        P("tp"),
        P("tp", None),
    )
    return jax.shard_map(
        on_device, mesh=mesh, in_specs=placed, out_specs=P(("ctx", "tp"), None), check_vma=False
    )
```

time: 103 us -> 101 us (0.981)
  other arithmetic: 1.06 us -> 0 us
    ppermute x3, waiting for transfers between devices: 0.93 us -> 2.45 us  [on_device(): lax.ppermute(outgoing, 'ctx', [(i, i + 2 * far) for i in range(devices -...]
    ppermute x1, waiting for transfers between devices: 1.21 us -> 0.05 us  [on_device(): sibling = lax.ppermute(send, 'ctx', swap)]
    concatenate x1 -> x0, other arithmetic: 1.06 us -> none  [line_reduce(): return jnp.concatenate(done, axis=1)]
    pallas_call x13 -> x14, Pallas kernels: 27.8 us -> 27.5 us  [in_vmem(): pl.pallas_call(kernel, in_specs=specs, out_specs=[pl.BlockSpec(memory_spa...]
  transfers between devices with their start and end apart: 15 -> 15, of which waited for: 8 -> 8; matrix products, arithmetic and copies ran while one was open for 0% -> 0% of each run, Pallas kernels for 19% -> 21%
where the time goes in v4:
time: 101 us; the launch traced here: 99.7 us
  starting transfers between devices  36.3 us (36%)
  waiting for transfers between devices  35.7 us (35%)
  Pallas kernels  27.5 us (27%)
    pallas_call x14, Pallas kernels, in_vmem(): pl.pallas_call(kernel, in_specs=specs, out_specs=[pl.BlockSpec(memory_spa...  27.5 us
    ppermute x4, waiting for transfers between devices, line_reduce(): right[half] = lax.ppermute(send_right, 'tp', to_right)  25.8 us
    ppermute x4, starting transfers between devices, line_reduce(): right[half] = lax.ppermute(send_right, 'tp', to_right)  17.4 us
    ppermute x3, starting transfers between devices, on_device(): lax.ppermute(outgoing, 'ctx', [(i, i + 2 * far) for i in range(devices -...  9.51 us
    ppermute x2, waiting for transfers between devices, line_reduce(): lax.ppermute(first[half], 'tp', to_right + to_left)  5.87 us
    ppermute x2, starting transfers between devices, line_reduce(): lax.ppermute(first[half], 'tp', to_right + to_left)  4.84 us
    ppermute x4, starting transfers between devices, line_reduce(): left[half] = lax.ppermute(send_left, 'tp', to_left)  3.97 us
    ppermute x3, waiting for transfers between devices, on_device(): lax.ppermute(outgoing, 'ctx', [(i, i + 2 * far) for i in range(devices -...  2.45 us
  transfers between devices with their start and end apart: 15, of which 8 were waited for; matrix products, arithmetic and copies ran while one was open for 0% of the time, Pallas kernels for 21%

profile of v4, /device:TPU:0, one launch (start us, length us, event | category | flops | bytes accessed | tf_op | source)
XLA Modules:
  0.0 99.7 jit_solution(11747342343498036883)
XLA Ops:
  0.0 2.5 %end_state_sent.1 = (bf16[1040,128]{1,0:T(8,128)(2,1)S(1)}, bf16[512,2048]{1,0:T(8,128)(2,1)S(1)}, bf16[512,256]{1,0:T(8,128)(2,1)S(1)}, f32[32,512]{1,0:T(8,128...) custom-call(s32[1]{0:T(128)} %bitcast.1.core_ref, s32[1]{0:T(128)} %bitcast.here_ref, ...), custom_call_target="tpu_custom_call" | custom-call | flops 1 | bytes 1 | tf_op jit(solution)/shard_map/end_state_sent/pallas_call | solution.py:361
  3.1 1.1 %end_state_kept.1.own_ref = bf16[1040,128]{1,0:T(8,128)(2,1)S(1)} custom-call(s32[1]{0:T(128)} %bitcast.1.core_ref, bf16[512,2048]{1,0:T(8,128)(2,1)S(1)} %get-tuple-element.28.x_ref, bf16[512,256]{1,0:T(8,128)(2,1)S(1)} %get-tuple-element.29.b_ref, f32[32,512]{1,0:T(8,128)S(1)} %get-tuple-element.30.step_ref, f32[32,512]{1,0:T(8,128)S(1)} %get-tuple-element.31.decay_ref, ...), custom_call_target="tpu_custom_call" | custom-call | flops 1000000000 | bytes 1 | tf_op jit(solution)/shard_map/end_state_kept/pallas_call | solution.py:361
  4.5 5.7 %collective-permute-start.3 = (bf16[1040,128]{1,0:T(8,128)(2,1)S(1)}, bf16[1040,128]{1,0:T(8,128)(2,1)S(1)}, u32[]{:S(2)}, u32[]{:S(2)}) collective-permute-start(bf16[1040,128]{1,0:T(8,128)(2,1)S(1)} %pair.1.after_ref), channel_id=1, source_target_pairs={{0,24},{4,28},{1,25},{5,29},{2,26},{6,30},{3,27},{7,31}} | collective-permute-start | bytes 798728 | tf_op jit(solution)/shard_map/ppermute | solution.py:441
  10.2 1.3 %collective-permute-start.2 = (bf16[1040,128]{1,0:T(8,128)(2,1)S(1)}, bf16[1040,128]{1,0:T(8,128)(2,1)S(1)}, u32[]{:S(2)}, u32[]{:S(2)}) collective-permute-start(bf16[1040,128]{1,0:T(8,128)(2,1)S(1)} %pair.1.after_ref), channel_id=1, source_target_pairs={{0,16},{4,20},{8,24},{12,28},{1,17},{5,21},{9,25},{13,29},{2,18},{... | collective-permute-start | bytes 798728 | tf_op jit(solution)/shard_map/ppermute | solution.py:441
  11.6 2.5 %collective-permute-start.1 = (bf16[1040,128]{1,0:T(8,128)(2,1)S(1)}, bf16[1040,128]{1,0:T(8,128)(2,1)S(1)}, u32[]{:S(2)}, u32[]{:S(2)}) collective-permute-start(bf16[1040,128]{1,0:T(8,128)(2,1)S(1)} %pair.1.after_ref), channel_id=1, source_target_pairs={{0,8},{4,12},{8,16},{12,20},{16,24},{20,28},{1,9},{5,13},{9,17},{1... | collective-permute-start | bytes 798728 | tf_op jit(solution)/shard_map/ppermute | solution.py:441
  14.1 6.7 %local_part.1 = (f32[512,2048]{1,0:T(8,128)S(1)}, f32[512,2048]{1,0:T(8,128)S(1)}, bf16[2048,4096]{1,0:T(8,128)(2,1)S(1)}, bf16[512,256]{1,0:T(8,128)(2,1)S(1)}, bf16[16,128]{1,0:T(8,128)(2,1)S(1)}) custom-call(bf16[512,2048]{1,0:T(8,128)(2,1)} %gate_hbm.1, bf16[512,256]{1,0:T(8,128)(2,1)} %c_hbm.1, bf16[2048,4096]{1,0:T(8,128)(2,1)} %w_hbm.1, ...), custom_call_target="tpu_custom_call" | custom-call | flops 8000000000 | bytes 1 | tf_op jit(solution)/shard_map/local_part/pallas_call | solution.py:361
  20.7 2.4 %collective-permute-done.2.refs_1_ = bf16[1040,128]{1,0:T(8,128)(2,1)S(1)} collective-permute-done((bf16[1040,128]{1,0:T(8,128)(2,1)S(1)}, bf16[1040,128]{1,0:T(8,128)(2,1)S(1)}, u32[]{:S(2)}, u32[]{:S(2)}) %collective-permute-start.2) | collective-permute-done | bytes 266272 | tf_op jit(solution)/shard_map/ppermute | solution.py:441
  23.8 1.5 %collective-permute-done.4.recv_ref = bf16[128,1024]{1,0:T(8,128)(2,1)S(1)} collective-permute-done((bf16[128,1024]{1,0:T(8,128)(2,1)S(1)}, bf16[128,1024]{1,0:T(8,128)(2,1)S(1)}, u32[]{:S(2)}, u32[]{:S(2)}) %collective-permute-start.4) | collective-permute-done | bytes 262176 | tf_op jit(solution)/shard_map/ppermute | solution.py:455
  25.3 2.3 %first_block.1 = (bf16[128,2048]{1,0:T(8,128)(2,1)S(1)}, bf16[128,2048]{1,0:T(8,128)(2,1)S(1)}) custom-call(s32[1]{0:T(128)} %bitcast.1.core_ref, s32[1]{0:T(128)} %bitcast.here_ref, f32[512,2048]{1,0:T(8,128)S(1)} %get-tuple-element.34.mixed_ref, f32[512,2048]{1,0:T(8,128)S(1)} %get-tuple-element.35.scale_ref, ...), custom_call_target="tpu_custom_call" | custom-call | flops 1 | bytes 1 | tf_op jit(solution)/shard_map/first_block/pallas_call | solution.py:361
  27.7 3.5 %collective-permute-start.10 = (bf16[128,2048]{1,0:T(8,128)(2,1)S(1)}, bf16[128,2048]{1,0:T(8,128)(2,1)S(1)}, u32[]{:S(2)}, u32[]{:S(2)}) collective-permute-start(bf16[128,2048]{1,0:T(8,128)(2,1)S(1)} %get-tuple-element.42.a_ref), channel_id=1, source_target_pairs={{0,1},{3,2},{4,5},{7,6},{8,9},{11,10},{12,13},{15,14},{16,17},{19,... | collective-permute-start | bytes 1572872 | tf_op jit(solution)/shard_map/ppermute | solution.py:385
  31.2 1.9 %first_block_rest.1.b_ref = bf16[128,2048]{1,0:T(8,128)(2,1)S(1)} custom-call(bf16[128,2048]{1,0:T(8,128)(2,1)S(1)} %get-tuple-element.41.normed_ref, bf16[2048,4096]{1,0:T(8,128)(2,1)S(1)} %get-tuple-element.40.w_ref), custom_call_target="tpu_custom_call" | custom-call | flops 1 | bytes 1 | tf_op jit(solution)/shard_map/first_block_rest/pallas_call | solution.py:361
  33.1 1.3 %collective-permute-start.5 = (bf16[128,2048]{1,0:T(8,128)(2,1)S(1)}, bf16[128,2048]{1,0:T(8,128)(2,1)S(1)}, u32[]{:S(2)}, u32[]{:S(2)}) collective-permute-start(bf16[128,2048]{1,0:T(8,128)(2,1)S(1)} %first_block_rest.1.b_ref), channel_id=1, source_target_pairs={{0,1},{3,2},{4,5},{7,6},{8,9},{11,10},{12,13},{15,14},{16,17},{19,... | collective-permute-start | bytes 1572872 | tf_op jit(solution)/shard_map/ppermute | solution.py:385
  34.4 9.3 %other_blocks.1.sums_ref = bf16[512,4096]{1,0:T(8,128)(2,1)S(1)} custom-call(s32[1]{0:T(128)} %bitcast.1.core_ref, s32[1]{0:T(128)} %bitcast.here_ref, f32[512,2048]{1,0:T(8,128)S(1)} %get-tuple-element.34.mixed_ref, f32[512,2048]{1,0:T(8,128)S(1)} %get-tuple-element.35.scale_ref, bf16[512,256]{1,0:T(8,128)(2,1)S(1)} %get-tuple-element.36.c_ref, ...), custom_call_target="tpu_custom_call" | custom-call | flops 1 | bytes 1 | tf_op jit(solution)/shard_map/other_blocks/pallas_call | solution.py:361
  44.0 4.2 %collective-permute-start.11 = (bf16[128,2048]{1,0:T(8,128)(2,1)S(1)}, bf16[128,2048]{1,0:T(8,128)(2,1)S(1)}, u32[]{:S(2)}, u32[]{:S(2)}) collective-permute-start(bf16[128,2048]{1,0:T(8,128)(2,1)S(1)} %get-tuple-element.47), channel_id=1, source_target_pairs={{0,1},{1,2},{4,5},{5,6},{8,9},{9,10},{12,13},{13,14},{16,17},{17,1... | collective-permute-start | bytes 1572872 | tf_op jit(solution)/shard_map/ppermute | solution.py:389
  48.8 5.9 %collective-permute-done.5.right_ref.left_ref = bf16[128,2048]{1,0:T(8,128)(2,1)S(1)} collective-permute-done((bf16[128,2048]{1,0:T(8,128)(2,1)S(1)}, bf16[128,2048]{1,0:T(8,128)(2,1)S(1)}, u32[]{:S(2)}, u32[]{:S(2)}) %collective-permute-start.5) | collective-permute-done | bytes 524320 | tf_op jit(solution)/shard_map/ppermute | solution.py:385
  54.9 4.4 %collective-permute-start.6 = (bf16[128,2048]{1,0:T(8,128)(2,1)S(1)}, bf16[128,2048]{1,0:T(8,128)(2,1)S(1)}, u32[]{:S(2)}, u32[]{:S(2)}) collective-permute-start(bf16[128,2048]{1,0:T(8,128)(2,1)S(1)} %get-tuple-element.43), channel_id=1, source_target_pairs={{0,1},{1,2},{4,5},{5,6},{8,9},{9,10},{12,13},{13,14},{16,17},{17,1... | collective-permute-start | bytes 1572872 | tf_op jit(solution)/shard_map/ppermute | solution.py:389
  60.1 5.9 %collective-permute-done.11.right_ref = bf16[128,2048]{1,0:T(8,128)(2,1)S(1)} collective-permute-done((bf16[128,2048]{1,0:T(8,128)(2,1)S(1)}, bf16[128,2048]{1,0:T(8,128)(2,1)S(1)}, u32[]{:S(2)}, u32[]{:S(2)}) %collective-permute-start.11) | collective-permute-done | bytes 524320 | tf_op jit(solution)/shard_map/ppermute | solution.py:389
  66.2 4.4 %collective-permute-start.13 = (bf16[128,2048]{1,0:T(8,128)(2,1)S(1)}, bf16[128,2048]{1,0:T(8,128)(2,1)S(1)}, u32[]{:S(2)}, u32[]{:S(2)}) collective-permute-start(bf16[128,2048]{1,0:T(8,128)(2,1)S(1)} %get-tuple-element.49), channel_id=1, source_target_pairs={{0,1},{1,2},{2,3},{4,5},{5,6},{6,7},{8,9},{9,10},{10,11},{12,13},{... | collective-permute-start | bytes 1572872 | tf_op jit(solution)/shard_map/ppermute | solution.py:389
  70.7 1.3 %collective-permute-start.14 = (bf16[128,2048]{1,0:T(8,128)(2,1)S(1)}, bf16[128,2048]{1,0:T(8,128)(2,1)S(1)}, u32[]{:S(2)}, u32[]{:S(2)}) collective-permute-start(bf16[128,2048]{1,0:T(8,128)(2,1)S(1)} %get-tuple-element.50), channel_id=1, source_target_pairs={{1,0},{2,1},{3,2},{5,4},{6,5},{7,6},{9,8},{10,9},{11,10},{13,12},{... | collective-permute-start | bytes 1572872 | tf_op jit(solution)/shard_map/ppermute | solution.py:390
  72.0 5.2 %collective-permute-done.6.right_ref = bf16[128,2048]{1,0:T(8,128)(2,1)S(1)} collective-permute-done((bf16[128,2048]{1,0:T(8,128)(2,1)S(1)}, bf16[128,2048]{1,0:T(8,128)(2,1)S(1)}, u32[]{:S(2)}, u32[]{:S(2)}) %collective-permute-start.6) | collective-permute-done | bytes 524320 | tf_op jit(solution)/shard_map/ppermute | solution.py:389
  77.5 4.4 %collective-permute-start.8 = (bf16[128,2048]{1,0:T(8,128)(2,1)S(1)}, bf16[128,2048]{1,0:T(8,128)(2,1)S(1)}, u32[]{:S(2)}, u32[]{:S(2)}) collective-permute-start(bf16[128,2048]{1,0:T(8,128)(2,1)S(1)} %get-tuple-element.45), channel_id=1, source_target_pairs={{0,1},{1,2},{2,3},{4,5},{5,6},{6,7},{8,9},{9,10},{10,11},{12,13},{... | collective-permute-start | bytes 1572872 | tf_op jit(solution)/shard_map/ppermute | solution.py:389
  81.9 1.3 %collective-permute-start.9 = (bf16[128,2048]{1,0:T(8,128)(2,1)S(1)}, bf16[128,2048]{1,0:T(8,128)(2,1)S(1)}, u32[]{:S(2)}, u32[]{:S(2)}) collective-permute-start(bf16[128,2048]{1,0:T(8,128)(2,1)S(1)} %get-tuple-element.46), channel_id=1, source_target_pairs={{1,0},{2,1},{3,2},{5,4},{6,5},{7,6},{9,8},{10,9},{11,10},{13,12},{... | collective-permute-start | bytes 1572872 | tf_op jit(solution)/shard_map/ppermute | solution.py:390
  83.2 5.2 %collective-permute-done.13.right_ref = bf16[128,2048]{1,0:T(8,128)(2,1)S(1)} collective-permute-done((bf16[128,2048]{1,0:T(8,128)(2,1)S(1)}, bf16[128,2048]{1,0:T(8,128)(2,1)S(1)}, u32[]{:S(2)}, u32[]{:S(2)}) %collective-permute-start.13) | collective-permute-done | bytes 524320 | tf_op jit(solution)/shard_map/ppermute | solution.py:389
  89.3 9.5 %collective-permute-done.8.right_ref = bf16[128,2048]{1,0:T(8,128)(2,1)S(1)} collective-permute-done((bf16[128,2048]{1,0:T(8,128)(2,1)S(1)}, bf16[128,2048]{1,0:T(8,128)(2,1)S(1)}, u32[]{:S(2)}, u32[]{:S(2)}) %collective-permute-start.8) | collective-permute-done | bytes 524320 | tf_op jit(solution)/shard_map/ppermute | solution.py:389
  (24 shorter events, 5.7 us)
Async XLA Ops:
  0.0 14.0 %copy-start.1 = (f32[32]{0:T(128)S(1)}, f32[32]{0:T(128)}, u32[]{:S(2)}) copy-start(f32[32]{0:T(128)} %param.15) | copy-start | bytes 388
  2.6 1.7 %collective-permute-start = (bf16[1040,128]{1,0:T(8,128)(2,1)S(1)}, bf16[1040,128]{1,0:T(8,128)(2,1)S(1)}, u32[]{:S(2)}, u32[]{:S(2)}) collective-permute-start(bf16[1040,128]{1,0:T(8,128)(2,1)S(1)} %get-tuple-element.33), channel_id=1, source_target_pairs={{0,4},{4,0},{8,12},{12,8},{16,20},{20,16},{24,28},{28,24},{1,5},{5... | collective-permute-start | bytes 798728 | tf_op jit(solution)/shard_map/ppermute | solution.py:428
  4.5 16.2 %collective-permute-start.3 = (bf16[1040,128]{1,0:T(8,128)(2,1)S(1)}, bf16[1040,128]{1,0:T(8,128)(2,1)S(1)}, u32[]{:S(2)}, u32[]{:S(2)}) collective-permute-start(bf16[1040,128]{1,0:T(8,128)(2,1)S(1)} %pair.1.after_ref), channel_id=1, source_target_pairs={{0,24},{4,28},{1,25},{5,29},{2,26},{6,30},{3,27},{7,31}} | collective-permute-start | bytes 798728 | tf_op jit(solution)/shard_map/ppermute | solution.py:441
  10.2 12.9 %collective-permute-start.2 = (bf16[1040,128]{1,0:T(8,128)(2,1)S(1)}, bf16[1040,128]{1,0:T(8,128)(2,1)S(1)}, u32[]{:S(2)}, u32[]{:S(2)}) collective-permute-start(bf16[1040,128]{1,0:T(8,128)(2,1)S(1)} %pair.1.after_ref), channel_id=1, source_target_pairs={{0,16},{4,20},{8,24},{12,28},{1,17},{5,21},{9,25},{13,29},{2,18},{... | collective-permute-start | bytes 798728 | tf_op jit(solution)/shard_map/ppermute | solution.py:441
  11.6 11.6 %collective-permute-start.1 = (bf16[1040,128]{1,0:T(8,128)(2,1)S(1)}, bf16[1040,128]{1,0:T(8,128)(2,1)S(1)}, u32[]{:S(2)}, u32[]{:S(2)}) collective-permute-start(bf16[1040,128]{1,0:T(8,128)(2,1)S(1)} %pair.1.after_ref), channel_id=1, source_target_pairs={{0,8},{4,12},{8,16},{12,20},{16,24},{20,28},{1,9},{5,13},{9,17},{1... | collective-permute-start | bytes 798728 | tf_op jit(solution)/shard_map/ppermute | solution.py:441
  14.1 11.3 %copy-start = (f32[2048]{0:T(1024)S(1)}, f32[2048]{0:T(1024)}, u32[]{:S(2)}) copy-start(f32[2048]{0:T(1024)} %param.16) | copy-start | bytes 24580
  23.7 1.6 %collective-permute-start.4 = (bf16[128,1024]{1,0:T(8,128)(2,1)S(1)}, bf16[128,1024]{1,0:T(8,128)(2,1)S(1)}, u32[]{:S(2)}, u32[]{:S(2)}) collective-permute-start(bf16[128,1024]{1,0:T(8,128)(2,1)S(1)} %get-tuple-element.39), channel_id=1, source_target_pairs={{0,4},{4,0},{8,12},{12,8},{16,20},{20,16},{24,28},{28,24},{1,5},{5... | collective-permute-start | bytes 786440 | tf_op jit(solution)/shard_map/ppermute | solution.py:455
  27.7 16.0 %collective-permute-start.10 = (bf16[128,2048]{1,0:T(8,128)(2,1)S(1)}, bf16[128,2048]{1,0:T(8,128)(2,1)S(1)}, u32[]{:S(2)}, u32[]{:S(2)}) collective-permute-start(bf16[128,2048]{1,0:T(8,128)(2,1)S(1)} %get-tuple-element.42.a_ref), channel_id=1, source_target_pairs={{0,1},{3,2},{4,5},{7,6},{8,9},{11,10},{12,13},{15,14},{16,17},{19,... | collective-permute-start | bytes 1572872 | tf_op jit(solution)/shard_map/ppermute | solution.py:385
  33.1 21.6 %collective-permute-start.5 = (bf16[128,2048]{1,0:T(8,128)(2,1)S(1)}, bf16[128,2048]{1,0:T(8,128)(2,1)S(1)}, u32[]{:S(2)}, u32[]{:S(2)}) collective-permute-start(bf16[128,2048]{1,0:T(8,128)(2,1)S(1)} %first_block_rest.1.b_ref), channel_id=1, source_target_pairs={{0,1},{3,2},{4,5},{7,6},{8,9},{11,10},{12,13},{15,14},{16,17},{19,... | collective-permute-start | bytes 1572872 | tf_op jit(solution)/shard_map/ppermute | solution.py:385
  44.0 22.0 %collective-permute-start.11 = (bf16[128,2048]{1,0:T(8,128)(2,1)S(1)}, bf16[128,2048]{1,0:T(8,128)(2,1)S(1)}, u32[]{:S(2)}, u32[]{:S(2)}) collective-permute-start(bf16[128,2048]{1,0:T(8,128)(2,1)S(1)} %get-tuple-element.47), channel_id=1, source_target_pairs={{0,1},{1,2},{4,5},{5,6},{8,9},{9,10},{12,13},{13,14},{16,17},{17,1... | collective-permute-start | bytes 1572872 | tf_op jit(solution)/shard_map/ppermute | solution.py:389
  48.1 17.8 %collective-permute-start.12 = (bf16[128,2048]{1,0:T(8,128)(2,1)S(1)}, bf16[128,2048]{1,0:T(8,128)(2,1)S(1)}, u32[]{:S(2)}, u32[]{:S(2)}) collective-permute-start(bf16[128,2048]{1,0:T(8,128)(2,1)S(1)} %get-tuple-element.48), channel_id=1, source_target_pairs={{2,1},{3,2},{6,5},{7,6},{10,9},{11,10},{14,13},{15,14},{18,17},{19... | collective-permute-start | bytes 1572872 | tf_op jit(solution)/shard_map/ppermute | solution.py:390
  54.9 22.2 %collective-permute-start.6 = (bf16[128,2048]{1,0:T(8,128)(2,1)S(1)}, bf16[128,2048]{1,0:T(8,128)(2,1)S(1)}, u32[]{:S(2)}, u32[]{:S(2)}) collective-permute-start(bf16[128,2048]{1,0:T(8,128)(2,1)S(1)} %get-tuple-element.43), channel_id=1, source_target_pairs={{0,1},{1,2},{4,5},{5,6},{8,9},{9,10},{12,13},{13,14},{16,17},{17,1... | collective-permute-start | bytes 1572872 | tf_op jit(solution)/shard_map/ppermute | solution.py:389
  59.4 17.8 %collective-permute-start.7 = (bf16[128,2048]{1,0:T(8,128)(2,1)S(1)}, bf16[128,2048]{1,0:T(8,128)(2,1)S(1)}, u32[]{:S(2)}, u32[]{:S(2)}) collective-permute-start(bf16[128,2048]{1,0:T(8,128)(2,1)S(1)} %get-tuple-element.44), channel_id=1, source_target_pairs={{2,1},{3,2},{6,5},{7,6},{10,9},{11,10},{14,13},{15,14},{18,17},{19... | collective-permute-start | bytes 1572872 | tf_op jit(solution)/shard_map/ppermute | solution.py:390
  66.2 22.2 %collective-permute-start.13 = (bf16[128,2048]{1,0:T(8,128)(2,1)S(1)}, bf16[128,2048]{1,0:T(8,128)(2,1)S(1)}, u32[]{:S(2)}, u32[]{:S(2)}) collective-permute-start(bf16[128,2048]{1,0:T(8,128)(2,1)S(1)} %get-tuple-element.49), channel_id=1, source_target_pairs={{0,1},{1,2},{2,3},{4,5},{5,6},{6,7},{8,9},{9,10},{10,11},{12,13},{... | collective-permute-start | bytes 1572872 | tf_op jit(solution)/shard_map/ppermute | solution.py:389
  70.7 17.7 %collective-permute-start.14 = (bf16[128,2048]{1,0:T(8,128)(2,1)S(1)}, bf16[128,2048]{1,0:T(8,128)(2,1)S(1)}, u32[]{:S(2)}, u32[]{:S(2)}) collective-permute-start(bf16[128,2048]{1,0:T(8,128)(2,1)S(1)} %get-tuple-element.50), channel_id=1, source_target_pairs={{1,0},{2,1},{3,2},{5,4},{6,5},{7,6},{9,8},{10,9},{11,10},{13,12},{... | collective-permute-start | bytes 1572872 | tf_op jit(solution)/shard_map/ppermute | solution.py:390
  77.5 21.4 %collective-permute-start.8 = (bf16[128,2048]{1,0:T(8,128)(2,1)S(1)}, bf16[128,2048]{1,0:T(8,128)(2,1)S(1)}, u32[]{:S(2)}, u32[]{:S(2)}) collective-permute-start(bf16[128,2048]{1,0:T(8,128)(2,1)S(1)} %get-tuple-element.45), channel_id=1, source_target_pairs={{0,1},{1,2},{2,3},{4,5},{5,6},{6,7},{8,9},{9,10},{10,11},{12,13},{... | collective-permute-start | bytes 1572872 | tf_op jit(solution)/shard_map/ppermute | solution.py:389
  81.9 17.0 %collective-permute-start.9 = (bf16[128,2048]{1,0:T(8,128)(2,1)S(1)}, bf16[128,2048]{1,0:T(8,128)(2,1)S(1)}, u32[]{:S(2)}, u32[]{:S(2)}) collective-permute-start(bf16[128,2048]{1,0:T(8,128)(2,1)S(1)} %get-tuple-element.46), channel_id=1, source_target_pairs={{1,0},{2,1},{3,2},{5,4},{6,5},{7,6},{9,8},{10,9},{11,10},{13,12},{... | collective-permute-start | bytes 1572872 | tf_op jit(solution)/shard_map/ppermute | solution.py:390

commit v5 on v4

--- a/solution.py
+++ b/solution.py
@@ -16,6 +16,7 @@
 HALVES = 2
 WEIGHT_COPIES = 8
 SUM_COPIES = 4
+PIECES = 2
 F32 = jnp.float32
 BF16 = jnp.bfloat16
 
@@ -110,11 +111,11 @@
     put_message(message_ref, state, jnp.transpose(logs)[:EXTRA])
 
 
-def send_kernel(groups, core_ref, here_ref, x_hbm, b_hbm, step_hbm, decay_hbm, send_ref, x_ref, b_ref, step_ref, decay_ref,
+def send_kernel(groups, ctx_ref, here_ref, x_hbm, b_hbm, step_hbm, decay_hbm, send_ref, x_ref, b_ref, step_ref, decay_ref,
                 spread_ref, weighted, semaphores):
     width = weighted.shape[1]
-    other = 1 - core_ref[0]
-    of_channels = [pl.ds(pl.multiple_of(half * width, width), width) for half in (other, core_ref[0])]
+    other = 1 - (ctx_ref[0] & 1)
+    of_channels = [pl.ds(pl.multiple_of(half * width, width), width) for half in (other, 1 - other)]
     copies = load(
         [(decay_hbm, decay_ref), (step_hbm, step_ref), (b_hbm, b_ref)]
         + [(x_hbm.at[:, cut], x_ref.at[:, cut]) for cut in of_channels],
@@ -128,60 +129,84 @@
     copies[4].wait()
 
 
-def keep_kernel(groups, core_ref, x_ref, b_ref, step_ref, decay_ref, spread_ref, keep_ref, weighted):
-    end_state(groups, core_ref[0], x_ref, b_ref, step_ref, decay_ref, weighted, keep_ref, spread_ref[...])
-
-
-def pair_kernel(core_ref, spread_ref, own_ref, sibling_ref, pair_ref):
+def keep_kernel(groups, ctx_ref, x_ref, b_ref, step_ref, decay_ref, spread_ref, keep_ref, weighted):
+    end_state(groups, (ctx_ref[0] & 1), x_ref, b_ref, step_ref, decay_ref, weighted, keep_ref, spread_ref[...])
+
+
+def pair_kernel(ctx_ref, spread_ref, own_ref, sibling_ref, *pieces_refs):
     spread = spread_ref[...]
     own_log, sibling_log = wide_log(logs_of(own_ref), spread), wide_log(logs_of(sibling_ref), spread)
-    early = core_ref[0] == 0
+    early = (ctx_ref[0] & 1) == 0
     own_scale = jnp.where(early, jnp.exp(sibling_log), 1.0)
     sibling_scale = jnp.where(early, 1.0, jnp.exp(own_log))
     logs = logs_of(own_ref).astype(F32) + logs_of(sibling_ref).astype(F32)
     logs = pieces(jnp.sum(logs, axis=0, keepdims=True), 0)
-    put_message(pair_ref, state_of(own_ref) * own_scale + state_of(sibling_ref) * sibling_scale, logs)
-
-
-def joined(stretches, spread):
-    total, log = state_of(stretches[0]), 0.0
-    for late, early in zip(stretches, stretches[1:]):
-        log = log + wide_log(logs_of(late), spread)
-        total = total + state_of(early) * jnp.exp(log)
-    return total
-
-
-def join_kernel(spread_ref, *refs):
-    logs = sum(jnp.sum(logs_of(ref).astype(F32), axis=0, keepdims=True) for ref in refs[:-1])
-    put_message(refs[-1], joined(refs[:-1], spread_ref[...]), pieces(logs, 0))
-
-
-def last_kernel(core_ref, after_ref, spread_ref, own_ref, sibling_ref, *refs):
+    state = state_of(own_ref) * own_scale + state_of(sibling_ref) * sibling_scale
+    width = state.shape[1] // len(pieces_refs)
+    for n, ref in enumerate(pieces_refs):
+        put_message(ref, state[:, n * width : (n + 1) * width], logs)
+
+
+def is_upper(ctx_ref, level):
+    return ((ctx_ref[0] >> (1 + level)) & 1) == 1
+
+
+def piece_of(spread_ref, piece, ref):
+    width = ref.shape[0] - EXTRA
+    return spread_ref[:, piece * width : (piece + 1) * width]
+
+
+def fold_kernel(level, piece, ctx_ref, after_ref, spread_ref, total_ref, other_ref, out_ref):
+    spread = piece_of(spread_ref, piece, total_ref)
+    upper = is_upper(ctx_ref, level)
+    total_scale = jnp.where(upper, 1.0, jnp.exp(wide_log(logs_of(other_ref), spread)))
+    other_scale = jnp.where(upper, jnp.exp(wide_log(logs_of(total_ref), spread)), 1.0)
+    logs = logs_of(total_ref).astype(F32) + logs_of(other_ref).astype(F32)
+    logs = pieces(jnp.sum(logs, axis=0, keepdims=True), 0)
+    put_message(out_ref, state_of(total_ref) * total_scale + state_of(other_ref) * other_scale, logs)
+
+
+def last_kernel(levels, ctx_ref, after_ref, spread_ref, own_ref, sibling_ref, *refs):
     keep_ref, send_ref = refs[-2:]
-    spread = spread_ref[...]
-    chip = joined(refs[:-2], spread)
+    count = len(refs[:-2]) // levels
+    parts = []
+    for piece in range(count):
+        state = log = 0.0
+        for level in range(levels):
+            ref = refs[level * count + piece]
+            upper = is_upper(ctx_ref, level)
+            spread = piece_of(spread_ref, piece, ref)
+            state = state + jnp.where(upper, state_of(ref), 0.0) * jnp.exp(log)
+            log = log + jnp.where(upper, wide_log(logs_of(ref), spread), 0.0)
+        parts.append(state)
+    chip = jnp.concatenate(parts, axis=1)
     for core, first, mine, other in ((0, own_ref, 0, 1), (1, sibling_ref, 1, 0)):
 
-        @pl.when(core_ref[0] == core)
+        @pl.when((ctx_ref[0] & 1) == core)
         def _():
-            after = chip * jnp.exp(wide_log(logs_of(first), spread)) + state_of(first)
+            after = chip * jnp.exp(wide_log(logs_of(first), spread_ref[...])) + state_of(first)
             both = (chip.astype(BF16), after.astype(BF16))
             keep_ref[...] = both[mine]
             send_ref[...] = both[other]
 
 
-def local_kernel(groups, gate_hbm, c_hbm, w_hbm, x_ref, b_ref, step_ref, decay_ref, skip_ref, after_ref, mixed_ref, scale_ref,
-                 w_ref, c_ref, token_ref, gate_ref, semaphores):
+def local_kernel(groups, part_index, gate_hbm, c_hbm, w_hbm, x_ref, b_ref, step_ref, decay_ref, skip_ref, after_ref, *refs):
+    if part_index:
+        refs = refs[5:]
+    mixed_ref, scale_ref, c_ref, state_ref, before_ref, w_ref, token_ref, gate_ref, semaphores = refs
     token_ref[...] = jnp.zeros_like(token_ref)
-    rows, channels = x_ref.shape
+    channels = x_ref.shape[1]
     heads = step_ref.shape[0]
     width = channels // groups
-    chunks = rows // CHUNK
-    small = load([(c_hbm, c_ref)], semaphores)
-    gates = [(gate_hbm.at[rows_of(n), :], gate_ref.at[rows_of(n), :]) for n in range(chunks)]
+    chunks = gate_ref.shape[0] // CHUNK
+    mine = range(part_index * chunks, (part_index + 1) * chunks)
+    own_rows = rows_of(part_index, chunks * CHUNK)
+    small = load([(c_hbm.at[own_rows, :], c_ref.at[own_rows, :])], semaphores)
+    gates = [(gate_hbm.at[rows_of(n), :], gate_ref.at[rows_of(n - mine[0]), :]) for n in mine]
     gates = load(gates, semaphores.at[pl.ds(1, chunks)])
     size = channels // WEIGHT_COPIES
-    weights = [(w_hbm.at[rows_of(n, size), :], w_ref.at[rows_of(n, size), :]) for n in range(WEIGHT_COPIES)]
+    columns = rows_of(part_index, w_ref.shape[1])
+    weights = [(w_hbm.at[rows_of(n, size), columns], w_ref.at[rows_of(n, size), :]) for n in range(WEIGHT_COPIES)]
     weights = load(weights, semaphores.at[pl.ds(1 + chunks, WEIGHT_COPIES)])
 
     spread = head_map(channels)
@@ -192,8 +217,11 @@
     skip = wide_log(skip.astype(BF16), spread)
     before = jnp.zeros((heads, 1), F32)
     state = [jnp.zeros((STATE, width), F32)] * groups
+    if part_index:
+        before = before_ref[:, 0:1]
+        state = [state_ref[:, rows_of(g, width)] for g in range(groups)]
     small[0].wait()
-    for n, running in enumerate(running_sums(decay_ref[...])):
+    for n, running in zip(mine, running_sums(decay_ref[:, own_rows])):
         here = rows_of(n)
         middle, total = running[:, MIDDLE : MIDDLE + 1], running[:, CHUNK - 1 :]
         inner = running - middle
@@ -208,7 +236,7 @@
             axis=0,
         )
         before = before + total
-        gates[n].wait()
+        gates[n - mine[0]].wait()
         for g in range(groups):
             cut = slice(g * width, (g + 1) * width)
             part = slice(g * STATE, (g + 1) * STATE)
@@ -222,15 +250,18 @@
             )
             scores = jnp.where(row >= column, scores, 0.0).astype(BF16)
             within = dot(jnp.concatenate([scores, c_ref[here, part]], axis=1), started)
-            if n < chunks - 1:
+            if n + 1 < x_ref.shape[0] // CHUNK:
                 fresh = lax.dot_general(
                     b_ref[here, part], weighted, (((0,), (0,)), ((), ())), preferred_element_type=F32
                 )
                 state[g] = state[g] * to_state + fresh * to_fresh
-            gate = gate_ref[here, cut].astype(F32)
+            gate = gate_ref[rows_of(n - mine[0]), cut].astype(F32)
             gate = gate / (1.0 + jnp.exp(-gate))
             mixed_ref[here, cut] = (within * wide[CHUNK : 2 * CHUNK] + x * skip[:, cut]) * gate
             scale_ref[here, cut] = wide[2 * CHUNK : 3 * CHUNK] * gate
+    before_ref[...] = jnp.broadcast_to(before, before_ref.shape)
+    for g in range(groups):
+        state_ref[:, rows_of(g, width)] = state[g]
     for copy in weights:
         copy.wait()
 
@@ -247,11 +278,11 @@
     return parts
 
 
-def fill_state(core_ref, keep_ref, recv_ref, state):
+def fill_state(ctx_ref, keep_ref, recv_ref, state):
     half = keep_ref.shape[1]
     for core in range(2):
 
-        @pl.when(core_ref[0] == core)
+        @pl.when((ctx_ref[0] & 1) == core)
         def _():
             state[:, core * half : (core + 1) * half] = keep_ref[...]
             state[:, (1 - core) * half : (2 - core) * half] = recv_ref[...]
@@ -264,9 +295,9 @@
     return pl.ds(pl.multiple_of(block * size, size), size)
 
 
-def first_kernel(groups, count, core_ref, here_ref, mixed_ref, scale_ref, c_ref, keep_ref, recv_ref, gain_ref, w_ref, out_ref,
+def first_kernel(groups, count, ctx_ref, here_ref, mixed_ref, scale_ref, c_ref, keep_ref, recv_ref, gain_ref, w_ref, out_ref,
                  normed_ref, state):
-    fill_state(core_ref, keep_ref, recv_ref, state)
+    fill_state(ctx_ref, keep_ref, recv_ref, state)
     width = normed_ref.shape[1] // groups
     here = block_at(here_ref[0], 0, count, normed_ref.shape[0])
     rows = norm_rows(groups, state, mixed_ref.at[here, :], scale_ref.at[here, :], c_ref.at[here, :], gain_ref)
@@ -280,22 +311,19 @@
 
 
 def second_kernel(normed_ref, w_ref, out_ref):
-    start = w_ref.shape[1] - out_ref.shape[1]
-
     @pl.loop(0, out_ref.shape[1] // COLUMN_TILE)
     def _(j):
         cut = pl.ds(pl.multiple_of(j * COLUMN_TILE, COLUMN_TILE), COLUMN_TILE)
-        from_ = pl.ds(pl.multiple_of(start + j * COLUMN_TILE, COLUMN_TILE), COLUMN_TILE)
-        out_ref[:, cut] = dot(normed_ref[...], w_ref[:, from_]).astype(BF16)
-
-
-def rest_kernel(groups, count, core_ref, here_ref, mixed_ref, scale_ref, c_ref, keep_ref, recv_ref, gain_ref, w_ref, a_ref,
-                b_ref, out_ref, state, normed):
+        out_ref[:, cut] = dot(normed_ref[...], w_ref[:, cut]).astype(BF16)
+
+
+def rest_kernel(groups, count, ctx_ref, here_ref, mixed_ref, scale_ref, c_ref, keep_ref, recv_ref, gain_ref, wa_ref, wb_ref,
+                a_ref, b_ref, out_ref, state, normed):
     size, half = a_ref.shape
     blocks = [block_at(here_ref[0], n, count, size) for n in range(count)]
     out_ref[blocks[0], :half] = a_ref[...]
     out_ref[blocks[0], half:] = b_ref[...]
-    fill_state(core_ref, keep_ref, recv_ref, state)
+    fill_state(ctx_ref, keep_ref, recv_ref, state)
     width = normed.shape[1] // groups
     for n in range(1, count):
         here = blocks[n]
@@ -303,32 +331,51 @@
         for g, part in enumerate(rows):
             normed[(n - 1) * size : n * size, g * width : (g + 1) * width] = part
 
-    @pl.loop(0, out_ref.shape[1] // COLUMN_TILE)
-    def _(j):
-        cut = pl.ds(pl.multiple_of(j * COLUMN_TILE, COLUMN_TILE), COLUMN_TILE)
-        product = dot(normed[...], w_ref[:, cut]).astype(BF16)
-        for n in range(1, count):
-            out_ref[blocks[n], cut] = product[(n - 1) * size : n * size]
-
-
-def pass_kernel(count, step, column, here_ref, right_ref, left_ref, sums_ref, to_right_ref, to_left_ref):
-    size, width = right_ref.shape
-    for shift, came, out in ((count - step, right_ref, to_right_ref), (step - count, left_ref, to_left_ref)):
-        block = jnp.clip(here_ref[0] + shift, 0, count - 1)
+    for first_column, w_ref in ((0, wa_ref), (half, wb_ref)):
+
+        @pl.loop(0, half // COLUMN_TILE)
+        def _(j):
+            cut = pl.ds(pl.multiple_of(j * COLUMN_TILE, COLUMN_TILE), COLUMN_TILE)
+            to = pl.ds(pl.multiple_of(first_column + j * COLUMN_TILE, COLUMN_TILE), COLUMN_TILE)
+            product = dot(normed[...], w_ref[:, cut]).astype(BF16)
+            for n in range(1, count):
+                out_ref[blocks[n], to] = product[(n - 1) * size : n * size]
+
+
+def pass_kernel(count, step, column, here_ref, *refs):
+    sums_ref, even_out, odd_out = refs[-3:]
+    arrived = refs[:-3]
+    size, width = even_out.shape
+    here = here_ref[0]
+
+    def send(shift, came, out):
+        block = jnp.clip(here + shift, 0, count - 1)
         rows = pl.ds(pl.multiple_of(block * size, size), size)
         own = sums_ref[rows, column : column + width].astype(F32)
-        out[...] = (own + came[...].astype(F32)).astype(BF16)
-
-
-def sum_kernel(column, here_ref, right_ref, left_ref, sums_ref, *refs):
+        for ref in came:
+            own = own + ref[...].astype(F32)
+        out[...] = own.astype(BF16)
+
+    for parity, to_right, to_left, from_left, from_right in (
+        (0, even_out, odd_out, arrived[1:], arrived[:1]),
+        (1, odd_out, even_out, arrived[:1], arrived[1:]),
+    ):
+
+        @pl.when((here & 1) == parity)
+        def _():
+            send(count - step, from_left, to_right)
+            send(step - count, from_right, to_left)
+
+
+def sum_kernel(column, here_ref, even_ref, odd_ref, sums_ref, *refs):
     out_hbm, total, semaphores = refs[-3:]
-    size, width = right_ref.shape
+    size, width = even_ref.shape
     rows = pl.ds(pl.multiple_of(here_ref[0] * size, size), size)
     copies = []
     for n in range(SUM_COPIES):
         part = rows_of(n, size // SUM_COPIES)
         own = sums_ref[rows, column : column + width][part, :].astype(F32)
-        total[part, :] = (own + right_ref[part, :].astype(F32) + left_ref[part, :].astype(F32)).astype(BF16)
+        total[part, :] = (own + even_ref[part, :].astype(F32) + odd_ref[part, :].astype(F32)).astype(BF16)
         to = out_hbm.at[part, column : column + width]
         copies.extend(load([(total.at[part, :], to)], semaphores.at[pl.ds(n, 1)]))
     for copy in copies:
@@ -344,7 +391,7 @@
     return order + [b for b in range(count) if b not in order]
 
 
-def in_vmem(kernel, name, ins, outs, scratch=(), vmem=4, flops=1, result=None):
+def in_vmem(kernel, name, ins, outs, scratch=(), vmem=4, flops=1, result=None, aliases=None):
     vm = pl.BlockSpec(memory_space=pltpu.VMEM)
     specs, arrays = [], []
     for v in ins:
@@ -364,7 +411,7 @@
         out_specs=[pl.BlockSpec(memory_space=pltpu.HBM)] if in_hbm else [vm for _ in outs],
         out_shape=[pltpu.HBM(*result)] if in_hbm else [pltpu.VMEM(shape, kind) for shape, kind in outs],
         scratch_shapes=list(scratch),
-        input_output_aliases={len(ins) - 1: 0} if in_hbm and isinstance(ins[-1], tuple) else {},
+        input_output_aliases={len(ins) - 1: 0} if in_hbm and isinstance(ins[-1], tuple) else aliases or {},
         compiler_params=pltpu.CompilerParams(vmem_limit_bytes=vmem * 2**20),
         cost_estimate=pl.CostEstimate(flops=flops, bytes_accessed=1, transcendentals=0),
         name=name,
@@ -375,22 +422,21 @@
     count = lax.axis_size("tp")
     width = columns // HALVES
     block = ((size, width), BF16)
-    right = [None] * HALVES
-    left = [None] * HALVES
+    even_edges = [(i, i ^ 1) for i in range(count)]
+    odd_edges = [(i, ((i + 1) ^ 1) - 1) for i in range(1, count - 1)]
+    arrived = [()] * HALVES
     for step in range(1, count):
-        to_right = [(i, i + 1) for i in range(step)]
-        to_left = [(i, i - 1) for i in range(count - step, count)]
         for half in range(HALVES):
             if step == 1:
-                right[half] = left[half] = lax.ppermute(first[half], "tp", to_right + to_left)
+                arrived[half] = (lax.ppermute(first[half], "tp", even_edges),)
                 continue
-            ins = (here, right[half], left[half], partial_sums)
-            send_right, send_left = in_vmem(partial(pass_kernel, count, step, half * width), "pass_on", ins, (block, block))
-            right[half] = lax.ppermute(send_right, "tp", to_right)
-            left[half] = lax.ppermute(send_left, "tp", to_left)
+            even, odd = in_vmem(
+                partial(pass_kernel, count, step, half * width), "pass_on", (here, *arrived[half], partial_sums), (block, block)
+            )
+            arrived[half] = (lax.ppermute(even, "tp", even_edges), lax.ppermute(odd, "tp", odd_edges))
     out = ()
     for half in range(HALVES):
-        ins = (here, right[half], left[half], partial_sums, *out)
+        ins = (here, *arrived[half], partial_sums, *out)
         scratch = [pltpu.VMEM((size, width), BF16), pltpu.SemaphoreType.DMA((SUM_COPIES,))]
         kernel = partial(sum_kernel, half * width)
         out = (tuple(in_vmem(kernel, "sum_up", ins, None, scratch, result=((size, columns), BF16))),)
@@ -408,7 +454,7 @@
     chips = devices // 2
     count = lax.axis_size("tp")
     size = rows // count
-    core = lax.rem(lax.axis_index("ctx"), 2).astype(jnp.int32).reshape(1)
+    ctx = lax.axis_index("ctx").astype(jnp.int32).reshape(1)
     here = lax.axis_index("tp").astype(jnp.int32).reshape(1)
     message = ((half + EXTRA, 128), BF16)
     whole = ((rows, channels), F32)
@@ -419,7 +465,7 @@
     send, x_here, b_here, step, decay, spread = in_vmem(
         partial(send_kernel, groups),
         "end_state_sent",
-        (core, here, (x_in,), (b_in,), (step_size.T,), (log_decay.T,)),
+        (ctx, here, (x_in,), (b_in,), (step_size.T,), (log_decay.T,)),
         (message, ((rows, channels), BF16), maps, by_head, by_head, ((128, half), BF16)),
         scratch=[weighted, pltpu.SemaphoreType.DMA((5,))],
         vmem=6,
@@ -427,45 +473,70 @@
     swap = [(i, i ^ 1) for i in range(devices)]
     sibling = lax.ppermute(send, "ctx", swap)
     (own,) = in_vmem(
-        partial(keep_kernel, groups), "end_state_kept", (core, x_here, b_here, step, decay, spread), (message,), [weighted],
+        partial(keep_kernel, groups), "end_state_kept", (ctx, x_here, b_here, step, decay, spread), (message,), [weighted],
         vmem=6, flops=10**9,
     )
-    (pair,) = in_vmem(pair_kernel, "pair", (core, spread, own, sibling), (message,))
-    incoming, outgoing, distance = [], pair, 1
-    while distance < chips:
-        if incoming:
-            (outgoing,) = in_vmem(join_kernel, "join", (spread, pair, *incoming), (message,))
-        reach = list(range(distance, min(chips, 4 * distance), distance))
-        arrived = {}
-        for far in reversed(reach):
-            arrived[far] = lax.ppermute(outgoing, "ctx", [(i, i + 2 * far) for i in range(devices - 2 * far)])
-        incoming.extend(arrived[far] for far in reach)
-        distance *= 4
-    mixed, scale, weight, c_here, token = in_vmem(
-        partial(local_kernel, groups),
-        "local_part",
-        ((gate_z,), (c_in,), (out_weight,), x_here, b_here, step, decay, skip.reshape(1, heads), pair),
-        (whole, whole, (out_weight.shape, BF16), maps, ((EXTRA, 128), BF16)),
-        scratch=[pltpu.VMEM((rows, channels), BF16), pltpu.SemaphoreType.DMA((1 + chunks + WEIGHT_COPIES,))],
-        vmem=12,
-        flops=8 * 10**9,
-    )
+    piece = ((half // PIECES + EXTRA, 128), BF16)
+    totals = in_vmem(pair_kernel, "pair", (ctx, spread, own, sibling), (piece,) * PIECES)
+    levels = chips.bit_length() - 1
+
+    def swap_chips(level, blocks):
+        return [lax.ppermute(v, "ctx", [(i, i ^ (2 << level)) for i in range(devices)]) for v in blocks]
+
+    def local_part(part_index, after, carried):
+        return in_vmem(
+            partial(local_kernel, groups, part_index),
+            "local_part",
+            ((gate_z,), (c_in,), (out_weight,), x_here, b_here, step, decay, skip.reshape(1, heads), after, *carried),
+            (
+                whole,
+                whole,
+                maps,
+                ((STATE, channels), F32),
+                ((heads, 128), F32),
+                ((channels, columns // 2), BF16),
+                ((EXTRA, 128), BF16),
+            ),
+            scratch=[
+                pltpu.VMEM((rows // 2, channels), BF16),
+                pltpu.SemaphoreType.DMA((1 + chunks // 2 + WEIGHT_COPIES,)),
+            ],
+            vmem=10,
+            flops=4 * 10**9,
+            aliases={9 + n: n for n in range(len(carried))},
+        )
+
+    received = swap_chips(0, totals)
+    *carried, weight_a, token = local_part(0, totals[-1], ())
+    arrived = list(received)
+    for level in range(1, levels):
+        folded = []
+        for n in range(PIECES):
+            kernel = partial(fold_kernel, level - 1, n)
+            after = folded[-1] if folded else token
+            folded.extend(in_vmem(kernel, "fold", (ctx, after, spread, totals[n], received[n]), (piece,)))
+        totals = folded
+        received = swap_chips(level, totals)
+        arrived.extend(received)
+    mixed, scale, c_here, _, _, weight_b, token = local_part(1, totals[-1], carried)
     state = ((STATE, half), BF16)
-    keep, send = in_vmem(last_kernel, "incoming", (core, token, spread, own, sibling, *incoming), (state, state))
+    keep, send = in_vmem(
+        partial(last_kernel, levels), "incoming", (ctx, token, spread, own, sibling, *arrived), (state, state)
+    )
     recv = lax.ppermute(send, "ctx", swap)
 
     first = ((size, columns // 2), BF16)
     gain = norm_gain.reshape(1, channels)
-    inputs = (core, here, mixed, scale, c_here, keep, recv, gain, weight)
+    inputs = (ctx, here, mixed, scale, c_here, keep, recv, gain, weight_a)
     whole_state = pltpu.VMEM((STATE, channels), BF16)
     first_a, normed = in_vmem(
         partial(first_kernel, groups, count), "first_block", inputs, (first, ((size, channels), BF16)), [whole_state]
     )
-    (first_b,) = in_vmem(second_kernel, "first_block_rest", (normed, weight), (first,))
+    (first_b,) = in_vmem(second_kernel, "first_block_rest", (normed, weight_b), (first,))
     (partial_sums,) = in_vmem(
         partial(rest_kernel, groups, count),
         "other_blocks",
-        (*inputs, first_a, first_b),
+        (*inputs, weight_b, first_a, first_b),
         (((rows, columns), BF16),),
         [whole_state, pltpu.VMEM((rows - size, channels), BF16)],
         vmem=6,

time: 101 us -> 96.1 us (0.951); the launches traced: 99.7 us -> 95.9 us
  starting transfers between devices: 36.3 us -> 23.4 us
  waiting for transfers between devices: 35.7 us -> 43.8 us
    ppermute x13 -> x14, starting transfers between devices: 35.7 us -> 22.8 us  [the longest x4 10.9 us: line_reduce(): lax.ppermute(even, 'tp', even_edges)]
    ppermute x13 -> x14, waiting for transfers between devices: 34.1 us -> 42.2 us  [the longest x4 31.7 us: line_reduce(): lax.ppermute(even, 'tp', even_edges)]
    pallas_call x14 -> x17, Pallas kernels: 27.5 us -> 28.4 us  [in_vmem(): pl.pallas_call(kernel, in_specs=specs, out_specs=[pl.BlockSpec(memory_spa...]
  transfers between devices with their start and end apart: 15 -> 16, of which waited for: 8 -> 8; matrix products, arithmetic and copies ran while one was open for 0% -> 0% of each run, Pallas kernels for 21% -> 23%
where the time goes in v5:
time: 96.1 us; the launch traced here: 95.9 us
  waiting for transfers between devices  43.8 us (46%)
  Pallas kernels  28.4 us (30%)
  starting transfers between devices  23.4 us (24%)
    ppermute x4, waiting for transfers between devices, line_reduce(): lax.ppermute(even, 'tp', even_edges)  31.7 us
    pallas_call x17, Pallas kernels, in_vmem(): pl.pallas_call(kernel, in_specs=specs, out_specs=[pl.BlockSpec(memory_spa...  28.4 us
    ppermute x4, starting transfers between devices, line_reduce(): lax.ppermute(even, 'tp', even_edges)  10.9 us
    ppermute x2, waiting for transfers between devices, line_reduce(): arrived[half] = (lax.ppermute(first[half], 'tp', even_edges),)  10.1 us
    ppermute x4, starting transfers between devices, swap_chips(): lax.ppermute(v, 'ctx', [(i, i ^ 2 << level) for i in range(devices)])  7 us
    ppermute x4, starting transfers between devices, line_reduce(): lax.ppermute(odd, 'tp', odd_edges)  2.74 us
    ppermute x2, starting transfers between devices, line_reduce(): arrived[half] = (lax.ppermute(first[half], 'tp', even_edges),)  2.18 us
  transfers between devices with their start and end apart: 16, of which 8 were waited for; matrix products, arithmetic and copies ran while one was open for 0% of the time, Pallas kernels for 23%

profile of v5, /device:TPU:0, one launch (start us, length us, event | category | flops | bytes accessed | tf_op | source)
XLA Modules:
  0.0 95.9 jit_solution(13743936303487405567)
XLA Ops:
  0.0 2.5 %end_state_sent.1 = (bf16[1040,128]{1,0:T(8,128)(2,1)S(1)}, bf16[512,2048]{1,0:T(8,128)(2,1)S(1)}, bf16[512,256]{1,0:T(8,128)(2,1)S(1)}, f32[32,512]{1,0:T(8,128...) custom-call(s32[1]{0:T(128)} %bitcast.1.ctx_ref, s32[1]{0:T(128)} %bitcast.here_ref, ...), custom_call_target="tpu_custom_call" | custom-call | flops 1 | bytes 1 | tf_op jit(solution)/shard_map/end_state_sent/pallas_call | solution.py:408
  3.1 1.1 %end_state_kept.1.own_ref = bf16[1040,128]{1,0:T(8,128)(2,1)S(1)} custom-call(s32[1]{0:T(128)} %bitcast.1.ctx_ref, bf16[512,2048]{1,0:T(8,128)(2,1)S(1)} %get-tuple-element.37.x_ref, bf16[512,256]{1,0:T(8,128)(2,1)S(1)} %get-tuple-element.38.b_ref, f32[32,512]{1,0:T(8,128)S(1)} %get-tuple-element.39.step_ref, f32[32,512]{1,0:T(8,128)S(1)} %get-tuple-element.40.decay_ref, ...), custom_call_target="tpu_custom_call" | custom-call | flops 1000000000 | bytes 1 | tf_op jit(solution)/shard_map/end_state_kept/pallas_call | solution.py:408
  4.5 2.9 %collective-permute-start.1 = (bf16[528,128]{1,0:T(8,128)(2,1)S(1)}, bf16[528,128]{1,0:T(8,128)(2,1)S(1)}, u32[]{:S(2)}, u32[]{:S(2)}) collective-permute-start(bf16[528,128]{1,0:T(8,128)(2,1)S(1)} %get-tuple-element.45.total_ref), channel_id=1, source_target_pairs={{0,8},{4,12},{8,0},{12,4},{16,24},{20,28},{24,16},{28,20},{1,9},{5... | collective-permute-start | bytes 405512 | tf_op jit(solution)/shard_map/ppermute | solution.py:484
  7.5 3.9 %local_part.2 = (f32[512,2048]{1,0:T(8,128)S(1)}, f32[512,2048]{1,0:T(8,128)S(1)}, bf16[512,256]{1,0:T(8,128)(2,1)S(1)}, f32[128,2048]{1,0:T(8,128)S(1)}, f32[32...) custom-call(bf16[512,2048]{1,0:T(8,128)(2,1)} %gate_hbm.3, bf16[512,256]{1,0:T(8,128)(2,1)} %c_hbm.3, ...), custom_call_target="tpu_custom_call" | custom-call | flops 4000000000 | bytes 1 | tf_op jit(solution)/shard_map/local_part/pallas_call | solution.py:408
  12.0 2.2 %collective-permute-start.3 = (bf16[528,128]{1,0:T(8,128)(2,1)S(1)}, bf16[528,128]{1,0:T(8,128)(2,1)S(1)}, u32[]{:S(2)}, u32[]{:S(2)}) collective-permute-start(bf16[528,128]{1,0:T(8,128)(2,1)S(1)} %fold.2.after_ref), channel_id=1, source_target_pairs={{0,16},{4,20},{8,24},{12,28},{16,0},{20,4},{24,8},{28,12},{1,17},{... | collective-permute-start | bytes 405512 | tf_op jit(solution)/shard_map/ppermute | solution.py:484
  14.4 1.8 %collective-permute-start.4 = (bf16[528,128]{1,0:T(8,128)(2,1)S(1)}, bf16[528,128]{1,0:T(8,128)(2,1)S(1)}, u32[]{:S(2)}, u32[]{:S(2)}) collective-permute-start(bf16[528,128]{1,0:T(8,128)(2,1)S(1)} %fold.3.after_ref), channel_id=1, source_target_pairs={{0,16},{4,20},{8,24},{12,28},{16,0},{20,4},{24,8},{28,12},{1,17},{... | collective-permute-start | bytes 405512 | tf_op jit(solution)/shard_map/ppermute | solution.py:484
  16.3 3.9 %local_part.3 = (f32[512,2048]{1,0:T(8,128)S(1)}, f32[512,2048]{1,0:T(8,128)S(1)}, bf16[512,256]{1,0:T(8,128)(2,1)S(1)}, f32[128,2048]{1,0:T(8,128)S(1)}, f32[32...) custom-call(bf16[512,2048]{1,0:T(8,128)(2,1)} %gate_hbm.3, ...), custom_call_target="tpu_custom_call", output_to_operand_aliasing={{0}: (9, {}), {1}: (10, {}), {2}: (11, {}), {3}: (12, {}), ... | custom-call | flops 4000000000 | bytes 1 | tf_op jit(solution)/shard_map/local_part/pallas_call | solution.py:408
  20.7 1.5 %collective-permute-done.5.recv_ref = bf16[128,1024]{1,0:T(8,128)(2,1)S(1)} collective-permute-done((bf16[128,1024]{1,0:T(8,128)(2,1)S(1)}, bf16[128,1024]{1,0:T(8,128)(2,1)S(1)}, u32[]{:S(2)}, u32[]{:S(2)}) %collective-permute-start.5) | collective-permute-done | bytes 262176 | tf_op jit(solution)/shard_map/ppermute | solution.py:526
  22.3 2.3 %first_block.1 = (bf16[128,2048]{1,0:T(8,128)(2,1)S(1)}, bf16[128,2048]{1,0:T(8,128)(2,1)S(1)}) custom-call(s32[1]{0:T(128)} %bitcast.1.ctx_ref, s32[1]{0:T(128)} %bitcast.here_ref, f32[512,2048]{1,0:T(8,128)S(1)} %get-tuple-element.51.mixed_ref, f32[512,2048]{1,0:T(8,128)S(1)} %get-tuple-element.52.scale_ref, bf16[512,256]{1,0:T(8,128)(2,1)S(1)} %get-tuple-element.53.c_ref, ...), custom_call_target="tpu_custom_call" | custom-call | flops 1 | bytes 1 | tf_op jit(solution)/shard_map/first_block/pallas_call | solution.py:408
  24.6 2.0 %collective-permute-start.11 = (bf16[128,2048]{1,0:T(8,128)(2,1)S(1)}, bf16[128,2048]{1,0:T(8,128)(2,1)S(1)}, u32[]{:S(2)}, u32[]{:S(2)}) collective-permute-start(bf16[128,2048]{1,0:T(8,128)(2,1)S(1)} %get-tuple-element.60.a_ref), channel_id=1, source_target_pairs={{0,1},{1,0},{2,3},{3,2},{4,5},{5,4},{6,7},{7,6},{8,9},{9,8},{10,11... | collective-permute-start | bytes 1572872 | tf_op jit(solution)/shard_map/ppermute | solution.py:431
  26.6 1.8 %first_block_rest.1.b_ref = bf16[128,2048]{1,0:T(8,128)(2,1)S(1)} custom-call(bf16[128,2048]{1,0:T(8,128)(2,1)S(1)} %get-tuple-element.58.normed_ref, bf16[2048,2048]{1,0:T(8,128)(2,1)S(1)} %get-tuple-element.59.w_ref.wb_ref), custom_call_target="tpu_custom_call" | custom-call | flops 1 | bytes 1 | tf_op jit(solution)/shard_map/first_block_rest/pallas_call | solution.py:408
  28.6 9.0 %other_blocks.1.refs_1_.refs_2_.sums_ref = bf16[512,4096]{1,0:T(8,128)(2,1)S(1)} custom-call(s32[1]{0:T(128)} %bitcast.1.ctx_ref, s32[1]{0:T(128)} %bitcast.here_ref, f32[512,2048]{1,0:T(8,128)S(1)} %get-tuple-element.51.mixed_ref, f32[512,2048]{1,0:T(8,128)S(1)} %get-tuple-element.52.scale_ref, bf16[512,256]{1,0:T(8,128)(2,1)S(1)} %get-tuple-element.53.c_ref, ...), custom_call_target="tpu_custom_call" | custom-call | flops 1 | bytes 1 | tf_op jit(solution)/shard_map/other_blocks/pallas_call | solution.py:408
  37.6 1.7 %collective-permute-done.11.refs_0_ = bf16[128,2048]{1,0:T(8,128)(2,1)S(1)} collective-permute-done((bf16[128,2048]{1,0:T(8,128)(2,1)S(1)}, bf16[128,2048]{1,0:T(8,128)(2,1)S(1)}, u32[]{:S(2)}, u32[]{:S(2)}) %collective-permute-start.11) | collective-permute-done | bytes 524320 | tf_op jit(solution)/shard_map/ppermute | solution.py:431
  39.5 2.0 %collective-permute-start.12 = (bf16[128,2048]{1,0:T(8,128)(2,1)S(1)}, bf16[128,2048]{1,0:T(8,128)(2,1)S(1)}, u32[]{:S(2)}, u32[]{:S(2)}) collective-permute-start(bf16[128,2048]{1,0:T(8,128)(2,1)S(1)} %get-tuple-element.65), channel_id=1, source_target_pairs={{0,1},{1,0},{2,3},{3,2},{4,5},{5,4},{6,7},{7,6},{8,9},{9,8},{10,11... | collective-permute-start | bytes 1572872 | tf_op jit(solution)/shard_map/ppermute | solution.py:436
  42.2 8.4 %collective-permute-done.6.refs_0_ = bf16[128,2048]{1,0:T(8,128)(2,1)S(1)} collective-permute-done((bf16[128,2048]{1,0:T(8,128)(2,1)S(1)}, bf16[128,2048]{1,0:T(8,128)(2,1)S(1)}, u32[]{:S(2)}, u32[]{:S(2)}) %collective-permute-start.6) | collective-permute-done | bytes 524320 | tf_op jit(solution)/shard_map/ppermute | solution.py:431
  50.8 2.0 %collective-permute-start.7 = (bf16[128,2048]{1,0:T(8,128)(2,1)S(1)}, bf16[128,2048]{1,0:T(8,128)(2,1)S(1)}, u32[]{:S(2)}, u32[]{:S(2)}) collective-permute-start(bf16[128,2048]{1,0:T(8,128)(2,1)S(1)} %get-tuple-element.61), channel_id=1, source_target_pairs={{0,1},{1,0},{2,3},{3,2},{4,5},{5,4},{6,7},{7,6},{8,9},{9,8},{10,11... | collective-permute-start | bytes 1572872 | tf_op jit(solution)/shard_map/ppermute | solution.py:436
  53.5 8.4 %collective-permute-done.12.refs_0_ = bf16[128,2048]{1,0:T(8,128)(2,1)S(1)} collective-permute-done((bf16[128,2048]{1,0:T(8,128)(2,1)S(1)}, bf16[128,2048]{1,0:T(8,128)(2,1)S(1)}, u32[]{:S(2)}, u32[]{:S(2)}) %collective-permute-start.12) | collective-permute-done | bytes 524320 | tf_op jit(solution)/shard_map/ppermute | solution.py:436
  62.1 2.0 %collective-permute-start.14 = (bf16[128,2048]{1,0:T(8,128)(2,1)S(1)}, bf16[128,2048]{1,0:T(8,128)(2,1)S(1)}, u32[]{:S(2)}, u32[]{:S(2)}) collective-permute-start(bf16[128,2048]{1,0:T(8,128)(2,1)S(1)} %get-tuple-element.67), channel_id=1, source_target_pairs={{0,1},{1,0},{2,3},{3,2},{4,5},{5,4},{6,7},{7,6},{8,9},{9,8},{10,11... | collective-permute-start | bytes 1572872 | tf_op jit(solution)/shard_map/ppermute | solution.py:436
  64.9 8.2 %collective-permute-done.7.refs_0_ = bf16[128,2048]{1,0:T(8,128)(2,1)S(1)} collective-permute-done((bf16[128,2048]{1,0:T(8,128)(2,1)S(1)}, bf16[128,2048]{1,0:T(8,128)(2,1)S(1)}, u32[]{:S(2)}, u32[]{:S(2)}) %collective-permute-start.7) | collective-permute-done | bytes 524320 | tf_op jit(solution)/shard_map/ppermute | solution.py:436
  74.1 4.8 %collective-permute-start.9 = (bf16[128,2048]{1,0:T(8,128)(2,1)S(1)}, bf16[128,2048]{1,0:T(8,128)(2,1)S(1)}, u32[]{:S(2)}, u32[]{:S(2)}) collective-permute-start(bf16[128,2048]{1,0:T(8,128)(2,1)S(1)} %get-tuple-element.63), channel_id=1, source_target_pairs={{0,1},{1,0},{2,3},{3,2},{4,5},{5,4},{6,7},{7,6},{8,9},{9,8},{10,11... | collective-permute-start | bytes 1572872 | tf_op jit(solution)/shard_map/ppermute | solution.py:436
  78.9 5.4 %collective-permute-done.14.even_ref = bf16[128,2048]{1,0:T(8,128)(2,1)S(1)} collective-permute-done((bf16[128,2048]{1,0:T(8,128)(2,1)S(1)}, bf16[128,2048]{1,0:T(8,128)(2,1)S(1)}, u32[]{:S(2)}, u32[]{:S(2)}) %collective-permute-start.14) | collective-permute-done | bytes 524320 | tf_op jit(solution)/shard_map/ppermute | solution.py:436
  84.3 0.9 sum_up.2.refs_0_
  85.2 9.8 %collective-permute-done.9.even_ref = bf16[128,2048]{1,0:T(8,128)(2,1)S(1)} collective-permute-done((bf16[128,2048]{1,0:T(8,128)(2,1)S(1)}, bf16[128,2048]{1,0:T(8,128)(2,1)S(1)}, u32[]{:S(2)}, u32[]{:S(2)}) %collective-permute-start.9) | collective-permute-done | bytes 524320 | tf_op jit(solution)/shard_map/ppermute | solution.py:436
  95.0 0.9 sum_up.3
  (29 shorter events, 6.1 us)
Async XLA Ops:
  0.0 7.5 %copy-start.1 = (f32[32]{0:T(128)S(1)}, f32[32]{0:T(128)}, u32[]{:S(2)}) copy-start(f32[32]{0:T(128)} %param.15) | copy-start | bytes 388
  2.6 1.7 %collective-permute-start = (bf16[1040,128]{1,0:T(8,128)(2,1)S(1)}, bf16[1040,128]{1,0:T(8,128)(2,1)S(1)}, u32[]{:S(2)}, u32[]{:S(2)}) collective-permute-start(bf16[1040,128]{1,0:T(8,128)(2,1)S(1)} %get-tuple-element.42), channel_id=1, source_target_pairs={{0,4},{4,0},{8,12},{12,8},{16,20},{20,16},{24,28},{28,24},{1,5},{5... | collective-permute-start | bytes 798728 | tf_op jit(solution)/shard_map/ppermute | solution.py:474
  4.5 7.3 %collective-permute-start.1 = (bf16[528,128]{1,0:T(8,128)(2,1)S(1)}, bf16[528,128]{1,0:T(8,128)(2,1)S(1)}, u32[]{:S(2)}, u32[]{:S(2)}) collective-permute-start(bf16[528,128]{1,0:T(8,128)(2,1)S(1)} %get-tuple-element.45.total_ref), channel_id=1, source_target_pairs={{0,8},{4,12},{8,0},{12,4},{16,24},{20,28},{24,16},{28,20},{1,9},{5... | collective-permute-start | bytes 405512 | tf_op jit(solution)/shard_map/ppermute | solution.py:484
  7.4 6.8 %collective-permute-start.2 = (bf16[528,128]{1,0:T(8,128)(2,1)S(1)}, bf16[528,128]{1,0:T(8,128)(2,1)S(1)}, u32[]{:S(2)}, u32[]{:S(2)}) collective-permute-start(bf16[528,128]{1,0:T(8,128)(2,1)S(1)} %get-tuple-element.43.after_ref.total_ref), channel_id=1, source_target_pairs={{0,8},{4,12},{8,0},{12,4},{16,24},{20,28},{24,16},{28,20},{1,9},{5... | collective-permute-start | bytes 405512 | tf_op jit(solution)/shard_map/ppermute | solution.py:484
  12.0 8.2 %collective-permute-start.3 = (bf16[528,128]{1,0:T(8,128)(2,1)S(1)}, bf16[528,128]{1,0:T(8,128)(2,1)S(1)}, u32[]{:S(2)}, u32[]{:S(2)}) collective-permute-start(bf16[528,128]{1,0:T(8,128)(2,1)S(1)} %fold.2.after_ref), channel_id=1, source_target_pairs={{0,16},{4,20},{8,24},{12,28},{16,0},{20,4},{24,8},{28,12},{1,17},{... | collective-permute-start | bytes 405512 | tf_op jit(solution)/shard_map/ppermute | solution.py:484
  14.4 5.7 %collective-permute-start.4 = (bf16[528,128]{1,0:T(8,128)(2,1)S(1)}, bf16[528,128]{1,0:T(8,128)(2,1)S(1)}, u32[]{:S(2)}, u32[]{:S(2)}) collective-permute-start(bf16[528,128]{1,0:T(8,128)(2,1)S(1)} %fold.3.after_ref), channel_id=1, source_target_pairs={{0,16},{4,20},{8,24},{12,28},{16,0},{20,4},{24,8},{28,12},{1,17},{... | collective-permute-start | bytes 405512 | tf_op jit(solution)/shard_map/ppermute | solution.py:484
  16.3 6.0 %copy-start = (f32[2048]{0:T(1024)S(1)}, f32[2048]{0:T(1024)}, u32[]{:S(2)}) copy-start(f32[2048]{0:T(1024)} %param.16) | copy-start | bytes 24580
  20.7 1.6 %collective-permute-start.5 = (bf16[128,1024]{1,0:T(8,128)(2,1)S(1)}, bf16[128,1024]{1,0:T(8,128)(2,1)S(1)}, u32[]{:S(2)}, u32[]{:S(2)}) collective-permute-start(bf16[128,1024]{1,0:T(8,128)(2,1)S(1)} %get-tuple-element.56), channel_id=1, source_target_pairs={{0,4},{4,0},{8,12},{12,8},{16,20},{20,16},{24,28},{28,24},{1,5},{5... | collective-permute-start | bytes 786440 | tf_op jit(solution)/shard_map/ppermute | solution.py:526
  24.6 14.8 %collective-permute-start.11 = (bf16[128,2048]{1,0:T(8,128)(2,1)S(1)}, bf16[128,2048]{1,0:T(8,128)(2,1)S(1)}, u32[]{:S(2)}, u32[]{:S(2)}) collective-permute-start(bf16[128,2048]{1,0:T(8,128)(2,1)S(1)} %get-tuple-element.60.a_ref), channel_id=1, source_target_pairs={{0,1},{1,0},{2,3},{3,2},{4,5},{5,4},{6,7},{7,6},{8,9},{9,8},{10,11... | collective-permute-start | bytes 1572872 | tf_op jit(solution)/shard_map/ppermute | solution.py:431
  28.4 22.2 %collective-permute-start.6 = (bf16[128,2048]{1,0:T(8,128)(2,1)S(1)}, bf16[128,2048]{1,0:T(8,128)(2,1)S(1)}, u32[]{:S(2)}, u32[]{:S(2)}) collective-permute-start(bf16[128,2048]{1,0:T(8,128)(2,1)S(1)} %first_block_rest.1.b_ref), channel_id=1, source_target_pairs={{0,1},{1,0},{2,3},{3,2},{4,5},{5,4},{6,7},{7,6},{8,9},{9,8},{10,11... | collective-permute-start | bytes 1572872 | tf_op jit(solution)/shard_map/ppermute | solution.py:431
  39.5 22.3 %collective-permute-start.12 = (bf16[128,2048]{1,0:T(8,128)(2,1)S(1)}, bf16[128,2048]{1,0:T(8,128)(2,1)S(1)}, u32[]{:S(2)}, u32[]{:S(2)}) collective-permute-start(bf16[128,2048]{1,0:T(8,128)(2,1)S(1)} %get-tuple-element.65), channel_id=1, source_target_pairs={{0,1},{1,0},{2,3},{3,2},{4,5},{5,4},{6,7},{7,6},{8,9},{9,8},{10,11... | collective-permute-start | bytes 1572872 | tf_op jit(solution)/shard_map/ppermute | solution.py:436
  41.6 20.3 %collective-permute-start.13 = (bf16[128,2048]{1,0:T(8,128)(2,1)S(1)}, bf16[128,2048]{1,0:T(8,128)(2,1)S(1)}, u32[]{:S(2)}, u32[]{:S(2)}) collective-permute-start(bf16[128,2048]{1,0:T(8,128)(2,1)S(1)} %get-tuple-element.66), channel_id=1, source_target_pairs={{1,2},{2,1},{5,6},{6,5},{9,10},{10,9},{13,14},{14,13},{17,18},{18,... | collective-permute-start | bytes 1572872 | tf_op jit(solution)/shard_map/ppermute | solution.py:436
  50.8 22.3 %collective-permute-start.7 = (bf16[128,2048]{1,0:T(8,128)(2,1)S(1)}, bf16[128,2048]{1,0:T(8,128)(2,1)S(1)}, u32[]{:S(2)}, u32[]{:S(2)}) collective-permute-start(bf16[128,2048]{1,0:T(8,128)(2,1)S(1)} %get-tuple-element.61), channel_id=1, source_target_pairs={{0,1},{1,0},{2,3},{3,2},{4,5},{5,4},{6,7},{7,6},{8,9},{9,8},{10,11... | collective-permute-start | bytes 1572872 | tf_op jit(solution)/shard_map/ppermute | solution.py:436
  52.8 20.3 %collective-permute-start.8 = (bf16[128,2048]{1,0:T(8,128)(2,1)S(1)}, bf16[128,2048]{1,0:T(8,128)(2,1)S(1)}, u32[]{:S(2)}, u32[]{:S(2)}) collective-permute-start(bf16[128,2048]{1,0:T(8,128)(2,1)S(1)} %get-tuple-element.62), channel_id=1, source_target_pairs={{1,2},{2,1},{5,6},{6,5},{9,10},{10,9},{13,14},{14,13},{17,18},{18,... | collective-permute-start | bytes 1572872 | tf_op jit(solution)/shard_map/ppermute | solution.py:436
  62.1 22.2 %collective-permute-start.14 = (bf16[128,2048]{1,0:T(8,128)(2,1)S(1)}, bf16[128,2048]{1,0:T(8,128)(2,1)S(1)}, u32[]{:S(2)}, u32[]{:S(2)}) collective-permute-start(bf16[128,2048]{1,0:T(8,128)(2,1)S(1)} %get-tuple-element.67), channel_id=1, source_target_pairs={{0,1},{1,0},{2,3},{3,2},{4,5},{5,4},{6,7},{7,6},{8,9},{9,8},{10,11... | collective-permute-start | bytes 1572872 | tf_op jit(solution)/shard_map/ppermute | solution.py:436
  64.2 20.1 %collective-permute-start.15 = (bf16[128,2048]{1,0:T(8,128)(2,1)S(1)}, bf16[128,2048]{1,0:T(8,128)(2,1)S(1)}, u32[]{:S(2)}, u32[]{:S(2)}) collective-permute-start(bf16[128,2048]{1,0:T(8,128)(2,1)S(1)} %get-tuple-element.68), channel_id=1, source_target_pairs={{1,2},{2,1},{5,6},{6,5},{9,10},{10,9},{13,14},{14,13},{17,18},{18,... | collective-permute-start | bytes 1572872 | tf_op jit(solution)/shard_map/ppermute | solution.py:436
  73.4 11.8 %collective-permute-start.10 = (bf16[128,2048]{1,0:T(8,128)(2,1)S(1)}, bf16[128,2048]{1,0:T(8,128)(2,1)S(1)}, u32[]{:S(2)}, u32[]{:S(2)}) collective-permute-start(bf16[128,2048]{1,0:T(8,128)(2,1)S(1)} %get-tuple-element.64), channel_id=1, source_target_pairs={{1,2},{2,1},{5,6},{6,5},{9,10},{10,9},{13,14},{14,13},{17,18},{18,... | collective-permute-start | bytes 1572872 | tf_op jit(solution)/shard_map/ppermute | solution.py:436
  74.1 20.9 %collective-permute-start.9 = (bf16[128,2048]{1,0:T(8,128)(2,1)S(1)}, bf16[128,2048]{1,0:T(8,128)(2,1)S(1)}, u32[]{:S(2)}, u32[]{:S(2)}) collective-permute-start(bf16[128,2048]{1,0:T(8,128)(2,1)S(1)} %get-tuple-element.63), channel_id=1, source_target_pairs={{0,1},{1,0},{2,3},{3,2},{4,5},{5,4},{6,7},{7,6},{8,9},{9,8},{10,11... | collective-permute-start | bytes 1572872 | tf_op jit(solution)/shard_map/ppermute | solution.py:436

commit v6 on v5

--- a/solution.py
+++ b/solution.py
@@ -13,7 +13,7 @@
 MIDDLE = CHUNK // 2 - 1
 EXTRA = 16
 COLUMN_TILE = 512
-HALVES = 2
+PARTS = 4
 WEIGHT_COPIES = 8
 SUM_COPIES = 4
 PIECES = 2
@@ -90,7 +90,7 @@
     return jnp.sum(dot(logs, spread), axis=0, keepdims=True)
 
 
-def end_state(groups, half, x_ref, b_ref, step_ref, decay_ref, weighted, message_ref, spread):
+def end_state(groups, half, x_ref, b_ref, step_ref, decay_ref, weighted, message_ref, spread, x_copies=(), b_copies=()):
     rows, width = weighted.shape
     heads = width // HEAD_DIM
     of_heads = pl.ds(pl.multiple_of(half * heads, heads), heads)
@@ -100,10 +100,15 @@
     for sums in running_sums(decay_ref[of_heads, :]):
         running.append(before + sums)
         before = before + sums[:, CHUNK - 1 :]
-    for n, sums in enumerate(running):
+    factors = [by_row(step_ref[of_heads, rows_of(n)] * jnp.exp(before - sums)) for n, sums in enumerate(running)]
+    for n, factor in enumerate(factors):
         here = rows_of(n)
-        factor = dot(by_row(step_ref[of_heads, here] * jnp.exp(before - sums)), spread)
+        factor = dot(factor, spread)
+        for copy in x_copies[n : n + 1]:
+            copy.wait()
         weighted[here, :] = (x_ref[here, of_channels].astype(F32) * factor).astype(BF16)
+    for copy in b_copies:
+        copy.wait()
     state = lax.dot_general(
         b_ref[:, of_group], weighted[...], (((0,), (0,)), ((), ())), preferred_element_type=F32
     )
@@ -115,18 +120,22 @@
                 spread_ref, weighted, semaphores):
     width = weighted.shape[1]
     other = 1 - (ctx_ref[0] & 1)
-    of_channels = [pl.ds(pl.multiple_of(half * width, width), width) for half in (other, 1 - other)]
+    first, second = [pl.ds(pl.multiple_of(half * width, width), width) for half in (other, 1 - other)]
+    rows = [rows_of(n) for n in range(x_ref.shape[0] // CHUNK)]
     copies = load(
-        [(decay_hbm, decay_ref), (step_hbm, step_ref), (b_hbm, b_ref)]
-        + [(x_hbm.at[:, cut], x_ref.at[:, cut]) for cut in of_channels],
+        [(decay_hbm, decay_ref), (step_hbm, step_ref)]
+        + [(x_hbm.at[here, first], x_ref.at[here, first]) for here in rows]
+        + [(b_hbm, b_ref), (x_hbm.at[:, second], x_ref.at[:, second])],
         semaphores,
     )
     spread = head_map(width)
     spread_ref[...] = spread
-    for copy in copies[:4]:
+    for copy in copies[:2]:
         copy.wait()
-    end_state(groups, other, x_ref, b_ref, step_ref, decay_ref, weighted, send_ref, spread)
-    copies[4].wait()
+    end_state(
+        groups, other, x_ref, b_ref, step_ref, decay_ref, weighted, send_ref, spread, copies[2:-2], copies[-2:-1]
+    )
+    copies[-1].wait()
 
 
 def keep_kernel(groups, ctx_ref, x_ref, b_ref, step_ref, decay_ref, spread_ref, keep_ref, weighted):
@@ -266,15 +275,19 @@
         copy.wait()
 
 
+def norm_group(mixed, scale, c_rows, gain, state):
+    whole = mixed + scale * dot(c_rows, state)
+    meansq = jnp.mean(whole * whole, axis=1, keepdims=True)
+    return (whole * lax.rsqrt(meansq + 1e-05) * gain).astype(BF16)
+
+
 def norm_rows(groups, state, mixed, scale, c_rows, gain):
     width = mixed.shape[1] // groups
     parts = []
     for g in range(groups):
         cut = slice(g * width, (g + 1) * width)
-        carried = dot(c_rows[:, g * STATE : (g + 1) * STATE], state[:, cut])
-        whole = mixed[:, cut] + scale[:, cut] * carried
-        meansq = jnp.mean(whole * whole, axis=1, keepdims=True)
-        parts.append((whole * lax.rsqrt(meansq + 1e-05) * gain[:, cut]).astype(BF16))
+        of_state = c_rows[:, g * STATE : (g + 1) * STATE]
+        parts.append(norm_group(mixed[:, cut], scale[:, cut], of_state, gain[:, cut], state[:, cut]))
     return parts
 
 
@@ -295,34 +308,69 @@
     return pl.ds(pl.multiple_of(block * size, size), size)
 
 
-def first_kernel(groups, count, ctx_ref, here_ref, mixed_ref, scale_ref, c_ref, keep_ref, recv_ref, gain_ref, w_ref, out_ref,
-                 normed_ref, state):
+def one_group(group, here, mixed_ref, scale_ref, c_ref, gain_ref, state):
+    width = state.shape[1]
+    cut = pl.ds(pl.multiple_of(group * width, width), width)
+    part = pl.ds(pl.multiple_of(group * STATE, STATE), STATE)
+    return norm_group(mixed_ref[here, cut], scale_ref[here, cut], c_ref[here, part], gain_ref[:, cut], state)
+
+
+def times_rows(group, normed, w_ref, columns):
+    width = normed.shape[1]
+    return dot(normed, w_ref[pl.ds(pl.multiple_of(group * width, width), width), :columns])
+
+
+def own_group_kernel(count, ctx_ref, here_ref, mixed_ref, scale_ref, c_ref, gain_ref, w_ref, keep_ref, normed_ref, product_ref):
+    size, columns = product_ref.shape
+    here = block_at(here_ref[0], 0, count, size)
+    group = ctx_ref[0] & 1
+    normed = one_group(group, here, mixed_ref, scale_ref, c_ref, gain_ref, keep_ref[...])
+    normed_ref[...] = normed
+    product_ref[...] = times_rows(group, normed, w_ref, columns)
+
+
+def other_group_kernel(count, ctx_ref, here_ref, mixed_ref, scale_ref, c_ref, gain_ref, w_ref, recv_ref, own_ref, product_ref,
+                       out_ref, normed_ref):
+    size, columns = product_ref.shape
+    here = block_at(here_ref[0], 0, count, size)
+    group = 1 - (ctx_ref[0] & 1)
+    normed = one_group(group, here, mixed_ref, scale_ref, c_ref, gain_ref, recv_ref[...])
+    out_ref[...] = (product_ref[...] + times_rows(group, normed, w_ref, columns)).astype(BF16)
+    width = normed.shape[1]
+    for g in range(2):
+
+        @pl.when(group == g)
+        def _():
+            normed_ref[:, rows_of(g, width)] = normed
+            normed_ref[:, rows_of(1 - g, width)] = own_ref[...]
+
+
+def both_groups_kernel(groups, count, ctx_ref, here_ref, mixed_ref, scale_ref, c_ref, gain_ref, w_ref, keep_ref, recv_ref,
+                       out_ref, normed_ref, state):
     fill_state(ctx_ref, keep_ref, recv_ref, state)
     width = normed_ref.shape[1] // groups
     here = block_at(here_ref[0], 0, count, normed_ref.shape[0])
     rows = norm_rows(groups, state, mixed_ref.at[here, :], scale_ref.at[here, :], c_ref.at[here, :], gain_ref)
     for g, part in enumerate(rows):
         normed_ref[:, g * width : (g + 1) * width] = part
-
-    @pl.loop(0, out_ref.shape[1] // COLUMN_TILE)
-    def _(j):
-        cut = pl.ds(pl.multiple_of(j * COLUMN_TILE, COLUMN_TILE), COLUMN_TILE)
-        out_ref[:, cut] = dot(normed_ref[...], w_ref[:, cut]).astype(BF16)
-
-
-def second_kernel(normed_ref, w_ref, out_ref):
-    @pl.loop(0, out_ref.shape[1] // COLUMN_TILE)
-    def _(j):
-        cut = pl.ds(pl.multiple_of(j * COLUMN_TILE, COLUMN_TILE), COLUMN_TILE)
-        out_ref[:, cut] = dot(normed_ref[...], w_ref[:, cut]).astype(BF16)
-
-
-def rest_kernel(groups, count, ctx_ref, here_ref, mixed_ref, scale_ref, c_ref, keep_ref, recv_ref, gain_ref, wa_ref, wb_ref,
-                a_ref, b_ref, out_ref, state, normed):
-    size, half = a_ref.shape
+    out_ref[...] = dot(normed_ref[...], w_ref[:, : out_ref.shape[1]]).astype(BF16)
+
+
+def project_kernel(start, normed_ref, w_ref, *outs):
+    for ref in outs:
+        columns = ref.shape[1]
+        ref[...] = dot(normed_ref[...], w_ref[:, start : start + columns]).astype(BF16)
+        start += columns
+
+
+def rest_kernel(groups, count, ctx_ref, here_ref, mixed_ref, scale_ref, c_ref, gain_ref, wa_ref, wb_ref, keep_ref, recv_ref,
+                *refs):
+    *first, out_ref, state, normed = refs
+    size, piece = first[0].shape
+    half = wa_ref.shape[1]
     blocks = [block_at(here_ref[0], n, count, size) for n in range(count)]
-    out_ref[blocks[0], :half] = a_ref[...]
-    out_ref[blocks[0], half:] = b_ref[...]
+    for n, ref in enumerate(first):
+        out_ref[blocks[0], n * piece : (n + 1) * piece] = ref[...]
     fill_state(ctx_ref, keep_ref, recv_ref, state)
     width = normed.shape[1] // groups
     for n in range(1, count):
@@ -420,13 +468,13 @@
 
 def line_reduce(first, partial_sums, here, size, columns):
     count = lax.axis_size("tp")
-    width = columns // HALVES
+    width = columns // PARTS
     block = ((size, width), BF16)
     even_edges = [(i, i ^ 1) for i in range(count)]
     odd_edges = [(i, ((i + 1) ^ 1) - 1) for i in range(1, count - 1)]
-    arrived = [()] * HALVES
+    arrived = [()] * PARTS
     for step in range(1, count):
-        for half in range(HALVES):
+        for half in range(PARTS):
             if step == 1:
                 arrived[half] = (lax.ppermute(first[half], "tp", even_edges),)
                 continue
@@ -435,7 +483,7 @@
             )
             arrived[half] = (lax.ppermute(even, "tp", even_edges), lax.ppermute(odd, "tp", odd_edges))
     out = ()
-    for half in range(HALVES):
+    for half in range(PARTS):
         ins = (here, *arrived[half], partial_sums, *out)
         scratch = [pltpu.VMEM((size, width), BF16), pltpu.SemaphoreType.DMA((SUM_COPIES,))]
         kernel = partial(sum_kernel, half * width)
@@ -467,7 +515,7 @@
         "end_state_sent",
         (ctx, here, (x_in,), (b_in,), (step_size.T,), (log_decay.T,)),
         (message, ((rows, channels), BF16), maps, by_head, by_head, ((128, half), BF16)),
-        scratch=[weighted, pltpu.SemaphoreType.DMA((5,))],
+        scratch=[weighted, pltpu.SemaphoreType.DMA((4 + chunks,))],
         vmem=6,
     )
     swap = [(i, i ^ 1) for i in range(devices)]
@@ -525,23 +573,37 @@
     )
     recv = lax.ppermute(send, "ctx", swap)
 
-    first = ((size, columns // 2), BF16)
     gain = norm_gain.reshape(1, channels)
-    inputs = (ctx, here, mixed, scale, c_here, keep, recv, gain, weight_a)
+    width = columns // PARTS
+    piece = ((size, width), BF16)
+    row_block = ((size, channels), BF16)
     whole_state = pltpu.VMEM((STATE, channels), BF16)
-    first_a, normed = in_vmem(
-        partial(first_kernel, groups, count), "first_block", inputs, (first, ((size, channels), BF16)), [whole_state]
-    )
-    (first_b,) = in_vmem(second_kernel, "first_block_rest", (normed, weight_b), (first,))
+    inputs = (ctx, here, mixed, scale, c_here, gain, weight_a)
+    if groups == 2:
+        own_group, product = in_vmem(
+            partial(own_group_kernel, count), "own_group", (*inputs, keep), (((size, half), BF16), ((size, width), F32)),
+            flops=10**9,
+        )
+        first, normed = in_vmem(
+            partial(other_group_kernel, count), "other_group", (*inputs, recv, own_group, product), (piece, row_block)
+        )
+    else:
+        first, normed = in_vmem(
+            partial(both_groups_kernel, groups, count), "both_groups", (*inputs, keep, recv), (piece, row_block), [whole_state]
+        )
+    pieces_out = [first]
+    for start, weight, number in ((1, weight_a, PARTS // 2 - 1), (0, weight_b, PARTS // 2)):
+        kernel = partial(project_kernel, start * width)
+        pieces_out.extend(in_vmem(kernel, "first_block_rest", (normed, weight), (piece,) * number))
     (partial_sums,) = in_vmem(
         partial(rest_kernel, groups, count),
         "other_blocks",
-        (*inputs, weight_b, first_a, first_b),
+        (*inputs, weight_b, keep, recv, *pieces_out),
         (((rows, columns), BF16),),
         [whole_state, pltpu.VMEM((rows - size, channels), BF16)],
         vmem=6,
     )
-    return line_reduce((first_a, first_b), partial_sums, here, size, columns)
+    return line_reduce(pieces_out, partial_sums, here, size, columns)
 
 
 def solution(mesh):

time: 96.1 us -> 94.9 us (0.988)
  waiting for transfers between devices: 43.8 us -> 17.4 us
  starting transfers between devices: 23.4 us -> 47 us
  Pallas kernels: 28.4 us -> 29.5 us
    ppermute x4 -> x8, starting transfers between devices: 10.9 us -> 29.8 us  [line_reduce(): lax.ppermute(even, 'tp', even_edges)]
    ppermute x4 -> x8, waiting for transfers between devices: 31.7 us -> 13.8 us  [line_reduce(): lax.ppermute(even, 'tp', even_edges)]
    ppermute x2 -> x4, waiting for transfers between devices: 10.1 us -> 2.33 us  [line_reduce(): arrived[half] = (lax.ppermute(first[half], 'tp', even_edges),)]
    ppermute x4 -> x8, starting transfers between devices: 2.74 us -> 5.38 us  [line_reduce(): lax.ppermute(odd, 'tp', odd_edges)]
    ppermute x2 -> x4, starting transfers between devices: 2.18 us -> 4.26 us  [line_reduce(): arrived[half] = (lax.ppermute(first[half], 'tp', even_edges),)]
    pallas_call x17 -> x25, Pallas kernels: 28.4 us -> 29.5 us  [in_vmem(): pl.pallas_call(kernel, in_specs=specs, out_specs=[pl.BlockSpec(memory_spa...]
  transfers between devices with their start and end apart: 16 -> 26, of which waited for: 8 -> 8; matrix products, arithmetic and copies ran while one was open for 0% -> 0% of each run, Pallas kernels for 23% -> 26%
where the time goes in v6:
time: 94.9 us; the launch traced here: 94.5 us
  starting transfers between devices  47 us (50%)
  Pallas kernels  29.5 us (31%)
  waiting for transfers between devices  17.4 us (18%)
    ppermute x8, starting transfers between devices, line_reduce(): lax.ppermute(even, 'tp', even_edges)  29.8 us
    pallas_call x25, Pallas kernels, in_vmem(): pl.pallas_call(kernel, in_specs=specs, out_specs=[pl.BlockSpec(memory_spa...  29.5 us
    ppermute x8, waiting for transfers between devices, line_reduce(): lax.ppermute(even, 'tp', even_edges)  13.8 us
    ppermute x4, starting transfers between devices, swap_chips(): lax.ppermute(v, 'ctx', [(i, i ^ 2 << level) for i in range(devices)])  6.99 us
    ppermute x8, starting transfers between devices, line_reduce(): lax.ppermute(odd, 'tp', odd_edges)  5.38 us
    ppermute x4, starting transfers between devices, line_reduce(): arrived[half] = (lax.ppermute(first[half], 'tp', even_edges),)  4.26 us
    ppermute x4, waiting for transfers between devices, line_reduce(): arrived[half] = (lax.ppermute(first[half], 'tp', even_edges),)  2.33 us
  transfers between devices with their start and end apart: 26, of which 8 were waited for; matrix products, arithmetic and copies ran while one was open for 0% of the time, Pallas kernels for 26%

profile of v6, /device:TPU:0, one launch (start us, length us, event | category | flops | bytes accessed | tf_op | source)
XLA Modules:
  0.0 94.5 jit_solution(2560920574105631258)
XLA Ops:
  0.0 2.7 %end_state_sent.1 = (bf16[1040,128]{1,0:T(8,128)(2,1)S(1)}, bf16[512,2048]{1,0:T(8,128)(2,1)S(1)}, bf16[512,256]{1,0:T(8,128)(2,1)S(1)}, f32[32,512]{1,0:T(8,128...) custom-call(s32[1]{0:T(128)} %bitcast.1.ctx_ref, s32[1]{0:T(128)} %bitcast.here_ref, ...), custom_call_target="tpu_custom_call" | custom-call | flops 1 | bytes 1 | tf_op jit(solution)/shard_map/end_state_sent/pallas_call | solution.py:456
  3.2 1.1 %end_state_kept.1.own_ref = bf16[1040,128]{1,0:T(8,128)(2,1)S(1)} custom-call(s32[1]{0:T(128)} %bitcast.1.ctx_ref, bf16[512,2048]{1,0:T(8,128)(2,1)S(1)} %get-tuple-element.49.x_ref, bf16[512,256]{1,0:T(8,128)(2,1)S(1)} %get-tuple-element.50.b_ref, f32[32,512]{1,0:T(8,128)S(1)} %get-tuple-element.51.step_ref, f32[32,512]{1,0:T(8,128)S(1)} %get-tuple-element.52.decay_ref, ...), custom_call_target="tpu_custom_call" | custom-call | flops 1000000000 | bytes 1 | tf_op jit(solution)/shard_map/end_state_kept/pallas_call | solution.py:456
  4.7 2.9 %collective-permute-start.1 = (bf16[528,128]{1,0:T(8,128)(2,1)S(1)}, bf16[528,128]{1,0:T(8,128)(2,1)S(1)}, u32[]{:S(2)}, u32[]{:S(2)}) collective-permute-start(bf16[528,128]{1,0:T(8,128)(2,1)S(1)} %get-tuple-element.57.total_ref), channel_id=1, source_target_pairs={{0,8},{4,12},{8,0},{12,4},{16,24},{20,28},{24,16},{28,20},{1,9},{5... | collective-permute-start | bytes 405512 | tf_op jit(solution)/shard_map/ppermute | solution.py:532
  7.7 3.9 %local_part.2 = (f32[512,2048]{1,0:T(8,128)S(1)}, f32[512,2048]{1,0:T(8,128)S(1)}, bf16[512,256]{1,0:T(8,128)(2,1)S(1)}, f32[128,2048]{1,0:T(8,128)S(1)}, f32[32...) custom-call(bf16[512,2048]{1,0:T(8,128)(2,1)} %gate_hbm.3, bf16[512,256]{1,0:T(8,128)(2,1)} %c_hbm.3, ...), custom_call_target="tpu_custom_call" | custom-call | flops 4000000000 | bytes 1 | tf_op jit(solution)/shard_map/local_part/pallas_call | solution.py:456
  12.2 2.2 %collective-permute-start.3 = (bf16[528,128]{1,0:T(8,128)(2,1)S(1)}, bf16[528,128]{1,0:T(8,128)(2,1)S(1)}, u32[]{:S(2)}, u32[]{:S(2)}) collective-permute-start(bf16[528,128]{1,0:T(8,128)(2,1)S(1)} %fold.2.after_ref), channel_id=1, source_target_pairs={{0,16},{4,20},{8,24},{12,28},{16,0},{20,4},{24,8},{28,12},{1,17},{... | collective-permute-start | bytes 405512 | tf_op jit(solution)/shard_map/ppermute | solution.py:532
  14.6 1.8 %collective-permute-start.4 = (bf16[528,128]{1,0:T(8,128)(2,1)S(1)}, bf16[528,128]{1,0:T(8,128)(2,1)S(1)}, u32[]{:S(2)}, u32[]{:S(2)}) collective-permute-start(bf16[528,128]{1,0:T(8,128)(2,1)S(1)} %fold.3.after_ref), channel_id=1, source_target_pairs={{0,16},{4,20},{8,24},{12,28},{16,0},{20,4},{24,8},{28,12},{1,17},{... | collective-permute-start | bytes 405512 | tf_op jit(solution)/shard_map/ppermute | solution.py:532
  16.4 3.9 %local_part.3 = (f32[512,2048]{1,0:T(8,128)S(1)}, f32[512,2048]{1,0:T(8,128)S(1)}, bf16[512,256]{1,0:T(8,128)(2,1)S(1)}, f32[128,2048]{1,0:T(8,128)S(1)}, f32[32...) custom-call(bf16[512,2048]{1,0:T(8,128)(2,1)} %gate_hbm.3, ...), custom_call_target="tpu_custom_call", output_to_operand_aliasing={{0}: (9, {}), {1}: (10, {}), {2}: (11, {}), {3}: (12, {}), ... | custom-call | flops 4000000000 | bytes 1 | tf_op jit(solution)/shard_map/local_part/pallas_call | solution.py:456
  23.1 2.0 %collective-permute-start.21 = (bf16[128,1024]{1,0:T(8,128)(2,1)S(1)}, bf16[128,1024]{1,0:T(8,128)(2,1)S(1)}, u32[]{:S(2)}, u32[]{:S(2)}) collective-permute-start(bf16[128,1024]{1,0:T(8,128)(2,1)S(1)} %get-tuple-element.75.refs_0_), channel_id=1, source_target_pairs={{0,1},{1,0},{2,3},{3,2},{4,5},{5,4},{6,7},{7,6},{8,9},{9,8},{10,11... | collective-permute-start | bytes 786440 | tf_op jit(solution)/shard_map/ppermute | solution.py:479
  26.0 1.3 %first_block_rest.2 = (bf16[128,1024]{1,0:T(8,128)(2,1)S(1)}, bf16[128,1024]{1,0:T(8,128)(2,1)S(1)}) custom-call(bf16[128,2048]{1,0:T(8,128)(2,1)S(1)} %get-tuple-element.72.normed_ref, bf16[2048,2048]{1,0:T(8,128)(2,1)S(1)} %get-tuple-element.73.w_ref.wb_ref), custom_call_target="tpu_custom_call" | custom-call | flops 1 | bytes 1 | tf_op jit(solution)/shard_map/first_block_rest/pallas_call | solution.py:456
  27.3 2.0 %collective-permute-start.11 = (bf16[128,1024]{1,0:T(8,128)(2,1)S(1)}, bf16[128,1024]{1,0:T(8,128)(2,1)S(1)}, u32[]{:S(2)}, u32[]{:S(2)}) collective-permute-start(bf16[128,1024]{1,0:T(8,128)(2,1)S(1)} %get-tuple-element.76.refs_2_), channel_id=1, source_target_pairs={{0,1},{1,0},{2,3},{3,2},{4,5},{5,4},{6,7},{7,6},{8,9},{9,8},{10,11... | collective-permute-start | bytes 786440 | tf_op jit(solution)/shard_map/ppermute | solution.py:479
  29.4 9.3 %other_blocks.1.refs_1_.refs_2_.sums_ref = bf16[512,4096]{1,0:T(8,128)(2,1)S(1)} custom-call(s32[1]{0:T(128)} %bitcast.1.ctx_ref, s32[1]{0:T(128)} %bitcast.here_ref, f32[512,2048]{1,0:T(8,128)S(1)} %get-tuple-element.63.mixed_ref, f32[512,2048]{1,0:T(8,128)S(1)} %get-tuple-element.64.scale_ref, bf16[512,256]{1,0:T(8,128)(2,1)S(1)} %get-tuple-element.65.c_ref, ...), custom_call_target="tpu_custom_call" | custom-call | flops 1 | bytes 1 | tf_op jit(solution)/shard_map/other_blocks/pallas_call | solution.py:456
  38.8 2.0 %collective-permute-start.22 = (bf16[128,1024]{1,0:T(8,128)(2,1)S(1)}, bf16[128,1024]{1,0:T(8,128)(2,1)S(1)}, u32[]{:S(2)}, u32[]{:S(2)}) collective-permute-start(bf16[128,1024]{1,0:T(8,128)(2,1)S(1)} %get-tuple-element.89), channel_id=1, source_target_pairs={{0,1},{1,0},{2,3},{3,2},{4,5},{5,4},{6,7},{7,6},{8,9},{9,8},{10,11... | collective-permute-start | bytes 786440 | tf_op jit(solution)/shard_map/ppermute | solution.py:484
  41.6 4.4 %collective-permute-start.17 = (bf16[128,1024]{1,0:T(8,128)(2,1)S(1)}, bf16[128,1024]{1,0:T(8,128)(2,1)S(1)}, u32[]{:S(2)}, u32[]{:S(2)}) collective-permute-start(bf16[128,1024]{1,0:T(8,128)(2,1)S(1)} %get-tuple-element.85), channel_id=1, source_target_pairs={{0,1},{1,0},{2,3},{3,2},{4,5},{5,4},{6,7},{7,6},{8,9},{9,8},{10,11... | collective-permute-start | bytes 786440 | tf_op jit(solution)/shard_map/ppermute | solution.py:484
  46.9 2.3 %collective-permute-done.6.refs_0_ = bf16[128,1024]{1,0:T(8,128)(2,1)S(1)} collective-permute-done((bf16[128,1024]{1,0:T(8,128)(2,1)S(1)}, bf16[128,1024]{1,0:T(8,128)(2,1)S(1)}, u32[]{:S(2)}, u32[]{:S(2)}) %collective-permute-start.6) | collective-permute-done | bytes 262176 | tf_op jit(solution)/shard_map/ppermute | solution.py:479
  49.2 2.0 %collective-permute-start.12 = (bf16[128,1024]{1,0:T(8,128)(2,1)S(1)}, bf16[128,1024]{1,0:T(8,128)(2,1)S(1)}, u32[]{:S(2)}, u32[]{:S(2)}) collective-permute-start(bf16[128,1024]{1,0:T(8,128)(2,1)S(1)} %get-tuple-element.81), channel_id=1, source_target_pairs={{0,1},{1,0},{2,3},{3,2},{4,5},{5,4},{6,7},{7,6},{8,9},{9,8},{10,11... | collective-permute-start | bytes 786440 | tf_op jit(solution)/shard_map/ppermute | solution.py:484
  51.2 3.6 %collective-permute-done.22.refs_0_ = bf16[128,1024]{1,0:T(8,128)(2,1)S(1)} collective-permute-done((bf16[128,1024]{1,0:T(8,128)(2,1)S(1)}, bf16[128,1024]{1,0:T(8,128)(2,1)S(1)}, u32[]{:S(2)}, u32[]{:S(2)}) %collective-permute-start.22) | collective-permute-done | bytes 262176 | tf_op jit(solution)/shard_map/ppermute | solution.py:484
  55.6 4.9 %collective-permute-start.7 = (bf16[128,1024]{1,0:T(8,128)(2,1)S(1)}, bf16[128,1024]{1,0:T(8,128)(2,1)S(1)}, u32[]{:S(2)}, u32[]{:S(2)}) collective-permute-start(bf16[128,1024]{1,0:T(8,128)(2,1)S(1)} %get-tuple-element.77), channel_id=1, source_target_pairs={{0,1},{1,0},{2,3},{3,2},{4,5},{5,4},{6,7},{7,6},{8,9},{9,8},{10,11... | collective-permute-start | bytes 786440 | tf_op jit(solution)/shard_map/ppermute | solution.py:484
  61.3 4.7 %collective-permute-start.24 = (bf16[128,1024]{1,0:T(8,128)(2,1)S(1)}, bf16[128,1024]{1,0:T(8,128)(2,1)S(1)}, u32[]{:S(2)}, u32[]{:S(2)}) collective-permute-start(bf16[128,1024]{1,0:T(8,128)(2,1)S(1)} %get-tuple-element.91), channel_id=1, source_target_pairs={{0,1},{1,0},{2,3},{3,2},{4,5},{5,4},{6,7},{7,6},{8,9},{9,8},{10,11... | collective-permute-start | bytes 786440 | tf_op jit(solution)/shard_map/ppermute | solution.py:484
  66.8 4.8 %collective-permute-start.19 = (bf16[128,1024]{1,0:T(8,128)(2,1)S(1)}, bf16[128,1024]{1,0:T(8,128)(2,1)S(1)}, u32[]{:S(2)}, u32[]{:S(2)}) collective-permute-start(bf16[128,1024]{1,0:T(8,128)(2,1)S(1)} %get-tuple-element.87), channel_id=1, source_target_pairs={{0,1},{1,0},{2,3},{3,2},{4,5},{5,4},{6,7},{7,6},{8,9},{9,8},{10,11... | collective-permute-start | bytes 786440 | tf_op jit(solution)/shard_map/ppermute | solution.py:484
  72.4 4.8 %collective-permute-start.14 = (bf16[128,1024]{1,0:T(8,128)(2,1)S(1)}, bf16[128,1024]{1,0:T(8,128)(2,1)S(1)}, u32[]{:S(2)}, u32[]{:S(2)}) collective-permute-start(bf16[128,1024]{1,0:T(8,128)(2,1)S(1)} %get-tuple-element.83), channel_id=1, source_target_pairs={{0,1},{1,0},{2,3},{3,2},{4,5},{5,4},{6,7},{7,6},{8,9},{9,8},{10,11... | collective-permute-start | bytes 786440 | tf_op jit(solution)/shard_map/ppermute | solution.py:484
  78.8 4.1 %collective-permute-done.19.even_ref = bf16[128,1024]{1,0:T(8,128)(2,1)S(1)} collective-permute-done((bf16[128,1024]{1,0:T(8,128)(2,1)S(1)}, bf16[128,1024]{1,0:T(8,128)(2,1)S(1)}, u32[]{:S(2)}, u32[]{:S(2)}) %collective-permute-start.19) | collective-permute-done | bytes 262176 | tf_op jit(solution)/shard_map/ppermute | solution.py:484
  82.9 2.3 %collective-permute-start.9 = (bf16[128,1024]{1,0:T(8,128)(2,1)S(1)}, bf16[128,1024]{1,0:T(8,128)(2,1)S(1)}, u32[]{:S(2)}, u32[]{:S(2)}) collective-permute-start(bf16[128,1024]{1,0:T(8,128)(2,1)S(1)} %get-tuple-element.79), channel_id=1, source_target_pairs={{0,1},{1,0},{2,3},{3,2},{4,5},{5,4},{6,7},{7,6},{8,9},{9,8},{10,11... | collective-permute-start | bytes 786440 | tf_op jit(solution)/shard_map/ppermute | solution.py:484
  86.8 1.7 %collective-permute-done.14.even_ref = bf16[128,1024]{1,0:T(8,128)(2,1)S(1)} collective-permute-done((bf16[128,1024]{1,0:T(8,128)(2,1)S(1)}, bf16[128,1024]{1,0:T(8,128)(2,1)S(1)}, u32[]{:S(2)}, u32[]{:S(2)}) %collective-permute-start.14) | collective-permute-done | bytes 262176 | tf_op jit(solution)/shard_map/ppermute | solution.py:484
  89.3 4.3 %collective-permute-done.9.even_ref = bf16[128,1024]{1,0:T(8,128)(2,1)S(1)} collective-permute-done((bf16[128,1024]{1,0:T(8,128)(2,1)S(1)}, bf16[128,1024]{1,0:T(8,128)(2,1)S(1)}, u32[]{:S(2)}, u32[]{:S(2)}) %collective-permute-start.9) | collective-permute-done | bytes 262176 | tf_op jit(solution)/shard_map/ppermute | solution.py:484
  (57 shorter events, 15.0 us)
Async XLA Ops:
  4.7 7.3 %collective-permute-start.1 = (bf16[528,128]{1,0:T(8,128)(2,1)S(1)}, bf16[528,128]{1,0:T(8,128)(2,1)S(1)}, u32[]{:S(2)}, u32[]{:S(2)}) collective-permute-start(bf16[528,128]{1,0:T(8,128)(2,1)S(1)} %get-tuple-element.57.total_ref), channel_id=1, source_target_pairs={{0,8},{4,12},{8,0},{12,4},{16,24},{20,28},{24,16},{28,20},{1,9},{5... | collective-permute-start | bytes 405512 | tf_op jit(solution)/shard_map/ppermute | solution.py:532
  7.6 6.8 %collective-permute-start.2 = (bf16[528,128]{1,0:T(8,128)(2,1)S(1)}, bf16[528,128]{1,0:T(8,128)(2,1)S(1)}, u32[]{:S(2)}, u32[]{:S(2)}) collective-permute-start(bf16[528,128]{1,0:T(8,128)(2,1)S(1)} %get-tuple-element.55.after_ref.total_ref), channel_id=1, source_target_pairs={{0,8},{4,12},{8,0},{12,4},{16,24},{20,28},{24,16},{28,20},{1,9},{5... | collective-permute-start | bytes 405512 | tf_op jit(solution)/shard_map/ppermute | solution.py:532
  12.2 8.2 %collective-permute-start.3 = (bf16[528,128]{1,0:T(8,128)(2,1)S(1)}, bf16[528,128]{1,0:T(8,128)(2,1)S(1)}, u32[]{:S(2)}, u32[]{:S(2)}) collective-permute-start(bf16[528,128]{1,0:T(8,128)(2,1)S(1)} %fold.2.after_ref), channel_id=1, source_target_pairs={{0,16},{4,20},{8,24},{12,28},{16,0},{20,4},{24,8},{28,12},{1,17},{... | collective-permute-start | bytes 405512 | tf_op jit(solution)/shard_map/ppermute | solution.py:532
  14.6 5.7 %collective-permute-start.4 = (bf16[528,128]{1,0:T(8,128)(2,1)S(1)}, bf16[528,128]{1,0:T(8,128)(2,1)S(1)}, u32[]{:S(2)}, u32[]{:S(2)}) collective-permute-start(bf16[528,128]{1,0:T(8,128)(2,1)S(1)} %fold.3.after_ref), channel_id=1, source_target_pairs={{0,16},{4,20},{8,24},{12,28},{16,0},{20,4},{24,8},{28,12},{1,17},{... | collective-permute-start | bytes 405512 | tf_op jit(solution)/shard_map/ppermute | solution.py:532
  23.1 15.6 %collective-permute-start.21 = (bf16[128,1024]{1,0:T(8,128)(2,1)S(1)}, bf16[128,1024]{1,0:T(8,128)(2,1)S(1)}, u32[]{:S(2)}, u32[]{:S(2)}) collective-permute-start(bf16[128,1024]{1,0:T(8,128)(2,1)S(1)} %get-tuple-element.75.refs_0_), channel_id=1, source_target_pairs={{0,1},{1,0},{2,3},{3,2},{4,5},{5,4},{6,7},{7,6},{8,9},{9,8},{10,11... | collective-permute-start | bytes 786440 | tf_op jit(solution)/shard_map/ppermute | solution.py:479
  25.9 15.6 %collective-permute-start.16 = (bf16[128,1024]{1,0:T(8,128)(2,1)S(1)}, bf16[128,1024]{1,0:T(8,128)(2,1)S(1)}, u32[]{:S(2)}, u32[]{:S(2)}) collective-permute-start(bf16[128,1024]{1,0:T(8,128)(2,1)S(1)} %first_block_rest.3.refs_1_), channel_id=1, source_target_pairs={{0,1},{1,0},{2,3},{3,2},{4,5},{5,4},{6,7},{7,6},{8,9},{9,8},{10,11... | collective-permute-start | bytes 786440 | tf_op jit(solution)/shard_map/ppermute | solution.py:479
  27.3 18.8 %collective-permute-start.11 = (bf16[128,1024]{1,0:T(8,128)(2,1)S(1)}, bf16[128,1024]{1,0:T(8,128)(2,1)S(1)}, u32[]{:S(2)}, u32[]{:S(2)}) collective-permute-start(bf16[128,1024]{1,0:T(8,128)(2,1)S(1)} %get-tuple-element.76.refs_2_), channel_id=1, source_target_pairs={{0,1},{1,0},{2,3},{3,2},{4,5},{5,4},{6,7},{7,6},{8,9},{9,8},{10,11... | collective-permute-start | bytes 786440 | tf_op jit(solution)/shard_map/ppermute | solution.py:479
  29.3 19.9 %collective-permute-start.6 = (bf16[128,1024]{1,0:T(8,128)(2,1)S(1)}, bf16[128,1024]{1,0:T(8,128)(2,1)S(1)}, u32[]{:S(2)}, u32[]{:S(2)}) collective-permute-start(bf16[128,1024]{1,0:T(8,128)(2,1)S(1)} %get-tuple-element.74.refs_3_), channel_id=1, source_target_pairs={{0,1},{1,0},{2,3},{3,2},{4,5},{5,4},{6,7},{7,6},{8,9},{9,8},{10,11... | collective-permute-start | bytes 786440 | tf_op jit(solution)/shard_map/ppermute | solution.py:479
  38.8 15.9 %collective-permute-start.22 = (bf16[128,1024]{1,0:T(8,128)(2,1)S(1)}, bf16[128,1024]{1,0:T(8,128)(2,1)S(1)}, u32[]{:S(2)}, u32[]{:S(2)}) collective-permute-start(bf16[128,1024]{1,0:T(8,128)(2,1)S(1)} %get-tuple-element.89), channel_id=1, source_target_pairs={{0,1},{1,0},{2,3},{3,2},{4,5},{5,4},{6,7},{7,6},{8,9},{9,8},{10,11... | collective-permute-start | bytes 786440 | tf_op jit(solution)/shard_map/ppermute | solution.py:484
  40.9 14.7 %collective-permute-start.23 = (bf16[128,1024]{1,0:T(8,128)(2,1)S(1)}, bf16[128,1024]{1,0:T(8,128)(2,1)S(1)}, u32[]{:S(2)}, u32[]{:S(2)}) collective-permute-start(bf16[128,1024]{1,0:T(8,128)(2,1)S(1)} %get-tuple-element.90), channel_id=1, source_target_pairs={{1,2},{2,1},{5,6},{6,5},{9,10},{10,9},{13,14},{14,13},{17,18},{18,... | collective-permute-start | bytes 786440 | tf_op jit(solution)/shard_map/ppermute | solution.py:484
  41.6 19.0 %collective-permute-start.17 = (bf16[128,1024]{1,0:T(8,128)(2,1)S(1)}, bf16[128,1024]{1,0:T(8,128)(2,1)S(1)}, u32[]{:S(2)}, u32[]{:S(2)}) collective-permute-start(bf16[128,1024]{1,0:T(8,128)(2,1)S(1)} %get-tuple-element.85), channel_id=1, source_target_pairs={{0,1},{1,0},{2,3},{3,2},{4,5},{5,4},{6,7},{7,6},{8,9},{9,8},{10,11... | collective-permute-start | bytes 786440 | tf_op jit(solution)/shard_map/ppermute | solution.py:484
  46.1 15.2 %collective-permute-start.18 = (bf16[128,1024]{1,0:T(8,128)(2,1)S(1)}, bf16[128,1024]{1,0:T(8,128)(2,1)S(1)}, u32[]{:S(2)}, u32[]{:S(2)}) collective-permute-start(bf16[128,1024]{1,0:T(8,128)(2,1)S(1)} %get-tuple-element.86), channel_id=1, source_target_pairs={{1,2},{2,1},{5,6},{6,5},{9,10},{10,9},{13,14},{14,13},{17,18},{18,... | collective-permute-start | bytes 786440 | tf_op jit(solution)/shard_map/ppermute | solution.py:484
  49.2 17.0 %collective-permute-start.12 = (bf16[128,1024]{1,0:T(8,128)(2,1)S(1)}, bf16[128,1024]{1,0:T(8,128)(2,1)S(1)}, u32[]{:S(2)}, u32[]{:S(2)}) collective-permute-start(bf16[128,1024]{1,0:T(8,128)(2,1)S(1)} %get-tuple-element.81), channel_id=1, source_target_pairs={{0,1},{1,0},{2,3},{3,2},{4,5},{5,4},{6,7},{7,6},{8,9},{9,8},{10,11... | collective-permute-start | bytes 786440 | tf_op jit(solution)/shard_map/ppermute | solution.py:484
  54.8 12.0 %collective-permute-start.13 = (bf16[128,1024]{1,0:T(8,128)(2,1)S(1)}, bf16[128,1024]{1,0:T(8,128)(2,1)S(1)}, u32[]{:S(2)}, u32[]{:S(2)}) collective-permute-start(bf16[128,1024]{1,0:T(8,128)(2,1)S(1)} %get-tuple-element.82), channel_id=1, source_target_pairs={{1,2},{2,1},{5,6},{6,5},{9,10},{10,9},{13,14},{14,13},{17,18},{18,... | collective-permute-start | bytes 786440 | tf_op jit(solution)/shard_map/ppermute | solution.py:484
  55.6 16.2 %collective-permute-start.7 = (bf16[128,1024]{1,0:T(8,128)(2,1)S(1)}, bf16[128,1024]{1,0:T(8,128)(2,1)S(1)}, u32[]{:S(2)}, u32[]{:S(2)}) collective-permute-start(bf16[128,1024]{1,0:T(8,128)(2,1)S(1)} %get-tuple-element.77), channel_id=1, source_target_pairs={{0,1},{1,0},{2,3},{3,2},{4,5},{5,4},{6,7},{7,6},{8,9},{9,8},{10,11... | collective-permute-start | bytes 786440 | tf_op jit(solution)/shard_map/ppermute | solution.py:484
  60.6 11.8 %collective-permute-start.8 = (bf16[128,1024]{1,0:T(8,128)(2,1)S(1)}, bf16[128,1024]{1,0:T(8,128)(2,1)S(1)}, u32[]{:S(2)}, u32[]{:S(2)}) collective-permute-start(bf16[128,1024]{1,0:T(8,128)(2,1)S(1)} %get-tuple-element.78), channel_id=1, source_target_pairs={{1,2},{2,1},{5,6},{6,5},{9,10},{10,9},{13,14},{14,13},{17,18},{18,... | collective-permute-start | bytes 786440 | tf_op jit(solution)/shard_map/ppermute | solution.py:484
  61.3 16.1 %collective-permute-start.24 = (bf16[128,1024]{1,0:T(8,128)(2,1)S(1)}, bf16[128,1024]{1,0:T(8,128)(2,1)S(1)}, u32[]{:S(2)}, u32[]{:S(2)}) collective-permute-start(bf16[128,1024]{1,0:T(8,128)(2,1)S(1)} %get-tuple-element.91), channel_id=1, source_target_pairs={{0,1},{1,0},{2,3},{3,2},{4,5},{5,4},{6,7},{7,6},{8,9},{9,8},{10,11... | collective-permute-start | bytes 786440 | tf_op jit(solution)/shard_map/ppermute | solution.py:484
  66.1 11.9 %collective-permute-start.25 = (bf16[128,1024]{1,0:T(8,128)(2,1)S(1)}, bf16[128,1024]{1,0:T(8,128)(2,1)S(1)}, u32[]{:S(2)}, u32[]{:S(2)}) collective-permute-start(bf16[128,1024]{1,0:T(8,128)(2,1)S(1)} %get-tuple-element.92), channel_id=1, source_target_pairs={{1,2},{2,1},{5,6},{6,5},{9,10},{10,9},{13,14},{14,13},{17,18},{18,... | collective-permute-start | bytes 786440 | tf_op jit(solution)/shard_map/ppermute | solution.py:484
  66.8 16.0 %collective-permute-start.19 = (bf16[128,1024]{1,0:T(8,128)(2,1)S(1)}, bf16[128,1024]{1,0:T(8,128)(2,1)S(1)}, u32[]{:S(2)}, u32[]{:S(2)}) collective-permute-start(bf16[128,1024]{1,0:T(8,128)(2,1)S(1)} %get-tuple-element.87), channel_id=1, source_target_pairs={{0,1},{1,0},{2,3},{3,2},{4,5},{5,4},{6,7},{7,6},{8,9},{9,8},{10,11... | collective-permute-start | bytes 786440 | tf_op jit(solution)/shard_map/ppermute | solution.py:484
  71.8 14.2 %collective-permute-start.20 = (bf16[128,1024]{1,0:T(8,128)(2,1)S(1)}, bf16[128,1024]{1,0:T(8,128)(2,1)S(1)}, u32[]{:S(2)}, u32[]{:S(2)}) collective-permute-start(bf16[128,1024]{1,0:T(8,128)(2,1)S(1)} %get-tuple-element.88), channel_id=1, source_target_pairs={{1,2},{2,1},{5,6},{6,5},{9,10},{10,9},{13,14},{14,13},{17,18},{18,... | collective-permute-start | bytes 786440 | tf_op jit(solution)/shard_map/ppermute | solution.py:484
  72.4 16.0 %collective-permute-start.14 = (bf16[128,1024]{1,0:T(8,128)(2,1)S(1)}, bf16[128,1024]{1,0:T(8,128)(2,1)S(1)}, u32[]{:S(2)}, u32[]{:S(2)}) collective-permute-start(bf16[128,1024]{1,0:T(8,128)(2,1)S(1)} %get-tuple-element.83), channel_id=1, source_target_pairs={{0,1},{1,0},{2,3},{3,2},{4,5},{5,4},{6,7},{7,6},{8,9},{9,8},{10,11... | collective-permute-start | bytes 786440 | tf_op jit(solution)/shard_map/ppermute | solution.py:484
  77.4 11.1 %collective-permute-start.15 = (bf16[128,1024]{1,0:T(8,128)(2,1)S(1)}, bf16[128,1024]{1,0:T(8,128)(2,1)S(1)}, u32[]{:S(2)}, u32[]{:S(2)}) collective-permute-start(bf16[128,1024]{1,0:T(8,128)(2,1)S(1)} %get-tuple-element.84), channel_id=1, source_target_pairs={{1,2},{2,1},{5,6},{6,5},{9,10},{10,9},{13,14},{14,13},{17,18},{18,... | collective-permute-start | bytes 786440 | tf_op jit(solution)/shard_map/ppermute | solution.py:484
  78.1 11.2 %collective-permute-start.10 = (bf16[128,1024]{1,0:T(8,128)(2,1)S(1)}, bf16[128,1024]{1,0:T(8,128)(2,1)S(1)}, u32[]{:S(2)}, u32[]{:S(2)}) collective-permute-start(bf16[128,1024]{1,0:T(8,128)(2,1)S(1)} %get-tuple-element.80), channel_id=1, source_target_pairs={{1,2},{2,1},{5,6},{6,5},{9,10},{10,9},{13,14},{14,13},{17,18},{18,... | collective-permute-start | bytes 786440 | tf_op jit(solution)/shard_map/ppermute | solution.py:484
  82.9 10.7 %collective-permute-start.9 = (bf16[128,1024]{1,0:T(8,128)(2,1)S(1)}, bf16[128,1024]{1,0:T(8,128)(2,1)S(1)}, u32[]{:S(2)}, u32[]{:S(2)}) collective-permute-start(bf16[128,1024]{1,0:T(8,128)(2,1)S(1)} %get-tuple-element.79), channel_id=1, source_target_pairs={{0,1},{1,0},{2,3},{3,2},{4,5},{5,4},{6,7},{7,6},{8,9},{9,8},{10,11... | collective-permute-start | bytes 786440 | tf_op jit(solution)/shard_map/ppermute | solution.py:484
  (4 other events, 15.4 us)

commit v7 on v6

v7 whole, which is shorter than its diff:
```python
from functools import partial

import jax
import jax.numpy as jnp
from jax import lax
from jax.experimental import pallas as pl
from jax.experimental.pallas import tpu as pltpu
from jax.sharding import PartitionSpec as P

HEAD_DIM = 64
STATE = 128
CHUNK = 128
MIDDLE = CHUNK // 2 - 1
EXTRA = 16
COLUMN_TILE = 512
PARTS = 4
SUM_COPIES = 4
F32 = jnp.float32
BF16 = jnp.bfloat16


def dot(a, b):
    return jnp.dot(a, b, preferred_element_type=F32)


def dot_exact(a, b):
    return jnp.dot(a, b, preferred_element_type=F32, precision=lax.Precision.HIGHEST)


def head_map(channels):
    head = lax.broadcasted_iota(jnp.int32, (128, channels), 0) & 63
    place = lax.broadcasted_iota(jnp.int32, (128, channels), 1) >> 6
    return jnp.where(head == place, 1.0, 0.0).astype(BF16)


def padded(values):
    return jnp.concatenate([values, jnp.zeros((64 - values.shape[0], values.shape[1]), F32)], axis=0)


def by_row(values):
    high = values.astype(BF16).astype(F32)
    return jnp.transpose(jnp.concatenate([padded(high), padded(values - high)], axis=0)).astype(BF16)


def pieces(values, axis):
    first = values.astype(BF16).astype(F32)
    second = (values - first).astype(BF16).astype(F32)
    third = values - first - second
    shape = (EXTRA, values.shape[1]) if axis == 0 else (values.shape[0], 128)
    at = lax.broadcasted_iota(jnp.int32, shape, axis)
    return jnp.where(at == 0, first, jnp.where(at == 1, second, jnp.where(at == 2, third, 0.0)))


def running_sums(decay):
    row = lax.broadcasted_iota(jnp.int32, (CHUNK, CHUNK), 0)
    column = lax.broadcasted_iota(jnp.int32, (CHUNK, CHUNK), 1)
    upper = jnp.where(row <= column, 1.0, 0.0)
    return [dot_exact(decay[:, rows_of(n)], upper) for n in range(decay.shape[1] // CHUNK)]


def load(pairs, semaphores):
    copies = [pltpu.make_async_copy(src, dst, semaphores.at[n]) for n, (src, dst) in enumerate(pairs)]
    for copy in copies:
        copy.start()
    return copies


def rows_of(chunk, size=CHUNK):
    return slice(chunk * size, (chunk + 1) * size)


def put_message(ref, state, logs):
    for j in range(state.shape[1] // 128):
        ref[j * STATE : (j + 1) * STATE, :] = state[:, j * 128 : (j + 1) * 128].astype(BF16)
    ref[state.shape[1] :, :] = logs.astype(BF16)


def state_of(ref):
    count = (ref.shape[0] - EXTRA) // STATE
    return jnp.concatenate([ref[j * STATE : (j + 1) * STATE, :] for j in range(count)], axis=1).astype(F32)


def logs_of(ref):
    return ref[ref.shape[0] - EXTRA :, :]


def wide_log(logs, spread):
    return jnp.sum(dot(logs, spread), axis=0, keepdims=True)


def end_state(groups, half, x_ref, b_ref, step_ref, decay_ref, weighted, message_ref, spread, x_copies=(), b_copies=()):
    rows, width = weighted.shape
    heads = width // HEAD_DIM
    of_heads = pl.ds(pl.multiple_of(half * heads, heads), heads)
    of_channels = pl.ds(pl.multiple_of(half * width, width), width)
    of_group = pl.ds(pl.multiple_of((half * groups // 2) * STATE, STATE), STATE)
    before, running = jnp.zeros((heads, 1), F32), []
    for sums in running_sums(decay_ref[of_heads, :]):
        running.append(before + sums)
        before = before + sums[:, CHUNK - 1 :]
    factors = [by_row(step_ref[of_heads, rows_of(n)] * jnp.exp(before - sums)) for n, sums in enumerate(running)]
    for n, factor in enumerate(factors):
        here = rows_of(n)
        factor = dot(factor, spread)
        for copy in x_copies[n : n + 1]:
            copy.wait()
        weighted[here, :] = (x_ref[here, of_channels].astype(F32) * factor).astype(BF16)
    for copy in b_copies:
        copy.wait()
    state = lax.dot_general(
        b_ref[:, of_group], weighted[...], (((0,), (0,)), ((), ())), preferred_element_type=F32
    )
    logs = jnp.concatenate([pieces(before, 1), jnp.zeros((128 - heads, 128), F32)], axis=0)
    put_message(message_ref, state, jnp.transpose(logs)[:EXTRA])


def send_kernel(groups, ctx_ref, here_ref, x_hbm, b_hbm, step_hbm, decay_hbm, send_ref, x_ref, b_ref, step_ref, decay_ref,
                spread_ref, weighted, semaphores):
    width = weighted.shape[1]
    other = 1 - (ctx_ref[0] & 1)
    first, second = [pl.ds(pl.multiple_of(half * width, width), width) for half in (other, 1 - other)]
    rows = [rows_of(n) for n in range(x_ref.shape[0] // CHUNK)]
    copies = load(
        [(decay_hbm, decay_ref), (step_hbm, step_ref)]
        + [(x_hbm.at[here, first], x_ref.at[here, first]) for here in rows]
        + [(b_hbm, b_ref), (x_hbm.at[:, second], x_ref.at[:, second])],
        semaphores,
    )
    spread = head_map(width)
    spread_ref[...] = spread
    for copy in copies[:2]:
        copy.wait()
    end_state(
        groups, other, x_ref, b_ref, step_ref, decay_ref, weighted, send_ref, spread, copies[2:-2], copies[-2:-1]
    )
    copies[-1].wait()


def weight_copies(w_hbm, refs, first, semaphores):
    return load([(w_hbm.at[:, rows_of(first + n, COLUMN_TILE)], ref) for n, ref in enumerate(refs)], semaphores)


def keep_kernel(groups, tile, ctx_ref, w_hbm, x_ref, b_ref, step_ref, decay_ref, spread_ref, keep_ref, w_ref, weighted,
                semaphores):
    copies = weight_copies(w_hbm, [w_ref], tile, semaphores)
    end_state(groups, ctx_ref[0] & 1, x_ref, b_ref, step_ref, decay_ref, weighted, keep_ref, spread_ref[...])
    for copy in copies:
        copy.wait()


def pair_kernel(ctx_ref, spread_ref, own_ref, sibling_ref, *pieces_refs):
    spread = spread_ref[...]
    own_log, sibling_log = wide_log(logs_of(own_ref), spread), wide_log(logs_of(sibling_ref), spread)
    early = (ctx_ref[0] & 1) == 0
    own_scale = jnp.where(early, jnp.exp(sibling_log), 1.0)
    sibling_scale = jnp.where(early, 1.0, jnp.exp(own_log))
    logs = logs_of(own_ref).astype(F32) + logs_of(sibling_ref).astype(F32)
    logs = pieces(jnp.sum(logs, axis=0, keepdims=True), 0)
    state = state_of(own_ref) * own_scale + state_of(sibling_ref) * sibling_scale
    start = 0
    for ref in pieces_refs:
        width = ref.shape[0] - EXTRA
        put_message(ref, state[:, start : start + width], logs)
        start += width


def is_upper(ctx_ref, level):
    return ((ctx_ref[0] >> (1 + level)) & 1) == 1


def piece_of(spread_ref, start, ref):
    return spread_ref[:, start : start + ref.shape[0] - EXTRA]


def fold_kernel(level, start, ctx_ref, after_ref, spread_ref, total_ref, other_ref, out_ref):
    spread = piece_of(spread_ref, start, total_ref)
    upper = is_upper(ctx_ref, level)
    total_scale = jnp.where(upper, 1.0, jnp.exp(wide_log(logs_of(other_ref), spread)))
    other_scale = jnp.where(upper, jnp.exp(wide_log(logs_of(total_ref), spread)), 1.0)
    logs = logs_of(total_ref).astype(F32) + logs_of(other_ref).astype(F32)
    logs = pieces(jnp.sum(logs, axis=0, keepdims=True), 0)
    put_message(out_ref, state_of(total_ref) * total_scale + state_of(other_ref) * other_scale, logs)


def last_kernel(start, ctx_ref, after_ref, spread_ref, own_ref, sibling_ref, *refs):
    keep_ref, send_ref = refs[-2:]
    spread = piece_of(spread_ref, start, refs[0])
    chip = log = 0.0
    for level, ref in enumerate(refs[:-2]):
        upper = is_upper(ctx_ref, level)
        chip = chip + jnp.where(upper, state_of(ref), 0.0) * jnp.exp(log)
        log = log + jnp.where(upper, wide_log(logs_of(ref), spread), 0.0)
    width = chip.shape[1]
    for core, first, mine, other in ((0, own_ref, 0, 1), (1, sibling_ref, 1, 0)):

        @pl.when((ctx_ref[0] & 1) == core)
        def _():
            piece = state_of(first)[:, start : start + width]
            after = chip * jnp.exp(wide_log(logs_of(first), spread)) + piece
            both = (chip.astype(BF16), after.astype(BF16))
            keep_ref[...] = both[mine]
            send_ref[...] = both[other]


def scan_kernel(groups, chunks, tile, w_hbm, x_ref, b_ref, step_ref, decay_ref, after_ref, *refs):
    first = chunks[0] == 0
    if not first:
        refs = refs[2:]
    rhs_ref, state_ref, token_ref, *w_refs, semaphores = refs
    token_ref[...] = jnp.zeros_like(token_ref)
    copies = weight_copies(w_hbm, w_refs, tile, semaphores)
    channels = x_ref.shape[1]
    heads = step_ref.shape[0]
    width = channels // groups
    spread = head_map(channels)
    lane = lax.broadcasted_iota(jnp.int32, (heads, CHUNK), 1)
    if first:
        state = [jnp.zeros((STATE, width), F32)] * groups
    else:
        state = [state_ref[:, rows_of(g, width)] for g in range(groups)]
    for n in chunks:
        here = rows_of(n)
        (running,) = running_sums(decay_ref[:, here])
        middle, total = running[:, MIDDLE : MIDDLE + 1], running[:, CHUNK - 1 :]
        ends = jnp.exp(jnp.where(lane == 0, total, jnp.where(lane == 1, total - middle, middle)))
        factors = [by_row(step_ref[:, here] * jnp.exp(middle - running)), by_row(ends)[:EXTRA]]
        factors = jnp.concatenate(factors, axis=0)
        start = n * (CHUNK + STATE)
        for g in range(groups):
            cut = rows_of(g, width)
            wide = dot(factors, spread[:, cut])
            to_state, to_fresh, to_middle = (wide[CHUNK + m : CHUNK + m + 1] for m in range(3))
            weighted = (x_ref[here, cut].astype(F32) * wide[:CHUNK]).astype(BF16)
            rhs_ref[start : start + CHUNK, cut] = weighted
            rhs_ref[start + CHUNK : start + CHUNK + STATE, cut] = (state[g] * to_middle).astype(BF16)
            if n + 1 < x_ref.shape[0] // CHUNK:
                fresh = lax.dot_general(
                    b_ref[here, rows_of(g, STATE)], weighted, (((0,), (0,)), ((), ())), preferred_element_type=F32
                )
                state[g] = state[g] * to_state + fresh * to_fresh
    for g in range(groups):
        state_ref[:, rows_of(g, width)] = state[g]
    for copy in copies:
        copy.wait()


def chunk_part(groups, here, rhs_rows, running, before, gate_rows, x_ref, b_ref, c_ref, skip_ref, rhs_ref, mixed_ref, scale_ref,
               out_rows):
    channels = x_ref.shape[1]
    heads = running.shape[0]
    width = channels // groups
    spread = head_map(channels)
    row = lax.broadcasted_iota(jnp.int32, (CHUNK, CHUNK), 0)
    column = lax.broadcasted_iota(jnp.int32, (CHUNK, CHUNK), 1)
    skip = jnp.concatenate([pieces(skip_ref[...], 0), jnp.zeros((EXTRA, 128 - heads), F32)], axis=1)
    skip = wide_log(skip.astype(BF16), spread)
    middle = running[:, MIDDLE : MIDDLE + 1]
    factors = jnp.concatenate([by_row(jnp.exp(running - middle)), by_row(jnp.exp(before + running))], axis=0)
    for g in range(groups):
        cut = rows_of(g, width)
        part = rows_of(g, STATE)
        wide = dot(factors, spread[:, cut])
        scores = lax.dot_general(
            c_ref[here, part], b_ref[here, part], (((1,), (1,)), ((), ())), preferred_element_type=F32
        )
        scores = jnp.where(row >= column, scores, 0.0).astype(BF16)
        within = dot(jnp.concatenate([scores, c_ref[here, part]], axis=1), rhs_ref[rhs_rows, cut])
        gate = gate_rows[:, cut].astype(F32)
        gate = gate * (0.5 * jnp.tanh(0.5 * gate) + 0.5)
        mixed_ref[out_rows, cut] = (within * wide[:CHUNK] + x_ref[here, cut].astype(F32) * skip[:, cut]) * gate
        scale_ref[out_rows, cut] = wide[CHUNK:] * gate


def first_part_kernel(groups, count, tile, here_ref, gate_hbm, c_hbm, w_hbm, x_ref, b_ref, step_ref, decay_ref, skip_ref, rhs_ref,
                      after_ref, mixed_ref, scale_ref, c_ref, token_ref, *refs):
    *w_refs, gate_ref, semaphores = refs
    token_ref[...] = jnp.zeros_like(token_ref)
    chunk, _ = first_chunk(here_ref, count, x_ref.shape[0] // count)
    here = pl.ds(pl.multiple_of(chunk * CHUNK, CHUNK), CHUNK)
    copies = load([(c_hbm, c_ref), (gate_hbm.at[here, :], gate_ref)], semaphores)
    weights = weight_copies(w_hbm, w_refs, tile, semaphores.at[pl.ds(2, len(w_refs))])
    lane = lax.broadcasted_iota(jnp.int32, decay_ref.shape, 1)
    before = jnp.sum(jnp.where(lane < chunk * CHUNK, decay_ref[...], 0.0), axis=1, keepdims=True)
    (running,) = running_sums(decay_ref[:, here])
    rhs_rows = pl.ds(pl.multiple_of(chunk * (CHUNK + STATE), CHUNK + STATE), CHUNK + STATE)
    for copy in copies:
        copy.wait()
    chunk_part(groups, here, rhs_rows, running, before, gate_ref, x_ref, b_ref, c_ref, skip_ref, rhs_ref, mixed_ref, scale_ref,
               slice(None))
    for copy in weights:
        copy.wait()


def norm_group(mixed, scale, c_rows, gain, state):
    whole = mixed + scale * dot(c_rows, state)
    meansq = jnp.mean(whole * whole, axis=1, keepdims=True)
    return (whole * lax.rsqrt(meansq + 1e-05) * gain).astype(BF16)


def norm_rows(groups, state, mixed, scale, c_rows, gain):
    width = mixed.shape[1] // groups
    parts = []
    for g in range(groups):
        cut = slice(g * width, (g + 1) * width)
        of_state = c_rows[:, g * STATE : (g + 1) * STATE]
        parts.append(norm_group(mixed[:, cut], scale[:, cut], of_state, gain[:, cut], state[:, cut]))
    return parts


def across(refs):
    return jnp.concatenate([ref[...] for ref in refs], axis=1)


def fill_state(ctx_ref, keep_refs, recv_refs, state):
    half = state.shape[1] // 2
    for core in range(2):

        @pl.when((ctx_ref[0] & 1) == core)
        def _():
            state[:, core * half : (core + 1) * half] = across(keep_refs)
            state[:, (1 - core) * half : (2 - core) * half] = across(recv_refs)


def block_at(here, position, count):
    block = 0
    for i in range(count):
        block = jnp.where(here == i, block_order(i, count)[position], block)
    return block


def rows_at(block, size):
    return pl.ds(pl.multiple_of(block * size, size), size)


def first_chunk(here_ref, count, size):
    start = block_at(here_ref[0], 0, count) * size
    chunk = start // CHUNK
    return chunk, pl.ds(pl.multiple_of(start - chunk * CHUNK, min(size, CHUNK)), size)


def one_group(group, count, here_ref, mixed_ref, scale_ref, c_ref, gain_ref, state):
    size = c_ref.shape[0] // count
    width = state.shape[1]
    cut = pl.ds(pl.multiple_of(group * width, width), width)
    part = pl.ds(pl.multiple_of(group * STATE, STATE), STATE)
    _, rows = first_chunk(here_ref, count, size)
    c_rows = c_ref[rows_at(block_at(here_ref[0], 0, count), size), part]
    return norm_group(mixed_ref[rows, cut], scale_ref[rows, cut], c_rows, gain_ref[:, cut], state)


def times_rows(group, normed, w_refs):
    width = normed.shape[1]
    rows = pl.ds(pl.multiple_of(group * width, width), width)
    return jnp.concatenate([dot(normed, ref[rows, :]) for ref in w_refs], axis=1)


def own_group_kernel(count, tiles, ctx_ref, here_ref, mixed_ref, scale_ref, c_ref, gain_ref, *refs):
    *keep_refs, normed_ref, product_ref = refs[tiles:]
    group = ctx_ref[0] & 1
    normed = one_group(group, count, here_ref, mixed_ref, scale_ref, c_ref, gain_ref, across(keep_refs))
    normed_ref[...] = normed
    product_ref[...] = times_rows(group, normed, refs[:tiles])


def other_group_kernel(count, tiles, ctx_ref, here_ref, mixed_ref, scale_ref, c_ref, gain_ref, *refs):
    *recv_refs, own_ref, product_ref, out_ref, normed_ref = refs[tiles:]
    group = 1 - (ctx_ref[0] & 1)
    normed = one_group(group, count, here_ref, mixed_ref, scale_ref, c_ref, gain_ref, across(recv_refs))
    out_ref[...] = (product_ref[...] + times_rows(group, normed, refs[:tiles])).astype(BF16)
    width = normed.shape[1]
    for g in range(2):

        @pl.when(group == g)
        def _():
            normed_ref[:, rows_of(g, width)] = normed
            normed_ref[:, rows_of(1 - g, width)] = own_ref[...]


def both_groups_kernel(groups, count, tiles, ctx_ref, here_ref, mixed_ref, scale_ref, c_ref, gain_ref, *refs):
    *state_refs, out_ref, normed_ref, state = refs[tiles:]
    fill_state(ctx_ref, state_refs[: len(state_refs) // 2], state_refs[len(state_refs) // 2 :], state)
    size = normed_ref.shape[0]
    width = normed_ref.shape[1] // groups
    _, rows = first_chunk(here_ref, count, size)
    c_rows = c_ref.at[rows_at(block_at(here_ref[0], 0, count), size), :]
    parts = norm_rows(groups, state, mixed_ref.at[rows, :], scale_ref.at[rows, :], c_rows, gain_ref)
    for g, part in enumerate(parts):
        normed_ref[:, g * width : (g + 1) * width] = part
    for n, ref in enumerate(refs[:tiles]):
        out_ref[:, rows_of(n, COLUMN_TILE)] = dot(normed_ref[...], ref[...]).astype(BF16)


def project_kernel(tiles, normed_ref, *refs):
    outs = refs[tiles:]
    for n, ref in enumerate(refs[:tiles]):
        out, column = divmod(n * COLUMN_TILE, outs[0].shape[1])
        outs[out][:, column : column + COLUMN_TILE] = dot(normed_ref[...], ref[...]).astype(BF16)


def rest_kernel(groups, count, tiles, ctx_ref, here_ref, gate_hbm, x_ref, b_ref, step_ref, decay_ref, skip_ref, rhs_ref, c_ref,
                first_mixed_ref, first_scale_ref, gain_ref, *refs):
    w_refs = refs[:tiles]
    *inputs, out_ref, state, normed, mixed_ref, scale_ref, gate_ref, semaphores = refs[tiles:]
    state_refs, first = inputs[:-PARTS], inputs[-PARTS:]
    size, piece = first[0].shape
    chunks = x_ref.shape[0] // CHUNK
    gates = [(gate_hbm.at[rows_of(n), :], gate_ref.at[rows_of(n), :]) for n in range(chunks)]
    gates = load(gates, semaphores)
    blocks = [rows_at(block_at(here_ref[0], n, count), size) for n in range(count)]
    for n, ref in enumerate(first):
        out_ref[blocks[0], n * piece : (n + 1) * piece] = ref[...]
    fill_state(ctx_ref, state_refs[: len(state_refs) // 2], state_refs[len(state_refs) // 2 :], state)
    done, _ = first_chunk(here_ref, count, size)
    before = jnp.zeros((decay_ref.shape[0], 1), F32)
    for n, running in enumerate(running_sums(decay_ref[...])):
        here = rows_of(n)
        gates[n].wait()

        @pl.when(done == n)
        def _():
            mixed_ref[here, :] = first_mixed_ref[...]
            scale_ref[here, :] = first_scale_ref[...]

        @pl.when(done != n)
        def _():
            chunk_part(groups, here, rows_of(n, CHUNK + STATE), running, before, gate_ref.at[here, :], x_ref, b_ref, c_ref,
                       skip_ref, rhs_ref, mixed_ref, scale_ref, here)

        before = before + running[:, CHUNK - 1 :]
    width = normed.shape[1] // groups
    for n in range(1, count):
        here = blocks[n]
        rows = norm_rows(groups, state, mixed_ref.at[here, :], scale_ref.at[here, :], c_ref.at[here, :], gain_ref)
        for g, part in enumerate(rows):
            normed[(n - 1) * size : n * size, g * width : (g + 1) * width] = part
    for tile, ref in enumerate(w_refs):
        product = dot(normed[...], ref[...]).astype(BF16)
        for n in range(1, count):
            out_ref[blocks[n], rows_of(tile, COLUMN_TILE)] = product[(n - 1) * size : n * size]


def pass_kernel(count, step, column, here_ref, *refs):
    sums_ref, even_out, odd_out = refs[-3:]
    arrived = refs[:-3]
    size, width = even_out.shape
    here = here_ref[0]

    def send(shift, came, out):
        block = jnp.clip(here + shift, 0, count - 1)
        rows = pl.ds(pl.multiple_of(block * size, size), size)
        own = sums_ref[rows, column : column + width].astype(F32)
        for ref in came:
            own = own + ref[...].astype(F32)
        out[...] = own.astype(BF16)

    for parity, to_right, to_left, from_left, from_right in (
        (0, even_out, odd_out, arrived[1:], arrived[:1]),
        (1, odd_out, even_out, arrived[:1], arrived[1:]),
    ):

        @pl.when((here & 1) == parity)
        def _():
            send(count - step, from_left, to_right)
            send(step - count, from_right, to_left)


def sum_kernel(column, here_ref, even_ref, odd_ref, sums_ref, *refs):
    out_hbm, total, semaphores = refs[-3:]
    size, width = even_ref.shape
    rows = pl.ds(pl.multiple_of(here_ref[0] * size, size), size)
    copies = []
    for n in range(SUM_COPIES):
        part = rows_of(n, size // SUM_COPIES)
        own = sums_ref[rows, column : column + width][part, :].astype(F32)
        total[part, :] = (own + even_ref[part, :].astype(F32) + odd_ref[part, :].astype(F32)).astype(BF16)
        to = out_hbm.at[part, column : column + width]
        copies.extend(load([(total.at[part, :], to)], semaphores.at[pl.ds(n, 1)]))
    for copy in copies:
        copy.wait()


def block_order(here, count):
    order = []
    for step in range(1, count):
        for block, sends in ((count - step + here, here <= step - 1), (step - count + here, here >= count - step)):
            if sends and block not in order:
                order.append(block)
    return order + [b for b in range(count) if b not in order]


def in_vmem(kernel, name, ins, outs, scratch=(), vmem=4, flops=1, result=None, aliases=None):
    vm = pl.BlockSpec(memory_space=pltpu.VMEM)
    specs, arrays = [], []
    for v in ins:
        if isinstance(v, tuple):
            specs.append(pl.BlockSpec(memory_space=pltpu.HBM))
            arrays.append(pltpu.with_memory_space_constraint(v[0], pltpu.HBM))
        elif v.dtype == jnp.int32:
            specs.append(pl.BlockSpec(memory_space=pltpu.SMEM))
            arrays.append(v)
        else:
            specs.append(vm)
            arrays.append(pltpu.with_memory_space_constraint(v, pltpu.VMEM))
    in_hbm = outs is None
    return pl.pallas_call(
        kernel,
        in_specs=specs,
        out_specs=[pl.BlockSpec(memory_space=pltpu.HBM)] if in_hbm else [vm for _ in outs],
        out_shape=[pltpu.HBM(*result)] if in_hbm else [pltpu.VMEM(shape, kind) for shape, kind in outs],
        scratch_shapes=list(scratch),
        input_output_aliases={len(ins) - 1: 0} if in_hbm and isinstance(ins[-1], tuple) else aliases or {},
        compiler_params=pltpu.CompilerParams(vmem_limit_bytes=vmem * 2**20),
        cost_estimate=pl.CostEstimate(flops=flops, bytes_accessed=1, transcendentals=0),
        name=name,
    )(*arrays)


def line_reduce(first, partial_sums, here, size, columns):
    count = lax.axis_size("tp")
    width = columns // PARTS
    block = ((size, width), BF16)
    even_edges = [(i, i ^ 1) for i in range(count)]
    odd_edges = [(i, ((i + 1) ^ 1) - 1) for i in range(1, count - 1)]
    arrived = [()] * PARTS
    for step in range(1, count):
        for half in range(PARTS):
            if step == 1:
                arrived[half] = (lax.ppermute(first[half], "tp", even_edges),)
                continue
            even, odd = in_vmem(
                partial(pass_kernel, count, step, half * width), "pass_on", (here, *arrived[half], partial_sums), (block, block)
            )
            arrived[half] = (lax.ppermute(even, "tp", even_edges), lax.ppermute(odd, "tp", odd_edges))
    out = ()
    for half in range(PARTS):
        ins = (here, *arrived[half], partial_sums, *out)
        scratch = [pltpu.VMEM((size, width), BF16), pltpu.SemaphoreType.DMA((SUM_COPIES,))]
        kernel = partial(sum_kernel, half * width)
        out = (tuple(in_vmem(kernel, "sum_up", ins, None, scratch, result=((size, columns), BF16))),)
    return out[0][0]


def on_device(x_in, gate_z, b_in, c_in, step_size, log_decay, skip, norm_gain, out_weight):
    rows, channels = x_in.shape
    heads = step_size.shape[1]
    groups = b_in.shape[1] // STATE
    chunks = rows // CHUNK
    columns = out_weight.shape[1]
    half = channels // 2
    devices = lax.axis_size("ctx")
    chips = devices // 2
    count = lax.axis_size("tp")
    size = rows // count
    ctx = lax.axis_index("ctx").astype(jnp.int32).reshape(1)
    here = lax.axis_index("tp").astype(jnp.int32).reshape(1)
    message = ((half + EXTRA, 128), BF16)
    by_head = ((heads, rows), F32)
    maps = ((rows, groups * STATE), BF16)
    weighted = pltpu.VMEM((rows, half), BF16)

    send, x_here, b_here, step, decay, spread = in_vmem(
        partial(send_kernel, groups),
        "end_state_sent",
        (ctx, here, (x_in,), (b_in,), (step_size.T,), (log_decay.T,)),
        (message, ((rows, channels), BF16), maps, by_head, by_head, ((128, half), BF16)),
        scratch=[weighted, pltpu.SemaphoreType.DMA((4 + chunks,))],
        vmem=6,
    )
    swap = [(i, i ^ 1) for i in range(devices)]
    sibling = lax.ppermute(send, "ctx", swap)
    tiles = columns // COLUMN_TILE
    weight = [None] * tiles
    w_tile = ((channels, COLUMN_TILE), BF16)
    token_shape = ((EXTRA, 128), BF16)
    own, weight[-1] = in_vmem(
        partial(keep_kernel, groups, tiles - 1),
        "end_state_kept",
        (ctx, (out_weight,), x_here, b_here, step, decay, spread),
        (message, w_tile),
        [weighted, pltpu.SemaphoreType.DMA((1,))],
        vmem=6,
        flops=10**9,
    )
    blocks = half // 128
    shares = [blocks // 4, (blocks - blocks // 4) // 2]
    shares.append(blocks - sum(shares))
    starts = [128 * sum(shares[:n]) for n in range(len(shares))]
    piece = [((128 * share + EXTRA, 128), BF16) for share in shares]
    totals = in_vmem(pair_kernel, "pair", (ctx, spread, own, sibling), piece)
    levels = chips.bit_length() - 1

    def swap_chips(level, block):
        return lax.ppermute(block, "ctx", [(i, i ^ (2 << level)) for i in range(devices)])

    def scan(mine, tile, number, after, carried):
        outs = (((chunks * (CHUNK + STATE), channels), BF16), ((STATE, channels), F32), token_shape, *(w_tile,) * number)
        rhs, state, token, *w_tiles = in_vmem(
            partial(scan_kernel, groups, mine, tile),
            "chunk_states",
            ((out_weight,), x_here, b_here, step, decay, after, *carried),
            outs,
            scratch=[pltpu.SemaphoreType.DMA((number,))],
            vmem=6,
            flops=2 * 10**9,
            aliases={6 + n: n for n in range(len(carried))},
        )
        weight[tile : tile + number] = w_tiles
        return (rhs, state), token

    received = [swap_chips(0, total) for total in totals]
    arrived = [[block] for block in received]
    middle = chunks // 2
    gaps = [list(range(middle)), [middle], list(range(middle + 1, chunks))]
    carried, after, tile = (), totals[-1], 0
    for level in range(1, levels):
        folded = []
        for n, start in enumerate(starts):
            if level == 1:
                number = 2 if n == 0 else 1
                carried, after = scan(gaps[n], tile, number, after, carried)
                tile += number
            kernel = partial(fold_kernel, level - 1, start)
            folded.extend(in_vmem(kernel, "fold", (ctx, after, spread, totals[n], received[n]), (piece[n],)))
            after = folded[-1]
            received[n] = swap_chips(level, after)
            arrived[n].append(received[n])
        totals = folded
    rhs = carried[0]
    number = tiles - 1 - tile
    chunk_rows = ((CHUNK, channels), F32)
    skip = skip.reshape(1, heads)
    mixed, scale, c_here, token, *w_tiles = in_vmem(
        partial(first_part_kernel, groups, count, tile),
        "first_part",
        (here, (gate_z,), (c_in,), (out_weight,), x_here, b_here, step, decay, skip, rhs, after),
        (chunk_rows, chunk_rows, maps, token_shape, *(w_tile,) * number),
        scratch=[pltpu.VMEM((CHUNK, channels), BF16), pltpu.SemaphoreType.DMA((2 + number,))],
        vmem=6,
        flops=4 * 10**9,
    )
    weight[tile : tiles - 1] = w_tiles
    keep, recv = [], []
    for n, start in enumerate(starts):
        state = ((STATE, 128 * shares[n]), BF16)
        kernel = partial(last_kernel, start)
        mine, send = in_vmem(kernel, "incoming", (ctx, token, spread, own, sibling, *arrived[n]), (state, state))
        keep.append(mine)
        recv.append(lax.ppermute(send, "ctx", swap))

    gain = norm_gain.reshape(1, channels)
    width = columns // PARTS
    part_tiles = width // COLUMN_TILE
    part = ((size, width), BF16)
    row_block = ((size, channels), BF16)
    whole_state = pltpu.VMEM((STATE, channels), BF16)
    inputs = (ctx, here, mixed, scale, c_here, gain, *weight[:part_tiles])
    if groups == 2:
        own_group, product = in_vmem(
            partial(own_group_kernel, count, part_tiles),
            "own_group",
            (*inputs, *keep),
            (((size, half), BF16), ((size, width), F32)),
            flops=10**9,
        )
        first, normed = in_vmem(
            partial(other_group_kernel, count, part_tiles),
            "other_group",
            (*inputs, *recv, own_group, product),
            (part, row_block),
        )
    else:
        first, normed = in_vmem(
            partial(both_groups_kernel, groups, count, part_tiles),
            "both_groups",
            (*inputs, *keep, *recv),
            (part, row_block),
            [whole_state],
        )
    parts = [first]
    for begin, end in ((1, 2), (2, PARTS)):
        mine = weight[begin * part_tiles : end * part_tiles]
        kernel = partial(project_kernel, len(mine))
        parts.extend(in_vmem(kernel, "first_block_rest", (normed, *mine), (part,) * (end - begin)))
    (partial_sums,) = in_vmem(
        partial(rest_kernel, groups, count, tiles),
        "other_blocks",
        (ctx, here, (gate_z,), x_here, b_here, step, decay, skip, rhs, c_here, mixed, scale, gain, *weight, *keep, *recv, *parts),
        (((rows, columns), BF16),),
        [
            whole_state,
            pltpu.VMEM((rows - size, channels), BF16),
            pltpu.VMEM((rows, channels), F32),
            pltpu.VMEM((rows, channels), F32),
            pltpu.VMEM((rows, channels), BF16),
            pltpu.SemaphoreType.DMA((chunks,)),
        ],
        vmem=20,
    )
    return line_reduce(parts, partial_sums, here, size, columns)


def solution(mesh):
    placed = (
        P("ctx", "tp"),
        P("ctx", "tp"),
        P("ctx", "tp"),
        P("ctx", "tp"),
        P("ctx", "tp"),
        P("ctx", "tp"),
        P("tp"),
        P("tp"),
        P("tp", None),
    )
    return jax.shard_map(
        on_device, mesh=mesh, in_specs=placed, out_specs=P(("ctx", "tp"), None), check_vma=False
    )
```

time: 94.9 us -> 103 us (1.085); the launches traced: 94.5 us -> 101 us
  waiting for transfers between devices: 17.4 us -> 26.1 us
  starting transfers between devices: 47 us -> 39.4 us
  Pallas kernels: 29.5 us -> 35 us
    ppermute x8, waiting for transfers between devices: 13.8 us -> 23.7 us  [line_reduce(): lax.ppermute(even, 'tp', even_edges)]
    ppermute x8, starting transfers between devices: 29.8 us -> 20.2 us  [line_reduce(): lax.ppermute(even, 'tp', even_edges)]
    pallas_call x25 -> x30, Pallas kernels: 29.5 us -> 35 us  [in_vmem(): pl.pallas_call(kernel, in_specs=specs, out_specs=[pl.BlockSpec(memory_spa...]
    ppermute x5 -> x9, starting transfers between devices: 7.06 us -> 9.11 us  [the longest x6 8.4 us: swap_chips(): lax.ppermute(block, 'ctx', [(i, i ^ 2 << level) for i in range(devices)])]
    ppermute x4, waiting for transfers between devices: 2.33 us -> 1.04 us  [line_reduce(): arrived[half] = (lax.ppermute(first[half], 'tp', even_edges),)]
  transfers between devices with their start and end apart: 26 -> 30, of which waited for: 8 -> 10; matrix products, arithmetic and copies ran while one was open for 0% -> 0% of each run, Pallas kernels for 26% -> 29%
where the time goes in v7:
time: 103 us; the launch traced here: 101 us
  starting transfers between devices  39.4 us (38%)
  Pallas kernels  35 us (34%)
  waiting for transfers between devices  26.1 us (25%)
    pallas_call x30, Pallas kernels, in_vmem(): pl.pallas_call(kernel, in_specs=specs, out_specs=[pl.BlockSpec(memory_spa...  35 us
    ppermute x8, waiting for transfers between devices, line_reduce(): lax.ppermute(even, 'tp', even_edges)  23.7 us
    ppermute x8, starting transfers between devices, line_reduce(): lax.ppermute(even, 'tp', even_edges)  20.2 us
    ppermute x6, starting transfers between devices, swap_chips(): lax.ppermute(block, 'ctx', [(i, i ^ 2 << level) for i in range(devices)])  8.4 us
    ppermute x8, starting transfers between devices, line_reduce(): lax.ppermute(odd, 'tp', odd_edges)  5.34 us
    ppermute x4, starting transfers between devices, line_reduce(): arrived[half] = (lax.ppermute(first[half], 'tp', even_edges),)  4.18 us
  transfers between devices with their start and end apart: 30, of which 10 were waited for; matrix products, arithmetic and copies ran while one was open for 0% of the time, Pallas kernels for 29%

profile of v7, /device:TPU:0, one launch (start us, length us, event | category | flops | bytes accessed | tf_op | source)
XLA Modules:
  0.0 101.0 jit_solution(10370238622954999593)
XLA Ops:
  0.0 2.7 %end_state_sent.1 = (bf16[1040,128]{1,0:T(8,128)(2,1)S(1)}, bf16[512,2048]{1,0:T(8,128)(2,1)S(1)}, bf16[512,256]{1,0:T(8,128)(2,1)S(1)}, f32[32,512]{1,0:T(8,128...) custom-call(s32[1]{0:T(128)} %bitcast.1.ctx_ref, s32[1]{0:T(128)} %bitcast.here_ref, ...), custom_call_target="tpu_custom_call" | custom-call | flops 1 | bytes 1 | tf_op jit(solution)/shard_map/end_state_sent/pallas_call | solution.py:505
  3.2 1.6 %end_state_kept.1 = (bf16[1040,128]{1,0:T(8,128)(2,1)S(1)}, bf16[2048,512]{1,0:T(8,128)(2,1)S(1)}) custom-call(s32[1]{0:T(128)} %bitcast.1.ctx_ref, bf16[2048,4096]{1,0:T(8,128)(2,1)} %w_hbm.9, bf16[512,2048]{1,0:T(8,128)(2,1)S(1)} %get-tuple-element.63.x_ref, bf16[512,256]{1,0:T(8,128)(2,1)S(1)} %get-tuple-element.64.b_ref, ...), custom_call_target="tpu_custom_call" | custom-call | flops 1000000000 | bytes 1 | tf_op jit(solution)/shard_map/end_state_kept/pallas_call | solution.py:505
  5.1 2.6 %collective-permute-start.1 = (bf16[272,128]{1,0:T(8,128)(2,1)S(1)}, bf16[272,128]{1,0:T(8,128)(2,1)S(1)}, u32[]{:S(2)}, u32[]{:S(2)}) collective-permute-start(bf16[272,128]{1,0:T(8,128)(2,1)S(1)} %get-tuple-element.72.total_ref), channel_id=1, source_target_pairs={{0,8},{4,12},{8,0},{12,4},{16,24},{20,28},{24,16},{28,20},{1,9},{5... | collective-permute-start | bytes 208904 | tf_op jit(solution)/shard_map/ppermute | solution.py:593
  7.7 2.9 %chunk_states.3 = (bf16[1024,2048]{1,0:T(8,128)(2,1)S(1)}, f32[128,2048]{1,0:T(8,128)S(1)}, bf16[16,128]{1,0:T(8,128)(2,1)S(1)}, bf16[2048,512]{1,0:T(8,128)(2,1)S(1)}, bf16[2048,512]{1,0:T(8,128)(2,1)S(1)}) custom-call(bf16[2048,4096]{1,0:T(8,128)(2,1)} %w_hbm.9, bf16[512,2048]{1,0:T(8,128)(2,1)S(1)} %get-tuple-element.63.x_ref, ...), custom_call_target="tpu_custom_call" | custom-call | flops 2000000000 | bytes 1 | tf_op jit(solution)/shard_map/chunk_states/pallas_call | solution.py:505
  10.6 2.0 %collective-permute-start.2 = (bf16[400,128]{1,0:T(8,128)(2,1)S(1)}, bf16[400,128]{1,0:T(8,128)(2,1)S(1)}, u32[]{:S(2)}, u32[]{:S(2)}) collective-permute-start(bf16[400,128]{1,0:T(8,128)(2,1)S(1)} %get-tuple-element.76.total_ref), channel_id=1, source_target_pairs={{0,8},{4,12},{8,0},{12,4},{16,24},{20,28},{24,16},{28,20},{1,9},{5... | collective-permute-start | bytes 307208 | tf_op jit(solution)/shard_map/ppermute | solution.py:593
  12.8 1.6 %collective-permute-start.4 = (bf16[272,128]{1,0:T(8,128)(2,1)S(1)}, bf16[272,128]{1,0:T(8,128)(2,1)S(1)}, u32[]{:S(2)}, u32[]{:S(2)}) collective-permute-start(bf16[272,128]{1,0:T(8,128)(2,1)S(1)} %fold.3.after_ref), channel_id=1, source_target_pairs={{0,16},{4,20},{8,24},{12,28},{16,0},{20,4},{24,8},{28,12},{1,17},{... | collective-permute-start | bytes 208904 | tf_op jit(solution)/shard_map/ppermute | solution.py:593
  14.4 1.6 %chunk_states.4 = (bf16[1024,2048]{1,0:T(8,128)(2,1)S(1)}, f32[128,2048]{1,0:T(8,128)S(1)}, bf16[16,128]{1,0:T(8,128)(2,1)S(1)}, bf16[2048,512]{1,0:T(8,128)(2,1)S(1)}) custom-call(bf16[2048,4096]{1,0:T(8,128)(2,1)} %w_hbm.9, bf16[512,2048]{1,0:T(8,128)(2,1)S(1)} %get-tuple-element.63.x_ref, ...), custom_call_target="tpu_custom_call", output_to_operand_aliasing={{0}: (6, {}), {1}: (7, {})} | custom-call | flops 2000000000 | bytes 1 | tf_op jit(solution)/shard_map/chunk_states/pallas_call | solution.py:505
  17.7 1.9 %chunk_states.5 = (bf16[1024,2048]{1,0:T(8,128)(2,1)S(1)}, f32[128,2048]{1,0:T(8,128)S(1)}, bf16[16,128]{1,0:T(8,128)(2,1)S(1)}, bf16[2048,512]{1,0:T(8,128)(2,1)S(1)}) custom-call(bf16[2048,4096]{1,0:T(8,128)(2,1)} %w_hbm.9, bf16[512,2048]{1,0:T(8,128)(2,1)S(1)} %get-tuple-element.63.x_ref, ...), custom_call_target="tpu_custom_call", output_to_operand_aliasing={{0}: (6, {}), {1}: (7, {})} | custom-call | flops 2000000000 | bytes 1 | tf_op jit(solution)/shard_map/chunk_states/pallas_call | solution.py:505
  20.5 3.2 %first_part.1 = (f32[128,2048]{1,0:T(8,128)S(1)}, f32[128,2048]{1,0:T(8,128)S(1)}, bf16[512,256]{1,0:T(8,128)(2,1)S(1)}, bf16[16,128]{1,0:T(8,128)(2,1)S(1)}, bf...) custom-call(s32[1]{0:T(128)} %bitcast.here_ref, ...), custom_call_target="tpu_custom_call" | custom-call | flops 4000000000 | bytes 1 | tf_op jit(solution)/shard_map/first_part/pallas_call | solution.py:505
  29.0 1.6 %collective-permute-start.20 = (bf16[128,1024]{1,0:T(8,128)(2,1)S(1)}, bf16[128,1024]{1,0:T(8,128)(2,1)S(1)}, u32[]{:S(2)}, u32[]{:S(2)}) collective-permute-start(bf16[128,1024]{1,0:T(8,128)(2,1)S(1)} %first_block_rest.3.refs_15_), channel_id=1, source_target_pairs={{0,1},{1,0},{2,3},{3,2},{4,5},{5,4},{6,7},{7,6},{8,9},{9,8},{10,11... | collective-permute-start | bytes 786440 | tf_op jit(solution)/shard_map/ppermute | solution.py:528
  32.5 1.6 %collective-permute-start.10 = (bf16[128,1024]{1,0:T(8,128)(2,1)S(1)}, bf16[128,1024]{1,0:T(8,128)(2,1)S(1)}, u32[]{:S(2)}, u32[]{:S(2)}) collective-permute-start(bf16[128,1024]{1,0:T(8,128)(2,1)S(1)} %get-tuple-element.100.refs_17_), channel_id=1, source_target_pairs={{0,1},{1,0},{2,3},{3,2},{4,5},{5,4},{6,7},{7,6},{8,9},{9,8},{10,11... | collective-permute-start | bytes 786440 | tf_op jit(solution)/shard_map/ppermute | solution.py:528
  34.6 11.7 %other_blocks.1.refs_1_.refs_2_.sums_ref = bf16[512,4096]{1,0:T(8,128)(2,1)S(1)} custom-call(s32[1]{0:T(128)} %bitcast.1.ctx_ref, s32[1]{0:T(128)} %bitcast.here_ref, bf16[512,2048]{1,0:T(8,128)(2,1)} %gate_hbm.3, bf16[512,2048]{1,0:T(8,128)(2,1)S(1)} %get-tuple-element.63.x_ref, bf16[512,256]{1,0:T(8,128)(2,1)S(1)} %get-tuple-element.64.b_ref, ...), custom_call_target="tpu_custom_call" | custom-call | flops 1 | bytes 1 | tf_op jit(solution)/shard_map/other_blocks/pallas_call | solution.py:505
  46.4 1.6 %collective-permute-start.21 = (bf16[128,1024]{1,0:T(8,128)(2,1)S(1)}, bf16[128,1024]{1,0:T(8,128)(2,1)S(1)}, u32[]{:S(2)}, u32[]{:S(2)}) collective-permute-start(bf16[128,1024]{1,0:T(8,128)(2,1)S(1)} %get-tuple-element.113), channel_id=1, source_target_pairs={{0,1},{1,0},{2,3},{3,2},{4,5},{5,4},{6,7},{7,6},{8,9},{9,8},{10,11... | collective-permute-start | bytes 786440 | tf_op jit(solution)/shard_map/ppermute | solution.py:533
  48.9 4.4 %collective-permute-start.26 = (bf16[128,1024]{1,0:T(8,128)(2,1)S(1)}, bf16[128,1024]{1,0:T(8,128)(2,1)S(1)}, u32[]{:S(2)}, u32[]{:S(2)}) collective-permute-start(bf16[128,1024]{1,0:T(8,128)(2,1)S(1)} %get-tuple-element.117), channel_id=1, source_target_pairs={{0,1},{1,0},{2,3},{3,2},{4,5},{5,4},{6,7},{7,6},{8,9},{9,8},{10,11... | collective-permute-start | bytes 786440 | tf_op jit(solution)/shard_map/ppermute | solution.py:533
  55.1 1.6 %collective-permute-start.11 = (bf16[128,1024]{1,0:T(8,128)(2,1)S(1)}, bf16[128,1024]{1,0:T(8,128)(2,1)S(1)}, u32[]{:S(2)}, u32[]{:S(2)}) collective-permute-start(bf16[128,1024]{1,0:T(8,128)(2,1)S(1)} %get-tuple-element.105), channel_id=1, source_target_pairs={{0,1},{1,0},{2,3},{3,2},{4,5},{5,4},{6,7},{7,6},{8,9},{9,8},{10,11... | collective-permute-start | bytes 786440 | tf_op jit(solution)/shard_map/ppermute | solution.py:533
  56.7 4.0 %collective-permute-done.21.refs_0_ = bf16[128,1024]{1,0:T(8,128)(2,1)S(1)} collective-permute-done((bf16[128,1024]{1,0:T(8,128)(2,1)S(1)}, bf16[128,1024]{1,0:T(8,128)(2,1)S(1)}, u32[]{:S(2)}, u32[]{:S(2)}) %collective-permute-start.21) | collective-permute-done | bytes 262176 | tf_op jit(solution)/shard_map/ppermute | solution.py:533
  61.5 4.4 %collective-permute-start.16 = (bf16[128,1024]{1,0:T(8,128)(2,1)S(1)}, bf16[128,1024]{1,0:T(8,128)(2,1)S(1)}, u32[]{:S(2)}, u32[]{:S(2)}) collective-permute-start(bf16[128,1024]{1,0:T(8,128)(2,1)S(1)} %get-tuple-element.109), channel_id=1, source_target_pairs={{0,1},{1,0},{2,3},{3,2},{4,5},{5,4},{6,7},{7,6},{8,9},{9,8},{10,11... | collective-permute-start | bytes 786440 | tf_op jit(solution)/shard_map/ppermute | solution.py:533
  67.2 4.5 %collective-permute-start.23 = (bf16[128,1024]{1,0:T(8,128)(2,1)S(1)}, bf16[128,1024]{1,0:T(8,128)(2,1)S(1)}, u32[]{:S(2)}, u32[]{:S(2)}) collective-permute-start(bf16[128,1024]{1,0:T(8,128)(2,1)S(1)} %get-tuple-element.115), channel_id=1, source_target_pairs={{0,1},{1,0},{2,3},{3,2},{4,5},{5,4},{6,7},{7,6},{8,9},{9,8},{10,11... | collective-permute-start | bytes 786440 | tf_op jit(solution)/shard_map/ppermute | solution.py:533
  72.0 1.6 %collective-permute-start.28 = (bf16[128,1024]{1,0:T(8,128)(2,1)S(1)}, bf16[128,1024]{1,0:T(8,128)(2,1)S(1)}, u32[]{:S(2)}, u32[]{:S(2)}) collective-permute-start(bf16[128,1024]{1,0:T(8,128)(2,1)S(1)} %get-tuple-element.119), channel_id=1, source_target_pairs={{0,1},{1,0},{2,3},{3,2},{4,5},{5,4},{6,7},{7,6},{8,9},{9,8},{10,11... | collective-permute-start | bytes 786440 | tf_op jit(solution)/shard_map/ppermute | solution.py:533
  74.4 3.2 %collective-permute-done.16.refs_0_ = bf16[128,1024]{1,0:T(8,128)(2,1)S(1)} collective-permute-done((bf16[128,1024]{1,0:T(8,128)(2,1)S(1)}, bf16[128,1024]{1,0:T(8,128)(2,1)S(1)}, u32[]{:S(2)}, u32[]{:S(2)}) %collective-permute-start.16) | collective-permute-done | bytes 262176 | tf_op jit(solution)/shard_map/ppermute | solution.py:533
  77.6 1.6 %collective-permute-start.13 = (bf16[128,1024]{1,0:T(8,128)(2,1)S(1)}, bf16[128,1024]{1,0:T(8,128)(2,1)S(1)}, u32[]{:S(2)}, u32[]{:S(2)}) collective-permute-start(bf16[128,1024]{1,0:T(8,128)(2,1)S(1)} %get-tuple-element.107), channel_id=1, source_target_pairs={{0,1},{1,0},{2,3},{3,2},{4,5},{5,4},{6,7},{7,6},{8,9},{9,8},{10,11... | collective-permute-start | bytes 786440 | tf_op jit(solution)/shard_map/ppermute | solution.py:533
  79.8 3.4 %collective-permute-done.23.even_ref = bf16[128,1024]{1,0:T(8,128)(2,1)S(1)} collective-permute-done((bf16[128,1024]{1,0:T(8,128)(2,1)S(1)}, bf16[128,1024]{1,0:T(8,128)(2,1)S(1)}, u32[]{:S(2)}, u32[]{:S(2)}) %collective-permute-start.23) | collective-permute-done | bytes 262176 | tf_op jit(solution)/shard_map/ppermute | solution.py:533
  83.9 4.9 %collective-permute-done.28.even_ref = bf16[128,1024]{1,0:T(8,128)(2,1)S(1)} collective-permute-done((bf16[128,1024]{1,0:T(8,128)(2,1)S(1)}, bf16[128,1024]{1,0:T(8,128)(2,1)S(1)}, u32[]{:S(2)}, u32[]{:S(2)}) %collective-permute-start.28) | collective-permute-done | bytes 262176 | tf_op jit(solution)/shard_map/ppermute | solution.py:533
  91.7 7.5 %collective-permute-done.18.even_ref = bf16[128,1024]{1,0:T(8,128)(2,1)S(1)} collective-permute-done((bf16[128,1024]{1,0:T(8,128)(2,1)S(1)}, bf16[128,1024]{1,0:T(8,128)(2,1)S(1)}, u32[]{:S(2)}, u32[]{:S(2)}) %collective-permute-start.18) | collective-permute-done | bytes 262176 | tf_op jit(solution)/shard_map/ppermute | solution.py:533
  (70 shorter events, 22.5 us)
Async XLA Ops:
  5.1 7.5 %collective-permute-start.1 = (bf16[272,128]{1,0:T(8,128)(2,1)S(1)}, bf16[272,128]{1,0:T(8,128)(2,1)S(1)}, u32[]{:S(2)}, u32[]{:S(2)}) collective-permute-start(bf16[272,128]{1,0:T(8,128)(2,1)S(1)} %get-tuple-element.72.total_ref), channel_id=1, source_target_pairs={{0,8},{4,12},{8,0},{12,4},{16,24},{20,28},{24,16},{28,20},{1,9},{5... | collective-permute-start | bytes 208904 | tf_op jit(solution)/shard_map/ppermute | solution.py:593
  7.7 11.9 %collective-permute-start.3 = (bf16[400,128]{1,0:T(8,128)(2,1)S(1)}, bf16[400,128]{1,0:T(8,128)(2,1)S(1)}, u32[]{:S(2)}, u32[]{:S(2)}) collective-permute-start(bf16[400,128]{1,0:T(8,128)(2,1)S(1)} %get-tuple-element.70.after_ref.total_ref), channel_id=1, source_target_pairs={{0,8},{4,12},{8,0},{12,4},{16,24},{20,28},{24,16},{28,20},{1,9},{5... | collective-permute-start | bytes 307208 | tf_op jit(solution)/shard_map/ppermute | solution.py:593
  12.8 13.0 %collective-permute-start.4 = (bf16[272,128]{1,0:T(8,128)(2,1)S(1)}, bf16[272,128]{1,0:T(8,128)(2,1)S(1)}, u32[]{:S(2)}, u32[]{:S(2)}) collective-permute-start(bf16[272,128]{1,0:T(8,128)(2,1)S(1)} %fold.3.after_ref), channel_id=1, source_target_pairs={{0,16},{4,20},{8,24},{12,28},{16,0},{20,4},{24,8},{28,12},{1,17},{... | collective-permute-start | bytes 208904 | tf_op jit(solution)/shard_map/ppermute | solution.py:593
  16.2 8.7 %collective-permute-start.6 = (bf16[400,128]{1,0:T(8,128)(2,1)S(1)}, bf16[400,128]{1,0:T(8,128)(2,1)S(1)}, u32[]{:S(2)}, u32[]{:S(2)}) collective-permute-start(bf16[400,128]{1,0:T(8,128)(2,1)S(1)} %fold.4.after_ref), channel_id=1, source_target_pairs={{0,16},{4,20},{8,24},{12,28},{16,0},{20,4},{24,8},{28,12},{1,17},{... | collective-permute-start | bytes 307208 | tf_op jit(solution)/shard_map/ppermute | solution.py:593
  29.0 17.3 %collective-permute-start.20 = (bf16[128,1024]{1,0:T(8,128)(2,1)S(1)}, bf16[128,1024]{1,0:T(8,128)(2,1)S(1)}, u32[]{:S(2)}, u32[]{:S(2)}) collective-permute-start(bf16[128,1024]{1,0:T(8,128)(2,1)S(1)} %first_block_rest.3.refs_15_), channel_id=1, source_target_pairs={{0,1},{1,0},{2,3},{3,2},{4,5},{5,4},{6,7},{7,6},{8,9},{9,8},{10,11... | collective-permute-start | bytes 786440 | tf_op jit(solution)/shard_map/ppermute | solution.py:528
  30.7 18.1 %collective-permute-start.25 = (bf16[128,1024]{1,0:T(8,128)(2,1)S(1)}, bf16[128,1024]{1,0:T(8,128)(2,1)S(1)}, u32[]{:S(2)}, u32[]{:S(2)}) collective-permute-start(bf16[128,1024]{1,0:T(8,128)(2,1)S(1)} %get-tuple-element.103.refs_14_), channel_id=1, source_target_pairs={{0,1},{1,0},{2,3},{3,2},{4,5},{5,4},{6,7},{7,6},{8,9},{9,8},{10,11... | collective-permute-start | bytes 786440 | tf_op jit(solution)/shard_map/ppermute | solution.py:528
  32.5 20.8 %collective-permute-start.10 = (bf16[128,1024]{1,0:T(8,128)(2,1)S(1)}, bf16[128,1024]{1,0:T(8,128)(2,1)S(1)}, u32[]{:S(2)}, u32[]{:S(2)}) collective-permute-start(bf16[128,1024]{1,0:T(8,128)(2,1)S(1)} %get-tuple-element.100.refs_17_), channel_id=1, source_target_pairs={{0,1},{1,0},{2,3},{3,2},{4,5},{5,4},{6,7},{7,6},{8,9},{9,8},{10,11... | collective-permute-start | bytes 786440 | tf_op jit(solution)/shard_map/ppermute | solution.py:528
  34.1 21.0 %collective-permute-start.15 = (bf16[128,1024]{1,0:T(8,128)(2,1)S(1)}, bf16[128,1024]{1,0:T(8,128)(2,1)S(1)}, u32[]{:S(2)}, u32[]{:S(2)}) collective-permute-start(bf16[128,1024]{1,0:T(8,128)(2,1)S(1)} %get-tuple-element.104.refs_16_), channel_id=1, source_target_pairs={{0,1},{1,0},{2,3},{3,2},{4,5},{5,4},{6,7},{7,6},{8,9},{9,8},{10,11... | collective-permute-start | bytes 786440 | tf_op jit(solution)/shard_map/ppermute | solution.py:528
  46.4 14.3 %collective-permute-start.21 = (bf16[128,1024]{1,0:T(8,128)(2,1)S(1)}, bf16[128,1024]{1,0:T(8,128)(2,1)S(1)}, u32[]{:S(2)}, u32[]{:S(2)}) collective-permute-start(bf16[128,1024]{1,0:T(8,128)(2,1)S(1)} %get-tuple-element.113), channel_id=1, source_target_pairs={{0,1},{1,0},{2,3},{3,2},{4,5},{5,4},{6,7},{7,6},{8,9},{9,8},{10,11... | collective-permute-start | bytes 786440 | tf_op jit(solution)/shard_map/ppermute | solution.py:533
  48.1 13.4 %collective-permute-start.22 = (bf16[128,1024]{1,0:T(8,128)(2,1)S(1)}, bf16[128,1024]{1,0:T(8,128)(2,1)S(1)}, u32[]{:S(2)}, u32[]{:S(2)}) collective-permute-start(bf16[128,1024]{1,0:T(8,128)(2,1)S(1)} %get-tuple-element.114), channel_id=1, source_target_pairs={{1,2},{2,1},{5,6},{6,5},{9,10},{10,9},{13,14},{14,13},{17,18},{18,... | collective-permute-start | bytes 786440 | tf_op jit(solution)/shard_map/ppermute | solution.py:533
  48.9 17.5 %collective-permute-start.26 = (bf16[128,1024]{1,0:T(8,128)(2,1)S(1)}, bf16[128,1024]{1,0:T(8,128)(2,1)S(1)}, u32[]{:S(2)}, u32[]{:S(2)}) collective-permute-start(bf16[128,1024]{1,0:T(8,128)(2,1)S(1)} %get-tuple-element.117), channel_id=1, source_target_pairs={{0,1},{1,0},{2,3},{3,2},{4,5},{5,4},{6,7},{7,6},{8,9},{9,8},{10,11... | collective-permute-start | bytes 786440 | tf_op jit(solution)/shard_map/ppermute | solution.py:533
  53.3 13.9 %collective-permute-start.27 = (bf16[128,1024]{1,0:T(8,128)(2,1)S(1)}, bf16[128,1024]{1,0:T(8,128)(2,1)S(1)}, u32[]{:S(2)}, u32[]{:S(2)}) collective-permute-start(bf16[128,1024]{1,0:T(8,128)(2,1)S(1)} %get-tuple-element.118), channel_id=1, source_target_pairs={{1,2},{2,1},{5,6},{6,5},{9,10},{10,9},{13,14},{14,13},{17,18},{18,... | collective-permute-start | bytes 786440 | tf_op jit(solution)/shard_map/ppermute | solution.py:533
  55.1 16.9 %collective-permute-start.11 = (bf16[128,1024]{1,0:T(8,128)(2,1)S(1)}, bf16[128,1024]{1,0:T(8,128)(2,1)S(1)}, u32[]{:S(2)}, u32[]{:S(2)}) collective-permute-start(bf16[128,1024]{1,0:T(8,128)(2,1)S(1)} %get-tuple-element.105), channel_id=1, source_target_pairs={{0,1},{1,0},{2,3},{3,2},{4,5},{5,4},{6,7},{7,6},{8,9},{9,8},{10,11... | collective-permute-start | bytes 786440 | tf_op jit(solution)/shard_map/ppermute | solution.py:533
  60.7 12.8 %collective-permute-start.12 = (bf16[128,1024]{1,0:T(8,128)(2,1)S(1)}, bf16[128,1024]{1,0:T(8,128)(2,1)S(1)}, u32[]{:S(2)}, u32[]{:S(2)}) collective-permute-start(bf16[128,1024]{1,0:T(8,128)(2,1)S(1)} %get-tuple-element.106), channel_id=1, source_target_pairs={{1,2},{2,1},{5,6},{6,5},{9,10},{10,9},{13,14},{14,13},{17,18},{18,... | collective-permute-start | bytes 786440 | tf_op jit(solution)/shard_map/ppermute | solution.py:533
  61.5 16.1 %collective-permute-start.16 = (bf16[128,1024]{1,0:T(8,128)(2,1)S(1)}, bf16[128,1024]{1,0:T(8,128)(2,1)S(1)}, u32[]{:S(2)}, u32[]{:S(2)}) collective-permute-start(bf16[128,1024]{1,0:T(8,128)(2,1)S(1)} %get-tuple-element.109), channel_id=1, source_target_pairs={{0,1},{1,0},{2,3},{3,2},{4,5},{5,4},{6,7},{7,6},{8,9},{9,8},{10,11... | collective-permute-start | bytes 786440 | tf_op jit(solution)/shard_map/ppermute | solution.py:533
  66.3 12.8 %collective-permute-start.17 = (bf16[128,1024]{1,0:T(8,128)(2,1)S(1)}, bf16[128,1024]{1,0:T(8,128)(2,1)S(1)}, u32[]{:S(2)}, u32[]{:S(2)}) collective-permute-start(bf16[128,1024]{1,0:T(8,128)(2,1)S(1)} %get-tuple-element.110), channel_id=1, source_target_pairs={{1,2},{2,1},{5,6},{6,5},{9,10},{10,9},{13,14},{14,13},{17,18},{18,... | collective-permute-start | bytes 786440 | tf_op jit(solution)/shard_map/ppermute | solution.py:533
  67.2 16.0 %collective-permute-start.23 = (bf16[128,1024]{1,0:T(8,128)(2,1)S(1)}, bf16[128,1024]{1,0:T(8,128)(2,1)S(1)}, u32[]{:S(2)}, u32[]{:S(2)}) collective-permute-start(bf16[128,1024]{1,0:T(8,128)(2,1)S(1)} %get-tuple-element.115), channel_id=1, source_target_pairs={{0,1},{1,0},{2,3},{3,2},{4,5},{5,4},{6,7},{7,6},{8,9},{9,8},{10,11... | collective-permute-start | bytes 786440 | tf_op jit(solution)/shard_map/ppermute | solution.py:533
  72.0 16.9 %collective-permute-start.28 = (bf16[128,1024]{1,0:T(8,128)(2,1)S(1)}, bf16[128,1024]{1,0:T(8,128)(2,1)S(1)}, u32[]{:S(2)}, u32[]{:S(2)}) collective-permute-start(bf16[128,1024]{1,0:T(8,128)(2,1)S(1)} %get-tuple-element.119), channel_id=1, source_target_pairs={{0,1},{1,0},{2,3},{3,2},{4,5},{5,4},{6,7},{7,6},{8,9},{9,8},{10,11... | collective-permute-start | bytes 786440 | tf_op jit(solution)/shard_map/ppermute | solution.py:533
  73.5 15.9 %collective-permute-start.29 = (bf16[128,1024]{1,0:T(8,128)(2,1)S(1)}, bf16[128,1024]{1,0:T(8,128)(2,1)S(1)}, u32[]{:S(2)}, u32[]{:S(2)}) collective-permute-start(bf16[128,1024]{1,0:T(8,128)(2,1)S(1)} %get-tuple-element.120), channel_id=1, source_target_pairs={{1,2},{2,1},{5,6},{6,5},{9,10},{10,9},{13,14},{14,13},{17,18},{18,... | collective-permute-start | bytes 786440 | tf_op jit(solution)/shard_map/ppermute | solution.py:533
  77.6 22.5 %collective-permute-start.13 = (bf16[128,1024]{1,0:T(8,128)(2,1)S(1)}, bf16[128,1024]{1,0:T(8,128)(2,1)S(1)}, u32[]{:S(2)}, u32[]{:S(2)}) collective-permute-start(bf16[128,1024]{1,0:T(8,128)(2,1)S(1)} %get-tuple-element.107), channel_id=1, source_target_pairs={{0,1},{1,0},{2,3},{3,2},{4,5},{5,4},{6,7},{7,6},{8,9},{9,8},{10,11... | collective-permute-start | bytes 786440 | tf_op jit(solution)/shard_map/ppermute | solution.py:533
  79.3 20.0 %collective-permute-start.18 = (bf16[128,1024]{1,0:T(8,128)(2,1)S(1)}, bf16[128,1024]{1,0:T(8,128)(2,1)S(1)}, u32[]{:S(2)}, u32[]{:S(2)}) collective-permute-start(bf16[128,1024]{1,0:T(8,128)(2,1)S(1)} %get-tuple-element.111), channel_id=1, source_target_pairs={{0,1},{1,0},{2,3},{3,2},{4,5},{5,4},{6,7},{7,6},{8,9},{9,8},{10,11... | collective-permute-start | bytes 786440 | tf_op jit(solution)/shard_map/ppermute | solution.py:533
  83.2 7.8 %collective-permute-start.24 = (bf16[128,1024]{1,0:T(8,128)(2,1)S(1)}, bf16[128,1024]{1,0:T(8,128)(2,1)S(1)}, u32[]{:S(2)}, u32[]{:S(2)}) collective-permute-start(bf16[128,1024]{1,0:T(8,128)(2,1)S(1)} %get-tuple-element.116), channel_id=1, source_target_pairs={{1,2},{2,1},{5,6},{6,5},{9,10},{10,9},{13,14},{14,13},{17,18},{18,... | collective-permute-start | bytes 786440 | tf_op jit(solution)/shard_map/ppermute | solution.py:533
  88.8 10.4 %collective-permute-start.19 = (bf16[128,1024]{1,0:T(8,128)(2,1)S(1)}, bf16[128,1024]{1,0:T(8,128)(2,1)S(1)}, u32[]{:S(2)}, u32[]{:S(2)}) collective-permute-start(bf16[128,1024]{1,0:T(8,128)(2,1)S(1)} %get-tuple-element.112), channel_id=1, source_target_pairs={{1,2},{2,1},{5,6},{6,5},{9,10},{10,9},{13,14},{14,13},{17,18},{18,... | collective-permute-start | bytes 786440 | tf_op jit(solution)/shard_map/ppermute | solution.py:533
  89.5 10.5 %collective-permute-start.14 = (bf16[128,1024]{1,0:T(8,128)(2,1)S(1)}, bf16[128,1024]{1,0:T(8,128)(2,1)S(1)}, u32[]{:S(2)}, u32[]{:S(2)}) collective-permute-start(bf16[128,1024]{1,0:T(8,128)(2,1)S(1)} %get-tuple-element.108), channel_id=1, source_target_pairs={{1,2},{2,1},{5,6},{6,5},{9,10},{10,9},{13,14},{14,13},{17,18},{18,... | collective-permute-start | bytes 786440 | tf_op jit(solution)/shard_map/ppermute | solution.py:533
  (8 other events, 23.9 us)

commit v8 on v6

--- a/solution.py
+++ b/solution.py
@@ -25,10 +25,6 @@
     return jnp.dot(a, b, preferred_element_type=F32)
 
 
-def dot_exact(a, b):
-    return jnp.dot(a, b, preferred_element_type=F32, precision=lax.Precision.HIGHEST)
-
-
 def head_map(channels):
     head = lax.broadcasted_iota(jnp.int32, (128, channels), 0) & 63
     place = lax.broadcasted_iota(jnp.int32, (128, channels), 1) >> 6
@@ -54,10 +50,18 @@
 
 
 def running_sums(decay):
+    heads, rows = decay.shape
+    chunks = rows // CHUNK
+    values = jnp.concatenate([decay[:, rows_of(n)] for n in range(chunks)], axis=0)
+    first = values.astype(BF16)
+    rest = values - first.astype(F32)
+    second = rest.astype(BF16)
+    third = (rest - second.astype(F32)).astype(BF16)
     row = lax.broadcasted_iota(jnp.int32, (CHUNK, CHUNK), 0)
     column = lax.broadcasted_iota(jnp.int32, (CHUNK, CHUNK), 1)
-    upper = jnp.where(row <= column, 1.0, 0.0)
-    return [dot_exact(decay[:, rows_of(n)], upper) for n in range(decay.shape[1] // CHUNK)]
+    upper = jnp.where(row <= column, 1.0, 0.0).astype(BF16)
+    sums = dot(jnp.concatenate([first, second, third], axis=1), jnp.concatenate([upper] * 3, axis=0))
+    return [sums[rows_of(n, heads)] for n in range(chunks)]
 
 
 def load(pairs, semaphores):
@@ -265,7 +269,7 @@
                 )
                 state[g] = state[g] * to_state + fresh * to_fresh
             gate = gate_ref[rows_of(n - mine[0]), cut].astype(F32)
-            gate = gate / (1.0 + jnp.exp(-gate))
+            gate = gate * (0.5 * jnp.tanh(0.5 * gate) + 0.5)
             mixed_ref[here, cut] = (within * wide[CHUNK : 2 * CHUNK] + x * skip[:, cut]) * gate
             scale_ref[here, cut] = wide[2 * CHUNK : 3 * CHUNK] * gate
     before_ref[...] = jnp.broadcast_to(before, before_ref.shape)

time: 94.9 us -> 94.6 us (level)
  transfers between devices with their start and end apart: 26 -> 26, of which waited for: 8 -> 9; matrix products, arithmetic and copies ran while one was open for 0% -> 0% of each run, Pallas kernels for 26% -> 26%
where the time goes in v8:
time: 94.6 us; the launch traced here: 94.3 us
  starting transfers between devices  47 us (50%)
  Pallas kernels  29.2 us (31%)
  waiting for transfers between devices  17.7 us (19%)
    ppermute x8, starting transfers between devices, line_reduce(): lax.ppermute(even, 'tp', even_edges)  29.7 us
    pallas_call x25, Pallas kernels, in_vmem(): pl.pallas_call(kernel, in_specs=specs, out_specs=[pl.BlockSpec(memory_spa...  29.2 us
    ppermute x8, waiting for transfers between devices, line_reduce(): lax.ppermute(even, 'tp', even_edges)  13.8 us
    ppermute x4, starting transfers between devices, swap_chips(): lax.ppermute(v, 'ctx', [(i, i ^ 2 << level) for i in range(devices)])  6.99 us
    ppermute x8, starting transfers between devices, line_reduce(): lax.ppermute(odd, 'tp', odd_edges)  5.38 us
    ppermute x4, starting transfers between devices, line_reduce(): arrived[half] = (lax.ppermute(first[half], 'tp', even_edges),)  4.25 us
    ppermute x4, waiting for transfers between devices, line_reduce(): arrived[half] = (lax.ppermute(first[half], 'tp', even_edges),)  2.34 us
  transfers between devices with their start and end apart: 26, of which 9 were waited for; matrix products, arithmetic and copies ran while one was open for 0% of the time, Pallas kernels for 26%

profile of v8, /device:TPU:0, one launch (start us, length us, event | category | flops | bytes accessed | tf_op | source)
XLA Modules:
  0.0 94.3 jit_solution(16712546929660148689)
XLA Ops:
  0.0 2.5 %end_state_sent.1 = (bf16[1040,128]{1,0:T(8,128)(2,1)S(1)}, bf16[512,2048]{1,0:T(8,128)(2,1)S(1)}, bf16[512,256]{1,0:T(8,128)(2,1)S(1)}, f32[32,512]{1,0:T(8,128...) custom-call(s32[1]{0:T(128)} %bitcast.1.ctx_ref, s32[1]{0:T(128)} %bitcast.here_ref, ...), custom_call_target="tpu_custom_call" | custom-call | flops 1 | bytes 1 | tf_op jit(solution)/shard_map/end_state_sent/pallas_call | solution.py:460
  3.1 0.9 end_state_kept.1.own_ref
  4.5 2.9 %collective-permute-start.1 = (bf16[528,128]{1,0:T(8,128)(2,1)S(1)}, bf16[528,128]{1,0:T(8,128)(2,1)S(1)}, u32[]{:S(2)}, u32[]{:S(2)}) collective-permute-start(bf16[528,128]{1,0:T(8,128)(2,1)S(1)} %get-tuple-element.57.total_ref), channel_id=1, source_target_pairs={{0,8},{4,12},{8,0},{12,4},{16,24},{20,28},{24,16},{28,20},{1,9},{5... | collective-permute-start | bytes 405512 | tf_op jit(solution)/shard_map/ppermute | solution.py:536
  7.5 3.9 %local_part.2 = (f32[512,2048]{1,0:T(8,128)S(1)}, f32[512,2048]{1,0:T(8,128)S(1)}, bf16[512,256]{1,0:T(8,128)(2,1)S(1)}, f32[128,2048]{1,0:T(8,128)S(1)}, f32[32...) custom-call(bf16[512,2048]{1,0:T(8,128)(2,1)} %gate_hbm.3, bf16[512,256]{1,0:T(8,128)(2,1)} %c_hbm.3, ...), custom_call_target="tpu_custom_call" | custom-call | flops 4000000000 | bytes 1 | tf_op jit(solution)/shard_map/local_part/pallas_call | solution.py:460
  12.0 2.2 %collective-permute-start.3 = (bf16[528,128]{1,0:T(8,128)(2,1)S(1)}, bf16[528,128]{1,0:T(8,128)(2,1)S(1)}, u32[]{:S(2)}, u32[]{:S(2)}) collective-permute-start(bf16[528,128]{1,0:T(8,128)(2,1)S(1)} %fold.2.after_ref), channel_id=1, source_target_pairs={{0,16},{4,20},{8,24},{12,28},{16,0},{20,4},{24,8},{28,12},{1,17},{... | collective-permute-start | bytes 405512 | tf_op jit(solution)/shard_map/ppermute | solution.py:536
  14.4 1.8 %collective-permute-start.4 = (bf16[528,128]{1,0:T(8,128)(2,1)S(1)}, bf16[528,128]{1,0:T(8,128)(2,1)S(1)}, u32[]{:S(2)}, u32[]{:S(2)}) collective-permute-start(bf16[528,128]{1,0:T(8,128)(2,1)S(1)} %fold.3.after_ref), channel_id=1, source_target_pairs={{0,16},{4,20},{8,24},{12,28},{16,0},{20,4},{24,8},{28,12},{1,17},{... | collective-permute-start | bytes 405512 | tf_op jit(solution)/shard_map/ppermute | solution.py:536
  16.2 3.9 %local_part.3 = (f32[512,2048]{1,0:T(8,128)S(1)}, f32[512,2048]{1,0:T(8,128)S(1)}, bf16[512,256]{1,0:T(8,128)(2,1)S(1)}, f32[128,2048]{1,0:T(8,128)S(1)}, f32[32...) custom-call(bf16[512,2048]{1,0:T(8,128)(2,1)} %gate_hbm.3, ...), custom_call_target="tpu_custom_call", output_to_operand_aliasing={{0}: (9, {}), {1}: (10, {}), {2}: (11, {}), {3}: (12, {}), ... | custom-call | flops 4000000000 | bytes 1 | tf_op jit(solution)/shard_map/local_part/pallas_call | solution.py:460
  23.0 2.0 %collective-permute-start.21 = (bf16[128,1024]{1,0:T(8,128)(2,1)S(1)}, bf16[128,1024]{1,0:T(8,128)(2,1)S(1)}, u32[]{:S(2)}, u32[]{:S(2)}) collective-permute-start(bf16[128,1024]{1,0:T(8,128)(2,1)S(1)} %get-tuple-element.75.refs_0_), channel_id=1, source_target_pairs={{0,1},{1,0},{2,3},{3,2},{4,5},{5,4},{6,7},{7,6},{8,9},{9,8},{10,11... | collective-permute-start | bytes 786440 | tf_op jit(solution)/shard_map/ppermute | solution.py:483
  25.9 1.3 %first_block_rest.2 = (bf16[128,1024]{1,0:T(8,128)(2,1)S(1)}, bf16[128,1024]{1,0:T(8,128)(2,1)S(1)}) custom-call(bf16[128,2048]{1,0:T(8,128)(2,1)S(1)} %get-tuple-element.72.normed_ref, bf16[2048,2048]{1,0:T(8,128)(2,1)S(1)} %get-tuple-element.73.w_ref.wb_ref), custom_call_target="tpu_custom_call" | custom-call | flops 1 | bytes 1 | tf_op jit(solution)/shard_map/first_block_rest/pallas_call | solution.py:460
  27.1 2.0 %collective-permute-start.11 = (bf16[128,1024]{1,0:T(8,128)(2,1)S(1)}, bf16[128,1024]{1,0:T(8,128)(2,1)S(1)}, u32[]{:S(2)}, u32[]{:S(2)}) collective-permute-start(bf16[128,1024]{1,0:T(8,128)(2,1)S(1)} %get-tuple-element.76.refs_2_), channel_id=1, source_target_pairs={{0,1},{1,0},{2,3},{3,2},{4,5},{5,4},{6,7},{7,6},{8,9},{9,8},{10,11... | collective-permute-start | bytes 786440 | tf_op jit(solution)/shard_map/ppermute | solution.py:483
  29.2 9.3 %other_blocks.1.refs_1_.refs_2_.sums_ref = bf16[512,4096]{1,0:T(8,128)(2,1)S(1)} custom-call(s32[1]{0:T(128)} %bitcast.1.ctx_ref, s32[1]{0:T(128)} %bitcast.here_ref, f32[512,2048]{1,0:T(8,128)S(1)} %get-tuple-element.63.mixed_ref, f32[512,2048]{1,0:T(8,128)S(1)} %get-tuple-element.64.scale_ref, bf16[512,256]{1,0:T(8,128)(2,1)S(1)} %get-tuple-element.65.c_ref, ...), custom_call_target="tpu_custom_call" | custom-call | flops 1 | bytes 1 | tf_op jit(solution)/shard_map/other_blocks/pallas_call | solution.py:460
  38.7 2.0 %collective-permute-start.22 = (bf16[128,1024]{1,0:T(8,128)(2,1)S(1)}, bf16[128,1024]{1,0:T(8,128)(2,1)S(1)}, u32[]{:S(2)}, u32[]{:S(2)}) collective-permute-start(bf16[128,1024]{1,0:T(8,128)(2,1)S(1)} %get-tuple-element.89), channel_id=1, source_target_pairs={{0,1},{1,0},{2,3},{3,2},{4,5},{5,4},{6,7},{7,6},{8,9},{9,8},{10,11... | collective-permute-start | bytes 786440 | tf_op jit(solution)/shard_map/ppermute | solution.py:488
  41.5 4.4 %collective-permute-start.17 = (bf16[128,1024]{1,0:T(8,128)(2,1)S(1)}, bf16[128,1024]{1,0:T(8,128)(2,1)S(1)}, u32[]{:S(2)}, u32[]{:S(2)}) collective-permute-start(bf16[128,1024]{1,0:T(8,128)(2,1)S(1)} %get-tuple-element.85), channel_id=1, source_target_pairs={{0,1},{1,0},{2,3},{3,2},{4,5},{5,4},{6,7},{7,6},{8,9},{9,8},{10,11... | collective-permute-start | bytes 786440 | tf_op jit(solution)/shard_map/ppermute | solution.py:488
  46.7 2.3 %collective-permute-done.6.refs_0_ = bf16[128,1024]{1,0:T(8,128)(2,1)S(1)} collective-permute-done((bf16[128,1024]{1,0:T(8,128)(2,1)S(1)}, bf16[128,1024]{1,0:T(8,128)(2,1)S(1)}, u32[]{:S(2)}, u32[]{:S(2)}) %collective-permute-start.6) | collective-permute-done | bytes 262176 | tf_op jit(solution)/shard_map/ppermute | solution.py:483
  49.0 2.0 %collective-permute-start.12 = (bf16[128,1024]{1,0:T(8,128)(2,1)S(1)}, bf16[128,1024]{1,0:T(8,128)(2,1)S(1)}, u32[]{:S(2)}, u32[]{:S(2)}) collective-permute-start(bf16[128,1024]{1,0:T(8,128)(2,1)S(1)} %get-tuple-element.81), channel_id=1, source_target_pairs={{0,1},{1,0},{2,3},{3,2},{4,5},{5,4},{6,7},{7,6},{8,9},{9,8},{10,11... | collective-permute-start | bytes 786440 | tf_op jit(solution)/shard_map/ppermute | solution.py:488
  51.0 3.6 %collective-permute-done.22.refs_0_ = bf16[128,1024]{1,0:T(8,128)(2,1)S(1)} collective-permute-done((bf16[128,1024]{1,0:T(8,128)(2,1)S(1)}, bf16[128,1024]{1,0:T(8,128)(2,1)S(1)}, u32[]{:S(2)}, u32[]{:S(2)}) %collective-permute-start.22) | collective-permute-done | bytes 262176 | tf_op jit(solution)/shard_map/ppermute | solution.py:488
  55.4 4.8 %collective-permute-start.7 = (bf16[128,1024]{1,0:T(8,128)(2,1)S(1)}, bf16[128,1024]{1,0:T(8,128)(2,1)S(1)}, u32[]{:S(2)}, u32[]{:S(2)}) collective-permute-start(bf16[128,1024]{1,0:T(8,128)(2,1)S(1)} %get-tuple-element.77), channel_id=1, source_target_pairs={{0,1},{1,0},{2,3},{3,2},{4,5},{5,4},{6,7},{7,6},{8,9},{9,8},{10,11... | collective-permute-start | bytes 786440 | tf_op jit(solution)/shard_map/ppermute | solution.py:488
  61.1 4.7 %collective-permute-start.24 = (bf16[128,1024]{1,0:T(8,128)(2,1)S(1)}, bf16[128,1024]{1,0:T(8,128)(2,1)S(1)}, u32[]{:S(2)}, u32[]{:S(2)}) collective-permute-start(bf16[128,1024]{1,0:T(8,128)(2,1)S(1)} %get-tuple-element.91), channel_id=1, source_target_pairs={{0,1},{1,0},{2,3},{3,2},{4,5},{5,4},{6,7},{7,6},{8,9},{9,8},{10,11... | collective-permute-start | bytes 786440 | tf_op jit(solution)/shard_map/ppermute | solution.py:488
  66.7 4.8 %collective-permute-start.19 = (bf16[128,1024]{1,0:T(8,128)(2,1)S(1)}, bf16[128,1024]{1,0:T(8,128)(2,1)S(1)}, u32[]{:S(2)}, u32[]{:S(2)}) collective-permute-start(bf16[128,1024]{1,0:T(8,128)(2,1)S(1)} %get-tuple-element.87), channel_id=1, source_target_pairs={{0,1},{1,0},{2,3},{3,2},{4,5},{5,4},{6,7},{7,6},{8,9},{9,8},{10,11... | collective-permute-start | bytes 786440 | tf_op jit(solution)/shard_map/ppermute | solution.py:488
  72.3 4.8 %collective-permute-start.14 = (bf16[128,1024]{1,0:T(8,128)(2,1)S(1)}, bf16[128,1024]{1,0:T(8,128)(2,1)S(1)}, u32[]{:S(2)}, u32[]{:S(2)}) collective-permute-start(bf16[128,1024]{1,0:T(8,128)(2,1)S(1)} %get-tuple-element.83), channel_id=1, source_target_pairs={{0,1},{1,0},{2,3},{3,2},{4,5},{5,4},{6,7},{7,6},{8,9},{9,8},{10,11... | collective-permute-start | bytes 786440 | tf_op jit(solution)/shard_map/ppermute | solution.py:488
  78.6 4.1 %collective-permute-done.19.even_ref = bf16[128,1024]{1,0:T(8,128)(2,1)S(1)} collective-permute-done((bf16[128,1024]{1,0:T(8,128)(2,1)S(1)}, bf16[128,1024]{1,0:T(8,128)(2,1)S(1)}, u32[]{:S(2)}, u32[]{:S(2)}) %collective-permute-start.19) | collective-permute-done | bytes 262176 | tf_op jit(solution)/shard_map/ppermute | solution.py:488
  82.7 2.3 %collective-permute-start.9 = (bf16[128,1024]{1,0:T(8,128)(2,1)S(1)}, bf16[128,1024]{1,0:T(8,128)(2,1)S(1)}, u32[]{:S(2)}, u32[]{:S(2)}) collective-permute-start(bf16[128,1024]{1,0:T(8,128)(2,1)S(1)} %get-tuple-element.79), channel_id=1, source_target_pairs={{0,1},{1,0},{2,3},{3,2},{4,5},{5,4},{6,7},{7,6},{8,9},{9,8},{10,11... | collective-permute-start | bytes 786440 | tf_op jit(solution)/shard_map/ppermute | solution.py:488
  86.6 1.8 %collective-permute-done.14.even_ref = bf16[128,1024]{1,0:T(8,128)(2,1)S(1)} collective-permute-done((bf16[128,1024]{1,0:T(8,128)(2,1)S(1)}, bf16[128,1024]{1,0:T(8,128)(2,1)S(1)}, u32[]{:S(2)}, u32[]{:S(2)}) %collective-permute-start.14) | collective-permute-done | bytes 262176 | tf_op jit(solution)/shard_map/ppermute | solution.py:488
  89.1 4.3 %collective-permute-done.9.even_ref = bf16[128,1024]{1,0:T(8,128)(2,1)S(1)} collective-permute-done((bf16[128,1024]{1,0:T(8,128)(2,1)S(1)}, bf16[128,1024]{1,0:T(8,128)(2,1)S(1)}, u32[]{:S(2)}, u32[]{:S(2)}) %collective-permute-start.9) | collective-permute-done | bytes 262176 | tf_op jit(solution)/shard_map/ppermute | solution.py:488
  (57 shorter events, 15.1 us)
Async XLA Ops:
  4.5 7.3 %collective-permute-start.1 = (bf16[528,128]{1,0:T(8,128)(2,1)S(1)}, bf16[528,128]{1,0:T(8,128)(2,1)S(1)}, u32[]{:S(2)}, u32[]{:S(2)}) collective-permute-start(bf16[528,128]{1,0:T(8,128)(2,1)S(1)} %get-tuple-element.57.total_ref), channel_id=1, source_target_pairs={{0,8},{4,12},{8,0},{12,4},{16,24},{20,28},{24,16},{28,20},{1,9},{5... | collective-permute-start | bytes 405512 | tf_op jit(solution)/shard_map/ppermute | solution.py:536
  7.4 6.8 %collective-permute-start.2 = (bf16[528,128]{1,0:T(8,128)(2,1)S(1)}, bf16[528,128]{1,0:T(8,128)(2,1)S(1)}, u32[]{:S(2)}, u32[]{:S(2)}) collective-permute-start(bf16[528,128]{1,0:T(8,128)(2,1)S(1)} %get-tuple-element.55.after_ref.total_ref), channel_id=1, source_target_pairs={{0,8},{4,12},{8,0},{12,4},{16,24},{20,28},{24,16},{28,20},{1,9},{5... | collective-permute-start | bytes 405512 | tf_op jit(solution)/shard_map/ppermute | solution.py:536
  12.0 8.2 %collective-permute-start.3 = (bf16[528,128]{1,0:T(8,128)(2,1)S(1)}, bf16[528,128]{1,0:T(8,128)(2,1)S(1)}, u32[]{:S(2)}, u32[]{:S(2)}) collective-permute-start(bf16[528,128]{1,0:T(8,128)(2,1)S(1)} %fold.2.after_ref), channel_id=1, source_target_pairs={{0,16},{4,20},{8,24},{12,28},{16,0},{20,4},{24,8},{28,12},{1,17},{... | collective-permute-start | bytes 405512 | tf_op jit(solution)/shard_map/ppermute | solution.py:536
  14.4 5.7 %collective-permute-start.4 = (bf16[528,128]{1,0:T(8,128)(2,1)S(1)}, bf16[528,128]{1,0:T(8,128)(2,1)S(1)}, u32[]{:S(2)}, u32[]{:S(2)}) collective-permute-start(bf16[528,128]{1,0:T(8,128)(2,1)S(1)} %fold.3.after_ref), channel_id=1, source_target_pairs={{0,16},{4,20},{8,24},{12,28},{16,0},{20,4},{24,8},{28,12},{1,17},{... | collective-permute-start | bytes 405512 | tf_op jit(solution)/shard_map/ppermute | solution.py:536
  23.0 15.6 %collective-permute-start.21 = (bf16[128,1024]{1,0:T(8,128)(2,1)S(1)}, bf16[128,1024]{1,0:T(8,128)(2,1)S(1)}, u32[]{:S(2)}, u32[]{:S(2)}) collective-permute-start(bf16[128,1024]{1,0:T(8,128)(2,1)S(1)} %get-tuple-element.75.refs_0_), channel_id=1, source_target_pairs={{0,1},{1,0},{2,3},{3,2},{4,5},{5,4},{6,7},{7,6},{8,9},{9,8},{10,11... | collective-permute-start | bytes 786440 | tf_op jit(solution)/shard_map/ppermute | solution.py:483
  25.7 15.6 %collective-permute-start.16 = (bf16[128,1024]{1,0:T(8,128)(2,1)S(1)}, bf16[128,1024]{1,0:T(8,128)(2,1)S(1)}, u32[]{:S(2)}, u32[]{:S(2)}) collective-permute-start(bf16[128,1024]{1,0:T(8,128)(2,1)S(1)} %first_block_rest.3.refs_1_), channel_id=1, source_target_pairs={{0,1},{1,0},{2,3},{3,2},{4,5},{5,4},{6,7},{7,6},{8,9},{9,8},{10,11... | collective-permute-start | bytes 786440 | tf_op jit(solution)/shard_map/ppermute | solution.py:483
  27.1 18.8 %collective-permute-start.11 = (bf16[128,1024]{1,0:T(8,128)(2,1)S(1)}, bf16[128,1024]{1,0:T(8,128)(2,1)S(1)}, u32[]{:S(2)}, u32[]{:S(2)}) collective-permute-start(bf16[128,1024]{1,0:T(8,128)(2,1)S(1)} %get-tuple-element.76.refs_2_), channel_id=1, source_target_pairs={{0,1},{1,0},{2,3},{3,2},{4,5},{5,4},{6,7},{7,6},{8,9},{9,8},{10,11... | collective-permute-start | bytes 786440 | tf_op jit(solution)/shard_map/ppermute | solution.py:483
  29.1 19.9 %collective-permute-start.6 = (bf16[128,1024]{1,0:T(8,128)(2,1)S(1)}, bf16[128,1024]{1,0:T(8,128)(2,1)S(1)}, u32[]{:S(2)}, u32[]{:S(2)}) collective-permute-start(bf16[128,1024]{1,0:T(8,128)(2,1)S(1)} %get-tuple-element.74.refs_3_), channel_id=1, source_target_pairs={{0,1},{1,0},{2,3},{3,2},{4,5},{5,4},{6,7},{7,6},{8,9},{9,8},{10,11... | collective-permute-start | bytes 786440 | tf_op jit(solution)/shard_map/ppermute | solution.py:483
  38.7 16.0 %collective-permute-start.22 = (bf16[128,1024]{1,0:T(8,128)(2,1)S(1)}, bf16[128,1024]{1,0:T(8,128)(2,1)S(1)}, u32[]{:S(2)}, u32[]{:S(2)}) collective-permute-start(bf16[128,1024]{1,0:T(8,128)(2,1)S(1)} %get-tuple-element.89), channel_id=1, source_target_pairs={{0,1},{1,0},{2,3},{3,2},{4,5},{5,4},{6,7},{7,6},{8,9},{9,8},{10,11... | collective-permute-start | bytes 786440 | tf_op jit(solution)/shard_map/ppermute | solution.py:488
  40.7 14.7 %collective-permute-start.23 = (bf16[128,1024]{1,0:T(8,128)(2,1)S(1)}, bf16[128,1024]{1,0:T(8,128)(2,1)S(1)}, u32[]{:S(2)}, u32[]{:S(2)}) collective-permute-start(bf16[128,1024]{1,0:T(8,128)(2,1)S(1)} %get-tuple-element.90), channel_id=1, source_target_pairs={{1,2},{2,1},{5,6},{6,5},{9,10},{10,9},{13,14},{14,13},{17,18},{18,... | collective-permute-start | bytes 786440 | tf_op jit(solution)/shard_map/ppermute | solution.py:488
  41.5 19.0 %collective-permute-start.17 = (bf16[128,1024]{1,0:T(8,128)(2,1)S(1)}, bf16[128,1024]{1,0:T(8,128)(2,1)S(1)}, u32[]{:S(2)}, u32[]{:S(2)}) collective-permute-start(bf16[128,1024]{1,0:T(8,128)(2,1)S(1)} %get-tuple-element.85), channel_id=1, source_target_pairs={{0,1},{1,0},{2,3},{3,2},{4,5},{5,4},{6,7},{7,6},{8,9},{9,8},{10,11... | collective-permute-start | bytes 786440 | tf_op jit(solution)/shard_map/ppermute | solution.py:488
  45.9 15.2 %collective-permute-start.18 = (bf16[128,1024]{1,0:T(8,128)(2,1)S(1)}, bf16[128,1024]{1,0:T(8,128)(2,1)S(1)}, u32[]{:S(2)}, u32[]{:S(2)}) collective-permute-start(bf16[128,1024]{1,0:T(8,128)(2,1)S(1)} %get-tuple-element.86), channel_id=1, source_target_pairs={{1,2},{2,1},{5,6},{6,5},{9,10},{10,9},{13,14},{14,13},{17,18},{18,... | collective-permute-start | bytes 786440 | tf_op jit(solution)/shard_map/ppermute | solution.py:488
  49.0 16.9 %collective-permute-start.12 = (bf16[128,1024]{1,0:T(8,128)(2,1)S(1)}, bf16[128,1024]{1,0:T(8,128)(2,1)S(1)}, u32[]{:S(2)}, u32[]{:S(2)}) collective-permute-start(bf16[128,1024]{1,0:T(8,128)(2,1)S(1)} %get-tuple-element.81), channel_id=1, source_target_pairs={{0,1},{1,0},{2,3},{3,2},{4,5},{5,4},{6,7},{7,6},{8,9},{9,8},{10,11... | collective-permute-start | bytes 786440 | tf_op jit(solution)/shard_map/ppermute | solution.py:488
  54.6 12.0 %collective-permute-start.13 = (bf16[128,1024]{1,0:T(8,128)(2,1)S(1)}, bf16[128,1024]{1,0:T(8,128)(2,1)S(1)}, u32[]{:S(2)}, u32[]{:S(2)}) collective-permute-start(bf16[128,1024]{1,0:T(8,128)(2,1)S(1)} %get-tuple-element.82), channel_id=1, source_target_pairs={{1,2},{2,1},{5,6},{6,5},{9,10},{10,9},{13,14},{14,13},{17,18},{18,... | collective-permute-start | bytes 786440 | tf_op jit(solution)/shard_map/ppermute | solution.py:488
  55.4 16.1 %collective-permute-start.7 = (bf16[128,1024]{1,0:T(8,128)(2,1)S(1)}, bf16[128,1024]{1,0:T(8,128)(2,1)S(1)}, u32[]{:S(2)}, u32[]{:S(2)}) collective-permute-start(bf16[128,1024]{1,0:T(8,128)(2,1)S(1)} %get-tuple-element.77), channel_id=1, source_target_pairs={{0,1},{1,0},{2,3},{3,2},{4,5},{5,4},{6,7},{7,6},{8,9},{9,8},{10,11... | collective-permute-start | bytes 786440 | tf_op jit(solution)/shard_map/ppermute | solution.py:488
  60.4 11.8 %collective-permute-start.8 = (bf16[128,1024]{1,0:T(8,128)(2,1)S(1)}, bf16[128,1024]{1,0:T(8,128)(2,1)S(1)}, u32[]{:S(2)}, u32[]{:S(2)}) collective-permute-start(bf16[128,1024]{1,0:T(8,128)(2,1)S(1)} %get-tuple-element.78), channel_id=1, source_target_pairs={{1,2},{2,1},{5,6},{6,5},{9,10},{10,9},{13,14},{14,13},{17,18},{18,... | collective-permute-start | bytes 786440 | tf_op jit(solution)/shard_map/ppermute | solution.py:488
  61.1 16.1 %collective-permute-start.24 = (bf16[128,1024]{1,0:T(8,128)(2,1)S(1)}, bf16[128,1024]{1,0:T(8,128)(2,1)S(1)}, u32[]{:S(2)}, u32[]{:S(2)}) collective-permute-start(bf16[128,1024]{1,0:T(8,128)(2,1)S(1)} %get-tuple-element.91), channel_id=1, source_target_pairs={{0,1},{1,0},{2,3},{3,2},{4,5},{5,4},{6,7},{7,6},{8,9},{9,8},{10,11... | collective-permute-start | bytes 786440 | tf_op jit(solution)/shard_map/ppermute | solution.py:488
  66.0 11.9 %collective-permute-start.25 = (bf16[128,1024]{1,0:T(8,128)(2,1)S(1)}, bf16[128,1024]{1,0:T(8,128)(2,1)S(1)}, u32[]{:S(2)}, u32[]{:S(2)}) collective-permute-start(bf16[128,1024]{1,0:T(8,128)(2,1)S(1)} %get-tuple-element.92), channel_id=1, source_target_pairs={{1,2},{2,1},{5,6},{6,5},{9,10},{10,9},{13,14},{14,13},{17,18},{18,... | collective-permute-start | bytes 786440 | tf_op jit(solution)/shard_map/ppermute | solution.py:488
  66.7 16.1 %collective-permute-start.19 = (bf16[128,1024]{1,0:T(8,128)(2,1)S(1)}, bf16[128,1024]{1,0:T(8,128)(2,1)S(1)}, u32[]{:S(2)}, u32[]{:S(2)}) collective-permute-start(bf16[128,1024]{1,0:T(8,128)(2,1)S(1)} %get-tuple-element.87), channel_id=1, source_target_pairs={{0,1},{1,0},{2,3},{3,2},{4,5},{5,4},{6,7},{7,6},{8,9},{9,8},{10,11... | collective-permute-start | bytes 786440 | tf_op jit(solution)/shard_map/ppermute | solution.py:488
  71.6 14.2 %collective-permute-start.20 = (bf16[128,1024]{1,0:T(8,128)(2,1)S(1)}, bf16[128,1024]{1,0:T(8,128)(2,1)S(1)}, u32[]{:S(2)}, u32[]{:S(2)}) collective-permute-start(bf16[128,1024]{1,0:T(8,128)(2,1)S(1)} %get-tuple-element.88), channel_id=1, source_target_pairs={{1,2},{2,1},{5,6},{6,5},{9,10},{10,9},{13,14},{14,13},{17,18},{18,... | collective-permute-start | bytes 786440 | tf_op jit(solution)/shard_map/ppermute | solution.py:488
  72.3 16.1 %collective-permute-start.14 = (bf16[128,1024]{1,0:T(8,128)(2,1)S(1)}, bf16[128,1024]{1,0:T(8,128)(2,1)S(1)}, u32[]{:S(2)}, u32[]{:S(2)}) collective-permute-start(bf16[128,1024]{1,0:T(8,128)(2,1)S(1)} %get-tuple-element.83), channel_id=1, source_target_pairs={{0,1},{1,0},{2,3},{3,2},{4,5},{5,4},{6,7},{7,6},{8,9},{9,8},{10,11... | collective-permute-start | bytes 786440 | tf_op jit(solution)/shard_map/ppermute | solution.py:488
  77.2 11.1 %collective-permute-start.15 = (bf16[128,1024]{1,0:T(8,128)(2,1)S(1)}, bf16[128,1024]{1,0:T(8,128)(2,1)S(1)}, u32[]{:S(2)}, u32[]{:S(2)}) collective-permute-start(bf16[128,1024]{1,0:T(8,128)(2,1)S(1)} %get-tuple-element.84), channel_id=1, source_target_pairs={{1,2},{2,1},{5,6},{6,5},{9,10},{10,9},{13,14},{14,13},{17,18},{18,... | collective-permute-start | bytes 786440 | tf_op jit(solution)/shard_map/ppermute | solution.py:488
  77.9 11.2 %collective-permute-start.10 = (bf16[128,1024]{1,0:T(8,128)(2,1)S(1)}, bf16[128,1024]{1,0:T(8,128)(2,1)S(1)}, u32[]{:S(2)}, u32[]{:S(2)}) collective-permute-start(bf16[128,1024]{1,0:T(8,128)(2,1)S(1)} %get-tuple-element.80), channel_id=1, source_target_pairs={{1,2},{2,1},{5,6},{6,5},{9,10},{10,9},{13,14},{14,13},{17,18},{18,... | collective-permute-start | bytes 786440 | tf_op jit(solution)/shard_map/ppermute | solution.py:488
  82.7 10.7 %collective-permute-start.9 = (bf16[128,1024]{1,0:T(8,128)(2,1)S(1)}, bf16[128,1024]{1,0:T(8,128)(2,1)S(1)}, u32[]{:S(2)}, u32[]{:S(2)}) collective-permute-start(bf16[128,1024]{1,0:T(8,128)(2,1)S(1)} %get-tuple-element.79), channel_id=1, source_target_pairs={{0,1},{1,0},{2,3},{3,2},{4,5},{5,4},{6,7},{7,6},{8,9},{9,8},{10,11... | collective-permute-start | bytes 786440 | tf_op jit(solution)/shard_map/ppermute | solution.py:488
  (4 other events, 15.2 us)

commit v9 on v8

--- a/solution.py
+++ b/solution.py
@@ -142,7 +142,8 @@
     copies[-1].wait()
 
 
-def keep_kernel(groups, ctx_ref, x_ref, b_ref, step_ref, decay_ref, spread_ref, keep_ref, weighted):
+def keep_kernel(groups, ctx_ref, x_ref, b_ref, step_ref, decay_ref, spread_ref, keep_ref, all_spread_ref, weighted):
+    all_spread_ref[...] = head_map(x_ref.shape[1])
     end_state(groups, (ctx_ref[0] & 1), x_ref, b_ref, step_ref, decay_ref, weighted, keep_ref, spread_ref[...])
 
 
@@ -203,7 +204,7 @@
             send_ref[...] = both[other]
 
 
-def local_kernel(groups, part_index, gate_hbm, c_hbm, w_hbm, x_ref, b_ref, step_ref, decay_ref, skip_ref, after_ref, *refs):
+def local_kernel(groups, part_index, gate_hbm, c_hbm, w_hbm, x_ref, b_ref, step_ref, decay_ref, skip_ref, spread_ref, after_ref, *refs):
     if part_index:
         refs = refs[5:]
     mixed_ref, scale_ref, c_ref, state_ref, before_ref, w_ref, token_ref, gate_ref, semaphores = refs
@@ -222,12 +223,11 @@
     weights = [(w_hbm.at[rows_of(n, size), columns], w_ref.at[rows_of(n, size), :]) for n in range(WEIGHT_COPIES)]
     weights = load(weights, semaphores.at[pl.ds(1 + chunks, WEIGHT_COPIES)])
 
-    spread = head_map(channels)
     row = lax.broadcasted_iota(jnp.int32, (CHUNK, CHUNK), 0)
     column = lax.broadcasted_iota(jnp.int32, (CHUNK, CHUNK), 1)
     lane = lax.broadcasted_iota(jnp.int32, (heads, CHUNK), 1)
     skip = jnp.concatenate([pieces(skip_ref[...], 0), jnp.zeros((EXTRA, 128 - heads), F32)], axis=1)
-    skip = wide_log(skip.astype(BF16), spread)
+    skip = wide_log(skip.astype(BF16), spread_ref[...])
     before = jnp.zeros((heads, 1), F32)
     state = [jnp.zeros((STATE, width), F32)] * groups
     if part_index:
@@ -253,7 +253,7 @@
         for g in range(groups):
             cut = slice(g * width, (g + 1) * width)
             part = slice(g * STATE, (g + 1) * STATE)
-            wide = dot(factors, spread[:, cut])
+            wide = dot(factors, spread_ref[:, cut])
             to_state, to_fresh, to_middle = (wide[3 * CHUNK + n : 3 * CHUNK + n + 1] for n in range(3))
             x = x_ref[here, cut].astype(F32)
             weighted = (x * wide[:CHUNK]).astype(BF16)
@@ -524,8 +524,9 @@
     )
     swap = [(i, i ^ 1) for i in range(devices)]
     sibling = lax.ppermute(send, "ctx", swap)
-    (own,) = in_vmem(
-        partial(keep_kernel, groups), "end_state_kept", (ctx, x_here, b_here, step, decay, spread), (message,), [weighted],
+    own, all_spread = in_vmem(
+        partial(keep_kernel, groups), "end_state_kept", (ctx, x_here, b_here, step, decay, spread),
+        (message, ((128, channels), BF16)), [weighted],
         vmem=6, flops=10**9,
     )
     piece = ((half // PIECES + EXTRA, 128), BF16)
@@ -539,7 +540,7 @@
         return in_vmem(
             partial(local_kernel, groups, part_index),
             "local_part",
-            ((gate_z,), (c_in,), (out_weight,), x_here, b_here, step, decay, skip.reshape(1, heads), after, *carried),
+            ((gate_z,), (c_in,), (out_weight,), x_here, b_here, step, decay, skip.reshape(1, heads), all_spread, after, *carried),
             (
                 whole,
                 whole,
@@ -555,7 +556,7 @@
             ],
             vmem=10,
             flops=4 * 10**9,
-            aliases={9 + n: n for n in range(len(carried))},
+            aliases={10 + n: n for n in range(len(carried))},
         )
 
     received = swap_chips(0, totals)

time: 94.6 us -> 94.6 us (level)
  transfers between devices with their start and end apart: 26 -> 26, of which waited for: 9 -> 8; matrix products, arithmetic and copies ran while one was open for 0% -> 0% of each run, Pallas kernels for 26% -> 26%
where the time goes in v9:
time: 94.6 us; the launch traced here: 94.3 us
  starting transfers between devices  47 us (50%)
  Pallas kernels  29.3 us (31%)
  waiting for transfers between devices  17.5 us (18%)
    ppermute x8, starting transfers between devices, line_reduce(): lax.ppermute(even, 'tp', even_edges)  29.8 us
    pallas_call x25, Pallas kernels, in_vmem(): pl.pallas_call(kernel, in_specs=specs, out_specs=[pl.BlockSpec(memory_spa...  29.3 us
    ppermute x8, waiting for transfers between devices, line_reduce(): lax.ppermute(even, 'tp', even_edges)  13.8 us
    ppermute x4, starting transfers between devices, swap_chips(): lax.ppermute(v, 'ctx', [(i, i ^ 2 << level) for i in range(devices)])  6.98 us
    ppermute x8, starting transfers between devices, line_reduce(): lax.ppermute(odd, 'tp', odd_edges)  5.38 us
    ppermute x4, starting transfers between devices, line_reduce(): arrived[half] = (lax.ppermute(first[half], 'tp', even_edges),)  4.26 us
    ppermute x4, waiting for transfers between devices, line_reduce(): arrived[half] = (lax.ppermute(first[half], 'tp', even_edges),)  2.28 us
  transfers between devices with their start and end apart: 26, of which 8 were waited for; matrix products, arithmetic and copies ran while one was open for 0% of the time, Pallas kernels for 26%

profile of v9, /device:TPU:0, one launch (start us, length us, event | category | flops | bytes accessed | tf_op | source)
XLA Modules:
  0.0 94.3 jit_solution(18022506934081221814)
XLA Ops:
  0.0 2.5 %end_state_sent.1 = (bf16[1040,128]{1,0:T(8,128)(2,1)S(1)}, bf16[512,2048]{1,0:T(8,128)(2,1)S(1)}, bf16[512,256]{1,0:T(8,128)(2,1)S(1)}, f32[32,512]{1,0:T(8,128...) custom-call(s32[1]{0:T(128)} %bitcast.1.ctx_ref, s32[1]{0:T(128)} %bitcast.here_ref, ...), custom_call_target="tpu_custom_call" | custom-call | flops 1 | bytes 1 | tf_op jit(solution)/shard_map/end_state_sent/pallas_call | solution.py:460
  3.1 1.0 %end_state_kept.1 = (bf16[1040,128]{1,0:T(8,128)(2,1)S(1)}, bf16[128,2048]{1,0:T(8,128)(2,1)S(1)}) custom-call(s32[1]{0:T(128)} %bitcast.1.ctx_ref, bf16[512,2048]{1,0:T(8,128)(2,1)S(1)} %get-tuple-element.51.x_ref, bf16[512,256]{1,0:T(8,128)(2,1)S(1)} %get-tuple-element.52.b_ref, f32[32,512]{1,0:T(8,128)S(1)} %get-tuple-element.53.step_ref, ...), custom_call_target="tpu_custom_call" | custom-call | flops 1000000000 | bytes 1 | tf_op jit(solution)/shard_map/end_state_kept/pallas_call | solution.py:460
  4.5 2.9 %collective-permute-start.1 = (bf16[528,128]{1,0:T(8,128)(2,1)S(1)}, bf16[528,128]{1,0:T(8,128)(2,1)S(1)}, u32[]{:S(2)}, u32[]{:S(2)}) collective-permute-start(bf16[528,128]{1,0:T(8,128)(2,1)S(1)} %get-tuple-element.61.total_ref), channel_id=1, source_target_pairs={{0,8},{4,12},{8,0},{12,4},{16,24},{20,28},{24,16},{28,20},{1,9},{5... | collective-permute-start | bytes 405512 | tf_op jit(solution)/shard_map/ppermute | solution.py:537
  7.5 3.9 %local_part.2 = (f32[512,2048]{1,0:T(8,128)S(1)}, f32[512,2048]{1,0:T(8,128)S(1)}, bf16[512,256]{1,0:T(8,128)(2,1)S(1)}, f32[128,2048]{1,0:T(8,128)S(1)}, f32[32...) custom-call(bf16[512,2048]{1,0:T(8,128)(2,1)} %gate_hbm.3, bf16[512,256]{1,0:T(8,128)(2,1)} %c_hbm.3, ...), custom_call_target="tpu_custom_call" | custom-call | flops 4000000000 | bytes 1 | tf_op jit(solution)/shard_map/local_part/pallas_call | solution.py:460
  12.0 2.2 %collective-permute-start.3 = (bf16[528,128]{1,0:T(8,128)(2,1)S(1)}, bf16[528,128]{1,0:T(8,128)(2,1)S(1)}, u32[]{:S(2)}, u32[]{:S(2)}) collective-permute-start(bf16[528,128]{1,0:T(8,128)(2,1)S(1)} %fold.2.after_ref), channel_id=1, source_target_pairs={{0,16},{4,20},{8,24},{12,28},{16,0},{20,4},{24,8},{28,12},{1,17},{... | collective-permute-start | bytes 405512 | tf_op jit(solution)/shard_map/ppermute | solution.py:537
  14.4 1.8 %collective-permute-start.4 = (bf16[528,128]{1,0:T(8,128)(2,1)S(1)}, bf16[528,128]{1,0:T(8,128)(2,1)S(1)}, u32[]{:S(2)}, u32[]{:S(2)}) collective-permute-start(bf16[528,128]{1,0:T(8,128)(2,1)S(1)} %fold.3.after_ref), channel_id=1, source_target_pairs={{0,16},{4,20},{8,24},{12,28},{16,0},{20,4},{24,8},{28,12},{1,17},{... | collective-permute-start | bytes 405512 | tf_op jit(solution)/shard_map/ppermute | solution.py:537
  16.3 3.9 %local_part.3 = (f32[512,2048]{1,0:T(8,128)S(1)}, f32[512,2048]{1,0:T(8,128)S(1)}, bf16[512,256]{1,0:T(8,128)(2,1)S(1)}, f32[128,2048]{1,0:T(8,128)S(1)}, f32[32...) custom-call(bf16[512,2048]{1,0:T(8,128)(2,1)} %gate_hbm.3, ...), custom_call_target="tpu_custom_call", output_to_operand_aliasing={{0}: (10, {}), {1}: (11, {}), {2}: (12, {}), {3}: (13, {}),... | custom-call | flops 4000000000 | bytes 1 | tf_op jit(solution)/shard_map/local_part/pallas_call | solution.py:460
  23.0 2.0 %collective-permute-start.21 = (bf16[128,1024]{1,0:T(8,128)(2,1)S(1)}, bf16[128,1024]{1,0:T(8,128)(2,1)S(1)}, u32[]{:S(2)}, u32[]{:S(2)}) collective-permute-start(bf16[128,1024]{1,0:T(8,128)(2,1)S(1)} %get-tuple-element.79.refs_0_), channel_id=1, source_target_pairs={{0,1},{1,0},{2,3},{3,2},{4,5},{5,4},{6,7},{7,6},{8,9},{9,8},{10,11... | collective-permute-start | bytes 786440 | tf_op jit(solution)/shard_map/ppermute | solution.py:483
  25.9 1.3 %first_block_rest.2 = (bf16[128,1024]{1,0:T(8,128)(2,1)S(1)}, bf16[128,1024]{1,0:T(8,128)(2,1)S(1)}) custom-call(bf16[128,2048]{1,0:T(8,128)(2,1)S(1)} %get-tuple-element.76.normed_ref, bf16[2048,2048]{1,0:T(8,128)(2,1)S(1)} %get-tuple-element.77.w_ref.wb_ref), custom_call_target="tpu_custom_call" | custom-call | flops 1 | bytes 1 | tf_op jit(solution)/shard_map/first_block_rest/pallas_call | solution.py:460
  27.2 2.0 %collective-permute-start.11 = (bf16[128,1024]{1,0:T(8,128)(2,1)S(1)}, bf16[128,1024]{1,0:T(8,128)(2,1)S(1)}, u32[]{:S(2)}, u32[]{:S(2)}) collective-permute-start(bf16[128,1024]{1,0:T(8,128)(2,1)S(1)} %get-tuple-element.80.refs_2_), channel_id=1, source_target_pairs={{0,1},{1,0},{2,3},{3,2},{4,5},{5,4},{6,7},{7,6},{8,9},{9,8},{10,11... | collective-permute-start | bytes 786440 | tf_op jit(solution)/shard_map/ppermute | solution.py:483
  29.3 9.3 %other_blocks.1.refs_1_.refs_2_.sums_ref = bf16[512,4096]{1,0:T(8,128)(2,1)S(1)} custom-call(s32[1]{0:T(128)} %bitcast.1.ctx_ref, s32[1]{0:T(128)} %bitcast.here_ref, f32[512,2048]{1,0:T(8,128)S(1)} %get-tuple-element.67.mixed_ref, f32[512,2048]{1,0:T(8,128)S(1)} %get-tuple-element.68.scale_ref, bf16[512,256]{1,0:T(8,128)(2,1)S(1)} %get-tuple-element.69.c_ref, ...), custom_call_target="tpu_custom_call" | custom-call | flops 1 | bytes 1 | tf_op jit(solution)/shard_map/other_blocks/pallas_call | solution.py:460
  38.7 2.0 %collective-permute-start.22 = (bf16[128,1024]{1,0:T(8,128)(2,1)S(1)}, bf16[128,1024]{1,0:T(8,128)(2,1)S(1)}, u32[]{:S(2)}, u32[]{:S(2)}) collective-permute-start(bf16[128,1024]{1,0:T(8,128)(2,1)S(1)} %get-tuple-element.93), channel_id=1, source_target_pairs={{0,1},{1,0},{2,3},{3,2},{4,5},{5,4},{6,7},{7,6},{8,9},{9,8},{10,11... | collective-permute-start | bytes 786440 | tf_op jit(solution)/shard_map/ppermute | solution.py:488
  41.5 4.4 %collective-permute-start.17 = (bf16[128,1024]{1,0:T(8,128)(2,1)S(1)}, bf16[128,1024]{1,0:T(8,128)(2,1)S(1)}, u32[]{:S(2)}, u32[]{:S(2)}) collective-permute-start(bf16[128,1024]{1,0:T(8,128)(2,1)S(1)} %get-tuple-element.89), channel_id=1, source_target_pairs={{0,1},{1,0},{2,3},{3,2},{4,5},{5,4},{6,7},{7,6},{8,9},{9,8},{10,11... | collective-permute-start | bytes 786440 | tf_op jit(solution)/shard_map/ppermute | solution.py:488
  46.8 2.3 %collective-permute-done.6.refs_0_ = bf16[128,1024]{1,0:T(8,128)(2,1)S(1)} collective-permute-done((bf16[128,1024]{1,0:T(8,128)(2,1)S(1)}, bf16[128,1024]{1,0:T(8,128)(2,1)S(1)}, u32[]{:S(2)}, u32[]{:S(2)}) %collective-permute-start.6) | collective-permute-done | bytes 262176 | tf_op jit(solution)/shard_map/ppermute | solution.py:483
  49.0 2.0 %collective-permute-start.12 = (bf16[128,1024]{1,0:T(8,128)(2,1)S(1)}, bf16[128,1024]{1,0:T(8,128)(2,1)S(1)}, u32[]{:S(2)}, u32[]{:S(2)}) collective-permute-start(bf16[128,1024]{1,0:T(8,128)(2,1)S(1)} %get-tuple-element.85), channel_id=1, source_target_pairs={{0,1},{1,0},{2,3},{3,2},{4,5},{5,4},{6,7},{7,6},{8,9},{9,8},{10,11... | collective-permute-start | bytes 786440 | tf_op jit(solution)/shard_map/ppermute | solution.py:488
  51.0 3.6 %collective-permute-done.22.refs_0_ = bf16[128,1024]{1,0:T(8,128)(2,1)S(1)} collective-permute-done((bf16[128,1024]{1,0:T(8,128)(2,1)S(1)}, bf16[128,1024]{1,0:T(8,128)(2,1)S(1)}, u32[]{:S(2)}, u32[]{:S(2)}) %collective-permute-start.22) | collective-permute-done | bytes 262176 | tf_op jit(solution)/shard_map/ppermute | solution.py:488
  55.4 4.8 %collective-permute-start.7 = (bf16[128,1024]{1,0:T(8,128)(2,1)S(1)}, bf16[128,1024]{1,0:T(8,128)(2,1)S(1)}, u32[]{:S(2)}, u32[]{:S(2)}) collective-permute-start(bf16[128,1024]{1,0:T(8,128)(2,1)S(1)} %get-tuple-element.81), channel_id=1, source_target_pairs={{0,1},{1,0},{2,3},{3,2},{4,5},{5,4},{6,7},{7,6},{8,9},{9,8},{10,11... | collective-permute-start | bytes 786440 | tf_op jit(solution)/shard_map/ppermute | solution.py:488
  61.1 4.7 %collective-permute-start.24 = (bf16[128,1024]{1,0:T(8,128)(2,1)S(1)}, bf16[128,1024]{1,0:T(8,128)(2,1)S(1)}, u32[]{:S(2)}, u32[]{:S(2)}) collective-permute-start(bf16[128,1024]{1,0:T(8,128)(2,1)S(1)} %get-tuple-element.95), channel_id=1, source_target_pairs={{0,1},{1,0},{2,3},{3,2},{4,5},{5,4},{6,7},{7,6},{8,9},{9,8},{10,11... | collective-permute-start | bytes 786440 | tf_op jit(solution)/shard_map/ppermute | solution.py:488
  66.7 4.8 %collective-permute-start.19 = (bf16[128,1024]{1,0:T(8,128)(2,1)S(1)}, bf16[128,1024]{1,0:T(8,128)(2,1)S(1)}, u32[]{:S(2)}, u32[]{:S(2)}) collective-permute-start(bf16[128,1024]{1,0:T(8,128)(2,1)S(1)} %get-tuple-element.91), channel_id=1, source_target_pairs={{0,1},{1,0},{2,3},{3,2},{4,5},{5,4},{6,7},{7,6},{8,9},{9,8},{10,11... | collective-permute-start | bytes 786440 | tf_op jit(solution)/shard_map/ppermute | solution.py:488
  72.3 4.8 %collective-permute-start.14 = (bf16[128,1024]{1,0:T(8,128)(2,1)S(1)}, bf16[128,1024]{1,0:T(8,128)(2,1)S(1)}, u32[]{:S(2)}, u32[]{:S(2)}) collective-permute-start(bf16[128,1024]{1,0:T(8,128)(2,1)S(1)} %get-tuple-element.87), channel_id=1, source_target_pairs={{0,1},{1,0},{2,3},{3,2},{4,5},{5,4},{6,7},{7,6},{8,9},{9,8},{10,11... | collective-permute-start | bytes 786440 | tf_op jit(solution)/shard_map/ppermute | solution.py:488
  78.6 4.1 %collective-permute-done.19.even_ref = bf16[128,1024]{1,0:T(8,128)(2,1)S(1)} collective-permute-done((bf16[128,1024]{1,0:T(8,128)(2,1)S(1)}, bf16[128,1024]{1,0:T(8,128)(2,1)S(1)}, u32[]{:S(2)}, u32[]{:S(2)}) %collective-permute-start.19) | collective-permute-done | bytes 262176 | tf_op jit(solution)/shard_map/ppermute | solution.py:488
  82.7 2.3 %collective-permute-start.9 = (bf16[128,1024]{1,0:T(8,128)(2,1)S(1)}, bf16[128,1024]{1,0:T(8,128)(2,1)S(1)}, u32[]{:S(2)}, u32[]{:S(2)}) collective-permute-start(bf16[128,1024]{1,0:T(8,128)(2,1)S(1)} %get-tuple-element.83), channel_id=1, source_target_pairs={{0,1},{1,0},{2,3},{3,2},{4,5},{5,4},{6,7},{7,6},{8,9},{9,8},{10,11... | collective-permute-start | bytes 786440 | tf_op jit(solution)/shard_map/ppermute | solution.py:488
  86.6 1.7 %collective-permute-done.14.even_ref = bf16[128,1024]{1,0:T(8,128)(2,1)S(1)} collective-permute-done((bf16[128,1024]{1,0:T(8,128)(2,1)S(1)}, bf16[128,1024]{1,0:T(8,128)(2,1)S(1)}, u32[]{:S(2)}, u32[]{:S(2)}) %collective-permute-start.14) | collective-permute-done | bytes 262176 | tf_op jit(solution)/shard_map/ppermute | solution.py:488
  89.1 4.3 %collective-permute-done.9.even_ref = bf16[128,1024]{1,0:T(8,128)(2,1)S(1)} collective-permute-done((bf16[128,1024]{1,0:T(8,128)(2,1)S(1)}, bf16[128,1024]{1,0:T(8,128)(2,1)S(1)}, u32[]{:S(2)}, u32[]{:S(2)}) %collective-permute-start.9) | collective-permute-done | bytes 262176 | tf_op jit(solution)/shard_map/ppermute | solution.py:488
  (57 shorter events, 15.1 us)
Async XLA Ops:
  4.5 7.3 %collective-permute-start.1 = (bf16[528,128]{1,0:T(8,128)(2,1)S(1)}, bf16[528,128]{1,0:T(8,128)(2,1)S(1)}, u32[]{:S(2)}, u32[]{:S(2)}) collective-permute-start(bf16[528,128]{1,0:T(8,128)(2,1)S(1)} %get-tuple-element.61.total_ref), channel_id=1, source_target_pairs={{0,8},{4,12},{8,0},{12,4},{16,24},{20,28},{24,16},{28,20},{1,9},{5... | collective-permute-start | bytes 405512 | tf_op jit(solution)/shard_map/ppermute | solution.py:537
  7.4 6.8 %collective-permute-start.2 = (bf16[528,128]{1,0:T(8,128)(2,1)S(1)}, bf16[528,128]{1,0:T(8,128)(2,1)S(1)}, u32[]{:S(2)}, u32[]{:S(2)}) collective-permute-start(bf16[528,128]{1,0:T(8,128)(2,1)S(1)} %get-tuple-element.59.after_ref.total_ref), channel_id=1, source_target_pairs={{0,8},{4,12},{8,0},{12,4},{16,24},{20,28},{24,16},{28,20},{1,9},{5... | collective-permute-start | bytes 405512 | tf_op jit(solution)/shard_map/ppermute | solution.py:537
  12.0 8.2 %collective-permute-start.3 = (bf16[528,128]{1,0:T(8,128)(2,1)S(1)}, bf16[528,128]{1,0:T(8,128)(2,1)S(1)}, u32[]{:S(2)}, u32[]{:S(2)}) collective-permute-start(bf16[528,128]{1,0:T(8,128)(2,1)S(1)} %fold.2.after_ref), channel_id=1, source_target_pairs={{0,16},{4,20},{8,24},{12,28},{16,0},{20,4},{24,8},{28,12},{1,17},{... | collective-permute-start | bytes 405512 | tf_op jit(solution)/shard_map/ppermute | solution.py:537
  14.4 5.7 %collective-permute-start.4 = (bf16[528,128]{1,0:T(8,128)(2,1)S(1)}, bf16[528,128]{1,0:T(8,128)(2,1)S(1)}, u32[]{:S(2)}, u32[]{:S(2)}) collective-permute-start(bf16[528,128]{1,0:T(8,128)(2,1)S(1)} %fold.3.after_ref), channel_id=1, source_target_pairs={{0,16},{4,20},{8,24},{12,28},{16,0},{20,4},{24,8},{28,12},{1,17},{... | collective-permute-start | bytes 405512 | tf_op jit(solution)/shard_map/ppermute | solution.py:537
  23.0 15.6 %collective-permute-start.21 = (bf16[128,1024]{1,0:T(8,128)(2,1)S(1)}, bf16[128,1024]{1,0:T(8,128)(2,1)S(1)}, u32[]{:S(2)}, u32[]{:S(2)}) collective-permute-start(bf16[128,1024]{1,0:T(8,128)(2,1)S(1)} %get-tuple-element.79.refs_0_), channel_id=1, source_target_pairs={{0,1},{1,0},{2,3},{3,2},{4,5},{5,4},{6,7},{7,6},{8,9},{9,8},{10,11... | collective-permute-start | bytes 786440 | tf_op jit(solution)/shard_map/ppermute | solution.py:483
  25.7 15.7 %collective-permute-start.16 = (bf16[128,1024]{1,0:T(8,128)(2,1)S(1)}, bf16[128,1024]{1,0:T(8,128)(2,1)S(1)}, u32[]{:S(2)}, u32[]{:S(2)}) collective-permute-start(bf16[128,1024]{1,0:T(8,128)(2,1)S(1)} %first_block_rest.3.refs_1_), channel_id=1, source_target_pairs={{0,1},{1,0},{2,3},{3,2},{4,5},{5,4},{6,7},{7,6},{8,9},{9,8},{10,11... | collective-permute-start | bytes 786440 | tf_op jit(solution)/shard_map/ppermute | solution.py:483
  27.2 18.8 %collective-permute-start.11 = (bf16[128,1024]{1,0:T(8,128)(2,1)S(1)}, bf16[128,1024]{1,0:T(8,128)(2,1)S(1)}, u32[]{:S(2)}, u32[]{:S(2)}) collective-permute-start(bf16[128,1024]{1,0:T(8,128)(2,1)S(1)} %get-tuple-element.80.refs_2_), channel_id=1, source_target_pairs={{0,1},{1,0},{2,3},{3,2},{4,5},{5,4},{6,7},{7,6},{8,9},{9,8},{10,11... | collective-permute-start | bytes 786440 | tf_op jit(solution)/shard_map/ppermute | solution.py:483
  29.2 19.8 %collective-permute-start.6 = (bf16[128,1024]{1,0:T(8,128)(2,1)S(1)}, bf16[128,1024]{1,0:T(8,128)(2,1)S(1)}, u32[]{:S(2)}, u32[]{:S(2)}) collective-permute-start(bf16[128,1024]{1,0:T(8,128)(2,1)S(1)} %get-tuple-element.78.refs_3_), channel_id=1, source_target_pairs={{0,1},{1,0},{2,3},{3,2},{4,5},{5,4},{6,7},{7,6},{8,9},{9,8},{10,11... | collective-permute-start | bytes 786440 | tf_op jit(solution)/shard_map/ppermute | solution.py:483
  38.7 15.9 %collective-permute-start.22 = (bf16[128,1024]{1,0:T(8,128)(2,1)S(1)}, bf16[128,1024]{1,0:T(8,128)(2,1)S(1)}, u32[]{:S(2)}, u32[]{:S(2)}) collective-permute-start(bf16[128,1024]{1,0:T(8,128)(2,1)S(1)} %get-tuple-element.93), channel_id=1, source_target_pairs={{0,1},{1,0},{2,3},{3,2},{4,5},{5,4},{6,7},{7,6},{8,9},{9,8},{10,11... | collective-permute-start | bytes 786440 | tf_op jit(solution)/shard_map/ppermute | solution.py:488
  40.7 14.7 %collective-permute-start.23 = (bf16[128,1024]{1,0:T(8,128)(2,1)S(1)}, bf16[128,1024]{1,0:T(8,128)(2,1)S(1)}, u32[]{:S(2)}, u32[]{:S(2)}) collective-permute-start(bf16[128,1024]{1,0:T(8,128)(2,1)S(1)} %get-tuple-element.94), channel_id=1, source_target_pairs={{1,2},{2,1},{5,6},{6,5},{9,10},{10,9},{13,14},{14,13},{17,18},{18,... | collective-permute-start | bytes 786440 | tf_op jit(solution)/shard_map/ppermute | solution.py:488
  41.5 18.9 %collective-permute-start.17 = (bf16[128,1024]{1,0:T(8,128)(2,1)S(1)}, bf16[128,1024]{1,0:T(8,128)(2,1)S(1)}, u32[]{:S(2)}, u32[]{:S(2)}) collective-permute-start(bf16[128,1024]{1,0:T(8,128)(2,1)S(1)} %get-tuple-element.89), channel_id=1, source_target_pairs={{0,1},{1,0},{2,3},{3,2},{4,5},{5,4},{6,7},{7,6},{8,9},{9,8},{10,11... | collective-permute-start | bytes 786440 | tf_op jit(solution)/shard_map/ppermute | solution.py:488
  46.0 15.1 %collective-permute-start.18 = (bf16[128,1024]{1,0:T(8,128)(2,1)S(1)}, bf16[128,1024]{1,0:T(8,128)(2,1)S(1)}, u32[]{:S(2)}, u32[]{:S(2)}) collective-permute-start(bf16[128,1024]{1,0:T(8,128)(2,1)S(1)} %get-tuple-element.90), channel_id=1, source_target_pairs={{1,2},{2,1},{5,6},{6,5},{9,10},{10,9},{13,14},{14,13},{17,18},{18,... | collective-permute-start | bytes 786440 | tf_op jit(solution)/shard_map/ppermute | solution.py:488
  49.0 16.9 %collective-permute-start.12 = (bf16[128,1024]{1,0:T(8,128)(2,1)S(1)}, bf16[128,1024]{1,0:T(8,128)(2,1)S(1)}, u32[]{:S(2)}, u32[]{:S(2)}) collective-permute-start(bf16[128,1024]{1,0:T(8,128)(2,1)S(1)} %get-tuple-element.85), channel_id=1, source_target_pairs={{0,1},{1,0},{2,3},{3,2},{4,5},{5,4},{6,7},{7,6},{8,9},{9,8},{10,11... | collective-permute-start | bytes 786440 | tf_op jit(solution)/shard_map/ppermute | solution.py:488
  54.6 12.0 %collective-permute-start.13 = (bf16[128,1024]{1,0:T(8,128)(2,1)S(1)}, bf16[128,1024]{1,0:T(8,128)(2,1)S(1)}, u32[]{:S(2)}, u32[]{:S(2)}) collective-permute-start(bf16[128,1024]{1,0:T(8,128)(2,1)S(1)} %get-tuple-element.86), channel_id=1, source_target_pairs={{1,2},{2,1},{5,6},{6,5},{9,10},{10,9},{13,14},{14,13},{17,18},{18,... | collective-permute-start | bytes 786440 | tf_op jit(solution)/shard_map/ppermute | solution.py:488
  55.4 16.1 %collective-permute-start.7 = (bf16[128,1024]{1,0:T(8,128)(2,1)S(1)}, bf16[128,1024]{1,0:T(8,128)(2,1)S(1)}, u32[]{:S(2)}, u32[]{:S(2)}) collective-permute-start(bf16[128,1024]{1,0:T(8,128)(2,1)S(1)} %get-tuple-element.81), channel_id=1, source_target_pairs={{0,1},{1,0},{2,3},{3,2},{4,5},{5,4},{6,7},{7,6},{8,9},{9,8},{10,11... | collective-permute-start | bytes 786440 | tf_op jit(solution)/shard_map/ppermute | solution.py:488
  60.4 11.8 %collective-permute-start.8 = (bf16[128,1024]{1,0:T(8,128)(2,1)S(1)}, bf16[128,1024]{1,0:T(8,128)(2,1)S(1)}, u32[]{:S(2)}, u32[]{:S(2)}) collective-permute-start(bf16[128,1024]{1,0:T(8,128)(2,1)S(1)} %get-tuple-element.82), channel_id=1, source_target_pairs={{1,2},{2,1},{5,6},{6,5},{9,10},{10,9},{13,14},{14,13},{17,18},{18,... | collective-permute-start | bytes 786440 | tf_op jit(solution)/shard_map/ppermute | solution.py:488
  61.1 16.1 %collective-permute-start.24 = (bf16[128,1024]{1,0:T(8,128)(2,1)S(1)}, bf16[128,1024]{1,0:T(8,128)(2,1)S(1)}, u32[]{:S(2)}, u32[]{:S(2)}) collective-permute-start(bf16[128,1024]{1,0:T(8,128)(2,1)S(1)} %get-tuple-element.95), channel_id=1, source_target_pairs={{0,1},{1,0},{2,3},{3,2},{4,5},{5,4},{6,7},{7,6},{8,9},{9,8},{10,11... | collective-permute-start | bytes 786440 | tf_op jit(solution)/shard_map/ppermute | solution.py:488
  66.0 11.9 %collective-permute-start.25 = (bf16[128,1024]{1,0:T(8,128)(2,1)S(1)}, bf16[128,1024]{1,0:T(8,128)(2,1)S(1)}, u32[]{:S(2)}, u32[]{:S(2)}) collective-permute-start(bf16[128,1024]{1,0:T(8,128)(2,1)S(1)} %get-tuple-element.96), channel_id=1, source_target_pairs={{1,2},{2,1},{5,6},{6,5},{9,10},{10,9},{13,14},{14,13},{17,18},{18,... | collective-permute-start | bytes 786440 | tf_op jit(solution)/shard_map/ppermute | solution.py:488
  66.7 16.1 %collective-permute-start.19 = (bf16[128,1024]{1,0:T(8,128)(2,1)S(1)}, bf16[128,1024]{1,0:T(8,128)(2,1)S(1)}, u32[]{:S(2)}, u32[]{:S(2)}) collective-permute-start(bf16[128,1024]{1,0:T(8,128)(2,1)S(1)} %get-tuple-element.91), channel_id=1, source_target_pairs={{0,1},{1,0},{2,3},{3,2},{4,5},{5,4},{6,7},{7,6},{8,9},{9,8},{10,11... | collective-permute-start | bytes 786440 | tf_op jit(solution)/shard_map/ppermute | solution.py:488
  71.6 14.2 %collective-permute-start.20 = (bf16[128,1024]{1,0:T(8,128)(2,1)S(1)}, bf16[128,1024]{1,0:T(8,128)(2,1)S(1)}, u32[]{:S(2)}, u32[]{:S(2)}) collective-permute-start(bf16[128,1024]{1,0:T(8,128)(2,1)S(1)} %get-tuple-element.92), channel_id=1, source_target_pairs={{1,2},{2,1},{5,6},{6,5},{9,10},{10,9},{13,14},{14,13},{17,18},{18,... | collective-permute-start | bytes 786440 | tf_op jit(solution)/shard_map/ppermute | solution.py:488
  72.3 16.1 %collective-permute-start.14 = (bf16[128,1024]{1,0:T(8,128)(2,1)S(1)}, bf16[128,1024]{1,0:T(8,128)(2,1)S(1)}, u32[]{:S(2)}, u32[]{:S(2)}) collective-permute-start(bf16[128,1024]{1,0:T(8,128)(2,1)S(1)} %get-tuple-element.87), channel_id=1, source_target_pairs={{0,1},{1,0},{2,3},{3,2},{4,5},{5,4},{6,7},{7,6},{8,9},{9,8},{10,11... | collective-permute-start | bytes 786440 | tf_op jit(solution)/shard_map/ppermute | solution.py:488
  77.2 11.1 %collective-permute-start.15 = (bf16[128,1024]{1,0:T(8,128)(2,1)S(1)}, bf16[128,1024]{1,0:T(8,128)(2,1)S(1)}, u32[]{:S(2)}, u32[]{:S(2)}) collective-permute-start(bf16[128,1024]{1,0:T(8,128)(2,1)S(1)} %get-tuple-element.88), channel_id=1, source_target_pairs={{1,2},{2,1},{5,6},{6,5},{9,10},{10,9},{13,14},{14,13},{17,18},{18,... | collective-permute-start | bytes 786440 | tf_op jit(solution)/shard_map/ppermute | solution.py:488
  77.9 11.2 %collective-permute-start.10 = (bf16[128,1024]{1,0:T(8,128)(2,1)S(1)}, bf16[128,1024]{1,0:T(8,128)(2,1)S(1)}, u32[]{:S(2)}, u32[]{:S(2)}) collective-permute-start(bf16[128,1024]{1,0:T(8,128)(2,1)S(1)} %get-tuple-element.84), channel_id=1, source_target_pairs={{1,2},{2,1},{5,6},{6,5},{9,10},{10,9},{13,14},{14,13},{17,18},{18,... | collective-permute-start | bytes 786440 | tf_op jit(solution)/shard_map/ppermute | solution.py:488
  82.7 10.7 %collective-permute-start.9 = (bf16[128,1024]{1,0:T(8,128)(2,1)S(1)}, bf16[128,1024]{1,0:T(8,128)(2,1)S(1)}, u32[]{:S(2)}, u32[]{:S(2)}) collective-permute-start(bf16[128,1024]{1,0:T(8,128)(2,1)S(1)} %get-tuple-element.83), channel_id=1, source_target_pairs={{0,1},{1,0},{2,3},{3,2},{4,5},{5,4},{6,7},{7,6},{8,9},{9,8},{10,11... | collective-permute-start | bytes 786440 | tf_op jit(solution)/shard_map/ppermute | solution.py:488
  (4 other events, 15.3 us)

commit v10 on v9

--- a/solution.py
+++ b/solution.py
@@ -15,7 +15,7 @@
 COLUMN_TILE = 512
 PARTS = 4
 WEIGHT_COPIES = 8
-SUM_COPIES = 4
+SUM_COPIES = 2
 PIECES = 2
 F32 = jnp.float32
 BF16 = jnp.bfloat16
@@ -38,6 +38,16 @@
 def by_row(values):
     high = values.astype(BF16).astype(F32)
     return jnp.transpose(jnp.concatenate([padded(high), padded(values - high)], axis=0)).astype(BF16)
+
+
+def by_lane(values):
+    return jnp.transpose(jnp.concatenate([values, jnp.zeros((128 - values.shape[0], values.shape[1]), F32)], axis=0))
+
+
+def spread_heads(values, first, heads):
+    lane = lax.broadcasted_iota(jnp.int32, values.shape, 1) >> 6
+    pairs = range(first, first + heads, 2)
+    return jnp.concatenate([jnp.take_along_axis(values, lane + pair, axis=1) for pair in pairs], axis=1)
 
 
 def pieces(values, axis):
@@ -239,24 +249,20 @@
         middle, total = running[:, MIDDLE : MIDDLE + 1], running[:, CHUNK - 1 :]
         inner = running - middle
         factors = jnp.exp(jnp.where(lane == 0, total, jnp.where(lane == 1, total - middle, middle)))
-        factors = jnp.concatenate(
-            [
-                by_row(step_ref[:, here] * jnp.exp(-inner)),
-                by_row(jnp.exp(inner)),
-                by_row(jnp.exp(before + running)),
-                by_row(factors)[:EXTRA],
-            ],
-            axis=0,
-        )
+        weights_by_lane = by_lane(step_ref[:, here] * jnp.exp(-inner))
+        inner_by_lane = by_lane(jnp.exp(inner))
+        outer_by_lane = by_lane(jnp.exp(before + running))
+        factors = by_row(factors)[:EXTRA]
         before = before + total
         gates[n - mine[0]].wait()
         for g in range(groups):
             cut = slice(g * width, (g + 1) * width)
             part = slice(g * STATE, (g + 1) * STATE)
-            wide = dot(factors, spread_ref[:, cut])
-            to_state, to_fresh, to_middle = (wide[3 * CHUNK + n : 3 * CHUNK + n + 1] for n in range(3))
+            ends = dot(factors, spread_ref[:, cut])
+            to_state, to_fresh, to_middle = (ends[n : n + 1] for n in range(3))
+            its_heads = (g * heads // groups, heads // groups)
             x = x_ref[here, cut].astype(F32)
-            weighted = (x * wide[:CHUNK]).astype(BF16)
+            weighted = (x * spread_heads(weights_by_lane, *its_heads)).astype(BF16)
             started = jnp.concatenate([weighted, (state[g] * to_middle).astype(BF16)], axis=0)
             scores = lax.dot_general(
                 c_ref[here, part], b_ref[here, part], (((1,), (1,)), ((), ())), preferred_element_type=F32
@@ -270,8 +276,8 @@
                 state[g] = state[g] * to_state + fresh * to_fresh
             gate = gate_ref[rows_of(n - mine[0]), cut].astype(F32)
             gate = gate * (0.5 * jnp.tanh(0.5 * gate) + 0.5)
-            mixed_ref[here, cut] = (within * wide[CHUNK : 2 * CHUNK] + x * skip[:, cut]) * gate
-            scale_ref[here, cut] = wide[2 * CHUNK : 3 * CHUNK] * gate
+            mixed_ref[here, cut] = (within * spread_heads(inner_by_lane, *its_heads) + x * skip[:, cut]) * gate
+            scale_ref[here, cut] = spread_heads(outer_by_lane, *its_heads) * gate
     before_ref[...] = jnp.broadcast_to(before, before_ref.shape)
     for g in range(groups):
         state_ref[:, rows_of(g, width)] = state[g]

time: 94.6 us -> 94.6 us (level)
  starting transfers between devices: 47 us -> 45.6 us
  waiting for transfers between devices: 17.5 us -> 18.5 us
    ppermute x8, starting transfers between devices: 29.8 us -> 28.5 us  [line_reduce(): lax.ppermute(even, 'tp', even_edges)]
  transfers between devices with their start and end apart: 26 -> 26, of which waited for: 8 -> 12; matrix products, arithmetic and copies ran while one was open for 0% -> 0% of each run, Pallas kernels for 26% -> 26%
where the time goes in v10:
time: 94.6 us; the launch traced here: 94.3 us
  starting transfers between devices  45.6 us (48%)
  Pallas kernels  29.6 us (31%)
  waiting for transfers between devices  18.5 us (20%)
    pallas_call x25, Pallas kernels, in_vmem(): pl.pallas_call(kernel, in_specs=specs, out_specs=[pl.BlockSpec(memory_spa...  29.6 us
    ppermute x8, starting transfers between devices, line_reduce(): lax.ppermute(even, 'tp', even_edges)  28.5 us
    ppermute x8, waiting for transfers between devices, line_reduce(): lax.ppermute(even, 'tp', even_edges)  14.7 us
    ppermute x4, starting transfers between devices, swap_chips(): lax.ppermute(v, 'ctx', [(i, i ^ 2 << level) for i in range(devices)])  6.98 us
    ppermute x8, starting transfers between devices, line_reduce(): lax.ppermute(odd, 'tp', odd_edges)  5.34 us
    ppermute x4, starting transfers between devices, line_reduce(): arrived[half] = (lax.ppermute(first[half], 'tp', even_edges),)  4.25 us
    ppermute x4, waiting for transfers between devices, line_reduce(): arrived[half] = (lax.ppermute(first[half], 'tp', even_edges),)  2.52 us
  transfers between devices with their start and end apart: 26, of which 12 were waited for; matrix products, arithmetic and copies ran while one was open for 0% of the time, Pallas kernels for 26%

profile of v10, /device:TPU:0, one launch (start us, length us, event | category | flops | bytes accessed | tf_op | source)
XLA Modules:
  0.0 94.3 jit_solution(7482260523561417468)
XLA Ops:
  0.0 2.5 %end_state_sent.1 = (bf16[1040,128]{1,0:T(8,128)(2,1)S(1)}, bf16[512,2048]{1,0:T(8,128)(2,1)S(1)}, bf16[512,256]{1,0:T(8,128)(2,1)S(1)}, f32[32,512]{1,0:T(8,128...) custom-call(s32[1]{0:T(128)} %bitcast.1.ctx_ref, s32[1]{0:T(128)} %bitcast.here_ref, ...), custom_call_target="tpu_custom_call" | custom-call | flops 1 | bytes 1 | tf_op jit(solution)/shard_map/end_state_sent/pallas_call | solution.py:466
  3.1 1.0 %end_state_kept.1 = (bf16[1040,128]{1,0:T(8,128)(2,1)S(1)}, bf16[128,2048]{1,0:T(8,128)(2,1)S(1)}) custom-call(s32[1]{0:T(128)} %bitcast.1.ctx_ref, bf16[512,2048]{1,0:T(8,128)(2,1)S(1)} %get-tuple-element.51.x_ref, bf16[512,256]{1,0:T(8,128)(2,1)S(1)} %get-tuple-element.52.b_ref, f32[32,512]{1,0:T(8,128)S(1)} %get-tuple-element.53.step_ref, ...), custom_call_target="tpu_custom_call" | custom-call | flops 1000000000 | bytes 1 | tf_op jit(solution)/shard_map/end_state_kept/pallas_call | solution.py:466
  4.5 2.9 %collective-permute-start.1 = (bf16[528,128]{1,0:T(8,128)(2,1)S(1)}, bf16[528,128]{1,0:T(8,128)(2,1)S(1)}, u32[]{:S(2)}, u32[]{:S(2)}) collective-permute-start(bf16[528,128]{1,0:T(8,128)(2,1)S(1)} %get-tuple-element.61.total_ref), channel_id=1, source_target_pairs={{0,8},{4,12},{8,0},{12,4},{16,24},{20,28},{24,16},{28,20},{1,9},{5... | collective-permute-start | bytes 405512 | tf_op jit(solution)/shard_map/ppermute | solution.py:543
  7.5 4.0 %local_part.2 = (f32[512,2048]{1,0:T(8,128)S(1)}, f32[512,2048]{1,0:T(8,128)S(1)}, bf16[512,256]{1,0:T(8,128)(2,1)S(1)}, f32[128,2048]{1,0:T(8,128)S(1)}, f32[32...) custom-call(bf16[512,2048]{1,0:T(8,128)(2,1)} %gate_hbm.3, bf16[512,256]{1,0:T(8,128)(2,1)} %c_hbm.3, ...), custom_call_target="tpu_custom_call" | custom-call | flops 4000000000 | bytes 1 | tf_op jit(solution)/shard_map/local_part/pallas_call | solution.py:466
  12.0 2.2 %collective-permute-start.3 = (bf16[528,128]{1,0:T(8,128)(2,1)S(1)}, bf16[528,128]{1,0:T(8,128)(2,1)S(1)}, u32[]{:S(2)}, u32[]{:S(2)}) collective-permute-start(bf16[528,128]{1,0:T(8,128)(2,1)S(1)} %fold.2.after_ref), channel_id=1, source_target_pairs={{0,16},{4,20},{8,24},{12,28},{16,0},{20,4},{24,8},{28,12},{1,17},{... | collective-permute-start | bytes 405512 | tf_op jit(solution)/shard_map/ppermute | solution.py:543
  14.4 1.8 %collective-permute-start.4 = (bf16[528,128]{1,0:T(8,128)(2,1)S(1)}, bf16[528,128]{1,0:T(8,128)(2,1)S(1)}, u32[]{:S(2)}, u32[]{:S(2)}) collective-permute-start(bf16[528,128]{1,0:T(8,128)(2,1)S(1)} %fold.3.after_ref), channel_id=1, source_target_pairs={{0,16},{4,20},{8,24},{12,28},{16,0},{20,4},{24,8},{28,12},{1,17},{... | collective-permute-start | bytes 405512 | tf_op jit(solution)/shard_map/ppermute | solution.py:543
  16.3 4.1 %local_part.3 = (f32[512,2048]{1,0:T(8,128)S(1)}, f32[512,2048]{1,0:T(8,128)S(1)}, bf16[512,256]{1,0:T(8,128)(2,1)S(1)}, f32[128,2048]{1,0:T(8,128)S(1)}, f32[32...) custom-call(bf16[512,2048]{1,0:T(8,128)(2,1)} %gate_hbm.3, ...), custom_call_target="tpu_custom_call", output_to_operand_aliasing={{0}: (10, {}), {1}: (11, {}), {2}: (12, {}), {3}: (13, {}),... | custom-call | flops 4000000000 | bytes 1 | tf_op jit(solution)/shard_map/local_part/pallas_call | solution.py:466
  23.2 1.8 %collective-permute-start.21 = (bf16[128,1024]{1,0:T(8,128)(2,1)S(1)}, bf16[128,1024]{1,0:T(8,128)(2,1)S(1)}, u32[]{:S(2)}, u32[]{:S(2)}) collective-permute-start(bf16[128,1024]{1,0:T(8,128)(2,1)S(1)} %get-tuple-element.79.refs_0_), channel_id=1, source_target_pairs={{0,1},{1,0},{2,3},{3,2},{4,5},{5,4},{6,7},{7,6},{8,9},{9,8},{10,11... | collective-permute-start | bytes 786440 | tf_op jit(solution)/shard_map/ppermute | solution.py:489
  26.1 1.3 %first_block_rest.2 = (bf16[128,1024]{1,0:T(8,128)(2,1)S(1)}, bf16[128,1024]{1,0:T(8,128)(2,1)S(1)}) custom-call(bf16[128,2048]{1,0:T(8,128)(2,1)S(1)} %get-tuple-element.76.normed_ref, bf16[2048,2048]{1,0:T(8,128)(2,1)S(1)} %get-tuple-element.77.w_ref.wb_ref), custom_call_target="tpu_custom_call" | custom-call | flops 1 | bytes 1 | tf_op jit(solution)/shard_map/first_block_rest/pallas_call | solution.py:466
  27.4 1.8 %collective-permute-start.11 = (bf16[128,1024]{1,0:T(8,128)(2,1)S(1)}, bf16[128,1024]{1,0:T(8,128)(2,1)S(1)}, u32[]{:S(2)}, u32[]{:S(2)}) collective-permute-start(bf16[128,1024]{1,0:T(8,128)(2,1)S(1)} %get-tuple-element.80.refs_2_), channel_id=1, source_target_pairs={{0,1},{1,0},{2,3},{3,2},{4,5},{5,4},{6,7},{7,6},{8,9},{9,8},{10,11... | collective-permute-start | bytes 786440 | tf_op jit(solution)/shard_map/ppermute | solution.py:489
  29.5 9.3 %other_blocks.1.refs_1_.refs_2_.sums_ref = bf16[512,4096]{1,0:T(8,128)(2,1)S(1)} custom-call(s32[1]{0:T(128)} %bitcast.1.ctx_ref, s32[1]{0:T(128)} %bitcast.here_ref, f32[512,2048]{1,0:T(8,128)S(1)} %get-tuple-element.67.mixed_ref, f32[512,2048]{1,0:T(8,128)S(1)} %get-tuple-element.68.scale_ref, bf16[512,256]{1,0:T(8,128)(2,1)S(1)} %get-tuple-element.69.c_ref, ...), custom_call_target="tpu_custom_call" | custom-call | flops 1 | bytes 1 | tf_op jit(solution)/shard_map/other_blocks/pallas_call | solution.py:466
  39.0 1.8 %collective-permute-start.22 = (bf16[128,1024]{1,0:T(8,128)(2,1)S(1)}, bf16[128,1024]{1,0:T(8,128)(2,1)S(1)}, u32[]{:S(2)}, u32[]{:S(2)}) collective-permute-start(bf16[128,1024]{1,0:T(8,128)(2,1)S(1)} %get-tuple-element.93), channel_id=1, source_target_pairs={{0,1},{1,0},{2,3},{3,2},{4,5},{5,4},{6,7},{7,6},{8,9},{9,8},{10,11... | collective-permute-start | bytes 786440 | tf_op jit(solution)/shard_map/ppermute | solution.py:494
  41.5 4.4 %collective-permute-start.17 = (bf16[128,1024]{1,0:T(8,128)(2,1)S(1)}, bf16[128,1024]{1,0:T(8,128)(2,1)S(1)}, u32[]{:S(2)}, u32[]{:S(2)}) collective-permute-start(bf16[128,1024]{1,0:T(8,128)(2,1)S(1)} %get-tuple-element.89), channel_id=1, source_target_pairs={{0,1},{1,0},{2,3},{3,2},{4,5},{5,4},{6,7},{7,6},{8,9},{9,8},{10,11... | collective-permute-start | bytes 786440 | tf_op jit(solution)/shard_map/ppermute | solution.py:494
  46.8 2.5 %collective-permute-done.6.refs_0_ = bf16[128,1024]{1,0:T(8,128)(2,1)S(1)} collective-permute-done((bf16[128,1024]{1,0:T(8,128)(2,1)S(1)}, bf16[128,1024]{1,0:T(8,128)(2,1)S(1)}, u32[]{:S(2)}, u32[]{:S(2)}) %collective-permute-start.6) | collective-permute-done | bytes 262176 | tf_op jit(solution)/shard_map/ppermute | solution.py:489
  49.3 1.7 %collective-permute-start.12 = (bf16[128,1024]{1,0:T(8,128)(2,1)S(1)}, bf16[128,1024]{1,0:T(8,128)(2,1)S(1)}, u32[]{:S(2)}, u32[]{:S(2)}) collective-permute-start(bf16[128,1024]{1,0:T(8,128)(2,1)S(1)} %get-tuple-element.85), channel_id=1, source_target_pairs={{0,1},{1,0},{2,3},{3,2},{4,5},{5,4},{6,7},{7,6},{8,9},{9,8},{10,11... | collective-permute-start | bytes 786440 | tf_op jit(solution)/shard_map/ppermute | solution.py:494
  51.0 3.9 %collective-permute-done.22.refs_0_ = bf16[128,1024]{1,0:T(8,128)(2,1)S(1)} collective-permute-done((bf16[128,1024]{1,0:T(8,128)(2,1)S(1)}, bf16[128,1024]{1,0:T(8,128)(2,1)S(1)}, u32[]{:S(2)}, u32[]{:S(2)}) %collective-permute-start.22) | collective-permute-done | bytes 262176 | tf_op jit(solution)/shard_map/ppermute | solution.py:494
  55.7 4.6 %collective-permute-start.7 = (bf16[128,1024]{1,0:T(8,128)(2,1)S(1)}, bf16[128,1024]{1,0:T(8,128)(2,1)S(1)}, u32[]{:S(2)}, u32[]{:S(2)}) collective-permute-start(bf16[128,1024]{1,0:T(8,128)(2,1)S(1)} %get-tuple-element.81), channel_id=1, source_target_pairs={{0,1},{1,0},{2,3},{3,2},{4,5},{5,4},{6,7},{7,6},{8,9},{9,8},{10,11... | collective-permute-start | bytes 786440 | tf_op jit(solution)/shard_map/ppermute | solution.py:494
  61.2 4.6 %collective-permute-start.24 = (bf16[128,1024]{1,0:T(8,128)(2,1)S(1)}, bf16[128,1024]{1,0:T(8,128)(2,1)S(1)}, u32[]{:S(2)}, u32[]{:S(2)}) collective-permute-start(bf16[128,1024]{1,0:T(8,128)(2,1)S(1)} %get-tuple-element.95), channel_id=1, source_target_pairs={{0,1},{1,0},{2,3},{3,2},{4,5},{5,4},{6,7},{7,6},{8,9},{9,8},{10,11... | collective-permute-start | bytes 786440 | tf_op jit(solution)/shard_map/ppermute | solution.py:494
  66.8 4.6 %collective-permute-start.19 = (bf16[128,1024]{1,0:T(8,128)(2,1)S(1)}, bf16[128,1024]{1,0:T(8,128)(2,1)S(1)}, u32[]{:S(2)}, u32[]{:S(2)}) collective-permute-start(bf16[128,1024]{1,0:T(8,128)(2,1)S(1)} %get-tuple-element.91), channel_id=1, source_target_pairs={{0,1},{1,0},{2,3},{3,2},{4,5},{5,4},{6,7},{7,6},{8,9},{9,8},{10,11... | collective-permute-start | bytes 786440 | tf_op jit(solution)/shard_map/ppermute | solution.py:494
  72.4 4.6 %collective-permute-start.14 = (bf16[128,1024]{1,0:T(8,128)(2,1)S(1)}, bf16[128,1024]{1,0:T(8,128)(2,1)S(1)}, u32[]{:S(2)}, u32[]{:S(2)}) collective-permute-start(bf16[128,1024]{1,0:T(8,128)(2,1)S(1)} %get-tuple-element.87), channel_id=1, source_target_pairs={{0,1},{1,0},{2,3},{3,2},{4,5},{5,4},{6,7},{7,6},{8,9},{9,8},{10,11... | collective-permute-start | bytes 786440 | tf_op jit(solution)/shard_map/ppermute | solution.py:494
  78.7 4.2 %collective-permute-done.19.even_ref = bf16[128,1024]{1,0:T(8,128)(2,1)S(1)} collective-permute-done((bf16[128,1024]{1,0:T(8,128)(2,1)S(1)}, bf16[128,1024]{1,0:T(8,128)(2,1)S(1)}, u32[]{:S(2)}, u32[]{:S(2)}) %collective-permute-start.19) | collective-permute-done | bytes 262176 | tf_op jit(solution)/shard_map/ppermute | solution.py:494
  83.0 2.1 %collective-permute-start.9 = (bf16[128,1024]{1,0:T(8,128)(2,1)S(1)}, bf16[128,1024]{1,0:T(8,128)(2,1)S(1)}, u32[]{:S(2)}, u32[]{:S(2)}) collective-permute-start(bf16[128,1024]{1,0:T(8,128)(2,1)S(1)} %get-tuple-element.83), channel_id=1, source_target_pairs={{0,1},{1,0},{2,3},{3,2},{4,5},{5,4},{6,7},{7,6},{8,9},{9,8},{10,11... | collective-permute-start | bytes 786440 | tf_op jit(solution)/shard_map/ppermute | solution.py:494
  86.6 2.0 %collective-permute-done.14.even_ref = bf16[128,1024]{1,0:T(8,128)(2,1)S(1)} collective-permute-done((bf16[128,1024]{1,0:T(8,128)(2,1)S(1)}, bf16[128,1024]{1,0:T(8,128)(2,1)S(1)}, u32[]{:S(2)}, u32[]{:S(2)}) %collective-permute-start.14) | collective-permute-done | bytes 262176 | tf_op jit(solution)/shard_map/ppermute | solution.py:494
  89.4 4.0 %collective-permute-done.9.even_ref = bf16[128,1024]{1,0:T(8,128)(2,1)S(1)} collective-permute-done((bf16[128,1024]{1,0:T(8,128)(2,1)S(1)}, bf16[128,1024]{1,0:T(8,128)(2,1)S(1)}, u32[]{:S(2)}, u32[]{:S(2)}) %collective-permute-start.9) | collective-permute-done | bytes 262176 | tf_op jit(solution)/shard_map/ppermute | solution.py:494
  (57 shorter events, 15.9 us)
Async XLA Ops:
  4.5 7.3 %collective-permute-start.1 = (bf16[528,128]{1,0:T(8,128)(2,1)S(1)}, bf16[528,128]{1,0:T(8,128)(2,1)S(1)}, u32[]{:S(2)}, u32[]{:S(2)}) collective-permute-start(bf16[528,128]{1,0:T(8,128)(2,1)S(1)} %get-tuple-element.61.total_ref), channel_id=1, source_target_pairs={{0,8},{4,12},{8,0},{12,4},{16,24},{20,28},{24,16},{28,20},{1,9},{5... | collective-permute-start | bytes 405512 | tf_op jit(solution)/shard_map/ppermute | solution.py:543
  7.4 6.8 %collective-permute-start.2 = (bf16[528,128]{1,0:T(8,128)(2,1)S(1)}, bf16[528,128]{1,0:T(8,128)(2,1)S(1)}, u32[]{:S(2)}, u32[]{:S(2)}) collective-permute-start(bf16[528,128]{1,0:T(8,128)(2,1)S(1)} %get-tuple-element.59.after_ref.total_ref), channel_id=1, source_target_pairs={{0,8},{4,12},{8,0},{12,4},{16,24},{20,28},{24,16},{28,20},{1,9},{5... | collective-permute-start | bytes 405512 | tf_op jit(solution)/shard_map/ppermute | solution.py:543
  12.0 8.4 %collective-permute-start.3 = (bf16[528,128]{1,0:T(8,128)(2,1)S(1)}, bf16[528,128]{1,0:T(8,128)(2,1)S(1)}, u32[]{:S(2)}, u32[]{:S(2)}) collective-permute-start(bf16[528,128]{1,0:T(8,128)(2,1)S(1)} %fold.2.after_ref), channel_id=1, source_target_pairs={{0,16},{4,20},{8,24},{12,28},{16,0},{20,4},{24,8},{28,12},{1,17},{... | collective-permute-start | bytes 405512 | tf_op jit(solution)/shard_map/ppermute | solution.py:543
  14.4 5.9 %collective-permute-start.4 = (bf16[528,128]{1,0:T(8,128)(2,1)S(1)}, bf16[528,128]{1,0:T(8,128)(2,1)S(1)}, u32[]{:S(2)}, u32[]{:S(2)}) collective-permute-start(bf16[528,128]{1,0:T(8,128)(2,1)S(1)} %fold.3.after_ref), channel_id=1, source_target_pairs={{0,16},{4,20},{8,24},{12,28},{16,0},{20,4},{24,8},{28,12},{1,17},{... | collective-permute-start | bytes 405512 | tf_op jit(solution)/shard_map/ppermute | solution.py:543
  23.2 15.6 %collective-permute-start.21 = (bf16[128,1024]{1,0:T(8,128)(2,1)S(1)}, bf16[128,1024]{1,0:T(8,128)(2,1)S(1)}, u32[]{:S(2)}, u32[]{:S(2)}) collective-permute-start(bf16[128,1024]{1,0:T(8,128)(2,1)S(1)} %get-tuple-element.79.refs_0_), channel_id=1, source_target_pairs={{0,1},{1,0},{2,3},{3,2},{4,5},{5,4},{6,7},{7,6},{8,9},{9,8},{10,11... | collective-permute-start | bytes 786440 | tf_op jit(solution)/shard_map/ppermute | solution.py:489
  25.7 15.7 %collective-permute-start.16 = (bf16[128,1024]{1,0:T(8,128)(2,1)S(1)}, bf16[128,1024]{1,0:T(8,128)(2,1)S(1)}, u32[]{:S(2)}, u32[]{:S(2)}) collective-permute-start(bf16[128,1024]{1,0:T(8,128)(2,1)S(1)} %first_block_rest.3.refs_1_), channel_id=1, source_target_pairs={{0,1},{1,0},{2,3},{3,2},{4,5},{5,4},{6,7},{7,6},{8,9},{9,8},{10,11... | collective-permute-start | bytes 786440 | tf_op jit(solution)/shard_map/ppermute | solution.py:489
  27.4 18.6 %collective-permute-start.11 = (bf16[128,1024]{1,0:T(8,128)(2,1)S(1)}, bf16[128,1024]{1,0:T(8,128)(2,1)S(1)}, u32[]{:S(2)}, u32[]{:S(2)}) collective-permute-start(bf16[128,1024]{1,0:T(8,128)(2,1)S(1)} %get-tuple-element.80.refs_2_), channel_id=1, source_target_pairs={{0,1},{1,0},{2,3},{3,2},{4,5},{5,4},{6,7},{7,6},{8,9},{9,8},{10,11... | collective-permute-start | bytes 786440 | tf_op jit(solution)/shard_map/ppermute | solution.py:489
  29.2 20.1 %collective-permute-start.6 = (bf16[128,1024]{1,0:T(8,128)(2,1)S(1)}, bf16[128,1024]{1,0:T(8,128)(2,1)S(1)}, u32[]{:S(2)}, u32[]{:S(2)}) collective-permute-start(bf16[128,1024]{1,0:T(8,128)(2,1)S(1)} %get-tuple-element.78.refs_3_), channel_id=1, source_target_pairs={{0,1},{1,0},{2,3},{3,2},{4,5},{5,4},{6,7},{7,6},{8,9},{9,8},{10,11... | collective-permute-start | bytes 786440 | tf_op jit(solution)/shard_map/ppermute | solution.py:489
  39.0 15.9 %collective-permute-start.22 = (bf16[128,1024]{1,0:T(8,128)(2,1)S(1)}, bf16[128,1024]{1,0:T(8,128)(2,1)S(1)}, u32[]{:S(2)}, u32[]{:S(2)}) collective-permute-start(bf16[128,1024]{1,0:T(8,128)(2,1)S(1)} %get-tuple-element.93), channel_id=1, source_target_pairs={{0,1},{1,0},{2,3},{3,2},{4,5},{5,4},{6,7},{7,6},{8,9},{9,8},{10,11... | collective-permute-start | bytes 786440 | tf_op jit(solution)/shard_map/ppermute | solution.py:494
  40.7 14.9 %collective-permute-start.23 = (bf16[128,1024]{1,0:T(8,128)(2,1)S(1)}, bf16[128,1024]{1,0:T(8,128)(2,1)S(1)}, u32[]{:S(2)}, u32[]{:S(2)}) collective-permute-start(bf16[128,1024]{1,0:T(8,128)(2,1)S(1)} %get-tuple-element.94), channel_id=1, source_target_pairs={{1,2},{2,1},{5,6},{6,5},{9,10},{10,9},{13,14},{14,13},{17,18},{18,... | collective-permute-start | bytes 786440 | tf_op jit(solution)/shard_map/ppermute | solution.py:494
  41.5 19.0 %collective-permute-start.17 = (bf16[128,1024]{1,0:T(8,128)(2,1)S(1)}, bf16[128,1024]{1,0:T(8,128)(2,1)S(1)}, u32[]{:S(2)}, u32[]{:S(2)}) collective-permute-start(bf16[128,1024]{1,0:T(8,128)(2,1)S(1)} %get-tuple-element.89), channel_id=1, source_target_pairs={{0,1},{1,0},{2,3},{3,2},{4,5},{5,4},{6,7},{7,6},{8,9},{9,8},{10,11... | collective-permute-start | bytes 786440 | tf_op jit(solution)/shard_map/ppermute | solution.py:494
  46.0 15.2 %collective-permute-start.18 = (bf16[128,1024]{1,0:T(8,128)(2,1)S(1)}, bf16[128,1024]{1,0:T(8,128)(2,1)S(1)}, u32[]{:S(2)}, u32[]{:S(2)}) collective-permute-start(bf16[128,1024]{1,0:T(8,128)(2,1)S(1)} %get-tuple-element.90), channel_id=1, source_target_pairs={{1,2},{2,1},{5,6},{6,5},{9,10},{10,9},{13,14},{14,13},{17,18},{18,... | collective-permute-start | bytes 786440 | tf_op jit(solution)/shard_map/ppermute | solution.py:494
  49.3 16.9 %collective-permute-start.12 = (bf16[128,1024]{1,0:T(8,128)(2,1)S(1)}, bf16[128,1024]{1,0:T(8,128)(2,1)S(1)}, u32[]{:S(2)}, u32[]{:S(2)}) collective-permute-start(bf16[128,1024]{1,0:T(8,128)(2,1)S(1)} %get-tuple-element.85), channel_id=1, source_target_pairs={{0,1},{1,0},{2,3},{3,2},{4,5},{5,4},{6,7},{7,6},{8,9},{9,8},{10,11... | collective-permute-start | bytes 786440 | tf_op jit(solution)/shard_map/ppermute | solution.py:494
  54.9 11.9 %collective-permute-start.13 = (bf16[128,1024]{1,0:T(8,128)(2,1)S(1)}, bf16[128,1024]{1,0:T(8,128)(2,1)S(1)}, u32[]{:S(2)}, u32[]{:S(2)}) collective-permute-start(bf16[128,1024]{1,0:T(8,128)(2,1)S(1)} %get-tuple-element.86), channel_id=1, source_target_pairs={{1,2},{2,1},{5,6},{6,5},{9,10},{10,9},{13,14},{14,13},{17,18},{18,... | collective-permute-start | bytes 786440 | tf_op jit(solution)/shard_map/ppermute | solution.py:494
  55.7 16.1 %collective-permute-start.7 = (bf16[128,1024]{1,0:T(8,128)(2,1)S(1)}, bf16[128,1024]{1,0:T(8,128)(2,1)S(1)}, u32[]{:S(2)}, u32[]{:S(2)}) collective-permute-start(bf16[128,1024]{1,0:T(8,128)(2,1)S(1)} %get-tuple-element.81), channel_id=1, source_target_pairs={{0,1},{1,0},{2,3},{3,2},{4,5},{5,4},{6,7},{7,6},{8,9},{9,8},{10,11... | collective-permute-start | bytes 786440 | tf_op jit(solution)/shard_map/ppermute | solution.py:494
  60.5 11.9 %collective-permute-start.8 = (bf16[128,1024]{1,0:T(8,128)(2,1)S(1)}, bf16[128,1024]{1,0:T(8,128)(2,1)S(1)}, u32[]{:S(2)}, u32[]{:S(2)}) collective-permute-start(bf16[128,1024]{1,0:T(8,128)(2,1)S(1)} %get-tuple-element.82), channel_id=1, source_target_pairs={{1,2},{2,1},{5,6},{6,5},{9,10},{10,9},{13,14},{14,13},{17,18},{18,... | collective-permute-start | bytes 786440 | tf_op jit(solution)/shard_map/ppermute | solution.py:494
  61.2 16.2 %collective-permute-start.24 = (bf16[128,1024]{1,0:T(8,128)(2,1)S(1)}, bf16[128,1024]{1,0:T(8,128)(2,1)S(1)}, u32[]{:S(2)}, u32[]{:S(2)}) collective-permute-start(bf16[128,1024]{1,0:T(8,128)(2,1)S(1)} %get-tuple-element.95), channel_id=1, source_target_pairs={{0,1},{1,0},{2,3},{3,2},{4,5},{5,4},{6,7},{7,6},{8,9},{9,8},{10,11... | collective-permute-start | bytes 786440 | tf_op jit(solution)/shard_map/ppermute | solution.py:494
  66.1 11.9 %collective-permute-start.25 = (bf16[128,1024]{1,0:T(8,128)(2,1)S(1)}, bf16[128,1024]{1,0:T(8,128)(2,1)S(1)}, u32[]{:S(2)}, u32[]{:S(2)}) collective-permute-start(bf16[128,1024]{1,0:T(8,128)(2,1)S(1)} %get-tuple-element.96), channel_id=1, source_target_pairs={{1,2},{2,1},{5,6},{6,5},{9,10},{10,9},{13,14},{14,13},{17,18},{18,... | collective-permute-start | bytes 786440 | tf_op jit(solution)/shard_map/ppermute | solution.py:494
  66.8 16.2 %collective-permute-start.19 = (bf16[128,1024]{1,0:T(8,128)(2,1)S(1)}, bf16[128,1024]{1,0:T(8,128)(2,1)S(1)}, u32[]{:S(2)}, u32[]{:S(2)}) collective-permute-start(bf16[128,1024]{1,0:T(8,128)(2,1)S(1)} %get-tuple-element.91), channel_id=1, source_target_pairs={{0,1},{1,0},{2,3},{3,2},{4,5},{5,4},{6,7},{7,6},{8,9},{9,8},{10,11... | collective-permute-start | bytes 786440 | tf_op jit(solution)/shard_map/ppermute | solution.py:494
  71.7 14.1 %collective-permute-start.20 = (bf16[128,1024]{1,0:T(8,128)(2,1)S(1)}, bf16[128,1024]{1,0:T(8,128)(2,1)S(1)}, u32[]{:S(2)}, u32[]{:S(2)}) collective-permute-start(bf16[128,1024]{1,0:T(8,128)(2,1)S(1)} %get-tuple-element.92), channel_id=1, source_target_pairs={{1,2},{2,1},{5,6},{6,5},{9,10},{10,9},{13,14},{14,13},{17,18},{18,... | collective-permute-start | bytes 786440 | tf_op jit(solution)/shard_map/ppermute | solution.py:494
  72.4 16.2 %collective-permute-start.14 = (bf16[128,1024]{1,0:T(8,128)(2,1)S(1)}, bf16[128,1024]{1,0:T(8,128)(2,1)S(1)}, u32[]{:S(2)}, u32[]{:S(2)}) collective-permute-start(bf16[128,1024]{1,0:T(8,128)(2,1)S(1)} %get-tuple-element.87), channel_id=1, source_target_pairs={{0,1},{1,0},{2,3},{3,2},{4,5},{5,4},{6,7},{7,6},{8,9},{9,8},{10,11... | collective-permute-start | bytes 786440 | tf_op jit(solution)/shard_map/ppermute | solution.py:494
  77.4 11.2 %collective-permute-start.15 = (bf16[128,1024]{1,0:T(8,128)(2,1)S(1)}, bf16[128,1024]{1,0:T(8,128)(2,1)S(1)}, u32[]{:S(2)}, u32[]{:S(2)}) collective-permute-start(bf16[128,1024]{1,0:T(8,128)(2,1)S(1)} %get-tuple-element.88), channel_id=1, source_target_pairs={{1,2},{2,1},{5,6},{6,5},{9,10},{10,9},{13,14},{14,13},{17,18},{18,... | collective-permute-start | bytes 786440 | tf_op jit(solution)/shard_map/ppermute | solution.py:494
  78.0 11.3 %collective-permute-start.10 = (bf16[128,1024]{1,0:T(8,128)(2,1)S(1)}, bf16[128,1024]{1,0:T(8,128)(2,1)S(1)}, u32[]{:S(2)}, u32[]{:S(2)}) collective-permute-start(bf16[128,1024]{1,0:T(8,128)(2,1)S(1)} %get-tuple-element.84), channel_id=1, source_target_pairs={{1,2},{2,1},{5,6},{6,5},{9,10},{10,9},{13,14},{14,13},{17,18},{18,... | collective-permute-start | bytes 786440 | tf_op jit(solution)/shard_map/ppermute | solution.py:494
  83.0 10.4 %collective-permute-start.9 = (bf16[128,1024]{1,0:T(8,128)(2,1)S(1)}, bf16[128,1024]{1,0:T(8,128)(2,1)S(1)}, u32[]{:S(2)}, u32[]{:S(2)}) collective-permute-start(bf16[128,1024]{1,0:T(8,128)(2,1)S(1)} %get-tuple-element.83), channel_id=1, source_target_pairs={{0,1},{1,0},{2,3},{3,2},{4,5},{5,4},{6,7},{7,6},{8,9},{9,8},{10,11... | collective-permute-start | bytes 786440 | tf_op jit(solution)/shard_map/ppermute | solution.py:494
  (4 other events, 15.5 us)
